TPU v7x, 32 devices: a whole 2x2x4 slice. The times are simulated.
32 devices in a mesh: sec: 8 (over z, x), op: 4 (over y, core).
Axes of the slice: x: 2, y: 2, z: 4, core: 2. Of those that a mesh axis runs over, the one named last changes fastest.
Arguments:
- wavefunction: bfloat16 [16, 512, 512], P('sec'), may hold values from -24 to 24
- left_blocks: bfloat16 [16, 16, 512, 512], P('op', 'sec'), may hold values from -5 to 5
- right_blocks: bfloat16 [16, 512, 512], P('op'), may hold values from -1 to 1
- charge_shifts: int32 [16], P('op'), may hold values from -2 to 2, as said below
- sector_rows: int32 [16], replicated, may hold values from 64 to 512, as said below
Outputs:
- next_vector: bfloat16 [16, 512, 512], P('sec')
- lanczos_coefficients: float32 [2, 3], replicated
Inputs may be any that keep to these rules, and one draw needn't show every extreme that they name: `charge_shifts`: some term has offset 2, some has offset -2, and some has offset 0. `sector_rows`: multiples of 64; some sector has 512 rows.
All inputs are finite; a program needn't handle non-finite values.
Results may differ from a plain program's by a relative error of at most 0.025.
Values may be sent and summed in bfloat16 or wider, within the bound.
No kernel may reach another device: no remote copies, remote signals or barrier semaphores. Data moves between devices by JAX's collectives and lax.ppermute only.
A program may use at most 64 MiB of HBM per device.

v0:
```python
import functools

import jax
import jax.numpy as jnp
from jax import lax
from jax.experimental import pallas as pl
from jax.experimental.pallas import tpu as pltpu
from jax.sharding import PartitionSpec as P

F32 = jnp.float32
BF16 = jnp.bfloat16
VMEM = pl.BlockSpec(memory_space=pltpu.VMEM)
SMEM = pl.BlockSpec(memory_space=pltpu.SMEM)


def call(kernel, name, out, scratch, *operands, flops=0):
    moved = sum(a.size * a.dtype.itemsize for a in operands)
    return pl.pallas_call(
        kernel,
        name=name,
        out_shape=out,
        in_specs=[SMEM if a.dtype == jnp.int32 else VMEM for a in operands],
        out_specs=jax.tree.map(lambda _: VMEM, out),
        scratch_shapes=scratch,
        compiler_params=pltpu.CompilerParams(vmem_limit_bytes=24 << 20),
        cost_estimate=pl.CostEstimate(flops=flops, bytes_accessed=moved, transcendentals=0),
    )(*operands)


def after(value, *others):
    return lax.optimization_barrier((value, *others))[0]


def my_core():
    return lax.axis_index("op") % 2


def half_of(which, half):
    core = my_core()
    return pl.ds(pl.multiple_of((core if which == 0 else 1 - core) * half, half), half)


def rows_of(rows_ref, target, sectors):
    return rows_ref[lax.axis_index("sec") * sectors + target]


def live_entries(rows_ref, columns):
    return sum(rows_ref[i] for i in range(rows_ref.shape[0])).astype(F32) * columns


def masked(value, first, rows):
    return jnp.where(lax.broadcasted_iota(jnp.int32, value.shape, 0) + first < rows, value, 0.0)


def inner(stats_ref, row, live):
    return jnp.sum(stats_ref[row : row + 1, :], axis=1, keepdims=True) / live


def write_sums(stats_ref, values, first=0):
    parts = [jnp.zeros((1, 128), F32)] * stats_ref.shape[0]
    for k, value in enumerate(values):
        folded = sum(value[:, i : i + 128] for i in range(0, value.shape[1], 128))
        parts[first + k] = jnp.sum(folded, axis=0, keepdims=True)
    stats_ref[...] = jnp.concatenate(parts, axis=0)


def first_scalars(start_stats, image_stats, live):
    norm = jnp.sqrt(inner(start_stats, 0, live))
    alpha = inner(image_stats, 1, live)
    beta = jnp.sqrt(jnp.maximum(inner(image_stats, 0, live) - alpha * alpha, 0.0))
    return norm, alpha, beta


def form(gram, a, b):
    return sum(a[i] * b[j] * gram[min(i, j)][max(i, j)] for i in a for j in b)


def plus(scale, *terms):
    out = {}
    for c, vector in terms:
        for i, v in vector.items():
            out[i] = out[i] + c * v if i in out else c * v
    return {i: scale * v for i, v in out.items()}


def start_kernel(rows_ref, x_ref, *refs):
    *halves, stats_ref = refs
    sectors, block_rows, _ = x_ref.shape
    square = 0.0
    for t in range(sectors):
        for which in range(2):
            part = half_of(which, block_rows // 2)
            value = x_ref[t, part, :].astype(F32)
            value = masked(value, part.start, rows_of(rows_ref, t, sectors))
            halves[2 * t + which][...] = value.astype(BF16)
            if which == 0:
                square = square + value * value
    write_sums(stats_ref, [square])


def split_kernel(left_ref, keep_ref, give_ref):
    half = keep_ref.shape[2]
    for w in range(left_ref.shape[0]):
        for t in range(left_ref.shape[1]):
            keep_ref[w, t] = left_ref[w, t, half_of(0, half), :]
            give_ref[w, t] = left_ref[w, t, half_of(1, half), :]


def gather_sources(refs, v_ref):
    half = refs[0].shape[0]
    even = lax.axis_index("sec") % 2 == 0
    pair = jnp.where(even, 2, 0)
    for k, place in enumerate((1, pair, 2 - pair)):
        for which in range(2):
            v_ref[place, half_of(which, half), :] = refs[2 * k + which][...]


def add_terms(parity, target, shifts_ref, left_ref, right_ref, v_ref, list_ref, acc_ref):
    count = jnp.int32(0)
    for w in range(shifts_ref.shape[0]):
        here = ((shifts_ref[w] + parity) & 1) == target

        @pl.when(here)
        def _():
            list_ref[count] = w

        count = count + here.astype(jnp.int32)

    def product(position):
        w = list_ref[position]
        source = v_ref[((target - shifts_ref[w]) >> 1) + 1]
        part = jnp.dot(left_ref[w, target], source, preferred_element_type=F32).astype(BF16)
        return jnp.dot(part, right_ref[w], preferred_element_type=F32)

    def two(k, carry):
        acc_ref[...] += product(2 * k) + product(2 * k + 1)
        return carry

    lax.fori_loop(0, count >> 1, two, 0)

    @pl.when(count & 1 == 1)
    def _():
        acc_ref[...] += product(count - 1)


def first_kernel(shifts_ref, left_ref, right_ref, *refs):
    *sources, acc_ref, v_ref, list_ref = refs
    gather_sources(sources, v_ref)
    for target in range(acc_ref.shape[0]):
        acc_ref[target] = jnp.zeros(acc_ref.shape[1:], F32)
        add_terms(
            0, target, shifts_ref, left_ref, right_ref, v_ref, list_ref, acc_ref.at[target]
        )


def second_kernel(target, shifts_ref, left_ref, right_ref, *refs):
    *sources, sum_ref, out_ref, v_ref, list_ref, acc_ref = refs
    gather_sources(sources, v_ref)
    acc_ref[...] = sum_ref[target]
    add_terms(1, target, shifts_ref, left_ref, right_ref, v_ref, list_ref, acc_ref)
    out_ref[...] = acc_ref[...].astype(BF16)


def add_kernel(a_ref, b_ref, out_ref):
    out_ref[...] = (a_ref[...].astype(F32) + b_ref[...].astype(F32)).astype(BF16)


def image_kernel(product, target, sectors, rows_ref, a_ref, b_ref, *refs):
    basis = [r[...].astype(F32) for r in refs[: product + 1]]
    *stats, out_ref, stats_ref = refs[product + 1 :]
    half, columns = out_ref.shape
    live = live_entries(rows_ref, columns)
    value = a_ref[...].astype(F32) + b_ref[...].astype(F32)
    if product == 0:
        scale = 1.0 / jnp.sqrt(inner(stats[0], 0, live))
        value = value * scale
        others = [basis[0] * scale]
    else:
        norm, alpha, beta = first_scalars(*stats, live)
        zeroth = basis[0] * (1.0 / norm)
        scale = 1.0 / beta
        first = (basis[1] - alpha * zeroth) * scale
        if product == 1:
            value = value - alpha * basis[1]
            others = [first, zeroth]
        else:
            others = [basis[2], first, zeroth]
        value = value * scale
    value = masked(value, my_core() * half, rows_of(rows_ref, target, sectors)).astype(BF16)
    out_ref[...] = value
    value = value.astype(F32)
    write_sums(stats_ref, [value * v for v in [value] + others], 3 if product == 2 else 0)


def last_kernel(rows_ref, *refs):
    out_ref, coef_ref = refs[-2:]
    start_stats, image_stats, last_stats = refs[-5:-2]
    sectors, block_rows, columns = out_ref.shape
    live = live_entries(rows_ref, columns)
    norm, alpha0, beta0 = first_scalars(start_stats, image_stats, live)
    one, none = jnp.ones_like(norm), jnp.zeros_like(norm)
    w11, w1q1, w1q0, zz, zw1, zq1, zq0 = (inner(last_stats, k, live) for k in range(7))
    gram = [[one, none, w1q0, zq0], [None, one, w1q1, zq1], [None, None, w11, zw1], [None] * 3 + [zz]]
    q0, q1, w1 = {0: one}, {1: one}, {2: one}
    alpha1 = w1q1
    r1 = plus(one, (one, w1), (-alpha1, q1), (-beta0, q0))
    beta1 = jnp.sqrt(jnp.maximum(form(gram, r1, r1), 0.0))
    q2 = plus(1.0 / beta1, (one, r1))
    w0 = {0: alpha0, 1: beta0}
    w2 = plus(1.0 / beta1, (beta0, {3: one}), (-alpha1, w1), (-beta0, w0))
    alpha2 = form(gram, q2, w2)
    r2 = plus(one, (one, w2), (-alpha2, q2), (-beta1, q1))
    beta2 = jnp.sqrt(jnp.maximum(form(gram, r2, r2), 0.0))
    q3 = plus(1.0 / beta2, (one, r2))
    c1 = q3[1] / beta0
    coefs = [(q3[0] - alpha0 * c1) / norm, c1, q3[2], q3[3]]
    for t in range(sectors):
        for which in range(2):
            blocks = [refs[8 * t + 2 * k + which][...].astype(F32) for k in range(4)]
            vector = sum(c * block for c, block in zip(coefs, blocks))
            out_ref[t, half_of(which, block_rows // 2), :] = vector.astype(BF16)
    row = lax.broadcasted_iota(jnp.int32, coef_ref.shape, 0)
    column = lax.broadcasted_iota(jnp.int32, coef_ref.shape, 1)
    value = jnp.zeros(coef_ref.shape, F32)
    for k, (alpha, beta) in enumerate(((alpha0, beta0), (alpha1, beta1), (alpha2, beta2))):
        value = jnp.where((row == 0) & (column == k), alpha, value)
        value = jnp.where((row == 1) & (column == k), beta, value)
    coef_ref[...] = value


def on_device(wavefunction, left_blocks, right_blocks, charge_shifts, sector_rows):
    sectors, block_rows, columns = wavefunction.shape
    half = block_rows // 2
    n_sec, n_op = lax.axis_size("sec"), lax.axis_size("op")
    assert sectors == 2 and n_sec % 2 == 0 and n_op % 4 == 0
    core_pairs = [(i, i ^ 1) for i in range(n_op)]
    pairs = [(i, i ^ 1) for i in range(n_sec)]
    onward = [(i, i + 2) for i in range(0, n_sec - 2, 2)]
    onward += [(i, i - 2) for i in range(3, n_sec, 2)]

    def across_cores(value):
        return lax.ppermute(value, "op", core_pairs)

    def sum_steps(stats):
        stats = stats + across_cores(stats)
        steps = []
        bit = 1
        while bit < n_sec:
            flips = [bit] if bit == 1 or 2 * bit >= n_sec else [bit, 2 * bit, 3 * bit]
            arrived = [
                lax.ppermute(stats, "sec", [(i, i ^ f) for i in range(n_sec)]) for f in flips
            ]
            if len(arrived) == 1:
                stats = stats + arrived[0]
            else:
                stats = (stats + arrived[0]) + (arrived[1] + arrived[2])
            steps.append(stats)
            bit <<= len(flips) - len(flips) // 2
        return steps

    half_type = jax.ShapeDtypeStruct((half, columns), BF16)
    stats_type = jax.ShapeDtypeStruct((8, 128), F32)
    acc_type = jax.ShapeDtypeStruct((sectors, half, columns), F32)
    terms = 2 * left_blocks.shape[0]
    term_scratch = [pltpu.VMEM((3, block_rows, columns), BF16), pltpu.SMEM((terms,), jnp.int32)]
    acc_scratch = pltpu.VMEM((half, columns), F32)

    *halves, sums = call(
        start_kernel, "start", [half_type] * (2 * sectors) + [stats_type], [],
        sector_rows, wavefunction,
    )
    basis = [[(halves[0], halves[1]), (halves[2], halves[3])]]
    half_left = jax.ShapeDtypeStruct((terms // 2, sectors, half, block_rows), BF16)
    keep, give = call(split_kernel, "split", [half_left] * 2, [], left_blocks)
    operators = [
        jnp.concatenate([mine, other])
        for mine, other in (
            (charge_shifts, across_cores(charge_shifts)),
            (keep, across_cores(give)),
            (right_blocks, across_cores(right_blocks)),
        )
    ]
    stats = []
    pair_flops = 2 * half * columns * (block_rows + columns)

    for product in range(3):
        (mine_0, other_0), (mine_1, other_1) = basis[-1]
        pair_0 = lax.ppermute(mine_0, "sec", pairs)
        pair_1 = lax.ppermute(mine_1, "sec", pairs)
        far_0 = lax.ppermute(pair_0, "sec", onward)
        far_1 = lax.ppermute(pair_1, "sec", onward)
        if product < 2:
            steps = sum_steps(after(sums, pair_1))
            stats.append(steps[-1])
        acc = call(
            first_kernel, "first", acc_type, term_scratch, *operators,
            mine_0, other_0, pair_0, across_cores(pair_0), far_0, across_cores(far_0),
            flops=terms * pair_flops,
        )
        far_1 = after(far_1, acc, steps[0]) if product < 2 else after(far_1, acc)
        sources = (mine_1, other_1, pair_1, across_cores(pair_1), far_1, across_cores(far_1))
        image = []
        parts = []
        for t in range(sectors):
            value = call(
                functools.partial(second_kernel, t), "second", half_type,
                term_scratch + [acc_scratch], *operators, *sources, acc,
                flops=terms * pair_flops // 2,
            )
            bit = 2
            while 2 * bit < n_op:
                arrived = lax.ppermute(value, "op", [(i, i ^ bit) for i in range(n_op)])
                value = call(add_kernel, "add", half_type, [], value, arrived)
                bit *= 2
            arrived = lax.ppermute(value, "op", [(i, i ^ bit) for i in range(n_op)])
            mine, part = call(
                functools.partial(image_kernel, product, t, sectors), "image",
                [half_type, stats_type], [], sector_rows,
                value, arrived, *[b[t][0] for b in basis], *stats,
            )
            image.append((mine, across_cores(mine)))
            parts.append(part)
        basis.append(image)
        if product < 2:
            sums = parts[0] + parts[1]
        else:
            sums = sums + (parts[0] + parts[1])
    stats.append(sum_steps(sums)[-1])

    flat = [h for t in range(sectors) for b in basis for h in b[t]]
    vector_type = jax.ShapeDtypeStruct(wavefunction.shape, BF16)
    coef_type = jax.ShapeDtypeStruct((2, 3), F32)
    vector, coef = call(
        last_kernel, "last", [vector_type, coef_type], [], sector_rows, *flat, *stats
    )
    return vector, coef


def solution(mesh):
    in_specs = (P("sec", None, None), P("op", "sec", None, None), P("op", None, None), P("op"), P())
    out_specs = (P("sec", None, None), P())
    return jax.shard_map(
        on_device, mesh=mesh, in_specs=in_specs, out_specs=out_specs, check_vma=False
    )
```

profile of v0, /device:TPU:0, one launch (start us, length us, event | category | flops | bytes accessed | tf_op | source)
XLA Modules:
  0.0 156.4 jit_solution(10721992063842469539)
XLA Ops:
  5.7 2.8 %collective-permute-start.3 = (bf16[256,512]{1,0:T(8,128)(2,1)S(1)}, bf16[256,512]{1,0:T(8,128)(2,1)S(1)}, u32[]{:S(2)}, u32[]{:S(2)}) collective-permute-start(bf16[256,512]{1,0:T(8,128)(2,1)S(1)} %get-tuple-element.30.refs_0_.refs_8_), channel_id=1, source_target_pairs={{0,4},{4,0},{8,12},{12,8},{16,20},{20,16},{24,28},{28,24},{1,5},{5... | collective-permute-start | bytes 786440 | tf_op jit(solution)/shard_map/ppermute | solution.py:289
  8.8 6.9 %collective-permute-done.3.refs_2_ = bf16[256,512]{1,0:T(8,128)(2,1)S(1)} collective-permute-done((bf16[256,512]{1,0:T(8,128)(2,1)S(1)}, bf16[256,512]{1,0:T(8,128)(2,1)S(1)}, u32[]{:S(2)}, u32[]{:S(2)}) %collective-permute-start.3) | collective-permute-done | bytes 262176 | tf_op jit(solution)/shard_map/ppermute | solution.py:289
  15.6 5.3 %collective-permute-done.6.refs_2_ = bf16[256,512]{1,0:T(8,128)(2,1)S(1)} collective-permute-done((bf16[256,512]{1,0:T(8,128)(2,1)S(1)}, bf16[256,512]{1,0:T(8,128)(2,1)S(1)}, u32[]{:S(2)}, u32[]{:S(2)}) %collective-permute-start.6) | collective-permute-done | bytes 262176 | tf_op jit(solution)/shard_map/ppermute | solution.py:288
  20.9 3.7 %collective-permute-start.8 = (bf16[256,512]{1,0:T(8,128)(2,1)S(1)}, bf16[256,512]{1,0:T(8,128)(2,1)S(1)}, u32[]{:S(2)}, u32[]{:S(2)}) collective-permute-start(bf16[256,512]{1,0:T(8,128)(2,1)S(1)} %collective-permute-done.6.refs_2_), channel_id=1, source_target_pairs={{0,8},{8,16},{16,24},{12,4},{20,12},{28,20},{1,9},{9,17},{17,25},{... | collective-permute-start | bytes 786440 | tf_op jit(solution)/shard_map/ppermute | solution.py:290
  25.0 3.5 %collective-permute-done.11 = f32[8,128]{1,0:T(8,128)S(1)} collective-permute-done((f32[8,128]{1,0:T(8,128)S(1)}, f32[8,128]{1,0:T(8,128)S(1)}, u32[]{:S(2)}, u32[]{:S(2)}) %collective-permute-start.11) | collective-permute-done | bytes 4128 | tf_op jit(solution)/shard_map/ppermute | solution.py:251
  28.4 3.5 %collective-permute-start.5 = (bf16[256,512]{1,0:T(8,128)(2,1)S(1)}, bf16[256,512]{1,0:T(8,128)(2,1)S(1)}, u32[]{:S(2)}, u32[]{:S(2)}) collective-permute-start(bf16[256,512]{1,0:T(8,128)(2,1)S(1)} %collective-permute-done.3.refs_2_), channel_id=1, source_target_pairs={{0,8},{8,16},{16,24},{12,4},{20,12},{28,20},{1,9},{9,17},{17,25},{... | collective-permute-start | bytes 786440 | tf_op jit(solution)/shard_map/ppermute | solution.py:291
  33.9 3.9 %first.3.refs_6_ = f32[2,256,512]{2,1,0:T(8,128)S(1)} custom-call(s32[8]{0:T(128)S(1)} %pad_add_fusion.shifts_ref, bf16[8,2,256,512]{3,2,1,0:T(8,128)(2,1)S(1)} %constant_dynamic-update-slice_fusion.left_ref, bf16[8,512,512]{2,1,0:T(8,128)(2,1)S(1)} %constant_dynamic-update-slice_fusion.2.right_ref, bf16[256,512]{1,0:T(8,128)(2,1)S(1)} %get-tuple-element.26.refs_0_, ...), custom_call_target="tpu_custom_call" | custom-call | flops 2147483648 | bytes 9961504 | tf_op jit(solution)/shard_map/first/pallas_call | solution.py:18
  52.5 3.1 %second.7.a_ref = bf16[256,512]{1,0:T(8,128)(2,1)S(1)} custom-call(s32[8]{0:T(128)S(1)} %pad_add_fusion.shifts_ref, bf16[8,2,256,512]{3,2,1,0:T(8,128)(2,1)S(1)} %constant_dynamic-update-slice_fusion.left_ref, bf16[8,512,512]{2,1,0:T(8,128)(2,1)S(1)} %constant_dynamic-update-slice_fusion.2.right_ref, bf16[256,512]{1,0:T(8,128)(2,1)S(1)} %get-tuple-element.30.refs_0_.refs_8_, ...), custom_call_target="tpu_custom_call" | custom-call | flops 1073741824 | bytes 11010080 | tf_op jit(solution)/shard_map/second/pallas_call | solution.py:18
  55.7 2.9 %collective-permute-done.23.refs_2_ = bf16[256,512]{1,0:T(8,128)(2,1)S(1)} collective-permute-done((bf16[256,512]{1,0:T(8,128)(2,1)S(1)}, bf16[256,512]{1,0:T(8,128)(2,1)S(1)}, u32[]{:S(2)}, u32[]{:S(2)}) %collective-permute-start.23) | collective-permute-done | bytes 262176 | tf_op jit(solution)/shard_map/ppermute | solution.py:288
  58.7 3.5 %collective-permute-start.25 = (bf16[256,512]{1,0:T(8,128)(2,1)S(1)}, bf16[256,512]{1,0:T(8,128)(2,1)S(1)}, u32[]{:S(2)}, u32[]{:S(2)}) collective-permute-start(bf16[256,512]{1,0:T(8,128)(2,1)S(1)} %collective-permute-done.23.refs_2_), channel_id=1, source_target_pairs={{0,8},{8,16},{16,24},{12,4},{20,12},{28,20},{1,9},{9,17},{17,25},{... | collective-permute-start | bytes 786440 | tf_op jit(solution)/shard_map/ppermute | solution.py:290
  66.6 3.2 %collective-permute-done.20.refs_2_ = bf16[256,512]{1,0:T(8,128)(2,1)S(1)} collective-permute-done((bf16[256,512]{1,0:T(8,128)(2,1)S(1)}, bf16[256,512]{1,0:T(8,128)(2,1)S(1)}, u32[]{:S(2)}, u32[]{:S(2)}) %collective-permute-start.20) | collective-permute-done | bytes 262176 | tf_op jit(solution)/shard_map/ppermute | solution.py:289
  69.8 3.2 %collective-permute-start.22 = (bf16[256,512]{1,0:T(8,128)(2,1)S(1)}, bf16[256,512]{1,0:T(8,128)(2,1)S(1)}, u32[]{:S(2)}, u32[]{:S(2)}) collective-permute-start(bf16[256,512]{1,0:T(8,128)(2,1)S(1)} %collective-permute-done.20.refs_2_), channel_id=1, source_target_pairs={{0,8},{8,16},{16,24},{12,4},{20,12},{28,20},{1,9},{9,17},{17,25},{... | collective-permute-start | bytes 786440 | tf_op jit(solution)/shard_map/ppermute | solution.py:291
  74.2 3.6 %collective-permute-done.28 = f32[8,128]{1,0:T(8,128)S(1)} collective-permute-done((f32[8,128]{1,0:T(8,128)S(1)}, f32[8,128]{1,0:T(8,128)S(1)}, u32[]{:S(2)}, u32[]{:S(2)}) %collective-permute-start.28) | collective-permute-done | bytes 4128 | tf_op jit(solution)/shard_map/ppermute | solution.py:251
  78.3 3.9 %first.4.refs_6_ = f32[2,256,512]{2,1,0:T(8,128)S(1)} custom-call(s32[8]{0:T(128)S(1)} %pad_add_fusion.shifts_ref, bf16[8,2,256,512]{3,2,1,0:T(8,128)(2,1)S(1)} %constant_dynamic-update-slice_fusion.left_ref, bf16[8,512,512]{2,1,0:T(8,128)(2,1)S(1)} %constant_dynamic-update-slice_fusion.2.right_ref, ...), custom_call_target="tpu_custom_call" | custom-call | flops 2147483648 | bytes 9961504 | tf_op jit(solution)/shard_map/first/pallas_call | solution.py:18
  96.7 3.3 %second.9.a_ref = bf16[256,512]{1,0:T(8,128)(2,1)S(1)} custom-call(s32[8]{0:T(128)S(1)} %pad_add_fusion.shifts_ref, bf16[8,2,256,512]{3,2,1,0:T(8,128)(2,1)S(1)} %constant_dynamic-update-slice_fusion.left_ref, bf16[8,512,512]{2,1,0:T(8,128)(2,1)S(1)} %constant_dynamic-update-slice_fusion.2.right_ref, ...), custom_call_target="tpu_custom_call" | custom-call | flops 1073741824 | bytes 11010080 | tf_op jit(solution)/shard_map/second/pallas_call | solution.py:18
  102.4 3.4 %collective-permute-start.42 = (bf16[256,512]{1,0:T(8,128)(2,1)S(1)}, bf16[256,512]{1,0:T(8,128)(2,1)S(1)}, u32[]{:S(2)}, u32[]{:S(2)}) collective-permute-start(bf16[256,512]{1,0:T(8,128)(2,1)S(1)} %collective-permute-done.40.refs_2_), channel_id=1, source_target_pairs={{0,8},{8,16},{16,24},{12,4},{20,12},{28,20},{1,9},{9,17},{17,25},{... | collective-permute-start | bytes 786440 | tf_op jit(solution)/shard_map/ppermute | solution.py:290
  109.9 4.0 %collective-permute-done.37.refs_2_ = bf16[256,512]{1,0:T(8,128)(2,1)S(1)} collective-permute-done((bf16[256,512]{1,0:T(8,128)(2,1)S(1)}, bf16[256,512]{1,0:T(8,128)(2,1)S(1)}, u32[]{:S(2)}, u32[]{:S(2)}) %collective-permute-start.37) | collective-permute-done | bytes 262176 | tf_op jit(solution)/shard_map/ppermute | solution.py:289
  113.9 3.2 %collective-permute-start.39 = (bf16[256,512]{1,0:T(8,128)(2,1)S(1)}, bf16[256,512]{1,0:T(8,128)(2,1)S(1)}, u32[]{:S(2)}, u32[]{:S(2)}) collective-permute-start(bf16[256,512]{1,0:T(8,128)(2,1)S(1)} %collective-permute-done.37.refs_2_), channel_id=1, source_target_pairs={{0,8},{8,16},{16,24},{12,4},{20,12},{28,20},{1,9},{9,17},{17,25},{... | collective-permute-start | bytes 786440 | tf_op jit(solution)/shard_map/ppermute | solution.py:291
  117.7 3.9 %first.5.refs_6_ = f32[2,256,512]{2,1,0:T(8,128)S(1)} custom-call(s32[8]{0:T(128)S(1)} %pad_add_fusion.shifts_ref, bf16[8,2,256,512]{3,2,1,0:T(8,128)(2,1)S(1)} %constant_dynamic-update-slice_fusion.left_ref, bf16[8,512,512]{2,1,0:T(8,128)(2,1)S(1)} %constant_dynamic-update-slice_fusion.2.right_ref, ...), custom_call_target="tpu_custom_call" | custom-call | flops 2147483648 | bytes 9961504 | tf_op jit(solution)/shard_map/first/pallas_call | solution.py:18
  126.8 3.1 %second.11.a_ref = bf16[256,512]{1,0:T(8,128)(2,1)S(1)} custom-call(s32[8]{0:T(128)S(1)} %pad_add_fusion.shifts_ref, bf16[8,2,256,512]{3,2,1,0:T(8,128)(2,1)S(1)} %constant_dynamic-update-slice_fusion.left_ref, bf16[8,512,512]{2,1,0:T(8,128)(2,1)S(1)} %constant_dynamic-update-slice_fusion.2.right_ref, ...), custom_call_target="tpu_custom_call" | custom-call | flops 1073741824 | bytes 11010080 | tf_op jit(solution)/shard_map/second/pallas_call | solution.py:18
  129.9 4.0 %collective-permute-done.45.b_ref = bf16[256,512]{1,0:T(8,128)(2,1)S(1)} collective-permute-done((bf16[256,512]{1,0:T(8,128)(2,1)S(1)}, bf16[256,512]{1,0:T(8,128)(2,1)S(1)}, u32[]{:S(2)}, u32[]{:S(2)}) %collective-permute-start.45) | collective-permute-done | bytes 262176 | tf_op jit(solution)/shard_map/ppermute | solution.py:315
  135.1 3.9 %collective-permute-done.47.b_ref = bf16[256,512]{1,0:T(8,128)(2,1)S(1)} collective-permute-done((bf16[256,512]{1,0:T(8,128)(2,1)S(1)}, bf16[256,512]{1,0:T(8,128)(2,1)S(1)}, u32[]{:S(2)}, u32[]{:S(2)}) %collective-permute-start.47) | collective-permute-done | bytes 262176 | tf_op jit(solution)/shard_map/ppermute | solution.py:315
  149.7 3.4 %collective-permute-done.53 = f32[8,128]{1,0:T(8,128)S(1)} collective-permute-done((f32[8,128]{1,0:T(8,128)S(1)}, f32[8,128]{1,0:T(8,128)S(1)}, u32[]{:S(2)}, u32[]{:S(2)}) %collective-permute-start.53) | collective-permute-done | bytes 4128 | tf_op jit(solution)/shard_map/ppermute | solution.py:251
  153.2 3.2 %last.1 = (bf16[2,512,512]{2,1,0:T(8,128)(2,1)}, f32[2,3]{1,0:T(2,128)}) custom-call(s32[16]{0:T(128)S(1)} %copy-done.2, bf16[256,512]{1,0:T(8,128)(2,1)S(1)} %get-tuple-element.26.refs_0_, bf16[256,512]{1,0:T(8,128)(2,1)S(1)} %get-tuple-element.27.refs_1_, bf16[256,512]{1,0:T(8,128)(2,1)S(1)} %get-tuple-element.35.refs_0_.refs_1_.refs_2_, ...), custom_call_target="tpu_custom_call" | custom-call | bytes 4206656 | tf_op jit(solution)/shard_map/last/pallas_call | solution.py:18
  (128 shorter events, 66.9 us)
Async XLA Ops:
  3.1 28.9 %collective-permute-start.1 = (bf16[4,2,256,512]{3,2,1,0:T(8,128)(2,1)S(1)}, bf16[4,2,256,512]{3,2,1,0:T(8,128)(2,1)S(1)}, u32[]{:S(2)}, u32[]{:S(2)}) collective-permute-start(bf16[4,2,256,512]{3,2,1,0:T(8,128)(2,1)S(1)} %get-tuple-element.29), channel_id=1, source_target_pairs={{0,1},{1,0},{2,3},{3,2},{4,5},{5,4},{6,7},{7,6},{8,9},{9,8},{10,11... | collective-permute-start | bytes 6291464 | tf_op jit(solution)/shard_map/ppermute | solution.py:242
  4.4 28.3 %collective-permute-start.2 = (bf16[4,512,512]{2,1,0:T(8,128)(2,1)S(1)}, bf16[4,512,512]{2,1,0:T(8,128)(2,1)S(1)}, u32[]{:S(2)}, u32[]{:S(2)}) collective-permute-start(bf16[4,512,512]{2,1,0:T(8,128)(2,1)S(1)} %copy-done.3), channel_id=1, source_target_pairs={{0,1},{1,0},{2,3},{3,2},{4,5},{5,4},{6,7},{7,6},{8,9},{9,8},{10,11... | collective-permute-start | bytes 6291464 | tf_op jit(solution)/shard_map/ppermute | solution.py:242
  5.7 9.9 %collective-permute-start.3 = (bf16[256,512]{1,0:T(8,128)(2,1)S(1)}, bf16[256,512]{1,0:T(8,128)(2,1)S(1)}, u32[]{:S(2)}, u32[]{:S(2)}) collective-permute-start(bf16[256,512]{1,0:T(8,128)(2,1)S(1)} %get-tuple-element.30.refs_0_.refs_8_), channel_id=1, source_target_pairs={{0,4},{4,0},{8,12},{12,8},{16,20},{20,16},{24,28},{28,24},{1,5},{5... | collective-permute-start | bytes 786440 | tf_op jit(solution)/shard_map/ppermute | solution.py:289
  8.5 12.3 %collective-permute-start.6 = (bf16[256,512]{1,0:T(8,128)(2,1)S(1)}, bf16[256,512]{1,0:T(8,128)(2,1)S(1)}, u32[]{:S(2)}, u32[]{:S(2)}) collective-permute-start(bf16[256,512]{1,0:T(8,128)(2,1)S(1)} %get-tuple-element.26.refs_0_), channel_id=1, source_target_pairs={{0,4},{4,0},{8,12},{12,8},{16,20},{20,16},{24,28},{28,24},{1,5},{5... | collective-permute-start | bytes 786440 | tf_op jit(solution)/shard_map/ppermute | solution.py:288
  8.6 16.2 %collective-permute-start = (s32[4]{0:T(128)S(1)}, s32[4]{0:T(128)S(1)}, u32[]{:S(2)}, u32[]{:S(2)}) collective-permute-start(s32[4]{0:T(128)S(1)} %copy-done.4), channel_id=1, source_target_pairs={{0,1},{1,0},{2,3},{3,2},{4,5},{5,4},{6,7},{7,6},{8,9},{9,8},{10,11... | collective-permute-start | bytes 56 | tf_op jit(solution)/shard_map/ppermute | solution.py:242
  15.6 9.2 %collective-permute-start.10 = (f32[8,128]{1,0:T(8,128)S(1)}, f32[8,128]{1,0:T(8,128)S(1)}, u32[]{:S(2)}, u32[]{:S(2)}) collective-permute-start(f32[8,128]{1,0:T(8,128)S(1)} %get-tuple-element.33), channel_id=1, source_target_pairs={{0,1},{1,0},{2,3},{3,2},{4,5},{5,4},{6,7},{7,6},{8,9},{9,8},{10,11... | collective-permute-start | bytes 12296 | tf_op jit(solution)/shard_map/ppermute | solution.py:242
  20.9 11.1 %collective-permute-start.8 = (bf16[256,512]{1,0:T(8,128)(2,1)S(1)}, bf16[256,512]{1,0:T(8,128)(2,1)S(1)}, u32[]{:S(2)}, u32[]{:S(2)}) collective-permute-start(bf16[256,512]{1,0:T(8,128)(2,1)S(1)} %collective-permute-done.6.refs_2_), channel_id=1, source_target_pairs={{0,8},{8,16},{16,24},{12,4},{20,12},{28,20},{1,9},{9,17},{17,25},{... | collective-permute-start | bytes 786440 | tf_op jit(solution)/shard_map/ppermute | solution.py:290
  24.9 13.1 %collective-permute-start.4 = (bf16[256,512]{1,0:T(8,128)(2,1)S(1)}, bf16[256,512]{1,0:T(8,128)(2,1)S(1)}, u32[]{:S(2)}, u32[]{:S(2)}) collective-permute-start(bf16[256,512]{1,0:T(8,128)(2,1)S(1)} %collective-permute-done.3.refs_2_), channel_id=1, source_target_pairs={{0,1},{1,0},{2,3},{3,2},{4,5},{5,4},{6,7},{7,6},{8,9},{9,8},{10,11... | collective-permute-start | bytes 786440 | tf_op jit(solution)/shard_map/ppermute | solution.py:242
  28.4 9.4 %collective-permute-start.5 = (bf16[256,512]{1,0:T(8,128)(2,1)S(1)}, bf16[256,512]{1,0:T(8,128)(2,1)S(1)}, u32[]{:S(2)}, u32[]{:S(2)}) collective-permute-start(bf16[256,512]{1,0:T(8,128)(2,1)S(1)} %collective-permute-done.3.refs_2_), channel_id=1, source_target_pairs={{0,8},{8,16},{16,24},{12,4},{20,12},{28,20},{1,9},{9,17},{17,25},{... | collective-permute-start | bytes 786440 | tf_op jit(solution)/shard_map/ppermute | solution.py:291
  41.0 9.9 %collective-permute-start.13 = (bf16[256,512]{1,0:T(8,128)(2,1)S(1)}, bf16[256,512]{1,0:T(8,128)(2,1)S(1)}, u32[]{:S(2)}, u32[]{:S(2)}) collective-permute-start(bf16[256,512]{1,0:T(8,128)(2,1)S(1)} %second.6.a_ref), channel_id=1, source_target_pairs={{0,2},{1,3},{2,0},{3,1},{4,6},{5,7},{6,4},{7,5},{8,10},{9,11},{10,... | collective-permute-start | bytes 786440 | tf_op jit(solution)/shard_map/ppermute | solution.py:315
  58.7 7.9 %collective-permute-start.25 = (bf16[256,512]{1,0:T(8,128)(2,1)S(1)}, bf16[256,512]{1,0:T(8,128)(2,1)S(1)}, u32[]{:S(2)}, u32[]{:S(2)}) collective-permute-start(bf16[256,512]{1,0:T(8,128)(2,1)S(1)} %collective-permute-done.23.refs_2_), channel_id=1, source_target_pairs={{0,8},{8,16},{16,24},{12,4},{20,12},{28,20},{1,9},{9,17},{17,25},{... | collective-permute-start | bytes 786440 | tf_op jit(solution)/shard_map/ppermute | solution.py:290
  64.5 13.3 %collective-permute-start.17 = (bf16[256,512]{1,0:T(8,128)(2,1)S(1)}, bf16[256,512]{1,0:T(8,128)(2,1)S(1)}, u32[]{:S(2)}, u32[]{:S(2)}) collective-permute-start(bf16[256,512]{1,0:T(8,128)(2,1)S(1)} %get-tuple-element.35.refs_0_.refs_1_.refs_2_), channel_id=1, source_target_pairs={{0,1},{1,0},{2,3},{3,2},{4,5},{5,4},{6,7},{7,6},{8,9},{9,8},{10,11... | collective-permute-start | bytes 786440 | tf_op jit(solution)/shard_map/ppermute | solution.py:242
  64.5 13.8 %collective-permute-start.24 = (bf16[256,512]{1,0:T(8,128)(2,1)S(1)}, bf16[256,512]{1,0:T(8,128)(2,1)S(1)}, u32[]{:S(2)}, u32[]{:S(2)}) collective-permute-start(bf16[256,512]{1,0:T(8,128)(2,1)S(1)} %collective-permute-done.23.refs_2_), channel_id=1, source_target_pairs={{0,1},{1,0},{2,3},{3,2},{4,5},{5,4},{6,7},{7,6},{8,9},{9,8},{10,11... | collective-permute-start | bytes 786440 | tf_op jit(solution)/shard_map/ppermute | solution.py:242
  66.6 11.7 %collective-permute-start.26 = (bf16[256,512]{1,0:T(8,128)(2,1)S(1)}, bf16[256,512]{1,0:T(8,128)(2,1)S(1)}, u32[]{:S(2)}, u32[]{:S(2)}) collective-permute-start(bf16[256,512]{1,0:T(8,128)(2,1)S(1)} %collective-permute-done.25.refs_4_), channel_id=1, source_target_pairs={{0,1},{1,0},{2,3},{3,2},{4,5},{5,4},{6,7},{7,6},{8,9},{9,8},{10,11... | collective-permute-start | bytes 786440 | tf_op jit(solution)/shard_map/ppermute | solution.py:242
  69.8 12.5 %collective-permute-start.22 = (bf16[256,512]{1,0:T(8,128)(2,1)S(1)}, bf16[256,512]{1,0:T(8,128)(2,1)S(1)}, u32[]{:S(2)}, u32[]{:S(2)}) collective-permute-start(bf16[256,512]{1,0:T(8,128)(2,1)S(1)} %collective-permute-done.20.refs_2_), channel_id=1, source_target_pairs={{0,8},{8,16},{16,24},{12,4},{20,12},{28,20},{1,9},{9,17},{17,25},{... | collective-permute-start | bytes 786440 | tf_op jit(solution)/shard_map/ppermute | solution.py:291
  85.4 9.2 %collective-permute-start.30 = (bf16[256,512]{1,0:T(8,128)(2,1)S(1)}, bf16[256,512]{1,0:T(8,128)(2,1)S(1)}, u32[]{:S(2)}, u32[]{:S(2)}) collective-permute-start(bf16[256,512]{1,0:T(8,128)(2,1)S(1)} %second.8.a_ref), channel_id=1, source_target_pairs={{0,2},{1,3},{2,0},{3,1},{4,6},{5,7},{6,4},{7,5},{8,10},{9,11},{10,... | collective-permute-start | bytes 786440 | tf_op jit(solution)/shard_map/ppermute | solution.py:315
  108.5 8.7 %collective-permute-start.34 = (bf16[256,512]{1,0:T(8,128)(2,1)S(1)}, bf16[256,512]{1,0:T(8,128)(2,1)S(1)}, u32[]{:S(2)}, u32[]{:S(2)}) collective-permute-start(bf16[256,512]{1,0:T(8,128)(2,1)S(1)} %get-tuple-element.41.refs_0_.refs_2_.refs_4_), channel_id=1, source_target_pairs={{0,1},{1,0},{2,3},{3,2},{4,5},{5,4},{6,7},{7,6},{8,9},{9,8},{10,11... | collective-permute-start | bytes 786440 | tf_op jit(solution)/shard_map/ppermute | solution.py:242
  108.5 9.2 %collective-permute-start.41 = (bf16[256,512]{1,0:T(8,128)(2,1)S(1)}, bf16[256,512]{1,0:T(8,128)(2,1)S(1)}, u32[]{:S(2)}, u32[]{:S(2)}) collective-permute-start(bf16[256,512]{1,0:T(8,128)(2,1)S(1)} %collective-permute-done.40.refs_2_), channel_id=1, source_target_pairs={{0,1},{1,0},{2,3},{3,2},{4,5},{5,4},{6,7},{7,6},{8,9},{9,8},{10,11... | collective-permute-start | bytes 786440 | tf_op jit(solution)/shard_map/ppermute | solution.py:242
  109.8 7.9 %collective-permute-start.43 = (bf16[256,512]{1,0:T(8,128)(2,1)S(1)}, bf16[256,512]{1,0:T(8,128)(2,1)S(1)}, u32[]{:S(2)}, u32[]{:S(2)}) collective-permute-start(bf16[256,512]{1,0:T(8,128)(2,1)S(1)} %collective-permute-done.42.refs_4_), channel_id=1, source_target_pairs={{0,1},{1,0},{2,3},{3,2},{4,5},{5,4},{6,7},{7,6},{8,9},{9,8},{10,11... | collective-permute-start | bytes 786440 | tf_op jit(solution)/shard_map/ppermute | solution.py:242
  113.9 7.8 %collective-permute-start.39 = (bf16[256,512]{1,0:T(8,128)(2,1)S(1)}, bf16[256,512]{1,0:T(8,128)(2,1)S(1)}, u32[]{:S(2)}, u32[]{:S(2)}) collective-permute-start(bf16[256,512]{1,0:T(8,128)(2,1)S(1)} %collective-permute-done.37.refs_2_), channel_id=1, source_target_pairs={{0,8},{8,16},{16,24},{12,4},{20,12},{28,20},{1,9},{9,17},{17,25},{... | collective-permute-start | bytes 786440 | tf_op jit(solution)/shard_map/ppermute | solution.py:291
  124.8 9.2 %collective-permute-start.45 = (bf16[256,512]{1,0:T(8,128)(2,1)S(1)}, bf16[256,512]{1,0:T(8,128)(2,1)S(1)}, u32[]{:S(2)}, u32[]{:S(2)}) collective-permute-start(bf16[256,512]{1,0:T(8,128)(2,1)S(1)} %second.10.a_ref), channel_id=1, source_target_pairs={{0,2},{1,3},{2,0},{3,1},{4,6},{5,7},{6,4},{7,5},{8,10},{9,11},{10,... | collective-permute-start | bytes 786440 | tf_op jit(solution)/shard_map/ppermute | solution.py:315
  129.9 9.1 %collective-permute-start.47 = (bf16[256,512]{1,0:T(8,128)(2,1)S(1)}, bf16[256,512]{1,0:T(8,128)(2,1)S(1)}, u32[]{:S(2)}, u32[]{:S(2)}) collective-permute-start(bf16[256,512]{1,0:T(8,128)(2,1)S(1)} %second.11.a_ref), channel_id=1, source_target_pairs={{0,2},{1,3},{2,0},{3,1},{4,6},{5,7},{6,4},{7,5},{8,10},{9,11},{10,... | collective-permute-start | bytes 786440 | tf_op jit(solution)/shard_map/ppermute | solution.py:315
  135.0 18.2 %collective-permute-start.46 = (bf16[256,512]{1,0:T(8,128)(2,1)S(1)}, bf16[256,512]{1,0:T(8,128)(2,1)S(1)}, u32[]{:S(2)}, u32[]{:S(2)}) collective-permute-start(bf16[256,512]{1,0:T(8,128)(2,1)S(1)} %get-tuple-element.44.refs_6_), channel_id=1, source_target_pairs={{0,1},{1,0},{2,3},{3,2},{4,5},{5,4},{6,7},{7,6},{8,9},{9,8},{10,11... | collective-permute-start | bytes 786440 | tf_op jit(solution)/shard_map/ppermute | solution.py:242
  140.0 13.2 %collective-permute-start.48 = (bf16[256,512]{1,0:T(8,128)(2,1)S(1)}, bf16[256,512]{1,0:T(8,128)(2,1)S(1)}, u32[]{:S(2)}, u32[]{:S(2)}) collective-permute-start(bf16[256,512]{1,0:T(8,128)(2,1)S(1)} %get-tuple-element.45.refs_14_), channel_id=1, source_target_pairs={{0,1},{1,0},{2,3},{3,2},{4,5},{5,4},{6,7},{7,6},{8,9},{9,8},{10,11... | collective-permute-start | bytes 786440 | tf_op jit(solution)/shard_map/ppermute | solution.py:242
  (35 other events, 142.3 us)
where the time goes:
time: 157 us; the launch traced here: 156 us
  waiting for transfers between devices  63.5 us (40%)
  starting transfers between devices  52.3 us (33%)
  Pallas kernels  35.8 us (23%)
  local copies, waits for them, and re-layouts  3.51 us (2%)
    pallas_call x18, Pallas kernels, call(): pl.pallas_call(kernel, name=name, out_shape=out, in_specs=[SMEM if a.dtyp...  35.8 us
    ppermute x12, waiting for transfers between devices, sum_steps(): lax.ppermute(stats, 'sec', [(i, i ^ f) for i in range(n_sec)])  20.5 us
    ppermute x3, waiting for transfers between devices, on_device(): pair_1 = lax.ppermute(mine_1, 'sec', pairs)  14.1 us
    ppermute x12, starting transfers between devices, sum_steps(): lax.ppermute(stats, 'sec', [(i, i ^ f) for i in range(n_sec)])  13.3 us
    ppermute x3, starting transfers between devices, on_device(): far_0 = lax.ppermute(pair_0, 'sec', onward)  10.6 us
    ppermute x3, waiting for transfers between devices, on_device(): pair_0 = lax.ppermute(mine_0, 'sec', pairs)  10.4 us
    ppermute x3, starting transfers between devices, on_device(): far_1 = lax.ppermute(pair_1, 'sec', onward)  9.89 us
    ppermute x6, waiting for transfers between devices, on_device(): arrived = lax.ppermute(value, 'op', [(i, i ^ bit) for i in range(n_op)])  8.63 us
  transfers between devices with their start and end apart: 54, of which 29 were waited for; matrix products, arithmetic and copies ran while one was open for 0% of the time, Pallas kernels for 17%

commit v1 on v0

--- a/solution.py
+++ b/solution.py
@@ -106,19 +106,29 @@
             give_ref[w, t] = left_ref[w, t, half_of(1, half), :]
 
 
-def gather_sources(refs, v_ref):
+def place_of(k):
+    pair = jnp.where(lax.axis_index("sec") % 2 == 0, 2, 0)
+    return (1, pair, 2 - pair)[k]
+
+
+def gather_sources(kinds, refs, v_ref):
     half = refs[0].shape[0]
-    even = lax.axis_index("sec") % 2 == 0
-    pair = jnp.where(even, 2, 0)
-    for k, place in enumerate((1, pair, 2 - pair)):
+    for i, k in enumerate(kinds):
         for which in range(2):
-            v_ref[place, half_of(which, half), :] = refs[2 * k + which][...]
-
-
-def add_terms(parity, target, shifts_ref, left_ref, right_ref, v_ref, list_ref, acc_ref):
+            v_ref[place_of(k), half_of(which, half), :] = refs[2 * i + which][...]
+
+
+def add_terms(
+    parity, kinds, target, shifts_ref, left_ref, right_ref, v_ref, list_ref, acc_ref
+):
+    far = place_of(2)
     count = jnp.int32(0)
     for w in range(shifts_ref.shape[0]):
         here = ((shifts_ref[w] + parity) & 1) == target
+        if 2 not in kinds:
+            here = here & (((target - shifts_ref[w]) >> 1) + 1 != far)
+        elif kinds == (2,):
+            here = here & (((target - shifts_ref[w]) >> 1) + 1 == far)
 
         @pl.when(here)
         def _():
@@ -145,19 +155,31 @@
 
 def first_kernel(shifts_ref, left_ref, right_ref, *refs):
     *sources, acc_ref, v_ref, list_ref = refs
-    gather_sources(sources, v_ref)
+    gather_sources((0, 1, 2), sources, v_ref)
     for target in range(acc_ref.shape[0]):
         acc_ref[target] = jnp.zeros(acc_ref.shape[1:], F32)
         add_terms(
-            0, target, shifts_ref, left_ref, right_ref, v_ref, list_ref, acc_ref.at[target]
-        )
-
-
-def second_kernel(target, shifts_ref, left_ref, right_ref, *refs):
+            0, (0, 1, 2), target, shifts_ref, left_ref, right_ref, v_ref, list_ref,
+            acc_ref.at[target],
+        )
+
+
+def near_kernel(shifts_ref, left_ref, right_ref, *refs):
+    *sources, sum_ref, acc_ref, v_ref, list_ref = refs
+    gather_sources((0, 1), sources, v_ref)
+    for target in range(acc_ref.shape[0]):
+        acc_ref[target] = sum_ref[target]
+        add_terms(
+            1, (0, 1), target, shifts_ref, left_ref, right_ref, v_ref, list_ref,
+            acc_ref.at[target],
+        )
+
+
+def far_kernel(target, shifts_ref, left_ref, right_ref, *refs):
     *sources, sum_ref, out_ref, v_ref, list_ref, acc_ref = refs
-    gather_sources(sources, v_ref)
+    gather_sources((2,), sources, v_ref)
     acc_ref[...] = sum_ref[target]
-    add_terms(1, target, shifts_ref, left_ref, right_ref, v_ref, list_ref, acc_ref)
+    add_terms(1, (2,), target, shifts_ref, left_ref, right_ref, v_ref, list_ref, acc_ref)
     out_ref[...] = acc_ref[...].astype(BF16)
 
 
@@ -241,12 +263,14 @@
     def across_cores(value):
         return lax.ppermute(value, "op", core_pairs)
 
-    def sum_steps(stats):
+    def sum_near(stats):
         stats = stats + across_cores(stats)
-        steps = []
-        bit = 1
+        return stats + lax.ppermute(stats, "sec", pairs)
+
+    def sum_far(stats):
+        bit = 2
         while bit < n_sec:
-            flips = [bit] if bit == 1 or 2 * bit >= n_sec else [bit, 2 * bit, 3 * bit]
+            flips = [bit] if 2 * bit >= n_sec else [bit, 2 * bit, 3 * bit]
             arrived = [
                 lax.ppermute(stats, "sec", [(i, i ^ f) for i in range(n_sec)]) for f in flips
             ]
@@ -254,9 +278,8 @@
                 stats = stats + arrived[0]
             else:
                 stats = (stats + arrived[0]) + (arrived[1] + arrived[2])
-            steps.append(stats)
-            bit <<= len(flips) - len(flips) // 2
-        return steps
+            bit *= len(flips) + 1
+        return stats
 
     half_type = jax.ShapeDtypeStruct((half, columns), BF16)
     stats_type = jax.ShapeDtypeStruct((8, 128), F32)
@@ -271,7 +294,7 @@
     )
     basis = [[(halves[0], halves[1]), (halves[2], halves[3])]]
     half_left = jax.ShapeDtypeStruct((terms // 2, sectors, half, block_rows), BF16)
-    keep, give = call(split_kernel, "split", [half_left] * 2, [], left_blocks)
+    keep, give = call(split_kernel, "split", [half_left] * 2, [], after(left_blocks, sums))
     operators = [
         jnp.concatenate([mine, other])
         for mine, other in (
@@ -286,27 +309,36 @@
     for product in range(3):
         (mine_0, other_0), (mine_1, other_1) = basis[-1]
         pair_0 = lax.ppermute(mine_0, "sec", pairs)
-        pair_1 = lax.ppermute(mine_1, "sec", pairs)
+        pair_1 = lax.ppermute(after(mine_1, pair_0), "sec", pairs)
         far_0 = lax.ppermute(pair_0, "sec", onward)
         far_1 = lax.ppermute(pair_1, "sec", onward)
         if product < 2:
-            steps = sum_steps(after(sums, pair_1))
-            stats.append(steps[-1])
+            near = sum_near(sums)
+            far_0 = after(far_0, near)
         acc = call(
             first_kernel, "first", acc_type, term_scratch, *operators,
             mine_0, other_0, pair_0, across_cores(pair_0), far_0, across_cores(far_0),
             flops=terms * pair_flops,
         )
-        far_1 = after(far_1, acc, steps[0]) if product < 2 else after(far_1, acc)
-        sources = (mine_1, other_1, pair_1, across_cores(pair_1), far_1, across_cores(far_1))
+        acc = call(
+            near_kernel, "near", acc_type, term_scratch, *operators,
+            mine_1, other_1, pair_1, across_cores(pair_1), acc, flops=terms * pair_flops // 2,
+        )
+        far_1 = after(far_1, acc)
+        sources = (far_1, across_cores(far_1))
+        values = [
+            call(
+                functools.partial(far_kernel, t), "far", half_type,
+                term_scratch + [acc_scratch], *operators, *sources, acc,
+                flops=terms * pair_flops // 4,
+            )
+            for t in range(sectors)
+        ]
+        if product < 2:
+            stats.append(sum_far(after(near, values[-1])))
         image = []
         parts = []
-        for t in range(sectors):
-            value = call(
-                functools.partial(second_kernel, t), "second", half_type,
-                term_scratch + [acc_scratch], *operators, *sources, acc,
-                flops=terms * pair_flops // 2,
-            )
+        for t, value in enumerate(values):
             bit = 2
             while 2 * bit < n_op:
                 arrived = lax.ppermute(value, "op", [(i, i ^ bit) for i in range(n_op)])
@@ -325,7 +357,7 @@
             sums = parts[0] + parts[1]
         else:
             sums = sums + (parts[0] + parts[1])
-    stats.append(sum_steps(sums)[-1])
+    stats.append(sum_far(sum_near(sums)))
 
     flat = [h for t in range(sectors) for b in basis for h in b[t]]
     vector_type = jax.ShapeDtypeStruct(wavefunction.shape, BF16)

time: 157 us -> 157 us (level)
  Pallas kernels: 35.8 us -> 39.4 us
  starting transfers between devices: 52.3 us -> 49.1 us
  local copies, waits for them, and re-layouts: 3.51 us -> 5.41 us
  waiting for transfers between devices: 63.5 us -> 61.6 us
    ppermute x15, waiting for transfers between devices: 34.5 us -> 24.4 us  [the longest x9 11.1 us: sum_far(): lax.ppermute(stats, 'sec', [(i, i ^ f) for i in range(n_sec)])]
    ppermute x3, waiting for transfers between devices: 10.4 us -> 18.2 us  [on_device(): pair_0 = lax.ppermute(mine_0, 'sec', pairs)]
    pallas_call x18 -> x21, Pallas kernels: 35.8 us -> 39.4 us  [call(): pl.pallas_call(kernel, name=name, out_shape=out, in_specs=[SMEM if a.dtyp...]
    ppermute x15, starting transfers between devices: 18.6 us -> 15.5 us  [the longest x9 11.4 us: sum_far(): lax.ppermute(stats, 'sec', [(i, i ^ f) for i in range(n_sec)])]
    ppermute x3, starting transfers between devices: 10.6 us -> 8.02 us  [on_device(): far_0 = lax.ppermute(pair_0, 'sec', onward)]
    unnamed x12 -> x14, local copies, waits for them, and re-layouts: 3.24 us -> 5.14 us
  transfers between devices with their start and end apart: 54 -> 54, of which waited for: 29 -> 24; matrix products, arithmetic and copies ran while one was open for 0% -> 0% of each run, Pallas kernels for 17% -> 19%
where the time goes in v1:
time: 157 us
  waiting for transfers between devices  61.6 us (39%)
  starting transfers between devices  49.1 us (31%)
  Pallas kernels  39.4 us (25%)
  local copies, waits for them, and re-layouts  5.41 us (3%)
    pallas_call x21, Pallas kernels, call(): pl.pallas_call(kernel, name=name, out_shape=out, in_specs=[SMEM if a.dtyp...  39.4 us
    ppermute x3, waiting for transfers between devices, on_device(): pair_0 = lax.ppermute(mine_0, 'sec', pairs)  18.2 us
    ppermute x9, starting transfers between devices, sum_far(): lax.ppermute(stats, 'sec', [(i, i ^ f) for i in range(n_sec)])  11.4 us
    ppermute x9, waiting for transfers between devices, sum_far(): lax.ppermute(stats, 'sec', [(i, i ^ f) for i in range(n_sec)])  11.1 us
    ppermute x3, starting transfers between devices, on_device(): far_1 = lax.ppermute(pair_1, 'sec', onward)  10.4 us
    ppermute x3, waiting for transfers between devices, sum_near(): return stats + lax.ppermute(stats, 'sec', pairs)  10.1 us
    ppermute x6, waiting for transfers between devices, on_device(): arrived = lax.ppermute(value, 'op', [(i, i ^ bit) for i in range(n_op)])  9.18 us
    ppermute x3, starting transfers between devices, on_device(): far_0 = lax.ppermute(pair_0, 'sec', onward)  8.02 us
  transfers between devices with their start and end apart: 54, of which 24 were waited for; matrix products, arithmetic and copies ran while one was open for 0% of the time, Pallas kernels for 19%

profile of v1, /device:TPU:0, one launch (start us, length us, event | category | flops | bytes accessed | tf_op | source)
XLA Modules:
  0.0 156.8 jit_solution(3487614116145327247)
XLA Ops:
  10.5 6.6 %collective-permute-done.3.refs_2_ = bf16[256,512]{1,0:T(8,128)(2,1)S(1)} collective-permute-done((bf16[256,512]{1,0:T(8,128)(2,1)S(1)}, bf16[256,512]{1,0:T(8,128)(2,1)S(1)}, u32[]{:S(2)}, u32[]{:S(2)}) %collective-permute-start.3) | collective-permute-done | bytes 262176 | tf_op jit(solution)/shard_map/ppermute | solution.py:311
  18.8 3.5 %collective-permute-start.8 = (bf16[256,512]{1,0:T(8,128)(2,1)S(1)}, bf16[256,512]{1,0:T(8,128)(2,1)S(1)}, u32[]{:S(2)}, u32[]{:S(2)}) collective-permute-start(bf16[256,512]{1,0:T(8,128)(2,1)S(1)} %collective-permute-done.3.refs_2_), channel_id=1, source_target_pairs={{0,8},{8,16},{16,24},{12,4},{20,12},{28,20},{1,9},{9,17},{17,25},{... | collective-permute-start | bytes 786440 | tf_op jit(solution)/shard_map/ppermute | solution.py:313
  23.7 3.5 %collective-permute-done.10 = f32[8,128]{1,0:T(8,128)S(1)} collective-permute-done((f32[8,128]{1,0:T(8,128)S(1)}, f32[8,128]{1,0:T(8,128)S(1)}, u32[]{:S(2)}, u32[]{:S(2)}) %collective-permute-start.10) | collective-permute-done | bytes 4128 | tf_op jit(solution)/shard_map/ppermute | solution.py:268
  27.8 4.1 %collective-permute-start.5 = (bf16[256,512]{1,0:T(8,128)(2,1)S(1)}, bf16[256,512]{1,0:T(8,128)(2,1)S(1)}, u32[]{:S(2)}, u32[]{:S(2)}) collective-permute-start(bf16[256,512]{1,0:T(8,128)(2,1)S(1)} %collective-permute-done.4.refs_2_), channel_id=1, source_target_pairs={{0,8},{8,16},{16,24},{12,4},{20,12},{28,20},{1,9},{9,17},{17,25},{... | collective-permute-start | bytes 786440 | tf_op jit(solution)/shard_map/ppermute | solution.py:314
  32.5 4.1 %first.3.refs_4_ = f32[2,256,512]{2,1,0:T(8,128)S(1)} custom-call(s32[8]{0:T(128)S(1)} %pad_add_fusion.shifts_ref, bf16[8,2,256,512]{3,2,1,0:T(8,128)(2,1)S(1)} %constant_dynamic-update-slice_fusion.left_ref, bf16[8,512,512]{2,1,0:T(8,128)(2,1)S(1)} %constant_dynamic-update-slice_fusion.2.right_ref, bf16[256,512]{1,0:T(8,128)(2,1)S(1)} %get-tuple-element.32.refs_0_, ...), custom_call_target="tpu_custom_call" | custom-call | flops 2147483648 | bytes 9961504 | tf_op jit(solution)/shard_map/first/pallas_call | solution.py:18
  36.6 2.9 %near.3.refs_2_ = f32[2,256,512]{2,1,0:T(8,128)S(1)} custom-call(s32[8]{0:T(128)S(1)} %pad_add_fusion.shifts_ref, bf16[8,2,256,512]{3,2,1,0:T(8,128)(2,1)S(1)} %constant_dynamic-update-slice_fusion.left_ref, bf16[8,512,512]{2,1,0:T(8,128)(2,1)S(1)} %constant_dynamic-update-slice_fusion.2.right_ref, bf16[256,512]{1,0:T(8,128)(2,1)S(1)} %get-tuple-element.39.refs_0_.refs_8_, ...), custom_call_target="tpu_custom_call" | custom-call | flops 1073741824 | bytes 10485792 | tf_op jit(solution)/shard_map/near/pallas_call | solution.py:18
  45.3 2.6 %collective-permute-start.15 = (f32[8,128]{1,0:T(8,128)S(1)}, f32[8,128]{1,0:T(8,128)S(1)}, u32[]{:S(2)}, u32[]{:S(2)}) collective-permute-start(f32[8,128]{1,0:T(8,128)S(1)} %add.58), channel_id=1, source_target_pairs={{0,16},{4,20},{8,24},{12,28},{16,0},{20,4},{24,8},{28,12},{1,17},{... | collective-permute-start | bytes 12296 | tf_op jit(solution)/shard_map/ppermute | solution.py:275
  49.9 3.5 %collective-permute-done.16 = f32[8,128]{1,0:T(8,128)S(1)} collective-permute-done((f32[8,128]{1,0:T(8,128)S(1)}, f32[8,128]{1,0:T(8,128)S(1)}, u32[]{:S(2)}, u32[]{:S(2)}) %collective-permute-start.16) | collective-permute-done | bytes 4128 | tf_op jit(solution)/shard_map/ppermute | solution.py:275
  54.9 6.2 %collective-permute-done.19.refs_2_ = bf16[256,512]{1,0:T(8,128)(2,1)S(1)} collective-permute-done((bf16[256,512]{1,0:T(8,128)(2,1)S(1)}, bf16[256,512]{1,0:T(8,128)(2,1)S(1)}, u32[]{:S(2)}, u32[]{:S(2)}) %collective-permute-start.19) | collective-permute-done | bytes 262176 | tf_op jit(solution)/shard_map/ppermute | solution.py:311
  67.1 3.3 %collective-permute-done.27 = f32[8,128]{1,0:T(8,128)S(1)} collective-permute-done((f32[8,128]{1,0:T(8,128)S(1)}, f32[8,128]{1,0:T(8,128)S(1)}, u32[]{:S(2)}, u32[]{:S(2)}) %collective-permute-start.27) | collective-permute-done | bytes 4128 | tf_op jit(solution)/shard_map/ppermute | solution.py:268
  71.4 3.5 %collective-permute-start.21 = (bf16[256,512]{1,0:T(8,128)(2,1)S(1)}, bf16[256,512]{1,0:T(8,128)(2,1)S(1)}, u32[]{:S(2)}, u32[]{:S(2)}) collective-permute-start(bf16[256,512]{1,0:T(8,128)(2,1)S(1)} %collective-permute-done.20.refs_2_), channel_id=1, source_target_pairs={{0,8},{8,16},{16,24},{12,4},{20,12},{28,20},{1,9},{9,17},{17,25},{... | collective-permute-start | bytes 786440 | tf_op jit(solution)/shard_map/ppermute | solution.py:314
  74.9 4.1 %first.4.refs_4_ = f32[2,256,512]{2,1,0:T(8,128)S(1)} custom-call(s32[8]{0:T(128)S(1)} %pad_add_fusion.shifts_ref, bf16[8,2,256,512]{3,2,1,0:T(8,128)(2,1)S(1)} %constant_dynamic-update-slice_fusion.left_ref, bf16[8,512,512]{2,1,0:T(8,128)(2,1)S(1)} %constant_dynamic-update-slice_fusion.2.right_ref, ...), custom_call_target="tpu_custom_call" | custom-call | flops 2147483648 | bytes 9961504 | tf_op jit(solution)/shard_map/first/pallas_call | solution.py:18
  79.1 3.0 %near.4.refs_2_ = f32[2,256,512]{2,1,0:T(8,128)S(1)} custom-call(s32[8]{0:T(128)S(1)} %pad_add_fusion.shifts_ref, bf16[8,2,256,512]{3,2,1,0:T(8,128)(2,1)S(1)} %constant_dynamic-update-slice_fusion.left_ref, bf16[8,512,512]{2,1,0:T(8,128)(2,1)S(1)} %constant_dynamic-update-slice_fusion.2.right_ref, ...), custom_call_target="tpu_custom_call" | custom-call | flops 1073741824 | bytes 10485792 | tf_op jit(solution)/shard_map/near/pallas_call | solution.py:18
  97.3 5.4 %collective-permute-done.36.refs_2_ = bf16[256,512]{1,0:T(8,128)(2,1)S(1)} collective-permute-done((bf16[256,512]{1,0:T(8,128)(2,1)S(1)}, bf16[256,512]{1,0:T(8,128)(2,1)S(1)}, u32[]{:S(2)}, u32[]{:S(2)}) %collective-permute-start.36) | collective-permute-done | bytes 262176 | tf_op jit(solution)/shard_map/ppermute | solution.py:311
  102.7 2.7 %collective-permute-start.42 = (bf16[256,512]{1,0:T(8,128)(2,1)S(1)}, bf16[256,512]{1,0:T(8,128)(2,1)S(1)}, u32[]{:S(2)}, u32[]{:S(2)}) collective-permute-start(bf16[256,512]{1,0:T(8,128)(2,1)S(1)} %collective-permute-done.36.refs_2_), channel_id=1, source_target_pairs={{0,8},{8,16},{16,24},{12,4},{20,12},{28,20},{1,9},{9,17},{17,25},{... | collective-permute-start | bytes 786440 | tf_op jit(solution)/shard_map/ppermute | solution.py:313
  109.8 3.1 %collective-permute-done.37.refs_2_ = bf16[256,512]{1,0:T(8,128)(2,1)S(1)} collective-permute-done((bf16[256,512]{1,0:T(8,128)(2,1)S(1)}, bf16[256,512]{1,0:T(8,128)(2,1)S(1)}, u32[]{:S(2)}, u32[]{:S(2)}) %collective-permute-start.37) | collective-permute-done | bytes 262176 | tf_op jit(solution)/shard_map/ppermute | solution.py:312
  112.9 2.9 %collective-permute-start.38 = (bf16[256,512]{1,0:T(8,128)(2,1)S(1)}, bf16[256,512]{1,0:T(8,128)(2,1)S(1)}, u32[]{:S(2)}, u32[]{:S(2)}) collective-permute-start(bf16[256,512]{1,0:T(8,128)(2,1)S(1)} %collective-permute-done.37.refs_2_), channel_id=1, source_target_pairs={{0,8},{8,16},{16,24},{12,4},{20,12},{28,20},{1,9},{9,17},{17,25},{... | collective-permute-start | bytes 786440 | tf_op jit(solution)/shard_map/ppermute | solution.py:314
  115.8 4.1 %first.5.refs_4_ = f32[2,256,512]{2,1,0:T(8,128)S(1)} custom-call(s32[8]{0:T(128)S(1)} %pad_add_fusion.shifts_ref, bf16[8,2,256,512]{3,2,1,0:T(8,128)(2,1)S(1)} %constant_dynamic-update-slice_fusion.left_ref, bf16[8,512,512]{2,1,0:T(8,128)(2,1)S(1)} %constant_dynamic-update-slice_fusion.2.right_ref, ...), custom_call_target="tpu_custom_call" | custom-call | flops 2147483648 | bytes 9961504 | tf_op jit(solution)/shard_map/first/pallas_call | solution.py:18
  120.0 2.8 %near.5.refs_2_ = f32[2,256,512]{2,1,0:T(8,128)S(1)} custom-call(s32[8]{0:T(128)S(1)} %pad_add_fusion.shifts_ref, bf16[8,2,256,512]{3,2,1,0:T(8,128)(2,1)S(1)} %constant_dynamic-update-slice_fusion.left_ref, bf16[8,512,512]{2,1,0:T(8,128)(2,1)S(1)} %constant_dynamic-update-slice_fusion.2.right_ref, ...), custom_call_target="tpu_custom_call" | custom-call | flops 1073741824 | bytes 10485792 | tf_op jit(solution)/shard_map/near/pallas_call | solution.py:18
  129.5 5.4 %collective-permute-done.45.b_ref = bf16[256,512]{1,0:T(8,128)(2,1)S(1)} collective-permute-done((bf16[256,512]{1,0:T(8,128)(2,1)S(1)}, bf16[256,512]{1,0:T(8,128)(2,1)S(1)}, u32[]{:S(2)}, u32[]{:S(2)}) %collective-permute-start.45) | collective-permute-done | bytes 262176 | tf_op jit(solution)/shard_map/ppermute | solution.py:347
  135.9 3.8 %collective-permute-done.47.b_ref = bf16[256,512]{1,0:T(8,128)(2,1)S(1)} collective-permute-done((bf16[256,512]{1,0:T(8,128)(2,1)S(1)}, bf16[256,512]{1,0:T(8,128)(2,1)S(1)}, u32[]{:S(2)}, u32[]{:S(2)}) %collective-permute-start.47) | collective-permute-done | bytes 262176 | tf_op jit(solution)/shard_map/ppermute | solution.py:347
  142.6 3.4 %collective-permute-done.50 = f32[8,128]{1,0:T(8,128)S(1)} collective-permute-done((f32[8,128]{1,0:T(8,128)S(1)}, f32[8,128]{1,0:T(8,128)S(1)}, u32[]{:S(2)}, u32[]{:S(2)}) %collective-permute-start.50) | collective-permute-done | bytes 4128 | tf_op jit(solution)/shard_map/ppermute | solution.py:268
  150.5 3.0 %collective-permute-done.53 = f32[8,128]{1,0:T(8,128)S(1)} collective-permute-done((f32[8,128]{1,0:T(8,128)S(1)}, f32[8,128]{1,0:T(8,128)S(1)}, u32[]{:S(2)}, u32[]{:S(2)}) %collective-permute-start.53) | collective-permute-done | bytes 4128 | tf_op jit(solution)/shard_map/ppermute | solution.py:275
  153.5 3.2 %last.1 = (bf16[2,512,512]{2,1,0:T(8,128)(2,1)}, f32[2,3]{1,0:T(2,128)}) custom-call(s32[16]{0:T(128)S(1)} %copy-done.3, bf16[256,512]{1,0:T(8,128)(2,1)S(1)} %get-tuple-element.32.refs_0_, bf16[256,512]{1,0:T(8,128)(2,1)S(1)} %get-tuple-element.33.refs_1_, bf16[256,512]{1,0:T(8,128)(2,1)S(1)} %get-tuple-element.44.refs_0_.refs_1_.refs_2_, ...), custom_call_target="tpu_custom_call" | custom-call | bytes 4206656 | tf_op jit(solution)/shard_map/last/pallas_call | solution.py:18
  (133 shorter events, 64.9 us)
Async XLA Ops:
  5.8 26.0 %collective-permute-start.1 = (bf16[4,2,256,512]{3,2,1,0:T(8,128)(2,1)S(1)}, bf16[4,2,256,512]{3,2,1,0:T(8,128)(2,1)S(1)}, u32[]{:S(2)}, u32[]{:S(2)}) collective-permute-start(bf16[4,2,256,512]{3,2,1,0:T(8,128)(2,1)S(1)} %get-tuple-element.37), channel_id=1, source_target_pairs={{0,1},{1,0},{2,3},{3,2},{4,5},{5,4},{6,7},{7,6},{8,9},{9,8},{10,11... | collective-permute-start | bytes 6291464 | tf_op jit(solution)/shard_map/ppermute | solution.py:264
  7.1 25.1 %collective-permute-start.2 = (bf16[4,512,512]{2,1,0:T(8,128)(2,1)S(1)}, bf16[4,512,512]{2,1,0:T(8,128)(2,1)S(1)}, u32[]{:S(2)}, u32[]{:S(2)}) collective-permute-start(bf16[4,512,512]{2,1,0:T(8,128)(2,1)S(1)} %copy-done.4), channel_id=1, source_target_pairs={{0,1},{1,0},{2,3},{3,2},{4,5},{5,4},{6,7},{7,6},{8,9},{9,8},{10,11... | collective-permute-start | bytes 6291464 | tf_op jit(solution)/shard_map/ppermute | solution.py:264
  7.6 9.5 %collective-permute-start.3 = (bf16[256,512]{1,0:T(8,128)(2,1)S(1)}, bf16[256,512]{1,0:T(8,128)(2,1)S(1)}, u32[]{:S(2)}, u32[]{:S(2)}) collective-permute-start(bf16[256,512]{1,0:T(8,128)(2,1)S(1)} %get-tuple-element.32.refs_0_), channel_id=1, source_target_pairs={{0,4},{4,0},{8,12},{12,8},{16,20},{20,16},{24,28},{28,24},{1,5},{5... | collective-permute-start | bytes 786440 | tf_op jit(solution)/shard_map/ppermute | solution.py:311
  10.1 12.4 %collective-permute-start.9 = (f32[8,128]{1,0:T(8,128)S(1)}, f32[8,128]{1,0:T(8,128)S(1)}, u32[]{:S(2)}, u32[]{:S(2)}) collective-permute-start(f32[8,128]{1,0:T(8,128)S(1)} %get-tuple-element.34), channel_id=1, source_target_pairs={{0,1},{1,0},{2,3},{3,2},{4,5},{5,4},{6,7},{7,6},{8,9},{9,8},{10,11... | collective-permute-start | bytes 12296 | tf_op jit(solution)/shard_map/ppermute | solution.py:264
  17.1 10.7 %collective-permute-start.4 = (bf16[256,512]{1,0:T(8,128)(2,1)S(1)}, bf16[256,512]{1,0:T(8,128)(2,1)S(1)}, u32[]{:S(2)}, u32[]{:S(2)}) collective-permute-start(bf16[256,512]{1,0:T(8,128)(2,1)S(1)} %get-tuple-element.39.refs_0_.refs_8_), channel_id=1, source_target_pairs={{0,4},{4,0},{8,12},{12,8},{16,20},{20,16},{24,28},{28,24},{1,5},{5... | collective-permute-start | bytes 786440 | tf_op jit(solution)/shard_map/ppermute | solution.py:312
  18.8 8.6 %collective-permute-start.8 = (bf16[256,512]{1,0:T(8,128)(2,1)S(1)}, bf16[256,512]{1,0:T(8,128)(2,1)S(1)}, u32[]{:S(2)}, u32[]{:S(2)}) collective-permute-start(bf16[256,512]{1,0:T(8,128)(2,1)S(1)} %collective-permute-done.3.refs_2_), channel_id=1, source_target_pairs={{0,8},{8,16},{16,24},{12,4},{20,12},{28,20},{1,9},{9,17},{17,25},{... | collective-permute-start | bytes 786440 | tf_op jit(solution)/shard_map/ppermute | solution.py:313
  27.8 11.7 %collective-permute-start.5 = (bf16[256,512]{1,0:T(8,128)(2,1)S(1)}, bf16[256,512]{1,0:T(8,128)(2,1)S(1)}, u32[]{:S(2)}, u32[]{:S(2)}) collective-permute-start(bf16[256,512]{1,0:T(8,128)(2,1)S(1)} %collective-permute-done.4.refs_2_), channel_id=1, source_target_pairs={{0,8},{8,16},{16,24},{12,4},{20,12},{28,20},{1,9},{9,17},{17,25},{... | collective-permute-start | bytes 786440 | tf_op jit(solution)/shard_map/ppermute | solution.py:314
  42.3 11.1 %collective-permute-start.13 = (bf16[256,512]{1,0:T(8,128)(2,1)S(1)}, bf16[256,512]{1,0:T(8,128)(2,1)S(1)}, u32[]{:S(2)}, u32[]{:S(2)}) collective-permute-start(bf16[256,512]{1,0:T(8,128)(2,1)S(1)} %far.6.a_ref), channel_id=1, source_target_pairs={{0,2},{1,3},{2,0},{3,1},{4,6},{5,7},{6,4},{7,5},{8,10},{9,11},{10,... | collective-permute-start | bytes 786440 | tf_op jit(solution)/shard_map/ppermute | solution.py:347
  54.3 8.6 %collective-permute-start.18 = (bf16[256,512]{1,0:T(8,128)(2,1)S(1)}, bf16[256,512]{1,0:T(8,128)(2,1)S(1)}, u32[]{:S(2)}, u32[]{:S(2)}) collective-permute-start(bf16[256,512]{1,0:T(8,128)(2,1)S(1)} %far.7.a_ref), channel_id=1, source_target_pairs={{0,2},{1,3},{2,0},{3,1},{4,6},{5,7},{6,4},{7,5},{8,10},{9,11},{10,... | collective-permute-start | bytes 786440 | tf_op jit(solution)/shard_map/ppermute | solution.py:347
  61.1 9.2 %collective-permute-start.25 = (bf16[256,512]{1,0:T(8,128)(2,1)S(1)}, bf16[256,512]{1,0:T(8,128)(2,1)S(1)}, u32[]{:S(2)}, u32[]{:S(2)}) collective-permute-start(bf16[256,512]{1,0:T(8,128)(2,1)S(1)} %collective-permute-done.19.refs_2_), channel_id=1, source_target_pairs={{0,8},{8,16},{16,24},{12,4},{20,12},{28,20},{1,9},{9,17},{17,25},{... | collective-permute-start | bytes 786440 | tf_op jit(solution)/shard_map/ppermute | solution.py:313
  63.8 7.1 %collective-permute-start.20 = (bf16[256,512]{1,0:T(8,128)(2,1)S(1)}, bf16[256,512]{1,0:T(8,128)(2,1)S(1)}, u32[]{:S(2)}, u32[]{:S(2)}) collective-permute-start(bf16[256,512]{1,0:T(8,128)(2,1)S(1)} %get-tuple-element.46.refs_0_.refs_1_.refs_10_), channel_id=1, source_target_pairs={{0,4},{4,0},{8,12},{12,8},{16,20},{20,16},{24,28},{28,24},{1,5},{5... | collective-permute-start | bytes 786440 | tf_op jit(solution)/shard_map/ppermute | solution.py:312
  70.9 8.2 %collective-permute-start.22 = (bf16[256,512]{1,0:T(8,128)(2,1)S(1)}, bf16[256,512]{1,0:T(8,128)(2,1)S(1)}, u32[]{:S(2)}, u32[]{:S(2)}) collective-permute-start(bf16[256,512]{1,0:T(8,128)(2,1)S(1)} %get-tuple-element.46.refs_0_.refs_1_.refs_10_), channel_id=1, source_target_pairs={{0,1},{1,0},{2,3},{3,2},{4,5},{5,4},{6,7},{7,6},{8,9},{9,8},{10,11... | collective-permute-start | bytes 786440 | tf_op jit(solution)/shard_map/ppermute | solution.py:264
  70.9 8.1 %collective-permute-start.23 = (bf16[256,512]{1,0:T(8,128)(2,1)S(1)}, bf16[256,512]{1,0:T(8,128)(2,1)S(1)}, u32[]{:S(2)}, u32[]{:S(2)}) collective-permute-start(bf16[256,512]{1,0:T(8,128)(2,1)S(1)} %collective-permute-done.20.refs_2_), channel_id=1, source_target_pairs={{0,1},{1,0},{2,3},{3,2},{4,5},{5,4},{6,7},{7,6},{8,9},{9,8},{10,11... | collective-permute-start | bytes 786440 | tf_op jit(solution)/shard_map/ppermute | solution.py:264
  71.4 10.7 %collective-permute-start.21 = (bf16[256,512]{1,0:T(8,128)(2,1)S(1)}, bf16[256,512]{1,0:T(8,128)(2,1)S(1)}, u32[]{:S(2)}, u32[]{:S(2)}) collective-permute-start(bf16[256,512]{1,0:T(8,128)(2,1)S(1)} %collective-permute-done.20.refs_2_), channel_id=1, source_target_pairs={{0,8},{8,16},{16,24},{12,4},{20,12},{28,20},{1,9},{9,17},{17,25},{... | collective-permute-start | bytes 786440 | tf_op jit(solution)/shard_map/ppermute | solution.py:314
  84.9 10.1 %collective-permute-start.30 = (bf16[256,512]{1,0:T(8,128)(2,1)S(1)}, bf16[256,512]{1,0:T(8,128)(2,1)S(1)}, u32[]{:S(2)}, u32[]{:S(2)}) collective-permute-start(bf16[256,512]{1,0:T(8,128)(2,1)S(1)} %far.8.a_ref), channel_id=1, source_target_pairs={{0,2},{1,3},{2,0},{3,1},{4,6},{5,7},{6,4},{7,5},{8,10},{9,11},{10,... | collective-permute-start | bytes 786440 | tf_op jit(solution)/shard_map/ppermute | solution.py:347
  96.9 8.6 %collective-permute-start.35 = (bf16[256,512]{1,0:T(8,128)(2,1)S(1)}, bf16[256,512]{1,0:T(8,128)(2,1)S(1)}, u32[]{:S(2)}, u32[]{:S(2)}) collective-permute-start(bf16[256,512]{1,0:T(8,128)(2,1)S(1)} %far.9.a_ref), channel_id=1, source_target_pairs={{0,2},{1,3},{2,0},{3,1},{4,6},{5,7},{6,4},{7,5},{8,10},{9,11},{10,... | collective-permute-start | bytes 786440 | tf_op jit(solution)/shard_map/ppermute | solution.py:347
  106.6 9.2 %collective-permute-start.41 = (bf16[256,512]{1,0:T(8,128)(2,1)S(1)}, bf16[256,512]{1,0:T(8,128)(2,1)S(1)}, u32[]{:S(2)}, u32[]{:S(2)}) collective-permute-start(bf16[256,512]{1,0:T(8,128)(2,1)S(1)} %collective-permute-done.36.refs_2_), channel_id=1, source_target_pairs={{0,1},{1,0},{2,3},{3,2},{4,5},{5,4},{6,7},{7,6},{8,9},{9,8},{10,11... | collective-permute-start | bytes 786440 | tf_op jit(solution)/shard_map/ppermute | solution.py:264
  109.3 10.6 %collective-permute-start.39 = (bf16[256,512]{1,0:T(8,128)(2,1)S(1)}, bf16[256,512]{1,0:T(8,128)(2,1)S(1)}, u32[]{:S(2)}, u32[]{:S(2)}) collective-permute-start(bf16[256,512]{1,0:T(8,128)(2,1)S(1)} %get-tuple-element.54.refs_0_.refs_2_.refs_12_), channel_id=1, source_target_pairs={{0,1},{1,0},{2,3},{3,2},{4,5},{5,4},{6,7},{7,6},{8,9},{9,8},{10,11... | collective-permute-start | bytes 786440 | tf_op jit(solution)/shard_map/ppermute | solution.py:264
  112.9 7.1 %collective-permute-start.40 = (bf16[256,512]{1,0:T(8,128)(2,1)S(1)}, bf16[256,512]{1,0:T(8,128)(2,1)S(1)}, u32[]{:S(2)}, u32[]{:S(2)}) collective-permute-start(bf16[256,512]{1,0:T(8,128)(2,1)S(1)} %collective-permute-done.37.refs_2_), channel_id=1, source_target_pairs={{0,1},{1,0},{2,3},{3,2},{4,5},{5,4},{6,7},{7,6},{8,9},{9,8},{10,11... | collective-permute-start | bytes 786440 | tf_op jit(solution)/shard_map/ppermute | solution.py:264
  112.9 9.9 %collective-permute-start.38 = (bf16[256,512]{1,0:T(8,128)(2,1)S(1)}, bf16[256,512]{1,0:T(8,128)(2,1)S(1)}, u32[]{:S(2)}, u32[]{:S(2)}) collective-permute-start(bf16[256,512]{1,0:T(8,128)(2,1)S(1)} %collective-permute-done.37.refs_2_), channel_id=1, source_target_pairs={{0,8},{8,16},{16,24},{12,4},{20,12},{28,20},{1,9},{9,17},{17,25},{... | collective-permute-start | bytes 786440 | tf_op jit(solution)/shard_map/ppermute | solution.py:314
  125.6 9.2 %collective-permute-start.45 = (bf16[256,512]{1,0:T(8,128)(2,1)S(1)}, bf16[256,512]{1,0:T(8,128)(2,1)S(1)}, u32[]{:S(2)}, u32[]{:S(2)}) collective-permute-start(bf16[256,512]{1,0:T(8,128)(2,1)S(1)} %far.10.a_ref), channel_id=1, source_target_pairs={{0,2},{1,3},{2,0},{3,1},{4,6},{5,7},{6,4},{7,5},{8,10},{9,11},{10,... | collective-permute-start | bytes 786440 | tf_op jit(solution)/shard_map/ppermute | solution.py:347
  128.0 11.7 %collective-permute-start.47 = (bf16[256,512]{1,0:T(8,128)(2,1)S(1)}, bf16[256,512]{1,0:T(8,128)(2,1)S(1)}, u32[]{:S(2)}, u32[]{:S(2)}) collective-permute-start(bf16[256,512]{1,0:T(8,128)(2,1)S(1)} %far.11.a_ref), channel_id=1, source_target_pairs={{0,2},{1,3},{2,0},{3,1},{4,6},{5,7},{6,4},{7,5},{8,10},{9,11},{10,... | collective-permute-start | bytes 786440 | tf_op jit(solution)/shard_map/ppermute | solution.py:347
  135.9 17.6 %collective-permute-start.46 = (bf16[256,512]{1,0:T(8,128)(2,1)S(1)}, bf16[256,512]{1,0:T(8,128)(2,1)S(1)}, u32[]{:S(2)}, u32[]{:S(2)}) collective-permute-start(bf16[256,512]{1,0:T(8,128)(2,1)S(1)} %get-tuple-element.56.refs_6_), channel_id=1, source_target_pairs={{0,1},{1,0},{2,3},{3,2},{4,5},{5,4},{6,7},{7,6},{8,9},{9,8},{10,11... | collective-permute-start | bytes 786440 | tf_op jit(solution)/shard_map/ppermute | solution.py:264
  140.8 12.7 %collective-permute-start.48 = (bf16[256,512]{1,0:T(8,128)(2,1)S(1)}, bf16[256,512]{1,0:T(8,128)(2,1)S(1)}, u32[]{:S(2)}, u32[]{:S(2)}) collective-permute-start(bf16[256,512]{1,0:T(8,128)(2,1)S(1)} %get-tuple-element.57.refs_14_), channel_id=1, source_target_pairs={{0,1},{1,0},{2,3},{3,2},{4,5},{5,4},{6,7},{7,6},{8,9},{9,8},{10,11... | collective-permute-start | bytes 786440 | tf_op jit(solution)/shard_map/ppermute | solution.py:264
  (36 other events, 161.7 us)

commit v2 on v1

--- a/solution.py
+++ b/solution.py
@@ -56,12 +56,15 @@
     return jnp.sum(stats_ref[row : row + 1, :], axis=1, keepdims=True) / live
 
 
-def write_sums(stats_ref, values, first=0):
-    parts = [jnp.zeros((1, 128), F32)] * stats_ref.shape[0]
+def write_sums(stats_ref, values, before=None):
+    parts = [jnp.zeros((1, 128), F32)] * 8
     for k, value in enumerate(values):
         folded = sum(value[:, i : i + 128] for i in range(0, value.shape[1], 128))
-        parts[first + k] = jnp.sum(folded, axis=0, keepdims=True)
-    stats_ref[...] = jnp.concatenate(parts, axis=0)
+        parts[k] = jnp.sum(folded, axis=0, keepdims=True)
+    rows = jnp.concatenate(parts, axis=0)
+    if stats_ref.shape[0] > 8:
+        stats_ref[...] = jnp.zeros_like(stats_ref)
+    stats_ref[:8] = rows if before is None else rows + before[:8]
 
 
 def first_scalars(start_stats, image_stats, live):
@@ -93,8 +96,7 @@
             value = x_ref[t, part, :].astype(F32)
             value = masked(value, part.start, rows_of(rows_ref, t, sectors))
             halves[2 * t + which][...] = value.astype(BF16)
-            if which == 0:
-                square = square + value * value
+            square = square + value * value
     write_sums(stats_ref, [square])
 
 
@@ -111,11 +113,17 @@
     return (1, pair, 2 - pair)[k]
 
 
-def gather_sources(kinds, refs, v_ref):
+def gather_sources(kinds, refs, scalars, v_ref):
     half = refs[0].shape[0]
+    if scalars:
+        rows_ref, *stats = scalars
+        scale = 1.0 / first_scalars(*stats, live_entries(rows_ref, v_ref.shape[2]))[2]
     for i, k in enumerate(kinds):
         for which in range(2):
-            v_ref[place_of(k), half_of(which, half), :] = refs[2 * i + which][...]
+            value = refs[2 * i + which][...]
+            if scalars:
+                value = (value.astype(F32) * scale).astype(BF16)
+            v_ref[place_of(k), half_of(which, half), :] = value
 
 
 def add_terms(
@@ -154,8 +162,8 @@
 
 
 def first_kernel(shifts_ref, left_ref, right_ref, *refs):
-    *sources, acc_ref, v_ref, list_ref = refs
-    gather_sources((0, 1, 2), sources, v_ref)
+    sources, (*scalars, acc_ref, v_ref, list_ref) = refs[:6], refs[6:]
+    gather_sources((0, 1, 2), sources, scalars, v_ref)
     for target in range(acc_ref.shape[0]):
         acc_ref[target] = jnp.zeros(acc_ref.shape[1:], F32)
         add_terms(
@@ -165,8 +173,8 @@
 
 
 def near_kernel(shifts_ref, left_ref, right_ref, *refs):
-    *sources, sum_ref, acc_ref, v_ref, list_ref = refs
-    gather_sources((0, 1), sources, v_ref)
+    sources, sum_ref, (*scalars, acc_ref, v_ref, list_ref) = refs[:4], refs[4], refs[5:]
+    gather_sources((0, 1), sources, scalars, v_ref)
     for target in range(acc_ref.shape[0]):
         acc_ref[target] = sum_ref[target]
         add_terms(
@@ -176,8 +184,8 @@
 
 
 def far_kernel(target, shifts_ref, left_ref, right_ref, *refs):
-    *sources, sum_ref, out_ref, v_ref, list_ref, acc_ref = refs
-    gather_sources((2,), sources, v_ref)
+    sources, sum_ref, (*scalars, out_ref, v_ref, list_ref, acc_ref) = refs[:2], refs[2], refs[3:]
+    gather_sources((2,), sources, scalars, v_ref)
     acc_ref[...] = sum_ref[target]
     add_terms(1, (2,), target, shifts_ref, left_ref, right_ref, v_ref, list_ref, acc_ref)
     out_ref[...] = acc_ref[...].astype(BF16)
@@ -188,30 +196,35 @@
 
 
 def image_kernel(product, target, sectors, rows_ref, a_ref, b_ref, *refs):
+    out_ref = refs[-2] if product != 1 else refs[-1]
+    half, columns = out_ref.shape
+    value = a_ref[...].astype(F32) + b_ref[...].astype(F32)
+    rows = rows_of(rows_ref, target, sectors)
+    if product == 1:
+        out_ref[...] = masked(value, my_core() * half, rows).astype(BF16)
+        return
+    stats_ref = refs[-1]
     basis = [r[...].astype(F32) for r in refs[: product + 1]]
-    *stats, out_ref, stats_ref = refs[product + 1 :]
-    half, columns = out_ref.shape
+    stats, before = refs[product + 1 : -2], None
+    if target:
+        *stats, before = stats
     live = live_entries(rows_ref, columns)
-    value = a_ref[...].astype(F32) + b_ref[...].astype(F32)
     if product == 0:
         scale = 1.0 / jnp.sqrt(inner(stats[0], 0, live))
         value = value * scale
-        others = [basis[0] * scale]
+        known, others = [], [basis[0] * scale]
     else:
         norm, alpha, beta = first_scalars(*stats, live)
+        scale = 1.0 / beta
         zeroth = basis[0] * (1.0 / norm)
-        scale = 1.0 / beta
         first = (basis[1] - alpha * zeroth) * scale
-        if product == 1:
-            value = value - alpha * basis[1]
-            others = [first, zeroth]
-        else:
-            others = [basis[2], first, zeroth]
-        value = value * scale
-    value = masked(value, my_core() * half, rows_of(rows_ref, target, sectors)).astype(BF16)
+        image = (basis[2] - alpha * basis[1]) * scale
+        value = (value - (alpha * scale) * basis[2]) * scale
+        known, others = [image * image, image * first, image * zeroth], [image, first, zeroth]
+    value = masked(value, my_core() * half, rows).astype(BF16)
     out_ref[...] = value
     value = value.astype(F32)
-    write_sums(stats_ref, [value * v for v in [value] + others], 3 if product == 2 else 0)
+    write_sums(stats_ref, known + [value * v for v in [value] + others], before)
 
 
 def last_kernel(rows_ref, *refs):
@@ -235,7 +248,8 @@
     beta2 = jnp.sqrt(jnp.maximum(form(gram, r2, r2), 0.0))
     q3 = plus(1.0 / beta2, (one, r2))
     c1 = q3[1] / beta0
-    coefs = [(q3[0] - alpha0 * c1) / norm, c1, q3[2], q3[3]]
+    c2 = q3[2] / beta0
+    coefs = [(q3[0] - alpha0 * c1) / norm, c1 - alpha0 * c2, c2, q3[3]]
     for t in range(sectors):
         for which in range(2):
             blocks = [refs[8 * t + 2 * k + which][...].astype(F32) for k in range(4)]
@@ -262,6 +276,10 @@
 
     def across_cores(value):
         return lax.ppermute(value, "op", core_pairs)
+
+    def gathered(stats):
+        parts = lax.all_gather(stats, "sec")
+        return jnp.sum(parts[:, :8], axis=0)
 
     def sum_near(stats):
         stats = stats + across_cores(stats)
@@ -283,18 +301,20 @@
 
     half_type = jax.ShapeDtypeStruct((half, columns), BF16)
     stats_type = jax.ShapeDtypeStruct((8, 128), F32)
+    tall_type = jax.ShapeDtypeStruct((128, 128), F32)
     acc_type = jax.ShapeDtypeStruct((sectors, half, columns), F32)
     terms = 2 * left_blocks.shape[0]
     term_scratch = [pltpu.VMEM((3, block_rows, columns), BF16), pltpu.SMEM((terms,), jnp.int32)]
     acc_scratch = pltpu.VMEM((half, columns), F32)
 
     *halves, sums = call(
-        start_kernel, "start", [half_type] * (2 * sectors) + [stats_type], [],
+        start_kernel, "start", [half_type] * (2 * sectors) + [tall_type], [],
         sector_rows, wavefunction,
     )
     basis = [[(halves[0], halves[1]), (halves[2], halves[3])]]
+    pair_0 = lax.ppermute(halves[0], "sec", pairs)
     half_left = jax.ShapeDtypeStruct((terms // 2, sectors, half, block_rows), BF16)
-    keep, give = call(split_kernel, "split", [half_left] * 2, [], after(left_blocks, sums))
+    keep, give = call(split_kernel, "split", [half_left] * 2, [], after(left_blocks, pair_0))
     operators = [
         jnp.concatenate([mine, other])
         for mine, other in (
@@ -303,26 +323,26 @@
             (right_blocks, across_cores(right_blocks)),
         )
     ]
-    stats = []
+    stats = [gathered(sums)]
     pair_flops = 2 * half * columns * (block_rows + columns)
 
     for product in range(3):
         (mine_0, other_0), (mine_1, other_1) = basis[-1]
-        pair_0 = lax.ppermute(mine_0, "sec", pairs)
+        if product:
+            pair_0 = lax.ppermute(mine_0, "sec", pairs)
         pair_1 = lax.ppermute(after(mine_1, pair_0), "sec", pairs)
         far_0 = lax.ppermute(pair_0, "sec", onward)
         far_1 = lax.ppermute(pair_1, "sec", onward)
-        if product < 2:
-            near = sum_near(sums)
-            far_0 = after(far_0, near)
+        scalars = (sector_rows, *stats) if product == 2 else ()
         acc = call(
             first_kernel, "first", acc_type, term_scratch, *operators,
             mine_0, other_0, pair_0, across_cores(pair_0), far_0, across_cores(far_0),
-            flops=terms * pair_flops,
+            *scalars, flops=terms * pair_flops,
         )
         acc = call(
             near_kernel, "near", acc_type, term_scratch, *operators,
-            mine_1, other_1, pair_1, across_cores(pair_1), acc, flops=terms * pair_flops // 2,
+            mine_1, other_1, pair_1, across_cores(pair_1), acc,
+            *scalars, flops=terms * pair_flops // 2,
         )
         far_1 = after(far_1, acc)
         sources = (far_1, across_cores(far_1))
@@ -330,14 +350,12 @@
             call(
                 functools.partial(far_kernel, t), "far", half_type,
                 term_scratch + [acc_scratch], *operators, *sources, acc,
-                flops=terms * pair_flops // 4,
+                *scalars, flops=terms * pair_flops // 4,
             )
             for t in range(sectors)
         ]
-        if product < 2:
-            stats.append(sum_far(after(near, values[-1])))
         image = []
-        parts = []
+        sums = []
         for t, value in enumerate(values):
             bit = 2
             while 2 * bit < n_op:
@@ -345,18 +363,18 @@
                 value = call(add_kernel, "add", half_type, [], value, arrived)
                 bit *= 2
             arrived = lax.ppermute(value, "op", [(i, i ^ bit) for i in range(n_op)])
-            mine, part = call(
-                functools.partial(image_kernel, product, t, sectors), "image",
-                [half_type, stats_type], [], sector_rows,
-                value, arrived, *[b[t][0] for b in basis], *stats,
+            out = [half_type] if product == 1 else [half_type, (tall_type, None, stats_type)[product]]
+            needed = () if product == 1 else (*[b[t][0] for b in basis], *stats, *sums)
+            mine, *sums = call(
+                functools.partial(image_kernel, product, t, sectors), "image", out, [],
+                sector_rows, value, arrived, *needed,
             )
             image.append((mine, across_cores(mine)))
-            parts.append(part)
         basis.append(image)
-        if product < 2:
-            sums = parts[0] + parts[1]
-        else:
-            sums = sums + (parts[0] + parts[1])
+        if product == 0:
+            total = gathered(sums[0])
+            stats.append(total + across_cores(total))
+    sums = sums[0]
     stats.append(sum_far(sum_near(sums)))
 
     flat = [h for t in range(sectors) for b in basis for h in b[t]]

time: 157 us -> 205 us (1.31)
  blocking collectives: 0 us -> 63.4 us
  waiting for transfers between devices: 61.6 us -> 52.5 us
  starting transfers between devices: 49.1 us -> 41.8 us
    all_gather x0 -> x2, blocking collectives: none -> 63.4 us  [gathered(): parts = lax.all_gather(stats, 'sec')]
    ppermute x3 -> x2, waiting for transfers between devices: 18.2 us -> 6.98 us  [on_device(): pair_0 = lax.ppermute(mine_0, 'sec', pairs)]
    ppermute x6, waiting for transfers between devices: 9.18 us -> 17.2 us  [on_device(): arrived = lax.ppermute(value, 'op', [(i, i ^ bit) for i in range(n_op)])]
    ppermute x3 -> x1, waiting for transfers between devices: 10.1 us -> 2.18 us  [sum_near(): return stats + lax.ppermute(stats, 'sec', pairs)]
    ppermute x9 -> x3, waiting for transfers between devices: 11.1 us -> 3.6 us  [sum_far(): lax.ppermute(stats, 'sec', [(i, i ^ f) for i in range(n_sec)])]
    ppermute x9 -> x3, starting transfers between devices: 11.4 us -> 3.97 us  [sum_far(): lax.ppermute(stats, 'sec', [(i, i ^ f) for i in range(n_sec)])]
    ppermute x0 -> x1, waiting for transfers between devices: none -> 6.3 us  [on_device(): pair_0 = lax.ppermute(halves[0], 'sec', pairs)]
    ppermute x3, waiting for transfers between devices: 3.09 us -> 6.28 us  [on_device(): pair_1 = lax.ppermute(after(mine_1, pair_0), 'sec', pairs)]
  transfers between devices with their start and end apart: 54 -> 45, of which waited for: 24 -> 20; matrix products, arithmetic and copies ran while one was open for 0% -> 0% of each run, Pallas kernels for 19% -> 15%
where the time goes in v2:
time: 205 us
  blocking collectives  63.4 us (31%)
  waiting for transfers between devices  52.5 us (26%)
  starting transfers between devices  41.8 us (20%)
  Pallas kernels  40.8 us (20%)
  local copies, waits for them, and re-layouts  5.52 us (3%)
    all_gather x2, blocking collectives, gathered(): parts = lax.all_gather(stats, 'sec')  63.4 us
    pallas_call x21, Pallas kernels, call(): pl.pallas_call(kernel, name=name, out_shape=out, in_specs=[SMEM if a.dtyp...  40.8 us
    ppermute x6, waiting for transfers between devices, on_device(): arrived = lax.ppermute(value, 'op', [(i, i ^ bit) for i in range(n_op)])  17.2 us
    ppermute x3, starting transfers between devices, on_device(): far_1 = lax.ppermute(pair_1, 'sec', onward)  8.62 us
    ppermute x3, starting transfers between devices, on_device(): far_0 = lax.ppermute(pair_0, 'sec', onward)  8.39 us
    ppermute x23, waiting for transfers between devices, across_cores(): return lax.ppermute(value, 'op', core_pairs)  7.29 us
    ppermute x2, waiting for transfers between devices, on_device(): pair_0 = lax.ppermute(mine_0, 'sec', pairs)  6.98 us
    ppermute x1, waiting for transfers between devices, on_device(): pair_0 = lax.ppermute(halves[0], 'sec', pairs)  6.3 us
  transfers between devices with their start and end apart: 45, of which 20 were waited for; matrix products, arithmetic and copies ran while one was open for 0% of the time, Pallas kernels for 15%

profile of v2, /device:TPU:0, one launch (start us, length us, event | category | flops | bytes accessed | tf_op | source)
XLA Modules:
  0.0 205.2 jit_solution(2619214158932274823)
XLA Ops:
  3.5 3.0 %collective-permute-start.1 = (bf16[256,512]{1,0:T(8,128)(2,1)S(1)}, bf16[256,512]{1,0:T(8,128)(2,1)S(1)}, u32[]{:S(2)}, u32[]{:S(2)}) collective-permute-start(bf16[256,512]{1,0:T(8,128)(2,1)S(1)} %get-tuple-element.24.refs_0_), channel_id=1, source_target_pairs={{0,4},{4,0},{8,12},{12,8},{16,20},{20,16},{24,28},{28,24},{1,5},{5... | collective-permute-start | bytes 786440 | tf_op jit(solution)/shard_map/ppermute | solution.py:315
  6.5 6.3 %collective-permute-done.1.refs_2_ = bf16[256,512]{1,0:T(8,128)(2,1)S(1)} collective-permute-done((bf16[256,512]{1,0:T(8,128)(2,1)S(1)}, bf16[256,512]{1,0:T(8,128)(2,1)S(1)}, u32[]{:S(2)}, u32[]{:S(2)}) %collective-permute-start.1) | collective-permute-done | bytes 262176 | tf_op jit(solution)/shard_map/ppermute | solution.py:315
  18.5 3.5 %collective-permute-start.8 = (bf16[256,512]{1,0:T(8,128)(2,1)S(1)}, bf16[256,512]{1,0:T(8,128)(2,1)S(1)}, u32[]{:S(2)}, u32[]{:S(2)}) collective-permute-start(bf16[256,512]{1,0:T(8,128)(2,1)S(1)} %collective-permute-done.1.refs_2_), channel_id=1, source_target_pairs={{0,8},{8,16},{16,24},{12,4},{20,12},{28,20},{1,9},{9,17},{17,25},{... | collective-permute-start | bytes 786440 | tf_op jit(solution)/shard_map/ppermute | solution.py:334
  24.3 3.7 %collective-permute-start.5 = (bf16[256,512]{1,0:T(8,128)(2,1)S(1)}, bf16[256,512]{1,0:T(8,128)(2,1)S(1)}, u32[]{:S(2)}, u32[]{:S(2)}) collective-permute-start(bf16[256,512]{1,0:T(8,128)(2,1)S(1)} %collective-permute-done.4.refs_2_), channel_id=1, source_target_pairs={{0,8},{8,16},{16,24},{12,4},{20,12},{28,20},{1,9},{9,17},{17,25},{... | collective-permute-start | bytes 786440 | tf_op jit(solution)/shard_map/ppermute | solution.py:335
  30.0 3.9 %first.3.refs_4_ = f32[2,256,512]{2,1,0:T(8,128)S(1)} custom-call(s32[8]{0:T(128)S(1)} %pad_add_fusion.shifts_ref, bf16[8,2,256,512]{3,2,1,0:T(8,128)(2,1)S(1)} %constant_dynamic-update-slice_fusion.left_ref, bf16[8,512,512]{2,1,0:T(8,128)(2,1)S(1)} %constant_dynamic-update-slice_fusion.2.right_ref, bf16[256,512]{1,0:T(8,128)(2,1)S(1)} %get-tuple-element.24.refs_0_, ...), custom_call_target="tpu_custom_call" | custom-call | flops 2147483648 | bytes 9961504 | tf_op jit(solution)/shard_map/first/pallas_call | solution.py:18
  33.9 2.6 %near.3.refs_2_ = f32[2,256,512]{2,1,0:T(8,128)S(1)} custom-call(s32[8]{0:T(128)S(1)} %pad_add_fusion.shifts_ref, bf16[8,2,256,512]{3,2,1,0:T(8,128)(2,1)S(1)} %constant_dynamic-update-slice_fusion.left_ref, bf16[8,512,512]{2,1,0:T(8,128)(2,1)S(1)} %constant_dynamic-update-slice_fusion.2.right_ref, bf16[256,512]{1,0:T(8,128)(2,1)S(1)} %get-tuple-element.30.refs_0_.refs_8_, ...), custom_call_target="tpu_custom_call" | custom-call | flops 1073741824 | bytes 10485792 | tf_op jit(solution)/shard_map/near/pallas_call | solution.py:18
  41.0 31.4 %all-gather = f32[1024,128]{1,0:T(8,128)S(1)} all-gather(f32[128,128]{1,0:T(8,128)S(1)} %get-tuple-element.33), channel_id=2, replica_groups=mesh['sec'=8,'op'=4] {'sec'}, dimensions={0}, use_global_device_ids=true | all-gather | bytes 589824 | tf_op jit(solution)/shard_map/all_gather | solution.py:281
  77.2 3.5 %collective-permute-done.14.refs_2_ = bf16[256,512]{1,0:T(8,128)(2,1)S(1)} collective-permute-done((bf16[256,512]{1,0:T(8,128)(2,1)S(1)}, bf16[256,512]{1,0:T(8,128)(2,1)S(1)}, u32[]{:S(2)}, u32[]{:S(2)}) %collective-permute-start.14) | collective-permute-done | bytes 262176 | tf_op jit(solution)/shard_map/ppermute | solution.py:332
  86.4 4.3 %collective-permute-done.15.refs_2_ = bf16[256,512]{1,0:T(8,128)(2,1)S(1)} collective-permute-done((bf16[256,512]{1,0:T(8,128)(2,1)S(1)}, bf16[256,512]{1,0:T(8,128)(2,1)S(1)}, u32[]{:S(2)}, u32[]{:S(2)}) %collective-permute-start.15) | collective-permute-done | bytes 262176 | tf_op jit(solution)/shard_map/ppermute | solution.py:333
  90.7 3.6 %collective-permute-start.16 = (bf16[256,512]{1,0:T(8,128)(2,1)S(1)}, bf16[256,512]{1,0:T(8,128)(2,1)S(1)}, u32[]{:S(2)}, u32[]{:S(2)}) collective-permute-start(bf16[256,512]{1,0:T(8,128)(2,1)S(1)} %collective-permute-done.15.refs_2_), channel_id=1, source_target_pairs={{0,8},{8,16},{16,24},{12,4},{20,12},{28,20},{1,9},{9,17},{17,25},{... | collective-permute-start | bytes 786440 | tf_op jit(solution)/shard_map/ppermute | solution.py:335
  94.3 3.9 %first.4.refs_4_ = f32[2,256,512]{2,1,0:T(8,128)S(1)} custom-call(s32[8]{0:T(128)S(1)} %pad_add_fusion.shifts_ref, bf16[8,2,256,512]{3,2,1,0:T(8,128)(2,1)S(1)} %constant_dynamic-update-slice_fusion.left_ref, bf16[8,512,512]{2,1,0:T(8,128)(2,1)S(1)} %constant_dynamic-update-slice_fusion.2.right_ref, ...), custom_call_target="tpu_custom_call" | custom-call | flops 2147483648 | bytes 9961504 | tf_op jit(solution)/shard_map/first/pallas_call | solution.py:18
  98.2 2.7 %near.4.refs_2_ = f32[2,256,512]{2,1,0:T(8,128)S(1)} custom-call(s32[8]{0:T(128)S(1)} %pad_add_fusion.shifts_ref, bf16[8,2,256,512]{3,2,1,0:T(8,128)(2,1)S(1)} %constant_dynamic-update-slice_fusion.left_ref, bf16[8,512,512]{2,1,0:T(8,128)(2,1)S(1)} %constant_dynamic-update-slice_fusion.2.right_ref, ...), custom_call_target="tpu_custom_call" | custom-call | flops 1073741824 | bytes 10485792 | tf_op jit(solution)/shard_map/near/pallas_call | solution.py:18
  104.9 7.4 %collective-permute-done.23.b_ref = bf16[256,512]{1,0:T(8,128)(2,1)S(1)} collective-permute-done((bf16[256,512]{1,0:T(8,128)(2,1)S(1)}, bf16[256,512]{1,0:T(8,128)(2,1)S(1)}, u32[]{:S(2)}, u32[]{:S(2)}) %collective-permute-start.23) | collective-permute-done | bytes 262176 | tf_op jit(solution)/shard_map/ppermute | solution.py:365
  117.2 3.5 %collective-permute-done.26.refs_2_ = bf16[256,512]{1,0:T(8,128)(2,1)S(1)} collective-permute-done((bf16[256,512]{1,0:T(8,128)(2,1)S(1)}, bf16[256,512]{1,0:T(8,128)(2,1)S(1)}, u32[]{:S(2)}, u32[]{:S(2)}) %collective-permute-start.26) | collective-permute-done | bytes 262176 | tf_op jit(solution)/shard_map/ppermute | solution.py:332
  120.6 3.6 %collective-permute-start.32 = (bf16[256,512]{1,0:T(8,128)(2,1)S(1)}, bf16[256,512]{1,0:T(8,128)(2,1)S(1)}, u32[]{:S(2)}, u32[]{:S(2)}) collective-permute-start(bf16[256,512]{1,0:T(8,128)(2,1)S(1)} %collective-permute-done.26.refs_2_), channel_id=1, source_target_pairs={{0,8},{8,16},{16,24},{12,4},{20,12},{28,20},{1,9},{9,17},{17,25},{... | collective-permute-start | bytes 786440 | tf_op jit(solution)/shard_map/ppermute | solution.py:334
  125.6 2.7 %collective-permute-done.32.refs_4_ = bf16[256,512]{1,0:T(8,128)(2,1)S(1)} collective-permute-done((bf16[256,512]{1,0:T(8,128)(2,1)S(1)}, bf16[256,512]{1,0:T(8,128)(2,1)S(1)}, u32[]{:S(2)}, u32[]{:S(2)}) %collective-permute-start.32) | collective-permute-done | bytes 262176 | tf_op jit(solution)/shard_map/ppermute | solution.py:334
  128.3 32.0 %all-gather.1 = f32[1024,128]{1,0:T(8,128)S(1)} all-gather(f32[128,128]{1,0:T(8,128)S(1)} %get-tuple-element.40), channel_id=3, replica_groups=mesh['sec'=8,'op'=4] {'sec'}, dimensions={0}, use_global_device_ids=true | all-gather | bytes 589824 | tf_op jit(solution)/shard_map/all_gather | solution.py:281
  163.4 4.3 %first.5.refs_4_ = f32[2,256,512]{2,1,0:T(8,128)S(1)} custom-call(s32[8]{0:T(128)S(1)} %pad_add_fusion.shifts_ref, bf16[8,2,256,512]{3,2,1,0:T(8,128)(2,1)S(1)} %constant_dynamic-update-slice_fusion.left_ref, bf16[8,512,512]{2,1,0:T(8,128)(2,1)S(1)} %constant_dynamic-update-slice_fusion.2.right_ref, bf16[256,512]{1,0:T(8,128)(2,1)S(1)} %image.8.refs_0_.refs_2_.refs_4_, ...), custom_call_target="tpu_custom_call" | custom-call | flops 2147483648 | bytes 9969760 | tf_op jit(solution)/shard_map/first/pallas_call | solution.py:18
  167.8 2.8 %near.5.refs_2_ = f32[2,256,512]{2,1,0:T(8,128)S(1)} custom-call(s32[8]{0:T(128)S(1)} %pad_add_fusion.shifts_ref, bf16[8,2,256,512]{3,2,1,0:T(8,128)(2,1)S(1)} %constant_dynamic-update-slice_fusion.left_ref, bf16[8,512,512]{2,1,0:T(8,128)(2,1)S(1)} %constant_dynamic-update-slice_fusion.2.right_ref, bf16[256,512]{1,0:T(8,128)(2,1)S(1)} %image.9.refs_0_.refs_2_.refs_12_, ...), custom_call_target="tpu_custom_call" | custom-call | flops 1073741824 | bytes 10494048 | tf_op jit(solution)/shard_map/near/pallas_call | solution.py:18
  174.5 2.3 %far.11.a_ref = bf16[256,512]{1,0:T(8,128)(2,1)S(1)} custom-call(s32[8]{0:T(128)S(1)} %pad_add_fusion.shifts_ref, bf16[8,2,256,512]{3,2,1,0:T(8,128)(2,1)S(1)} %constant_dynamic-update-slice_fusion.left_ref, bf16[8,512,512]{2,1,0:T(8,128)(2,1)S(1)} %constant_dynamic-update-slice_fusion.2.right_ref, bf16[256,512]{1,0:T(8,128)(2,1)S(1)} %collective-permute-done.28.refs_0_, ...), custom_call_target="tpu_custom_call" | custom-call | flops 536870912 | bytes 9969760 | tf_op jit(solution)/shard_map/far/pallas_call | solution.py:18
  177.4 5.2 %collective-permute-done.36.b_ref = bf16[256,512]{1,0:T(8,128)(2,1)S(1)} collective-permute-done((bf16[256,512]{1,0:T(8,128)(2,1)S(1)}, bf16[256,512]{1,0:T(8,128)(2,1)S(1)}, u32[]{:S(2)}, u32[]{:S(2)}) %collective-permute-start.36) | collective-permute-done | bytes 262176 | tf_op jit(solution)/shard_map/ppermute | solution.py:365
  184.4 3.1 %collective-permute-done.38.b_ref = bf16[256,512]{1,0:T(8,128)(2,1)S(1)} collective-permute-done((bf16[256,512]{1,0:T(8,128)(2,1)S(1)}, bf16[256,512]{1,0:T(8,128)(2,1)S(1)}, u32[]{:S(2)}, u32[]{:S(2)}) %collective-permute-start.38) | collective-permute-done | bytes 262176 | tf_op jit(solution)/shard_map/ppermute | solution.py:365
  198.9 2.6 %collective-permute-done.44 = f32[8,128]{1,0:T(8,128)S(1)} collective-permute-done((f32[8,128]{1,0:T(8,128)S(1)}, f32[8,128]{1,0:T(8,128)S(1)}, u32[]{:S(2)}, u32[]{:S(2)}) %collective-permute-start.44) | collective-permute-done | bytes 4128 | tf_op jit(solution)/shard_map/ppermute | solution.py:293
  202.0 3.2 %last.1 = (bf16[2,512,512]{2,1,0:T(8,128)(2,1)}, f32[2,3]{1,0:T(2,128)}) custom-call(s32[16]{0:T(128)S(1)} %copy-done.3, bf16[256,512]{1,0:T(8,128)(2,1)S(1)} %get-tuple-element.24.refs_0_, bf16[256,512]{1,0:T(8,128)(2,1)S(1)} %get-tuple-element.25.refs_1_, bf16[256,512]{1,0:T(8,128)(2,1)S(1)} %get-tuple-element.34.refs_0_.refs_1_.refs_2_, ...), custom_call_target="tpu_custom_call" | custom-call | bytes 4206656 | tf_op jit(solution)/shard_map/last/pallas_call | solution.py:18
  (112 shorter events, 59.0 us)
Async XLA Ops:
  3.5 9.3 %collective-permute-start.1 = (bf16[256,512]{1,0:T(8,128)(2,1)S(1)}, bf16[256,512]{1,0:T(8,128)(2,1)S(1)}, u32[]{:S(2)}, u32[]{:S(2)}) collective-permute-start(bf16[256,512]{1,0:T(8,128)(2,1)S(1)} %get-tuple-element.24.refs_0_), channel_id=1, source_target_pairs={{0,4},{4,0},{8,12},{12,8},{16,20},{20,16},{24,28},{28,24},{1,5},{5... | collective-permute-start | bytes 786440 | tf_op jit(solution)/shard_map/ppermute | solution.py:315
  6.5 21.7 %collective-permute-start.3 = (bf16[4,512,512]{2,1,0:T(8,128)(2,1)}, bf16[4,512,512]{2,1,0:T(8,128)(2,1)S(1)}, u32[]{:S(2)}, u32[]{:S(2)}) collective-permute-start(bf16[4,512,512]{2,1,0:T(8,128)(2,1)} %param.7), channel_id=1, source_target_pairs={{0,1},{1,0},{2,3},{3,2},{4,5},{5,4},{6,7},{7,6},{8,9},{9,8},{10,11... | collective-permute-start | bytes 6291464 | tf_op jit(solution)/shard_map/ppermute | solution.py:278
  15.2 13.6 %collective-permute-start.2 = (bf16[4,2,256,512]{3,2,1,0:T(8,128)(2,1)S(1)}, bf16[4,2,256,512]{3,2,1,0:T(8,128)(2,1)S(1)}, u32[]{:S(2)}, u32[]{:S(2)}) collective-permute-start(bf16[4,2,256,512]{3,2,1,0:T(8,128)(2,1)S(1)} %get-tuple-element.28), channel_id=1, source_target_pairs={{0,1},{1,0},{2,3},{3,2},{4,5},{5,4},{6,7},{7,6},{8,9},{9,8},{10,11... | collective-permute-start | bytes 6291464 | tf_op jit(solution)/shard_map/ppermute | solution.py:278
  16.7 7.6 %collective-permute-start.4 = (bf16[256,512]{1,0:T(8,128)(2,1)S(1)}, bf16[256,512]{1,0:T(8,128)(2,1)S(1)}, u32[]{:S(2)}, u32[]{:S(2)}) collective-permute-start(bf16[256,512]{1,0:T(8,128)(2,1)S(1)} %get-tuple-element.30.refs_0_.refs_8_), channel_id=1, source_target_pairs={{0,4},{4,0},{8,12},{12,8},{16,20},{20,16},{24,28},{28,24},{1,5},{5... | collective-permute-start | bytes 786440 | tf_op jit(solution)/shard_map/ppermute | solution.py:333
  18.5 9.6 %collective-permute-start.8 = (bf16[256,512]{1,0:T(8,128)(2,1)S(1)}, bf16[256,512]{1,0:T(8,128)(2,1)S(1)}, u32[]{:S(2)}, u32[]{:S(2)}) collective-permute-start(bf16[256,512]{1,0:T(8,128)(2,1)S(1)} %collective-permute-done.1.refs_2_), channel_id=1, source_target_pairs={{0,8},{8,16},{16,24},{12,4},{20,12},{28,20},{1,9},{9,17},{17,25},{... | collective-permute-start | bytes 786440 | tf_op jit(solution)/shard_map/ppermute | solution.py:334
  24.3 12.2 %collective-permute-start.5 = (bf16[256,512]{1,0:T(8,128)(2,1)S(1)}, bf16[256,512]{1,0:T(8,128)(2,1)S(1)}, u32[]{:S(2)}, u32[]{:S(2)}) collective-permute-start(bf16[256,512]{1,0:T(8,128)(2,1)S(1)} %collective-permute-done.4.refs_2_), channel_id=1, source_target_pairs={{0,8},{8,16},{16,24},{12,4},{20,12},{28,20},{1,9},{9,17},{17,25},{... | collective-permute-start | bytes 786440 | tf_op jit(solution)/shard_map/ppermute | solution.py:335
  39.3 33.0 %collective-permute-start.11 = (bf16[256,512]{1,0:T(8,128)(2,1)S(1)}, bf16[256,512]{1,0:T(8,128)(2,1)S(1)}, u32[]{:S(2)}, u32[]{:S(2)}) collective-permute-start(bf16[256,512]{1,0:T(8,128)(2,1)S(1)} %far.6.a_ref), channel_id=1, source_target_pairs={{0,2},{1,3},{2,0},{3,1},{4,6},{5,7},{6,4},{7,5},{8,10},{9,11},{10,... | collective-permute-start | bytes 786440 | tf_op jit(solution)/shard_map/ppermute | solution.py:365
  85.4 8.9 %collective-permute-start.19 = (bf16[256,512]{1,0:T(8,128)(2,1)S(1)}, bf16[256,512]{1,0:T(8,128)(2,1)S(1)}, u32[]{:S(2)}, u32[]{:S(2)}) collective-permute-start(bf16[256,512]{1,0:T(8,128)(2,1)S(1)} %collective-permute-done.14.refs_2_), channel_id=1, source_target_pairs={{0,1},{1,0},{2,3},{3,2},{4,5},{5,4},{6,7},{7,6},{8,9},{9,8},{10,11... | collective-permute-start | bytes 786440 | tf_op jit(solution)/shard_map/ppermute | solution.py:278
  85.9 8.4 %collective-permute-start.21 = (bf16[256,512]{1,0:T(8,128)(2,1)S(1)}, bf16[256,512]{1,0:T(8,128)(2,1)S(1)}, u32[]{:S(2)}, u32[]{:S(2)}) collective-permute-start(bf16[256,512]{1,0:T(8,128)(2,1)S(1)} %collective-permute-done.20.refs_4_), channel_id=1, source_target_pairs={{0,1},{1,0},{2,3},{3,2},{4,5},{5,4},{6,7},{7,6},{8,9},{9,8},{10,11... | collective-permute-start | bytes 786440 | tf_op jit(solution)/shard_map/ppermute | solution.py:278
  85.9 12.3 %collective-permute-start.17 = (bf16[256,512]{1,0:T(8,128)(2,1)S(1)}, bf16[256,512]{1,0:T(8,128)(2,1)S(1)}, u32[]{:S(2)}, u32[]{:S(2)}) collective-permute-start(bf16[256,512]{1,0:T(8,128)(2,1)S(1)} %get-tuple-element.37.refs_0_.refs_1_.refs_10_), channel_id=1, source_target_pairs={{0,1},{1,0},{2,3},{3,2},{4,5},{5,4},{6,7},{7,6},{8,9},{9,8},{10,11... | collective-permute-start | bytes 786440 | tf_op jit(solution)/shard_map/ppermute | solution.py:278
  90.7 10.3 %collective-permute-start.16 = (bf16[256,512]{1,0:T(8,128)(2,1)S(1)}, bf16[256,512]{1,0:T(8,128)(2,1)S(1)}, u32[]{:S(2)}, u32[]{:S(2)}) collective-permute-start(bf16[256,512]{1,0:T(8,128)(2,1)S(1)} %collective-permute-done.15.refs_2_), channel_id=1, source_target_pairs={{0,8},{8,16},{16,24},{12,4},{20,12},{28,20},{1,9},{9,17},{17,25},{... | collective-permute-start | bytes 786440 | tf_op jit(solution)/shard_map/ppermute | solution.py:335
  103.8 8.5 %collective-permute-start.23 = (bf16[256,512]{1,0:T(8,128)(2,1)S(1)}, bf16[256,512]{1,0:T(8,128)(2,1)S(1)}, u32[]{:S(2)}, u32[]{:S(2)}) collective-permute-start(bf16[256,512]{1,0:T(8,128)(2,1)S(1)} %far.8.a_ref), channel_id=1, source_target_pairs={{0,2},{1,3},{2,0},{3,1},{4,6},{5,7},{6,4},{7,5},{8,10},{9,11},{10,... | collective-permute-start | bytes 786440 | tf_op jit(solution)/shard_map/ppermute | solution.py:365
  112.9 7.7 %collective-permute-start.26 = (bf16[256,512]{1,0:T(8,128)(2,1)S(1)}, bf16[256,512]{1,0:T(8,128)(2,1)S(1)}, u32[]{:S(2)}, u32[]{:S(2)}) collective-permute-start(bf16[256,512]{1,0:T(8,128)(2,1)S(1)} %image.8.refs_0_.refs_2_.refs_4_), channel_id=1, source_target_pairs={{0,4},{4,0},{8,12},{12,8},{16,20},{20,16},{24,28},{28,24},{1,5},{5... | collective-permute-start | bytes 786440 | tf_op jit(solution)/shard_map/ppermute | solution.py:332
  116.6 7.8 %collective-permute-start.25 = (bf16[256,512]{1,0:T(8,128)(2,1)S(1)}, bf16[256,512]{1,0:T(8,128)(2,1)S(1)}, u32[]{:S(2)}, u32[]{:S(2)}) collective-permute-start(bf16[256,512]{1,0:T(8,128)(2,1)S(1)} %far.9.a_ref), channel_id=1, source_target_pairs={{0,2},{1,3},{2,0},{3,1},{4,6},{5,7},{6,4},{7,5},{8,10},{9,11},{10,... | collective-permute-start | bytes 786440 | tf_op jit(solution)/shard_map/ppermute | solution.py:365
  120.6 7.7 %collective-permute-start.32 = (bf16[256,512]{1,0:T(8,128)(2,1)S(1)}, bf16[256,512]{1,0:T(8,128)(2,1)S(1)}, u32[]{:S(2)}, u32[]{:S(2)}) collective-permute-start(bf16[256,512]{1,0:T(8,128)(2,1)S(1)} %collective-permute-done.26.refs_2_), channel_id=1, source_target_pairs={{0,8},{8,16},{16,24},{12,4},{20,12},{28,20},{1,9},{9,17},{17,25},{... | collective-permute-start | bytes 786440 | tf_op jit(solution)/shard_map/ppermute | solution.py:334
  124.2 37.9 %collective-permute-start.24 = (bf16[256,512]{1,0:T(8,128)(2,1)S(1)}, bf16[256,512]{1,0:T(8,128)(2,1)S(1)}, u32[]{:S(2)}, u32[]{:S(2)}) collective-permute-start(bf16[256,512]{1,0:T(8,128)(2,1)S(1)} %image.8.refs_0_.refs_2_.refs_4_), channel_id=1, source_target_pairs={{0,1},{1,0},{2,3},{3,2},{4,5},{5,4},{6,7},{7,6},{8,9},{9,8},{10,11... | collective-permute-start | bytes 786440 | tf_op jit(solution)/shard_map/ppermute | solution.py:278
  125.0 36.8 %collective-permute-start.27 = (bf16[256,512]{1,0:T(8,128)(2,1)S(1)}, bf16[256,512]{1,0:T(8,128)(2,1)S(1)}, u32[]{:S(2)}, u32[]{:S(2)}) collective-permute-start(bf16[256,512]{1,0:T(8,128)(2,1)S(1)} %image.9.refs_0_.refs_2_.refs_12_), channel_id=1, source_target_pairs={{0,4},{4,0},{8,12},{12,8},{16,20},{20,16},{24,28},{28,24},{1,5},{5... | collective-permute-start | bytes 786440 | tf_op jit(solution)/shard_map/ppermute | solution.py:333
  125.1 38.4 %collective-permute-start.31 = (bf16[256,512]{1,0:T(8,128)(2,1)S(1)}, bf16[256,512]{1,0:T(8,128)(2,1)S(1)}, u32[]{:S(2)}, u32[]{:S(2)}) collective-permute-start(bf16[256,512]{1,0:T(8,128)(2,1)S(1)} %collective-permute-done.26.refs_2_), channel_id=1, source_target_pairs={{0,1},{1,0},{2,3},{3,2},{4,5},{5,4},{6,7},{7,6},{8,9},{9,8},{10,11... | collective-permute-start | bytes 786440 | tf_op jit(solution)/shard_map/ppermute | solution.py:278
  128.3 35.1 %collective-permute-start.33 = (bf16[256,512]{1,0:T(8,128)(2,1)S(1)}, bf16[256,512]{1,0:T(8,128)(2,1)S(1)}, u32[]{:S(2)}, u32[]{:S(2)}) collective-permute-start(bf16[256,512]{1,0:T(8,128)(2,1)S(1)} %collective-permute-done.32.refs_4_), channel_id=1, source_target_pairs={{0,1},{1,0},{2,3},{3,2},{4,5},{5,4},{6,7},{7,6},{8,9},{9,8},{10,11... | collective-permute-start | bytes 786440 | tf_op jit(solution)/shard_map/ppermute | solution.py:278
  162.1 8.4 %collective-permute-start.28 = (bf16[256,512]{1,0:T(8,128)(2,1)S(1)}, bf16[256,512]{1,0:T(8,128)(2,1)S(1)}, u32[]{:S(2)}, u32[]{:S(2)}) collective-permute-start(bf16[256,512]{1,0:T(8,128)(2,1)S(1)} %collective-permute-done.27.refs_2_), channel_id=1, source_target_pairs={{0,8},{8,16},{16,24},{12,4},{20,12},{28,20},{1,9},{9,17},{17,25},{... | collective-permute-start | bytes 786440 | tf_op jit(solution)/shard_map/ppermute | solution.py:335
  173.5 9.2 %collective-permute-start.36 = (bf16[256,512]{1,0:T(8,128)(2,1)S(1)}, bf16[256,512]{1,0:T(8,128)(2,1)S(1)}, u32[]{:S(2)}, u32[]{:S(2)}) collective-permute-start(bf16[256,512]{1,0:T(8,128)(2,1)S(1)} %far.10.a_ref), channel_id=1, source_target_pairs={{0,2},{1,3},{2,0},{3,1},{4,6},{5,7},{6,4},{7,5},{8,10},{9,11},{10,... | collective-permute-start | bytes 786440 | tf_op jit(solution)/shard_map/ppermute | solution.py:365
  176.9 10.7 %collective-permute-start.38 = (bf16[256,512]{1,0:T(8,128)(2,1)S(1)}, bf16[256,512]{1,0:T(8,128)(2,1)S(1)}, u32[]{:S(2)}, u32[]{:S(2)}) collective-permute-start(bf16[256,512]{1,0:T(8,128)(2,1)S(1)} %far.11.a_ref), channel_id=1, source_target_pairs={{0,2},{1,3},{2,0},{3,1},{4,6},{5,7},{6,4},{7,5},{8,10},{9,11},{10,... | collective-permute-start | bytes 786440 | tf_op jit(solution)/shard_map/ppermute | solution.py:365
  184.3 17.6 %collective-permute-start.37 = (bf16[256,512]{1,0:T(8,128)(2,1)S(1)}, bf16[256,512]{1,0:T(8,128)(2,1)S(1)}, u32[]{:S(2)}, u32[]{:S(2)}) collective-permute-start(bf16[256,512]{1,0:T(8,128)(2,1)S(1)} %get-tuple-element.42.refs_6_), channel_id=1, source_target_pairs={{0,1},{1,0},{2,3},{3,2},{4,5},{5,4},{6,7},{7,6},{8,9},{9,8},{10,11... | collective-permute-start | bytes 786440 | tf_op jit(solution)/shard_map/ppermute | solution.py:278
  189.2 12.8 %collective-permute-start.39 = (bf16[256,512]{1,0:T(8,128)(2,1)S(1)}, bf16[256,512]{1,0:T(8,128)(2,1)S(1)}, u32[]{:S(2)}, u32[]{:S(2)}) collective-permute-start(bf16[256,512]{1,0:T(8,128)(2,1)S(1)} %get-tuple-element.44.refs_14_), channel_id=1, source_target_pairs={{0,1},{1,0},{2,3},{3,2},{4,5},{5,4},{6,7},{7,6},{8,9},{9,8},{10,11... | collective-permute-start | bytes 786440 | tf_op jit(solution)/shard_map/ppermute | solution.py:278
  (27 other events, 150.9 us)

commit v3 on v2

--- a/solution.py
+++ b/solution.py
@@ -13,8 +13,7 @@
 SMEM = pl.BlockSpec(memory_space=pltpu.SMEM)
 
 
-def call(kernel, name, out, scratch, *operands, flops=0):
-    moved = sum(a.size * a.dtype.itemsize for a in operands)
+def call(kernel, name, out, scratch, *operands):
     return pl.pallas_call(
         kernel,
         name=name,
@@ -23,7 +22,7 @@
         out_specs=jax.tree.map(lambda _: VMEM, out),
         scratch_shapes=scratch,
         compiler_params=pltpu.CompilerParams(vmem_limit_bytes=24 << 20),
-        cost_estimate=pl.CostEstimate(flops=flops, bytes_accessed=moved, transcendentals=0),
+        cost_estimate=pl.CostEstimate(flops=0, bytes_accessed=0, transcendentals=0),
     )(*operands)
 
 
@@ -62,9 +61,7 @@
         folded = sum(value[:, i : i + 128] for i in range(0, value.shape[1], 128))
         parts[k] = jnp.sum(folded, axis=0, keepdims=True)
     rows = jnp.concatenate(parts, axis=0)
-    if stats_ref.shape[0] > 8:
-        stats_ref[...] = jnp.zeros_like(stats_ref)
-    stats_ref[:8] = rows if before is None else rows + before[:8]
+    stats_ref[...] = rows if before is None else rows + before[...]
 
 
 def first_scalars(start_stats, image_stats, live):
@@ -113,30 +110,23 @@
     return (1, pair, 2 - pair)[k]
 
 
-def gather_sources(kinds, refs, scalars, v_ref):
+def gather_sources(slots, refs, scalars, v_ref):
     half = refs[0].shape[0]
     if scalars:
         rows_ref, *stats = scalars
         scale = 1.0 / first_scalars(*stats, live_entries(rows_ref, v_ref.shape[2]))[2]
-    for i, k in enumerate(kinds):
+    for i, slot in enumerate(slots):
         for which in range(2):
             value = refs[2 * i + which][...]
             if scalars:
                 value = (value.astype(F32) * scale).astype(BF16)
-            v_ref[place_of(k), half_of(which, half), :] = value
-
-
-def add_terms(
-    parity, kinds, target, shifts_ref, left_ref, right_ref, v_ref, list_ref, acc_ref
-):
-    far = place_of(2)
+            v_ref[slot, half_of(which, half), :] = value
+
+
+def add_terms(chosen, slot, target, shifts_ref, left_ref, right_ref, v_ref, list_ref, acc_ref):
     count = jnp.int32(0)
     for w in range(shifts_ref.shape[0]):
-        here = ((shifts_ref[w] + parity) & 1) == target
-        if 2 not in kinds:
-            here = here & (((target - shifts_ref[w]) >> 1) + 1 != far)
-        elif kinds == (2,):
-            here = here & (((target - shifts_ref[w]) >> 1) + 1 == far)
+        here = chosen(shifts_ref[w])
 
         @pl.when(here)
         def _():
@@ -146,7 +136,7 @@
 
     def product(position):
         w = list_ref[position]
-        source = v_ref[((target - shifts_ref[w]) >> 1) + 1]
+        source = v_ref[slot(shifts_ref[w])]
         part = jnp.dot(left_ref[w, target], source, preferred_element_type=F32).astype(BF16)
         return jnp.dot(part, right_ref[w], preferred_element_type=F32)
 
@@ -161,33 +151,39 @@
         acc_ref[...] += product(count - 1)
 
 
-def first_kernel(shifts_ref, left_ref, right_ref, *refs):
-    sources, (*scalars, acc_ref, v_ref, list_ref) = refs[:6], refs[6:]
-    gather_sources((0, 1, 2), sources, scalars, v_ref)
+def near_kernel(shifts_ref, left_ref, right_ref, *refs):
+    sources, (*scalars, acc_ref, v_ref, list_ref) = refs[:4], refs[4:]
+    gather_sources((place_of(0), place_of(1)), sources, scalars, v_ref)
+    far = place_of(2)
     for target in range(acc_ref.shape[0]):
         acc_ref[target] = jnp.zeros(acc_ref.shape[1:], F32)
+
+        def place(shift):
+            return ((target - shift) >> 1) + 1
+
         add_terms(
-            0, (0, 1, 2), target, shifts_ref, left_ref, right_ref, v_ref, list_ref,
-            acc_ref.at[target],
+            lambda shift: ((target - shift) & 1 == 0) & (place(shift) != far), place,
+            target, shifts_ref, left_ref, right_ref, v_ref, list_ref, acc_ref.at[target],
         )
 
 
-def near_kernel(shifts_ref, left_ref, right_ref, *refs):
-    sources, sum_ref, (*scalars, acc_ref, v_ref, list_ref) = refs[:4], refs[4], refs[5:]
-    gather_sources((0, 1), sources, scalars, v_ref)
-    for target in range(acc_ref.shape[0]):
-        acc_ref[target] = sum_ref[target]
-        add_terms(
-            1, (0, 1), target, shifts_ref, left_ref, right_ref, v_ref, list_ref,
-            acc_ref.at[target],
-        )
-
-
-def far_kernel(target, shifts_ref, left_ref, right_ref, *refs):
-    sources, sum_ref, (*scalars, out_ref, v_ref, list_ref, acc_ref) = refs[:2], refs[2], refs[3:]
-    gather_sources((2,), sources, scalars, v_ref)
+def rest_kernel(target, shifts_ref, left_ref, right_ref, *refs):
+    sources, sum_ref, (*scalars, out_ref, v_ref, list_ref, acc_ref) = refs[:8], refs[8], refs[9:]
+    places = place_of(0), place_of(1), place_of(2)
+    gather_sources((*places, 3), sources, scalars, v_ref)
     acc_ref[...] = sum_ref[target]
-    add_terms(1, (2,), target, shifts_ref, left_ref, right_ref, v_ref, list_ref, acc_ref)
+
+    def place(shift):
+        return ((target - shift) >> 1) + 1
+
+    def second(shift):
+        return (target - shift) & 1 == 1
+
+    add_terms(
+        lambda shift: second(shift) | (place(shift) == places[2]),
+        lambda shift: jnp.where(second(shift), place(shift), 3),
+        target, shifts_ref, left_ref, right_ref, v_ref, list_ref, acc_ref,
+    )
     out_ref[...] = acc_ref[...].astype(BF16)
 
 
@@ -273,48 +269,35 @@
     pairs = [(i, i ^ 1) for i in range(n_sec)]
     onward = [(i, i + 2) for i in range(0, n_sec - 2, 2)]
     onward += [(i, i - 2) for i in range(3, n_sec, 2)]
+    diagonal = [(i, i + 1) for i in range(1, n_sec - 1, 2)]
+    diagonal += [(j, i) for i, j in diagonal]
 
     def across_cores(value):
         return lax.ppermute(value, "op", core_pairs)
 
-    def gathered(stats):
-        parts = lax.all_gather(stats, "sec")
-        return jnp.sum(parts[:, :8], axis=0)
-
-    def sum_near(stats):
-        stats = stats + across_cores(stats)
-        return stats + lax.ppermute(stats, "sec", pairs)
-
-    def sum_far(stats):
-        bit = 2
-        while bit < n_sec:
-            flips = [bit] if 2 * bit >= n_sec else [bit, 2 * bit, 3 * bit]
-            arrived = [
-                lax.ppermute(stats, "sec", [(i, i ^ f) for i in range(n_sec)]) for f in flips
-            ]
-            if len(arrived) == 1:
-                stats = stats + arrived[0]
-            else:
-                stats = (stats + arrived[0]) + (arrived[1] + arrived[2])
-            bit *= len(flips) + 1
+    def flipped_sum(stats, bits):
+        for bit in bits:
+            stats = stats + lax.ppermute(stats, "sec", [(i, i ^ bit) for i in range(n_sec)])
         return stats
+
+    bits = [1 << k for k in range(n_sec.bit_length() - 1)]
 
     half_type = jax.ShapeDtypeStruct((half, columns), BF16)
     stats_type = jax.ShapeDtypeStruct((8, 128), F32)
-    tall_type = jax.ShapeDtypeStruct((128, 128), F32)
     acc_type = jax.ShapeDtypeStruct((sectors, half, columns), F32)
     terms = 2 * left_blocks.shape[0]
-    term_scratch = [pltpu.VMEM((3, block_rows, columns), BF16), pltpu.SMEM((terms,), jnp.int32)]
+    term_scratch = [pltpu.VMEM((4, block_rows, columns), BF16), pltpu.SMEM((terms,), jnp.int32)]
     acc_scratch = pltpu.VMEM((half, columns), F32)
 
     *halves, sums = call(
-        start_kernel, "start", [half_type] * (2 * sectors) + [tall_type], [],
+        start_kernel, "start", [half_type] * (2 * sectors) + [stats_type], [],
         sector_rows, wavefunction,
     )
     basis = [[(halves[0], halves[1]), (halves[2], halves[3])]]
     pair_0 = lax.ppermute(halves[0], "sec", pairs)
+    start_sums = flipped_sum(sums, bits[:1])
     half_left = jax.ShapeDtypeStruct((terms // 2, sectors, half, block_rows), BF16)
-    keep, give = call(split_kernel, "split", [half_left] * 2, [], after(left_blocks, pair_0))
+    keep, give = call(split_kernel, "split", [half_left] * 2, [], left_blocks)
     operators = [
         jnp.concatenate([mine, other])
         for mine, other in (
@@ -323,39 +306,41 @@
             (right_blocks, across_cores(right_blocks)),
         )
     ]
-    stats = [gathered(sums)]
-    pair_flops = 2 * half * columns * (block_rows + columns)
+    stats = []
+    pair_0 = after(pair_0, start_sums, keep)
 
     for product in range(3):
         (mine_0, other_0), (mine_1, other_1) = basis[-1]
         if product:
             pair_0 = lax.ppermute(mine_0, "sec", pairs)
-        pair_1 = lax.ppermute(after(mine_1, pair_0), "sec", pairs)
+        if product:
+            pair_0 = after(pair_0, mine_1)
+        else:
+            mine_1 = after(mine_1, pair_0)
+        if product == 2:
+            image_sums = flipped_sum(after(image_sums, mine_0), bits[2:])
+            pair_0 = after(pair_0, image_sums)
+            stats.append(image_sums)
+        pair_1 = lax.ppermute(mine_1, "sec", pairs)
         far_0 = lax.ppermute(pair_0, "sec", onward)
-        far_1 = lax.ppermute(pair_1, "sec", onward)
+        far_1 = lax.ppermute(mine_1, "sec", diagonal)
         scalars = (sector_rows, *stats) if product == 2 else ()
         acc = call(
-            first_kernel, "first", acc_type, term_scratch, *operators,
-            mine_0, other_0, pair_0, across_cores(pair_0), far_0, across_cores(far_0),
-            *scalars, flops=terms * pair_flops,
+            near_kernel, "near", acc_type, term_scratch, *operators,
+            mine_0, other_0, pair_0, across_cores(pair_0), *scalars,
         )
-        acc = call(
-            near_kernel, "near", acc_type, term_scratch, *operators,
-            mine_1, other_1, pair_1, across_cores(pair_1), acc,
-            *scalars, flops=terms * pair_flops // 2,
-        )
-        far_1 = after(far_1, acc)
-        sources = (far_1, across_cores(far_1))
+        sources = [mine_1, other_1]
+        for part in (pair_1, far_1, far_0):
+            sources += [part, across_cores(part)]
         values = [
             call(
-                functools.partial(far_kernel, t), "far", half_type,
-                term_scratch + [acc_scratch], *operators, *sources, acc,
-                *scalars, flops=terms * pair_flops // 4,
+                functools.partial(rest_kernel, t), "rest", half_type,
+                term_scratch + [acc_scratch], *operators, *sources, acc, *scalars,
             )
             for t in range(sectors)
         ]
         image = []
-        sums = []
+        earlier = []
         for t, value in enumerate(values):
             bit = 2
             while 2 * bit < n_op:
@@ -363,19 +348,25 @@
                 value = call(add_kernel, "add", half_type, [], value, arrived)
                 bit *= 2
             arrived = lax.ppermute(value, "op", [(i, i ^ bit) for i in range(n_op)])
-            out = [half_type] if product == 1 else [half_type, (tall_type, None, stats_type)[product]]
-            needed = () if product == 1 else (*[b[t][0] for b in basis], *stats, *sums)
-            mine, *sums = call(
+            if t == 0 and product == 0:
+                stats.append(flipped_sum(after(start_sums, values[-1]), bits[1:]))
+            elif t == 0 and product == 1:
+                image_sums = sums + across_cores(sums)
+                image_sums = flipped_sum(after(image_sums, values[-1]), bits[:2])
+                arrived = after(arrived, image_sums)
+            elif t == 0:
+                arrived = after(arrived, values[-1])
+            out = [half_type] if product == 1 else [half_type, stats_type]
+            needed = () if product == 1 else (*[b[t][0] for b in basis], *stats, *earlier)
+            mine, *earlier = call(
                 functools.partial(image_kernel, product, t, sectors), "image", out, [],
                 sector_rows, value, arrived, *needed,
             )
             image.append((mine, across_cores(mine)))
         basis.append(image)
-        if product == 0:
-            total = gathered(sums[0])
-            stats.append(total + across_cores(total))
-    sums = sums[0]
-    stats.append(sum_far(sum_near(sums)))
+        if earlier:
+            sums = earlier[0]
+    stats.append(flipped_sum(sums + across_cores(sums), bits))
 
     flat = [h for t in range(sectors) for b in basis for h in b[t]]
     vector_type = jax.ShapeDtypeStruct(wavefunction.shape, BF16)

time: 205 us -> 146 us (0.71)
  blocking collectives: 63.4 us -> 0 us
  starting transfers between devices: 41.8 us -> 56.7 us
  waiting for transfers between devices: 52.5 us -> 46.3 us
  Pallas kernels: 40.8 us -> 38.6 us
    all_gather x2 -> x0, blocking collectives: 63.4 us -> none  [gathered(): parts = lax.all_gather(stats, 'sec')]
    ppermute x10 -> x15, waiting for transfers between devices: 12.1 us -> 30 us  [the longest x9 19.2 us: flipped_sum(): lax.ppermute(stats, 'sec', [(i, i ^ bit) for i in range(n_sec)])]
    ppermute x3, starting transfers between devices: 8.39 us -> 16.7 us  [on_device(): far_0 = lax.ppermute(pair_0, 'sec', onward)]
    ppermute x10 -> x15, starting transfers between devices: 17 us -> 24.7 us  [the longest x9 20.1 us: flipped_sum(): lax.ppermute(stats, 'sec', [(i, i ^ bit) for i in range(n_sec)])]
    ppermute x1, waiting for transfers between devices: 6.3 us -> 0.01 us  [on_device(): pair_0 = lax.ppermute(halves[0], 'sec', pairs)]
    ppermute x2, waiting for transfers between devices: 6.98 us -> 0.75 us  [on_device(): pair_0 = lax.ppermute(mine_0, 'sec', pairs)]
    ppermute x23, waiting for transfers between devices: 7.29 us -> 2.57 us  [across_cores(): return lax.ppermute(value, 'op', core_pairs)]
    ppermute x6, waiting for transfers between devices: 17.2 us -> 12.8 us  [on_device(): arrived = lax.ppermute(value, 'op', [(i, i ^ bit) for i in range(n_op)])]
  transfers between devices with their start and end apart: 45 -> 50, of which waited for: 20 -> 21; matrix products, arithmetic and copies ran while one was open for 0% -> 1% of each run, Pallas kernels for 15% -> 18%
where the time goes in v3:
time: 146 us
  starting transfers between devices  56.7 us (39%)
  waiting for transfers between devices  46.3 us (32%)
  Pallas kernels  38.6 us (26%)
  local copies, waits for them, and re-layouts  3.59 us (2%)
    pallas_call x18, Pallas kernels, call(): pl.pallas_call(kernel, name=name, out_shape=out, in_specs=[SMEM if a.dtyp...  38.6 us
    ppermute x9, starting transfers between devices, flipped_sum(): lax.ppermute(stats, 'sec', [(i, i ^ bit) for i in range(n_sec)])  20.1 us
    ppermute x9, waiting for transfers between devices, flipped_sum(): lax.ppermute(stats, 'sec', [(i, i ^ bit) for i in range(n_sec)])  19.2 us
    ppermute x3, starting transfers between devices, on_device(): far_0 = lax.ppermute(pair_0, 'sec', onward)  16.7 us
    ppermute x6, waiting for transfers between devices, on_device(): arrived = lax.ppermute(value, 'op', [(i, i ^ bit) for i in range(n_op)])  12.8 us
    ppermute x3, waiting for transfers between devices, on_device(): pair_1 = lax.ppermute(mine_1, 'sec', pairs)  10.7 us
    ppermute x6, starting transfers between devices, on_device(): arrived = lax.ppermute(value, 'op', [(i, i ^ bit) for i in range(n_op)])  6.52 us
    ppermute x23, starting transfers between devices, across_cores(): return lax.ppermute(value, 'op', core_pairs)  5.04 us
  transfers between devices with their start and end apart: 50, of which 21 were waited for; matrix products, arithmetic and copies ran while one was open for 1% of the time, Pallas kernels for 18%

profile of v3, /device:TPU:0, one launch (start us, length us, event | category | flops | bytes accessed | tf_op | source)
XLA Modules:
  0.0 146.3 jit_solution(1502577766223387351)
XLA Ops:
  5.8 2.8 %collective-permute-start.3 = (bf16[256,512]{1,0:T(8,128)(2,1)S(1)}, bf16[256,512]{1,0:T(8,128)(2,1)S(1)}, u32[]{:S(2)}, u32[]{:S(2)}) collective-permute-start(bf16[256,512]{1,0:T(8,128)(2,1)S(1)} %get-tuple-element.27.refs_0_), channel_id=1, source_target_pairs={{0,4},{4,0},{8,12},{12,8},{16,20},{20,16},{24,28},{28,24},{1,5},{5... | collective-permute-start | bytes 786440 | tf_op jit(solution)/shard_map/ppermute | solution.py:297
  8.9 6.5 %collective-permute-done.4 = f32[8,128]{1,0:T(8,128)S(1)} collective-permute-done((f32[8,128]{1,0:T(8,128)S(1)}, f32[8,128]{1,0:T(8,128)S(1)}, u32[]{:S(2)}, u32[]{:S(2)}) %collective-permute-start.4) | collective-permute-done | bytes 4128 | tf_op jit(solution)/shard_map/ppermute | solution.py:280
  17.8 4.9 %collective-permute-start.9 = (bf16[256,512]{1,0:T(8,128)(2,1)S(1)}, bf16[256,512]{1,0:T(8,128)(2,1)S(1)}, u32[]{:S(2)}, u32[]{:S(2)}) collective-permute-start(bf16[256,512]{1,0:T(8,128)(2,1)S(1)} %collective-permute-done.3.refs_2_), channel_id=1, source_target_pairs={{0,8},{8,16},{16,24},{12,4},{20,12},{28,20},{1,9},{9,17},{17,25},{... | collective-permute-start | bytes 786440 | tf_op jit(solution)/shard_map/ppermute | solution.py:325
  23.0 5.0 %collective-permute-done.5.refs_2_ = bf16[256,512]{1,0:T(8,128)(2,1)S(1)} collective-permute-done((bf16[256,512]{1,0:T(8,128)(2,1)S(1)}, bf16[256,512]{1,0:T(8,128)(2,1)S(1)}, u32[]{:S(2)}, u32[]{:S(2)}) %collective-permute-start.5) | collective-permute-done | bytes 262176 | tf_op jit(solution)/shard_map/ppermute | solution.py:324
  29.5 2.8 %near.3.refs_8_ = f32[2,256,512]{2,1,0:T(8,128)S(1)} custom-call(s32[8]{0:T(128)S(1)} %pad_add_fusion.shifts_ref, bf16[8,2,256,512]{3,2,1,0:T(8,128)(2,1)S(1)} %constant_dynamic-update-slice_fusion.left_ref, bf16[8,512,512]{2,1,0:T(8,128)(2,1)S(1)} %constant_dynamic-update-slice_fusion.2.right_ref, bf16[256,512]{1,0:T(8,128)(2,1)S(1)} %get-tuple-element.27.refs_0_, ...), custom_call_target="tpu_custom_call" | custom-call | tf_op jit(solution)/shard_map/near/pallas_call | solution.py:17
  34.7 2.9 %collective-permute-start.12 = (bf16[256,512]{1,0:T(8,128)(2,1)S(1)}, bf16[256,512]{1,0:T(8,128)(2,1)S(1)}, u32[]{:S(2)}, u32[]{:S(2)}) collective-permute-start(bf16[256,512]{1,0:T(8,128)(2,1)S(1)} %rest.6.a_ref), channel_id=1, source_target_pairs={{0,2},{1,3},{2,0},{3,1},{4,6},{5,7},{6,4},{7,5},{8,10},{9,11},{10,... | collective-permute-start | bytes 786440 | tf_op jit(solution)/shard_map/ppermute | solution.py:350
  37.6 3.7 %rest.7.a_ref = bf16[256,512]{1,0:T(8,128)(2,1)S(1)} custom-call(s32[8]{0:T(128)S(1)} %pad_add_fusion.shifts_ref, bf16[8,2,256,512]{3,2,1,0:T(8,128)(2,1)S(1)} %constant_dynamic-update-slice_fusion.left_ref, bf16[8,512,512]{2,1,0:T(8,128)(2,1)S(1)} %constant_dynamic-update-slice_fusion.2.right_ref, bf16[256,512]{1,0:T(8,128)(2,1)S(1)} %get-tuple-element.34.refs_0_.refs_8_, ...), custom_call_target="tpu_custom_call" | custom-call | tf_op jit(solution)/shard_map/rest/pallas_call | solution.py:17
  45.5 3.0 %collective-permute-start.14 = (f32[8,128]{1,0:T(8,128)S(1)}, f32[8,128]{1,0:T(8,128)S(1)}, u32[]{:S(2)}, u32[]{:S(2)}) collective-permute-start(f32[8,128]{1,0:T(8,128)S(1)} %add.34), channel_id=1, source_target_pairs={{0,16},{4,20},{8,24},{12,28},{16,0},{20,4},{24,8},{28,12},{1,17},{... | collective-permute-start | bytes 12296 | tf_op jit(solution)/shard_map/ppermute | solution.py:280
  51.9 3.7 %collective-permute-done.16.b_ref = bf16[256,512]{1,0:T(8,128)(2,1)S(1)} collective-permute-done((bf16[256,512]{1,0:T(8,128)(2,1)S(1)}, bf16[256,512]{1,0:T(8,128)(2,1)S(1)}, u32[]{:S(2)}, u32[]{:S(2)}) %collective-permute-start.16) | collective-permute-done | bytes 262176 | tf_op jit(solution)/shard_map/ppermute | solution.py:350
  58.0 5.7 %collective-permute-start.23 = (bf16[256,512]{1,0:T(8,128)(2,1)S(1)}, bf16[256,512]{1,0:T(8,128)(2,1)S(1)}, u32[]{:S(2)}, u32[]{:S(2)}) collective-permute-start(bf16[256,512]{1,0:T(8,128)(2,1)S(1)} %collective-permute-done.22.refs_2_), channel_id=1, source_target_pairs={{0,8},{8,16},{16,24},{12,4},{20,12},{28,20},{1,9},{9,17},{17,25},{... | collective-permute-start | bytes 786440 | tf_op jit(solution)/shard_map/ppermute | solution.py:325
  64.3 2.6 %collective-permute-done.18.refs_2_ = bf16[256,512]{1,0:T(8,128)(2,1)S(1)} collective-permute-done((bf16[256,512]{1,0:T(8,128)(2,1)S(1)}, bf16[256,512]{1,0:T(8,128)(2,1)S(1)}, u32[]{:S(2)}, u32[]{:S(2)}) %collective-permute-start.18) | collective-permute-done | bytes 262176 | tf_op jit(solution)/shard_map/ppermute | solution.py:324
  67.6 2.8 %near.4.refs_8_ = f32[2,256,512]{2,1,0:T(8,128)S(1)} custom-call(s32[8]{0:T(128)S(1)} %pad_add_fusion.shifts_ref, bf16[8,2,256,512]{3,2,1,0:T(8,128)(2,1)S(1)} %constant_dynamic-update-slice_fusion.left_ref, bf16[8,512,512]{2,1,0:T(8,128)(2,1)S(1)} %constant_dynamic-update-slice_fusion.2.right_ref, ...), custom_call_target="tpu_custom_call" | custom-call | tf_op jit(solution)/shard_map/near/pallas_call | solution.py:17
  75.8 3.9 %rest.9.a_ref = bf16[256,512]{1,0:T(8,128)(2,1)S(1)} custom-call(s32[8]{0:T(128)S(1)} %pad_add_fusion.shifts_ref, bf16[8,2,256,512]{3,2,1,0:T(8,128)(2,1)S(1)} %constant_dynamic-update-slice_fusion.left_ref, bf16[8,512,512]{2,1,0:T(8,128)(2,1)S(1)} %constant_dynamic-update-slice_fusion.2.right_ref, ...), custom_call_target="tpu_custom_call" | custom-call | tf_op jit(solution)/shard_map/rest/pallas_call | solution.py:17
  83.3 3.6 %collective-permute-start.29 = (f32[8,128]{1,0:T(8,128)S(1)}, f32[8,128]{1,0:T(8,128)S(1)}, u32[]{:S(2)}, u32[]{:S(2)}) collective-permute-start(f32[8,128]{1,0:T(8,128)S(1)} %add.37), channel_id=1, source_target_pairs={{0,8},{4,12},{8,0},{12,4},{16,24},{20,28},{24,16},{28,20},{1,9},{5... | collective-permute-start | bytes 12296 | tf_op jit(solution)/shard_map/ppermute | solution.py:280
  95.9 6.1 %collective-permute-start.39 = (bf16[256,512]{1,0:T(8,128)(2,1)S(1)}, bf16[256,512]{1,0:T(8,128)(2,1)S(1)}, u32[]{:S(2)}, u32[]{:S(2)}) collective-permute-start(bf16[256,512]{1,0:T(8,128)(2,1)S(1)} %collective-permute-done.37.refs_2_), channel_id=1, source_target_pairs={{0,8},{8,16},{16,24},{12,4},{20,12},{28,20},{1,9},{9,17},{17,25},{... | collective-permute-start | bytes 786440 | tf_op jit(solution)/shard_map/ppermute | solution.py:325
  102.6 3.1 %collective-permute-done.33.refs_2_ = bf16[256,512]{1,0:T(8,128)(2,1)S(1)} collective-permute-done((bf16[256,512]{1,0:T(8,128)(2,1)S(1)}, bf16[256,512]{1,0:T(8,128)(2,1)S(1)}, u32[]{:S(2)}, u32[]{:S(2)}) %collective-permute-start.33) | collective-permute-done | bytes 262176 | tf_op jit(solution)/shard_map/ppermute | solution.py:324
  106.3 3.1 %near.5.refs_8_ = f32[2,256,512]{2,1,0:T(8,128)S(1)} custom-call(s32[8]{0:T(128)S(1)} %pad_add_fusion.shifts_ref, bf16[8,2,256,512]{3,2,1,0:T(8,128)(2,1)S(1)} %constant_dynamic-update-slice_fusion.left_ref, bf16[8,512,512]{2,1,0:T(8,128)(2,1)S(1)} %constant_dynamic-update-slice_fusion.2.right_ref, bf16[256,512]{1,0:T(8,128)(2,1)S(1)} %image.8.refs_0_.refs_2_.refs_4_, ...), custom_call_target="tpu_custom_call" | custom-call | tf_op jit(solution)/shard_map/near/pallas_call | solution.py:17
  109.4 2.8 %rest.10.a_ref = bf16[256,512]{1,0:T(8,128)(2,1)S(1)} custom-call(s32[8]{0:T(128)S(1)} %pad_add_fusion.shifts_ref, bf16[8,2,256,512]{3,2,1,0:T(8,128)(2,1)S(1)} %constant_dynamic-update-slice_fusion.left_ref, bf16[8,512,512]{2,1,0:T(8,128)(2,1)S(1)} %constant_dynamic-update-slice_fusion.2.right_ref, bf16[256,512]{1,0:T(8,128)(2,1)S(1)} %image.9.refs_0_.refs_2_.refs_12_, ...), custom_call_target="tpu_custom_call" | custom-call | tf_op jit(solution)/shard_map/rest/pallas_call | solution.py:17
  114.1 4.1 %rest.11.a_ref = bf16[256,512]{1,0:T(8,128)(2,1)S(1)} custom-call(s32[8]{0:T(128)S(1)} %pad_add_fusion.shifts_ref, bf16[8,2,256,512]{3,2,1,0:T(8,128)(2,1)S(1)} %constant_dynamic-update-slice_fusion.left_ref, bf16[8,512,512]{2,1,0:T(8,128)(2,1)S(1)} %constant_dynamic-update-slice_fusion.2.right_ref, bf16[256,512]{1,0:T(8,128)(2,1)S(1)} %image.9.refs_0_.refs_2_.refs_12_, ...), custom_call_target="tpu_custom_call" | custom-call | tf_op jit(solution)/shard_map/rest/pallas_call | solution.py:17
  118.2 2.8 %collective-permute-done.42.b_ref = bf16[256,512]{1,0:T(8,128)(2,1)S(1)} collective-permute-done((bf16[256,512]{1,0:T(8,128)(2,1)S(1)}, bf16[256,512]{1,0:T(8,128)(2,1)S(1)}, u32[]{:S(2)}, u32[]{:S(2)}) %collective-permute-start.42) | collective-permute-done | bytes 262176 | tf_op jit(solution)/shard_map/ppermute | solution.py:350
  122.7 4.0 %collective-permute-done.44.b_ref = bf16[256,512]{1,0:T(8,128)(2,1)S(1)} collective-permute-done((bf16[256,512]{1,0:T(8,128)(2,1)S(1)}, bf16[256,512]{1,0:T(8,128)(2,1)S(1)}, u32[]{:S(2)}, u32[]{:S(2)}) %collective-permute-start.44) | collective-permute-done | bytes 262176 | tf_op jit(solution)/shard_map/ppermute | solution.py:350
  134.2 2.8 %collective-permute-start.48 = (f32[8,128]{1,0:T(8,128)S(1)}, f32[8,128]{1,0:T(8,128)S(1)}, u32[]{:S(2)}, u32[]{:S(2)}) collective-permute-start(f32[8,128]{1,0:T(8,128)S(1)} %add.41), channel_id=1, source_target_pairs={{0,8},{4,12},{8,0},{12,4},{16,24},{20,28},{24,16},{28,20},{1,9},{5... | collective-permute-start | bytes 12296 | tf_op jit(solution)/shard_map/ppermute | solution.py:280
  140.5 2.6 %collective-permute-done.49 = f32[8,128]{1,0:T(8,128)S(1)} collective-permute-done((f32[8,128]{1,0:T(8,128)S(1)}, f32[8,128]{1,0:T(8,128)S(1)}, u32[]{:S(2)}, u32[]{:S(2)}) %collective-permute-start.49) | collective-permute-done | bytes 4128 | tf_op jit(solution)/shard_map/ppermute | solution.py:280
  143.1 3.2 %last.1 = (bf16[2,512,512]{2,1,0:T(8,128)(2,1)}, f32[2,3]{1,0:T(2,128)}) custom-call(s32[16]{0:T(128)S(1)} %copy-done.2, bf16[256,512]{1,0:T(8,128)(2,1)S(1)} %get-tuple-element.27.refs_0_, bf16[256,512]{1,0:T(8,128)(2,1)S(1)} %get-tuple-element.28.refs_1_, bf16[256,512]{1,0:T(8,128)(2,1)S(1)} %get-tuple-element.37.refs_0_.refs_1_.refs_2_, ...), custom_call_target="tpu_custom_call" | custom-call | tf_op jit(solution)/shard_map/last/pallas_call | solution.py:17
  (120 shorter events, 56.7 us)
Async XLA Ops:
  3.1 25.4 %collective-permute-start.1 = (bf16[4,2,256,512]{3,2,1,0:T(8,128)(2,1)S(1)}, bf16[4,2,256,512]{3,2,1,0:T(8,128)(2,1)S(1)}, u32[]{:S(2)}, u32[]{:S(2)}) collective-permute-start(bf16[4,2,256,512]{3,2,1,0:T(8,128)(2,1)S(1)} %get-tuple-element.30), channel_id=1, source_target_pairs={{0,1},{1,0},{2,3},{3,2},{4,5},{5,4},{6,7},{7,6},{8,9},{9,8},{10,11... | collective-permute-start | bytes 6291464 | tf_op jit(solution)/shard_map/ppermute | solution.py:276
  4.4 24.7 %collective-permute-start.2 = (bf16[4,512,512]{2,1,0:T(8,128)(2,1)S(1)}, bf16[4,512,512]{2,1,0:T(8,128)(2,1)S(1)}, u32[]{:S(2)}, u32[]{:S(2)}) collective-permute-start(bf16[4,512,512]{2,1,0:T(8,128)(2,1)S(1)} %copy-done.3), channel_id=1, source_target_pairs={{0,1},{1,0},{2,3},{3,2},{4,5},{5,4},{6,7},{7,6},{8,9},{9,8},{10,11... | collective-permute-start | bytes 6291464 | tf_op jit(solution)/shard_map/ppermute | solution.py:276
  5.8 9.6 %collective-permute-start.3 = (bf16[256,512]{1,0:T(8,128)(2,1)S(1)}, bf16[256,512]{1,0:T(8,128)(2,1)S(1)}, u32[]{:S(2)}, u32[]{:S(2)}) collective-permute-start(bf16[256,512]{1,0:T(8,128)(2,1)S(1)} %get-tuple-element.27.refs_0_), channel_id=1, source_target_pairs={{0,4},{4,0},{8,12},{12,8},{16,20},{20,16},{24,28},{28,24},{1,5},{5... | collective-permute-start | bytes 786440 | tf_op jit(solution)/shard_map/ppermute | solution.py:297
  8.7 9.2 %collective-permute-start = (s32[4]{0:T(128)S(1)}, s32[4]{0:T(128)S(1)}, u32[]{:S(2)}, u32[]{:S(2)}) collective-permute-start(s32[4]{0:T(128)S(1)} %copy-done.4), channel_id=1, source_target_pairs={{0,1},{1,0},{2,3},{3,2},{4,5},{5,4},{6,7},{7,6},{8,9},{9,8},{10,11... | collective-permute-start | bytes 56 | tf_op jit(solution)/shard_map/ppermute | solution.py:276
  15.4 12.5 %collective-permute-start.5 = (bf16[256,512]{1,0:T(8,128)(2,1)S(1)}, bf16[256,512]{1,0:T(8,128)(2,1)S(1)}, u32[]{:S(2)}, u32[]{:S(2)}) collective-permute-start(bf16[256,512]{1,0:T(8,128)(2,1)S(1)} %get-tuple-element.34.refs_0_.refs_8_), channel_id=1, source_target_pairs={{0,4},{4,0},{8,12},{12,8},{16,20},{20,16},{24,28},{28,24},{1,5},{5... | collective-permute-start | bytes 786440 | tf_op jit(solution)/shard_map/ppermute | solution.py:324
  17.2 10.8 %collective-permute-start.7 = (bf16[256,512]{1,0:T(8,128)(2,1)S(1)}, bf16[256,512]{1,0:T(8,128)(2,1)S(1)}, u32[]{:S(2)}, u32[]{:S(2)}) collective-permute-start(bf16[256,512]{1,0:T(8,128)(2,1)S(1)} %get-tuple-element.34.refs_0_.refs_8_), channel_id=1, source_target_pairs={{4,8},{12,16},{20,24},{8,4},{16,12},{24,20},{5,9},{13,17},{21,25},... | collective-permute-start | bytes 786440 | tf_op jit(solution)/shard_map/ppermute | solution.py:326
  17.8 10.6 %collective-permute-start.9 = (bf16[256,512]{1,0:T(8,128)(2,1)S(1)}, bf16[256,512]{1,0:T(8,128)(2,1)S(1)}, u32[]{:S(2)}, u32[]{:S(2)}) collective-permute-start(bf16[256,512]{1,0:T(8,128)(2,1)S(1)} %collective-permute-done.3.refs_2_), channel_id=1, source_target_pairs={{0,8},{8,16},{16,24},{12,4},{20,12},{28,20},{1,9},{9,17},{17,25},{... | collective-permute-start | bytes 786440 | tf_op jit(solution)/shard_map/ppermute | solution.py:325
  34.7 15.4 %collective-permute-start.12 = (bf16[256,512]{1,0:T(8,128)(2,1)S(1)}, bf16[256,512]{1,0:T(8,128)(2,1)S(1)}, u32[]{:S(2)}, u32[]{:S(2)}) collective-permute-start(bf16[256,512]{1,0:T(8,128)(2,1)S(1)} %rest.6.a_ref), channel_id=1, source_target_pairs={{0,2},{1,3},{2,0},{3,1},{4,6},{5,7},{6,4},{7,5},{8,10},{9,11},{10,... | collective-permute-start | bytes 786440 | tf_op jit(solution)/shard_map/ppermute | solution.py:350
  51.0 7.0 %collective-permute-start.22 = (bf16[256,512]{1,0:T(8,128)(2,1)S(1)}, bf16[256,512]{1,0:T(8,128)(2,1)S(1)}, u32[]{:S(2)}, u32[]{:S(2)}) collective-permute-start(bf16[256,512]{1,0:T(8,128)(2,1)S(1)} %get-tuple-element.37.refs_0_.refs_1_.refs_2_), channel_id=1, source_target_pairs={{0,4},{4,0},{8,12},{12,8},{16,20},{20,16},{24,28},{28,24},{1,5},{5... | collective-permute-start | bytes 786440 | tf_op jit(solution)/shard_map/ppermute | solution.py:315
  51.9 12.0 %collective-permute-start.15 = (bf16[256,512]{1,0:T(8,128)(2,1)S(1)}, bf16[256,512]{1,0:T(8,128)(2,1)S(1)}, u32[]{:S(2)}, u32[]{:S(2)}) collective-permute-start(bf16[256,512]{1,0:T(8,128)(2,1)S(1)} %get-tuple-element.37.refs_0_.refs_1_.refs_2_), channel_id=1, source_target_pairs={{0,1},{1,0},{2,3},{3,2},{4,5},{5,4},{6,7},{7,6},{8,9},{9,8},{10,11... | collective-permute-start | bytes 786440 | tf_op jit(solution)/shard_map/ppermute | solution.py:276
  56.4 10.6 %collective-permute-start.18 = (bf16[256,512]{1,0:T(8,128)(2,1)S(1)}, bf16[256,512]{1,0:T(8,128)(2,1)S(1)}, u32[]{:S(2)}, u32[]{:S(2)}) collective-permute-start(bf16[256,512]{1,0:T(8,128)(2,1)S(1)} %get-tuple-element.39.refs_0_.refs_1_.refs_10_), channel_id=1, source_target_pairs={{0,4},{4,0},{8,12},{12,8},{16,20},{20,16},{24,28},{28,24},{1,5},{5... | collective-permute-start | bytes 786440 | tf_op jit(solution)/shard_map/ppermute | solution.py:324
  56.9 10.1 %collective-permute-start.20 = (bf16[256,512]{1,0:T(8,128)(2,1)S(1)}, bf16[256,512]{1,0:T(8,128)(2,1)S(1)}, u32[]{:S(2)}, u32[]{:S(2)}) collective-permute-start(bf16[256,512]{1,0:T(8,128)(2,1)S(1)} %get-tuple-element.39.refs_0_.refs_1_.refs_10_), channel_id=1, source_target_pairs={{4,8},{12,16},{20,24},{8,4},{16,12},{24,20},{5,9},{13,17},{21,25},... | collective-permute-start | bytes 786440 | tf_op jit(solution)/shard_map/ppermute | solution.py:326
  58.0 9.6 %collective-permute-start.23 = (bf16[256,512]{1,0:T(8,128)(2,1)S(1)}, bf16[256,512]{1,0:T(8,128)(2,1)S(1)}, u32[]{:S(2)}, u32[]{:S(2)}) collective-permute-start(bf16[256,512]{1,0:T(8,128)(2,1)S(1)} %collective-permute-done.22.refs_2_), channel_id=1, source_target_pairs={{0,8},{8,16},{16,24},{12,4},{20,12},{28,20},{1,9},{9,17},{17,25},{... | collective-permute-start | bytes 786440 | tf_op jit(solution)/shard_map/ppermute | solution.py:325
  72.9 15.7 %collective-permute-start.26 = (bf16[256,512]{1,0:T(8,128)(2,1)S(1)}, bf16[256,512]{1,0:T(8,128)(2,1)S(1)}, u32[]{:S(2)}, u32[]{:S(2)}) collective-permute-start(bf16[256,512]{1,0:T(8,128)(2,1)S(1)} %rest.8.a_ref), channel_id=1, source_target_pairs={{0,2},{1,3},{2,0},{3,1},{4,6},{5,7},{6,4},{7,5},{8,10},{9,11},{10,... | collective-permute-start | bytes 786440 | tf_op jit(solution)/shard_map/ppermute | solution.py:350
  87.0 6.9 %collective-permute-start.31 = (bf16[256,512]{1,0:T(8,128)(2,1)S(1)}, bf16[256,512]{1,0:T(8,128)(2,1)S(1)}, u32[]{:S(2)}, u32[]{:S(2)}) collective-permute-start(bf16[256,512]{1,0:T(8,128)(2,1)S(1)} %rest.9.a_ref), channel_id=1, source_target_pairs={{0,2},{1,3},{2,0},{3,1},{4,6},{5,7},{6,4},{7,5},{8,10},{9,11},{10,... | collective-permute-start | bytes 786440 | tf_op jit(solution)/shard_map/ppermute | solution.py:350
  91.5 10.5 %collective-permute-start.30 = (bf16[256,512]{1,0:T(8,128)(2,1)S(1)}, bf16[256,512]{1,0:T(8,128)(2,1)S(1)}, u32[]{:S(2)}, u32[]{:S(2)}) collective-permute-start(bf16[256,512]{1,0:T(8,128)(2,1)S(1)} %image.8.refs_0_.refs_2_.refs_4_), channel_id=1, source_target_pairs={{0,1},{1,0},{2,3},{3,2},{4,5},{5,4},{6,7},{7,6},{8,9},{9,8},{10,11... | collective-permute-start | bytes 786440 | tf_op jit(solution)/shard_map/ppermute | solution.py:276
  94.6 11.1 %collective-permute-start.33 = (bf16[256,512]{1,0:T(8,128)(2,1)S(1)}, bf16[256,512]{1,0:T(8,128)(2,1)S(1)}, u32[]{:S(2)}, u32[]{:S(2)}) collective-permute-start(bf16[256,512]{1,0:T(8,128)(2,1)S(1)} %image.9.refs_0_.refs_2_.refs_12_), channel_id=1, source_target_pairs={{0,4},{4,0},{8,12},{12,8},{16,20},{20,16},{24,28},{28,24},{1,5},{5... | collective-permute-start | bytes 786440 | tf_op jit(solution)/shard_map/ppermute | solution.py:324
  94.9 10.8 %collective-permute-start.35 = (bf16[256,512]{1,0:T(8,128)(2,1)S(1)}, bf16[256,512]{1,0:T(8,128)(2,1)S(1)}, u32[]{:S(2)}, u32[]{:S(2)}) collective-permute-start(bf16[256,512]{1,0:T(8,128)(2,1)S(1)} %image.9.refs_0_.refs_2_.refs_12_), channel_id=1, source_target_pairs={{4,8},{12,16},{20,24},{8,4},{16,12},{24,20},{5,9},{13,17},{21,25},... | collective-permute-start | bytes 786440 | tf_op jit(solution)/shard_map/ppermute | solution.py:326
  95.9 10.4 %collective-permute-start.39 = (bf16[256,512]{1,0:T(8,128)(2,1)S(1)}, bf16[256,512]{1,0:T(8,128)(2,1)S(1)}, u32[]{:S(2)}, u32[]{:S(2)}) collective-permute-start(bf16[256,512]{1,0:T(8,128)(2,1)S(1)} %collective-permute-done.37.refs_2_), channel_id=1, source_target_pairs={{0,8},{8,16},{16,24},{12,4},{20,12},{28,20},{1,9},{9,17},{17,25},{... | collective-permute-start | bytes 786440 | tf_op jit(solution)/shard_map/ppermute | solution.py:325
  102.0 7.4 %collective-permute-start.32 = (bf16[256,512]{1,0:T(8,128)(2,1)S(1)}, bf16[256,512]{1,0:T(8,128)(2,1)S(1)}, u32[]{:S(2)}, u32[]{:S(2)}) collective-permute-start(bf16[256,512]{1,0:T(8,128)(2,1)S(1)} %image.9.refs_0_.refs_2_.refs_12_), channel_id=1, source_target_pairs={{0,1},{1,0},{2,3},{3,2},{4,5},{5,4},{6,7},{7,6},{8,9},{9,8},{10,11... | collective-permute-start | bytes 786440 | tf_op jit(solution)/shard_map/ppermute | solution.py:276
  112.2 8.8 %collective-permute-start.42 = (bf16[256,512]{1,0:T(8,128)(2,1)S(1)}, bf16[256,512]{1,0:T(8,128)(2,1)S(1)}, u32[]{:S(2)}, u32[]{:S(2)}) collective-permute-start(bf16[256,512]{1,0:T(8,128)(2,1)S(1)} %rest.10.a_ref), channel_id=1, source_target_pairs={{0,2},{1,3},{2,0},{3,1},{4,6},{5,7},{6,4},{7,5},{8,10},{9,11},{10,... | collective-permute-start | bytes 786440 | tf_op jit(solution)/shard_map/ppermute | solution.py:350
  118.2 8.5 %collective-permute-start.44 = (bf16[256,512]{1,0:T(8,128)(2,1)S(1)}, bf16[256,512]{1,0:T(8,128)(2,1)S(1)}, u32[]{:S(2)}, u32[]{:S(2)}) collective-permute-start(bf16[256,512]{1,0:T(8,128)(2,1)S(1)} %rest.11.a_ref), channel_id=1, source_target_pairs={{0,2},{1,3},{2,0},{3,1},{4,6},{5,7},{6,4},{7,5},{8,10},{9,11},{10,... | collective-permute-start | bytes 786440 | tf_op jit(solution)/shard_map/ppermute | solution.py:350
  128.3 14.8 %collective-permute-start.45 = (bf16[256,512]{1,0:T(8,128)(2,1)S(1)}, bf16[256,512]{1,0:T(8,128)(2,1)S(1)}, u32[]{:S(2)}, u32[]{:S(2)}) collective-permute-start(bf16[256,512]{1,0:T(8,128)(2,1)S(1)} %get-tuple-element.50.refs_14_), channel_id=1, source_target_pairs={{0,1},{1,0},{2,3},{3,2},{4,5},{5,4},{6,7},{7,6},{8,9},{9,8},{10,11... | collective-permute-start | bytes 786440 | tf_op jit(solution)/shard_map/ppermute | solution.py:276
  128.4 14.7 %collective-permute-start.43 = (bf16[256,512]{1,0:T(8,128)(2,1)S(1)}, bf16[256,512]{1,0:T(8,128)(2,1)S(1)}, u32[]{:S(2)}, u32[]{:S(2)}) collective-permute-start(bf16[256,512]{1,0:T(8,128)(2,1)S(1)} %get-tuple-element.48.refs_6_), channel_id=1, source_target_pairs={{0,1},{1,0},{2,3},{3,2},{4,5},{5,4},{6,7},{7,6},{8,9},{9,8},{10,11... | collective-permute-start | bytes 786440 | tf_op jit(solution)/shard_map/ppermute | solution.py:276
  (31 other events, 122.2 us)

commit v4 on v3

--- a/solution.py
+++ b/solution.py
@@ -21,7 +21,7 @@
         in_specs=[SMEM if a.dtype == jnp.int32 else VMEM for a in operands],
         out_specs=jax.tree.map(lambda _: VMEM, out),
         scratch_shapes=scratch,
-        compiler_params=pltpu.CompilerParams(vmem_limit_bytes=24 << 20),
+        compiler_params=pltpu.CompilerParams(vmem_limit_bytes=16 << 20),
         cost_estimate=pl.CostEstimate(flops=0, bytes_accessed=0, transcendentals=0),
     )(*operands)
 
@@ -97,17 +97,20 @@
     write_sums(stats_ref, [square])
 
 
-def split_kernel(left_ref, keep_ref, give_ref):
-    half = keep_ref.shape[2]
-    for w in range(left_ref.shape[0]):
-        for t in range(left_ref.shape[1]):
-            keep_ref[w, t] = left_ref[w, t, half_of(0, half), :]
-            give_ref[w, t] = left_ref[w, t, half_of(1, half), :]
-
-
 def place_of(k):
     pair = jnp.where(lax.axis_index("sec") % 2 == 0, 2, 0)
     return (1, pair, 2 - pair)[k]
+
+
+def stage_kernel(left_ref, right_ref, left_out, right_out, sems):
+    copies = [
+        pltpu.make_async_copy(left_ref, left_out, sems.at[0]),
+        pltpu.make_async_copy(right_ref, right_out, sems.at[1]),
+    ]
+    for copy in copies:
+        copy.start()
+    for copy in copies:
+        copy.wait()
 
 
 def gather_sources(slots, refs, scalars, v_ref):
@@ -123,68 +126,25 @@
             v_ref[slot, half_of(which, half), :] = value
 
 
-def add_terms(chosen, slot, target, shifts_ref, left_ref, right_ref, v_ref, list_ref, acc_ref):
-    count = jnp.int32(0)
-    for w in range(shifts_ref.shape[0]):
-        here = chosen(shifts_ref[w])
-
-        @pl.when(here)
-        def _():
-            list_ref[count] = w
-
-        count = count + here.astype(jnp.int32)
-
-    def product(position):
-        w = list_ref[position]
-        source = v_ref[slot(shifts_ref[w])]
-        part = jnp.dot(left_ref[w, target], source, preferred_element_type=F32).astype(BF16)
-        return jnp.dot(part, right_ref[w], preferred_element_type=F32)
-
-    def two(k, carry):
-        acc_ref[...] += product(2 * k) + product(2 * k + 1)
-        return carry
-
-    lax.fori_loop(0, count >> 1, two, 0)
-
-    @pl.when(count & 1 == 1)
-    def _():
-        acc_ref[...] += product(count - 1)
-
-
-def near_kernel(shifts_ref, left_ref, right_ref, *refs):
-    sources, (*scalars, acc_ref, v_ref, list_ref) = refs[:4], refs[4:]
-    gather_sources((place_of(0), place_of(1)), sources, scalars, v_ref)
+def full_kernel(target, *refs):
+    operators, sources, (*scalars, out_ref, v_ref) = refs[:6], refs[6:18], refs[18:]
+    gather_sources((0, 1, 2, 3, 4, 5), sources, scalars, v_ref)
     far = place_of(2)
-    for target in range(acc_ref.shape[0]):
-        acc_ref[target] = jnp.zeros(acc_ref.shape[1:], F32)
-
-        def place(shift):
-            return ((target - shift) >> 1) + 1
-
-        add_terms(
-            lambda shift: ((target - shift) & 1 == 0) & (place(shift) != far), place,
-            target, shifts_ref, left_ref, right_ref, v_ref, list_ref, acc_ref.at[target],
-        )
-
-
-def rest_kernel(target, shifts_ref, left_ref, right_ref, *refs):
-    sources, sum_ref, (*scalars, out_ref, v_ref, list_ref, acc_ref) = refs[:8], refs[8], refs[9:]
-    places = place_of(0), place_of(1), place_of(2)
-    gather_sources((*places, 3), sources, scalars, v_ref)
-    acc_ref[...] = sum_ref[target]
-
-    def place(shift):
-        return ((target - shift) >> 1) + 1
-
-    def second(shift):
-        return (target - shift) & 1 == 1
-
-    add_terms(
-        lambda shift: second(shift) | (place(shift) == places[2]),
-        lambda shift: jnp.where(second(shift), place(shift), 3),
-        target, shifts_ref, left_ref, right_ref, v_ref, list_ref, acc_ref,
-    )
-    out_ref[...] = acc_ref[...].astype(BF16)
+    half = out_ref.shape[0]
+    total = None
+    for shifts_ref, left_ref, right_ref in (operators[:3], operators[3:]):
+        for w in range(left_ref.shape[0]):
+            offset = target - shifts_ref[w]
+            place = (offset >> 1) + 1
+            kind = jnp.where(place == 1, 0, jnp.where(place == far, 4, 2))
+            part = jnp.dot(
+                left_ref[w, target, half_of(0, half), :],
+                v_ref[kind + (offset & 1)],
+                preferred_element_type=F32,
+            ).astype(BF16)
+            term = jnp.dot(part, right_ref[w], preferred_element_type=F32)
+            total = term if total is None else total + term
+    out_ref[...] = total.astype(BF16)
 
 
 def add_kernel(a_ref, b_ref, out_ref):
@@ -280,14 +240,18 @@
             stats = stats + lax.ppermute(stats, "sec", [(i, i ^ bit) for i in range(n_sec)])
         return stats
 
+    def sum_pairs(stats):
+        crossed = [(i, i ^ 1 ^ n_op) for i in range(n_op * n_sec)]
+        core = lax.ppermute(stats, "op", core_pairs)
+        pair = lax.ppermute(stats, "sec", pairs)
+        cross = lax.ppermute(stats, ("sec", "op"), crossed)
+        return (stats + cross) + (core + pair)
+
     bits = [1 << k for k in range(n_sec.bit_length() - 1)]
 
     half_type = jax.ShapeDtypeStruct((half, columns), BF16)
     stats_type = jax.ShapeDtypeStruct((8, 128), F32)
-    acc_type = jax.ShapeDtypeStruct((sectors, half, columns), F32)
-    terms = 2 * left_blocks.shape[0]
-    term_scratch = [pltpu.VMEM((4, block_rows, columns), BF16), pltpu.SMEM((terms,), jnp.int32)]
-    acc_scratch = pltpu.VMEM((half, columns), F32)
+    v_scratch = pltpu.VMEM((6, block_rows, columns), BF16)
 
     *halves, sums = call(
         start_kernel, "start", [half_type] * (2 * sectors) + [stats_type], [],
@@ -295,19 +259,11 @@
     )
     basis = [[(halves[0], halves[1]), (halves[2], halves[3])]]
     pair_0 = lax.ppermute(halves[0], "sec", pairs)
-    start_sums = flipped_sum(sums, bits[:1])
-    half_left = jax.ShapeDtypeStruct((terms // 2, sectors, half, block_rows), BF16)
-    keep, give = call(split_kernel, "split", [half_left] * 2, [], left_blocks)
-    operators = [
-        jnp.concatenate([mine, other])
-        for mine, other in (
-            (charge_shifts, across_cores(charge_shifts)),
-            (keep, across_cores(give)),
-            (right_blocks, across_cores(right_blocks)),
-        )
-    ]
+    start_sums = flipped_sum(sums, bits[1:])
+    operators = (charge_shifts, left_blocks, right_blocks)
+    others = tuple(across_cores(value) for value in operators)
     stats = []
-    pair_0 = after(pair_0, start_sums, keep)
+    pair_0 = after(pair_0, start_sums)
 
     for product in range(3):
         (mine_0, other_0), (mine_1, other_1) = basis[-1]
@@ -318,24 +274,44 @@
         else:
             mine_1 = after(mine_1, pair_0)
         if product == 2:
-            image_sums = flipped_sum(after(image_sums, mine_0), bits[2:])
+            image_sums = flipped_sum(after(image_sums, mine_0), bits[1:2])
             pair_0 = after(pair_0, image_sums)
-            stats.append(image_sums)
         pair_1 = lax.ppermute(mine_1, "sec", pairs)
+        if product == 0:
+            hbm = pl.BlockSpec(memory_space=pltpu.HBM)
+            left, right = pl.pallas_call(
+                stage_kernel,
+                name="stage",
+                out_shape=[jax.ShapeDtypeStruct(v.shape, v.dtype) for v in operators[1:]],
+                in_specs=[hbm] * 2,
+                out_specs=[VMEM] * 2,
+                scratch_shapes=[pltpu.SemaphoreType.DMA((2,))],
+                compiler_params=pltpu.CompilerParams(vmem_limit_bytes=16 << 20),
+                cost_estimate=pl.CostEstimate(flops=0, bytes_accessed=0, transcendentals=0),
+            )(after(operators[1], pair_0), operators[2])
+            operators = (charge_shifts, left, right) + others
+            pair_1 = after(pair_1, left)
         far_0 = lax.ppermute(pair_0, "sec", onward)
         far_1 = lax.ppermute(mine_1, "sec", diagonal)
+        if product == 0:
+            start_sums = flipped_sum(after(start_sums, pair_0), bits[:1])
+            stats.append(start_sums)
+            pair_1 = after(pair_1, start_sums)
+        elif product == 1:
+            image_sums = flipped_sum(sums + across_cores(sums), bits[:1])
+            pair_1 = after(pair_1, image_sums)
+        else:
+            image_sums = flipped_sum(after(image_sums, pair_0), bits[2:])
+            stats.append(image_sums)
+            pair_1 = after(pair_1, image_sums)
         scalars = (sector_rows, *stats) if product == 2 else ()
-        acc = call(
-            near_kernel, "near", acc_type, term_scratch, *operators,
-            mine_0, other_0, pair_0, across_cores(pair_0), *scalars,
-        )
-        sources = [mine_1, other_1]
-        for part in (pair_1, far_1, far_0):
+        sources = [mine_0, other_0, mine_1, other_1]
+        for part in (pair_0, pair_1, far_0, far_1):
             sources += [part, across_cores(part)]
         values = [
             call(
-                functools.partial(rest_kernel, t), "rest", half_type,
-                term_scratch + [acc_scratch], *operators, *sources, acc, *scalars,
+                functools.partial(full_kernel, t), "full", half_type,
+                [v_scratch], *operators, *sources, *scalars,
             )
             for t in range(sectors)
         ]
@@ -348,13 +324,7 @@
                 value = call(add_kernel, "add", half_type, [], value, arrived)
                 bit *= 2
             arrived = lax.ppermute(value, "op", [(i, i ^ bit) for i in range(n_op)])
-            if t == 0 and product == 0:
-                stats.append(flipped_sum(after(start_sums, values[-1]), bits[1:]))
-            elif t == 0 and product == 1:
-                image_sums = sums + across_cores(sums)
-                image_sums = flipped_sum(after(image_sums, values[-1]), bits[:2])
-                arrived = after(arrived, image_sums)
-            elif t == 0:
+            if t == 0:
                 arrived = after(arrived, values[-1])
             out = [half_type] if product == 1 else [half_type, stats_type]
             needed = () if product == 1 else (*[b[t][0] for b in basis], *stats, *earlier)
@@ -366,7 +336,7 @@
         basis.append(image)
         if earlier:
             sums = earlier[0]
-    stats.append(flipped_sum(sums + across_cores(sums), bits))
+    stats.append(flipped_sum(sum_pairs(sums), bits[1:]))
 
     flat = [h for t in range(sectors) for b in basis for h in b[t]]
     vector_type = jax.ShapeDtypeStruct(wavefunction.shape, BF16)

time: 146 us -> 142 us (0.973)
  Pallas kernels: 38.6 us -> 33.6 us
  waiting for transfers between devices: 46.3 us -> 43.2 us
  local copies, waits for them, and re-layouts: 3.59 us -> 5.66 us
  starting transfers between devices: 56.7 us -> 58.2 us
    ppermute x3, waiting for transfers between devices: 10.7 us -> 1.59 us  [on_device(): pair_1 = lax.ppermute(mine_1, 'sec', pairs)]
    ppermute x9 -> x8, starting transfers between devices: 20.1 us -> 13.3 us  [flipped_sum(): lax.ppermute(stats, 'sec', [(i, i ^ bit) for i in range(n_sec)])]
    ppermute x3, starting transfers between devices: 2.58 us -> 8.51 us  [on_device(): pair_1 = lax.ppermute(mine_1, 'sec', pairs)]
    pallas_call x18 -> x14, Pallas kernels: 38.6 us -> 33.2 us  [call(): pl.pallas_call(kernel, name=name, out_shape=out, in_specs=[SMEM if a.dtyp...]
    ppermute x2, starting transfers between devices: 0.89 us -> 5.9 us  [on_device(): pair_0 = lax.ppermute(mine_0, 'sec', pairs)]
    ppermute x3, starting transfers between devices: 16.7 us -> 11.9 us  [on_device(): far_0 = lax.ppermute(pair_0, 'sec', onward)]
    ppermute x23 -> x22, waiting for transfers between devices: 2.57 us -> 7.21 us  [across_cores(): return lax.ppermute(value, 'op', core_pairs)]
    ppermute x0 -> x3, waiting for transfers between devices: none -> 3 us  [the longest x1 1.61 us: sum_pairs(): cross = lax.ppermute(stats, ('sec', 'op'), crossed)]
  transfers between devices with their start and end apart: 50 -> 51, of which waited for: 21 -> 27; matrix products, arithmetic and copies ran while one was open for 1% -> 0% of each run, Pallas kernels for 18% -> 13%
where the time goes in v4:
time: 142 us
  starting transfers between devices  58.2 us (41%)
  waiting for transfers between devices  43.2 us (30%)
  Pallas kernels  33.6 us (24%)
  local copies, waits for them, and re-layouts  5.66 us (4%)
    pallas_call x14, Pallas kernels, call(): pl.pallas_call(kernel, name=name, out_shape=out, in_specs=[SMEM if a.dtyp...  33.2 us
    ppermute x8, waiting for transfers between devices, flipped_sum(): lax.ppermute(stats, 'sec', [(i, i ^ bit) for i in range(n_sec)])  17.7 us
    ppermute x6, waiting for transfers between devices, on_device(): arrived = lax.ppermute(value, 'op', [(i, i ^ bit) for i in range(n_op)])  13.8 us
    ppermute x8, starting transfers between devices, flipped_sum(): lax.ppermute(stats, 'sec', [(i, i ^ bit) for i in range(n_sec)])  13.3 us
    ppermute x3, starting transfers between devices, on_device(): far_0 = lax.ppermute(pair_0, 'sec', onward)  11.9 us
    ppermute x3, starting transfers between devices, on_device(): pair_1 = lax.ppermute(mine_1, 'sec', pairs)  8.51 us
    ppermute x22, waiting for transfers between devices, across_cores(): return lax.ppermute(value, 'op', core_pairs)  7.21 us
    ppermute x6, starting transfers between devices, on_device(): arrived = lax.ppermute(value, 'op', [(i, i ^ bit) for i in range(n_op)])  6.49 us
  transfers between devices with their start and end apart: 51, of which 27 were waited for; matrix products, arithmetic and copies ran while one was open for 0% of the time, Pallas kernels for 13%

profile of v4, /device:TPU:0, one launch (start us, length us, event | category | flops | bytes accessed | tf_op | source)
XLA Modules:
  0.0 141.7 jit_solution(14937099202275192027)
XLA Ops:
  4.1 3.0 %collective-permute-start = (bf16[256,512]{1,0:T(8,128)(2,1)S(1)}, bf16[256,512]{1,0:T(8,128)(2,1)S(1)}, u32[]{:S(2)}, u32[]{:S(2)}) collective-permute-start(bf16[256,512]{1,0:T(8,128)(2,1)S(1)} %get-tuple-element.33.refs_6_.refs_0_), channel_id=1, source_target_pairs={{0,4},{4,0},{8,12},{12,8},{16,20},{20,16},{24,28},{28,24},{1,5},{5... | collective-permute-start | bytes 786440 | tf_op jit(solution)/shard_map/ppermute | solution.py:261
  10.6 2.6 %collective-permute-start.2 = (f32[8,128]{1,0:T(8,128)S(1)}, f32[8,128]{1,0:T(8,128)S(1)}, u32[]{:S(2)}, u32[]{:S(2)}) collective-permute-start(f32[8,128]{1,0:T(8,128)S(1)} %add.36), channel_id=1, source_target_pairs={{0,16},{4,20},{8,24},{12,28},{16,0},{20,4},{24,8},{28,12},{1,17},{... | collective-permute-start | bytes 12296 | tf_op jit(solution)/shard_map/ppermute | solution.py:240
  19.1 2.5 %collective-permute-done.8 = f32[8,128]{1,0:T(8,128)S(1)} collective-permute-done((f32[8,128]{1,0:T(8,128)S(1)}, f32[8,128]{1,0:T(8,128)S(1)}, u32[]{:S(2)}, u32[]{:S(2)}) %collective-permute-start.8) | collective-permute-done | bytes 4128 | tf_op jit(solution)/shard_map/ppermute | solution.py:240
  21.6 3.5 %collective-permute-start.10 = (bf16[256,512]{1,0:T(8,128)(2,1)S(1)}, bf16[256,512]{1,0:T(8,128)(2,1)S(1)}, u32[]{:S(2)}, u32[]{:S(2)}) collective-permute-start(bf16[256,512]{1,0:T(8,128)(2,1)S(1)} %collective-permute-done.refs_10_), channel_id=1, source_target_pairs={{0,8},{8,16},{16,24},{12,4},{20,12},{28,20},{1,9},{9,17},{17,25},{... | collective-permute-start | bytes 786440 | tf_op jit(solution)/shard_map/ppermute | solution.py:294
  31.9 3.7 %full.6.a_ref = bf16[256,512]{1,0:T(8,128)(2,1)S(1)} custom-call(s32[4]{0:T(128)S(1)} %copy-done.5, bf16[4,2,512,512]{3,2,1,0:T(8,128)(2,1)S(1)} %get-tuple-element.38.refs_1_, bf16[4,512,512]{2,1,0:T(8,128)(2,1)S(1)} %get-tuple-element.39.refs_2_, s32[4]{0:T(128)S(1)} %collective-permute-done.3.refs_3_, ...), custom_call_target="tpu_custom_call" | custom-call | tf_op jit(solution)/shard_map/full/pallas_call | solution.py:17
  37.2 3.7 %full.7.a_ref = bf16[256,512]{1,0:T(8,128)(2,1)S(1)} custom-call(s32[4]{0:T(128)S(1)} %copy-done.5, bf16[4,2,512,512]{3,2,1,0:T(8,128)(2,1)S(1)} %get-tuple-element.38.refs_1_, bf16[4,512,512]{2,1,0:T(8,128)(2,1)S(1)} %get-tuple-element.39.refs_2_, s32[4]{0:T(128)S(1)} %collective-permute-done.3.refs_3_, ...), custom_call_target="tpu_custom_call" | custom-call | tf_op jit(solution)/shard_map/full/pallas_call | solution.py:17
  41.5 3.3 %collective-permute-done.14.b_ref = bf16[256,512]{1,0:T(8,128)(2,1)S(1)} collective-permute-done((bf16[256,512]{1,0:T(8,128)(2,1)S(1)}, bf16[256,512]{1,0:T(8,128)(2,1)S(1)}, u32[]{:S(2)}, u32[]{:S(2)}) %collective-permute-start.14) | collective-permute-done | bytes 262176 | tf_op jit(solution)/shard_map/ppermute | solution.py:326
  45.7 3.3 %collective-permute-start.18 = (bf16[256,512]{1,0:T(8,128)(2,1)S(1)}, bf16[256,512]{1,0:T(8,128)(2,1)S(1)}, u32[]{:S(2)}, u32[]{:S(2)}) collective-permute-start(bf16[256,512]{1,0:T(8,128)(2,1)S(1)} %get-tuple-element.47.refs_6_.refs_1_.refs_2_), channel_id=1, source_target_pairs={{0,4},{4,0},{8,12},{12,8},{16,20},{20,16},{24,28},{28,24},{1,5},{5... | collective-permute-start | bytes 786440 | tf_op jit(solution)/shard_map/ppermute | solution.py:271
  50.7 3.3 %collective-permute-start.20 = (bf16[256,512]{1,0:T(8,128)(2,1)S(1)}, bf16[256,512]{1,0:T(8,128)(2,1)S(1)}, u32[]{:S(2)}, u32[]{:S(2)}) collective-permute-start(bf16[256,512]{1,0:T(8,128)(2,1)S(1)} %get-tuple-element.49.refs_8_.refs_1_.refs_10_), channel_id=1, source_target_pairs={{0,4},{4,0},{8,12},{12,8},{16,20},{20,16},{24,28},{28,24},{1,5},{5... | collective-permute-start | bytes 786440 | tf_op jit(solution)/shard_map/ppermute | solution.py:279
  54.7 4.7 %collective-permute-start.24 = (bf16[256,512]{1,0:T(8,128)(2,1)S(1)}, bf16[256,512]{1,0:T(8,128)(2,1)S(1)}, u32[]{:S(2)}, u32[]{:S(2)}) collective-permute-start(bf16[256,512]{1,0:T(8,128)(2,1)S(1)} %collective-permute-done.18.refs_10_), channel_id=1, source_target_pairs={{0,8},{8,16},{16,24},{12,4},{20,12},{28,20},{1,9},{9,17},{17,25},{... | collective-permute-start | bytes 786440 | tf_op jit(solution)/shard_map/ppermute | solution.py:294
  61.5 3.5 %collective-permute-done.22 = f32[8,128]{1,0:T(8,128)S(1)} collective-permute-done((f32[8,128]{1,0:T(8,128)S(1)}, f32[8,128]{1,0:T(8,128)S(1)}, u32[]{:S(2)}, u32[]{:S(2)}) %collective-permute-start.22) | collective-permute-done | bytes 4128 | tf_op jit(solution)/shard_map/ppermute | solution.py:240
  68.0 3.7 %full.8.a_ref = bf16[256,512]{1,0:T(8,128)(2,1)S(1)} custom-call(s32[4]{0:T(128)S(1)} %copy-done.5, bf16[4,2,512,512]{3,2,1,0:T(8,128)(2,1)S(1)} %get-tuple-element.38.refs_1_, bf16[4,512,512]{2,1,0:T(8,128)(2,1)S(1)} %get-tuple-element.39.refs_2_, s32[4]{0:T(128)S(1)} %collective-permute-done.3.refs_3_, ...), custom_call_target="tpu_custom_call" | custom-call | tf_op jit(solution)/shard_map/full/pallas_call | solution.py:17
  73.1 3.7 %full.9.a_ref = bf16[256,512]{1,0:T(8,128)(2,1)S(1)} custom-call(s32[4]{0:T(128)S(1)} %copy-done.5, bf16[4,2,512,512]{3,2,1,0:T(8,128)(2,1)S(1)} %get-tuple-element.38.refs_1_, bf16[4,512,512]{2,1,0:T(8,128)(2,1)S(1)} %get-tuple-element.39.refs_2_, s32[4]{0:T(128)S(1)} %collective-permute-done.3.refs_3_, ...), custom_call_target="tpu_custom_call" | custom-call | tf_op jit(solution)/shard_map/full/pallas_call | solution.py:17
  77.6 3.4 %collective-permute-done.28.b_ref = bf16[256,512]{1,0:T(8,128)(2,1)S(1)} collective-permute-done((bf16[256,512]{1,0:T(8,128)(2,1)S(1)}, bf16[256,512]{1,0:T(8,128)(2,1)S(1)}, u32[]{:S(2)}, u32[]{:S(2)}) %collective-permute-start.28) | collective-permute-done | bytes 262176 | tf_op jit(solution)/shard_map/ppermute | solution.py:326
  81.6 2.6 %collective-permute-start.32 = (bf16[256,512]{1,0:T(8,128)(2,1)S(1)}, bf16[256,512]{1,0:T(8,128)(2,1)S(1)}, u32[]{:S(2)}, u32[]{:S(2)}) collective-permute-start(bf16[256,512]{1,0:T(8,128)(2,1)S(1)} %image.8.refs_6_.refs_2_.refs_4_), channel_id=1, source_target_pairs={{0,4},{4,0},{8,12},{12,8},{16,20},{20,16},{24,28},{28,24},{1,5},{5... | collective-permute-start | bytes 786440 | tf_op jit(solution)/shard_map/ppermute | solution.py:271
  87.1 5.0 %collective-permute-start.35 = (bf16[256,512]{1,0:T(8,128)(2,1)S(1)}, bf16[256,512]{1,0:T(8,128)(2,1)S(1)}, u32[]{:S(2)}, u32[]{:S(2)}) collective-permute-start(bf16[256,512]{1,0:T(8,128)(2,1)S(1)} %image.9.refs_8_.refs_2_.refs_12_), channel_id=1, source_target_pairs={{0,4},{4,0},{8,12},{12,8},{16,20},{20,16},{24,28},{28,24},{1,5},{5... | collective-permute-start | bytes 786440 | tf_op jit(solution)/shard_map/ppermute | solution.py:279
  92.2 3.7 %collective-permute-start.38 = (bf16[256,512]{1,0:T(8,128)(2,1)S(1)}, bf16[256,512]{1,0:T(8,128)(2,1)S(1)}, u32[]{:S(2)}, u32[]{:S(2)}) collective-permute-start(bf16[256,512]{1,0:T(8,128)(2,1)S(1)} %collective-permute-done.32.refs_10_), channel_id=1, source_target_pairs={{0,8},{8,16},{16,24},{12,4},{20,12},{28,20},{1,9},{9,17},{17,25},{... | collective-permute-start | bytes 786440 | tf_op jit(solution)/shard_map/ppermute | solution.py:294
  97.1 3.3 %collective-permute-done.36 = f32[8,128]{1,0:T(8,128)S(1)} collective-permute-done((f32[8,128]{1,0:T(8,128)S(1)}, f32[8,128]{1,0:T(8,128)S(1)}, u32[]{:S(2)}, u32[]{:S(2)}) %collective-permute-start.36) | collective-permute-done | bytes 4128 | tf_op jit(solution)/shard_map/ppermute | solution.py:240
  104.8 4.0 %full.10.a_ref = bf16[256,512]{1,0:T(8,128)(2,1)S(1)} custom-call(s32[4]{0:T(128)S(1)} %copy-done.5, bf16[4,2,512,512]{3,2,1,0:T(8,128)(2,1)S(1)} %get-tuple-element.38.refs_1_, bf16[4,512,512]{2,1,0:T(8,128)(2,1)S(1)} %get-tuple-element.39.refs_2_, s32[4]{0:T(128)S(1)} %collective-permute-done.3.refs_3_, ...), custom_call_target="tpu_custom_call" | custom-call | tf_op jit(solution)/shard_map/full/pallas_call | solution.py:17
  110.0 4.0 %full.11.a_ref = bf16[256,512]{1,0:T(8,128)(2,1)S(1)} custom-call(s32[4]{0:T(128)S(1)} %copy-done.5, bf16[4,2,512,512]{3,2,1,0:T(8,128)(2,1)S(1)} %get-tuple-element.38.refs_1_, bf16[4,512,512]{2,1,0:T(8,128)(2,1)S(1)} %get-tuple-element.39.refs_2_, s32[4]{0:T(128)S(1)} %collective-permute-done.3.refs_3_, ...), custom_call_target="tpu_custom_call" | custom-call | tf_op jit(solution)/shard_map/full/pallas_call | solution.py:17
  115.0 2.8 %collective-permute-done.42.b_ref = bf16[256,512]{1,0:T(8,128)(2,1)S(1)} collective-permute-done((bf16[256,512]{1,0:T(8,128)(2,1)S(1)}, bf16[256,512]{1,0:T(8,128)(2,1)S(1)}, u32[]{:S(2)}, u32[]{:S(2)}) %collective-permute-start.42) | collective-permute-done | bytes 262176 | tf_op jit(solution)/shard_map/ppermute | solution.py:326
  119.5 3.3 %collective-permute-done.44.b_ref = bf16[256,512]{1,0:T(8,128)(2,1)S(1)} collective-permute-done((bf16[256,512]{1,0:T(8,128)(2,1)S(1)}, bf16[256,512]{1,0:T(8,128)(2,1)S(1)}, u32[]{:S(2)}, u32[]{:S(2)}) %collective-permute-start.44) | collective-permute-done | bytes 262176 | tf_op jit(solution)/shard_map/ppermute | solution.py:326
  124.6 2.5 %collective-permute-start.48 = (f32[8,128]{1,0:T(8,128)S(1)}, f32[8,128]{1,0:T(8,128)S(1)}, u32[]{:S(2)}, u32[]{:S(2)}) collective-permute-start(f32[8,128]{1,0:T(8,128)S(1)} %get-tuple-element.63), channel_id=1, source_target_pairs={{0,4},{4,0},{8,12},{12,8},{16,20},{20,16},{24,28},{28,24},{1,5},{5... | collective-permute-start | bytes 12296 | tf_op jit(solution)/shard_map/ppermute | solution.py:246
  138.5 3.2 %last.1 = (bf16[2,512,512]{2,1,0:T(8,128)(2,1)}, f32[2,3]{1,0:T(2,128)}) custom-call(s32[16]{0:T(128)S(1)} %copy-done.4, bf16[256,512]{1,0:T(8,128)(2,1)S(1)} %get-tuple-element.33.refs_6_.refs_0_, bf16[256,512]{1,0:T(8,128)(2,1)S(1)} %get-tuple-element.34.refs_7_.refs_1_, bf16[256,512]{1,0:T(8,128)(2,1)S(1)} %get-tuple-element.47.refs_6_.refs_1_.refs_2_, ...), custom_call_target="tpu_custom_call" | custom-call | tf_op jit(solution)/shard_map/last/pallas_call | solution.py:17
  (115 shorter events, 58.5 us)
Async XLA Ops:
  0.6 31.3 %collective-permute-start.4 = (bf16[4,2,512,512]{3,2,1,0:T(8,128)(2,1)}, bf16[4,2,512,512]{3,2,1,0:T(8,128)(2,1)S(1)}, u32[]{:S(2)}, u32[]{:S(2)}) collective-permute-start(bf16[4,2,512,512]{3,2,1,0:T(8,128)(2,1)} %left_ref), channel_id=1, source_target_pairs={{0,1},{1,0},{2,3},{3,2},{4,5},{5,4},{6,7},{7,6},{8,9},{9,8},{10,11... | collective-permute-start | bytes 12582920 | tf_op jit(solution)/shard_map/ppermute | solution.py:236
  1.1 30.7 %collective-permute-start.5 = (bf16[4,512,512]{2,1,0:T(8,128)(2,1)}, bf16[4,512,512]{2,1,0:T(8,128)(2,1)S(1)}, u32[]{:S(2)}, u32[]{:S(2)}) collective-permute-start(bf16[4,512,512]{2,1,0:T(8,128)(2,1)} %right_ref.1), channel_id=1, source_target_pairs={{0,1},{1,0},{2,3},{3,2},{4,5},{5,4},{6,7},{7,6},{8,9},{9,8},{10,11... | collective-permute-start | bytes 6291464 | tf_op jit(solution)/shard_map/ppermute | solution.py:236
  4.1 11.1 %collective-permute-start = (bf16[256,512]{1,0:T(8,128)(2,1)S(1)}, bf16[256,512]{1,0:T(8,128)(2,1)S(1)}, u32[]{:S(2)}, u32[]{:S(2)}) collective-permute-start(bf16[256,512]{1,0:T(8,128)(2,1)S(1)} %get-tuple-element.33.refs_6_.refs_0_), channel_id=1, source_target_pairs={{0,4},{4,0},{8,12},{12,8},{16,20},{20,16},{24,28},{28,24},{1,5},{5... | collective-permute-start | bytes 786440 | tf_op jit(solution)/shard_map/ppermute | solution.py:261
  15.2 9.9 %collective-permute-start.7 = (bf16[256,512]{1,0:T(8,128)(2,1)S(1)}, bf16[256,512]{1,0:T(8,128)(2,1)S(1)}, u32[]{:S(2)}, u32[]{:S(2)}) collective-permute-start(bf16[256,512]{1,0:T(8,128)(2,1)S(1)} %get-tuple-element.41.refs_8_.refs_0_), channel_id=1, source_target_pairs={{0,4},{4,0},{8,12},{12,8},{16,20},{20,16},{24,28},{28,24},{1,5},{5... | collective-permute-start | bytes 786440 | tf_op jit(solution)/shard_map/ppermute | solution.py:279
  18.4 11.0 %collective-permute-start.12 = (bf16[256,512]{1,0:T(8,128)(2,1)S(1)}, bf16[256,512]{1,0:T(8,128)(2,1)S(1)}, u32[]{:S(2)}, u32[]{:S(2)}) collective-permute-start(bf16[256,512]{1,0:T(8,128)(2,1)S(1)} %get-tuple-element.41.refs_8_.refs_0_), channel_id=1, source_target_pairs={{4,8},{12,16},{20,24},{8,4},{16,12},{24,20},{5,9},{13,17},{21,25},... | collective-permute-start | bytes 786440 | tf_op jit(solution)/shard_map/ppermute | solution.py:295
  21.6 8.4 %collective-permute-start.10 = (bf16[256,512]{1,0:T(8,128)(2,1)S(1)}, bf16[256,512]{1,0:T(8,128)(2,1)S(1)}, u32[]{:S(2)}, u32[]{:S(2)}) collective-permute-start(bf16[256,512]{1,0:T(8,128)(2,1)S(1)} %collective-permute-done.refs_10_), channel_id=1, source_target_pairs={{0,8},{8,16},{16,24},{12,4},{20,12},{28,20},{1,9},{9,17},{17,25},{... | collective-permute-start | bytes 786440 | tf_op jit(solution)/shard_map/ppermute | solution.py:294
  35.6 9.2 %collective-permute-start.14 = (bf16[256,512]{1,0:T(8,128)(2,1)S(1)}, bf16[256,512]{1,0:T(8,128)(2,1)S(1)}, u32[]{:S(2)}, u32[]{:S(2)}) collective-permute-start(bf16[256,512]{1,0:T(8,128)(2,1)S(1)} %full.6.a_ref), channel_id=1, source_target_pairs={{0,2},{1,3},{2,0},{3,1},{4,6},{5,7},{6,4},{7,5},{8,10},{9,11},{10,... | collective-permute-start | bytes 786440 | tf_op jit(solution)/shard_map/ppermute | solution.py:326
  40.9 9.0 %collective-permute-start.16 = (bf16[256,512]{1,0:T(8,128)(2,1)S(1)}, bf16[256,512]{1,0:T(8,128)(2,1)S(1)}, u32[]{:S(2)}, u32[]{:S(2)}) collective-permute-start(bf16[256,512]{1,0:T(8,128)(2,1)S(1)} %full.7.a_ref), channel_id=1, source_target_pairs={{0,2},{1,3},{2,0},{3,1},{4,6},{5,7},{6,4},{7,5},{8,10},{9,11},{10,... | collective-permute-start | bytes 786440 | tf_op jit(solution)/shard_map/ppermute | solution.py:326
  45.7 9.0 %collective-permute-start.18 = (bf16[256,512]{1,0:T(8,128)(2,1)S(1)}, bf16[256,512]{1,0:T(8,128)(2,1)S(1)}, u32[]{:S(2)}, u32[]{:S(2)}) collective-permute-start(bf16[256,512]{1,0:T(8,128)(2,1)S(1)} %get-tuple-element.47.refs_6_.refs_1_.refs_2_), channel_id=1, source_target_pairs={{0,4},{4,0},{8,12},{12,8},{16,20},{20,16},{24,28},{28,24},{1,5},{5... | collective-permute-start | bytes 786440 | tf_op jit(solution)/shard_map/ppermute | solution.py:271
  50.7 14.3 %collective-permute-start.20 = (bf16[256,512]{1,0:T(8,128)(2,1)S(1)}, bf16[256,512]{1,0:T(8,128)(2,1)S(1)}, u32[]{:S(2)}, u32[]{:S(2)}) collective-permute-start(bf16[256,512]{1,0:T(8,128)(2,1)S(1)} %get-tuple-element.49.refs_8_.refs_1_.refs_10_), channel_id=1, source_target_pairs={{0,4},{4,0},{8,12},{12,8},{16,20},{20,16},{24,28},{28,24},{1,5},{5... | collective-permute-start | bytes 786440 | tf_op jit(solution)/shard_map/ppermute | solution.py:279
  54.0 11.5 %collective-permute-start.15 = (bf16[256,512]{1,0:T(8,128)(2,1)S(1)}, bf16[256,512]{1,0:T(8,128)(2,1)S(1)}, u32[]{:S(2)}, u32[]{:S(2)}) collective-permute-start(bf16[256,512]{1,0:T(8,128)(2,1)S(1)} %get-tuple-element.47.refs_6_.refs_1_.refs_2_), channel_id=1, source_target_pairs={{0,1},{1,0},{2,3},{3,2},{4,5},{5,4},{6,7},{7,6},{8,9},{9,8},{10,11... | collective-permute-start | bytes 786440 | tf_op jit(solution)/shard_map/ppermute | solution.py:236
  54.0 11.6 %collective-permute-start.26 = (bf16[256,512]{1,0:T(8,128)(2,1)S(1)}, bf16[256,512]{1,0:T(8,128)(2,1)S(1)}, u32[]{:S(2)}, u32[]{:S(2)}) collective-permute-start(bf16[256,512]{1,0:T(8,128)(2,1)S(1)} %get-tuple-element.49.refs_8_.refs_1_.refs_10_), channel_id=1, source_target_pairs={{4,8},{12,16},{20,24},{8,4},{16,12},{24,20},{5,9},{13,17},{21,25},... | collective-permute-start | bytes 786440 | tf_op jit(solution)/shard_map/ppermute | solution.py:295
  54.7 11.3 %collective-permute-start.24 = (bf16[256,512]{1,0:T(8,128)(2,1)S(1)}, bf16[256,512]{1,0:T(8,128)(2,1)S(1)}, u32[]{:S(2)}, u32[]{:S(2)}) collective-permute-start(bf16[256,512]{1,0:T(8,128)(2,1)S(1)} %collective-permute-done.18.refs_10_), channel_id=1, source_target_pairs={{0,8},{8,16},{16,24},{12,4},{20,12},{28,20},{1,9},{9,17},{17,25},{... | collective-permute-start | bytes 786440 | tf_op jit(solution)/shard_map/ppermute | solution.py:294
  71.7 9.2 %collective-permute-start.28 = (bf16[256,512]{1,0:T(8,128)(2,1)S(1)}, bf16[256,512]{1,0:T(8,128)(2,1)S(1)}, u32[]{:S(2)}, u32[]{:S(2)}) collective-permute-start(bf16[256,512]{1,0:T(8,128)(2,1)S(1)} %full.8.a_ref), channel_id=1, source_target_pairs={{0,2},{1,3},{2,0},{3,1},{4,6},{5,7},{6,4},{7,5},{8,10},{9,11},{10,... | collective-permute-start | bytes 786440 | tf_op jit(solution)/shard_map/ppermute | solution.py:326
  76.8 9.0 %collective-permute-start.30 = (bf16[256,512]{1,0:T(8,128)(2,1)S(1)}, bf16[256,512]{1,0:T(8,128)(2,1)S(1)}, u32[]{:S(2)}, u32[]{:S(2)}) collective-permute-start(bf16[256,512]{1,0:T(8,128)(2,1)S(1)} %full.9.a_ref), channel_id=1, source_target_pairs={{0,2},{1,3},{2,0},{3,1},{4,6},{5,7},{6,4},{7,5},{8,10},{9,11},{10,... | collective-permute-start | bytes 786440 | tf_op jit(solution)/shard_map/ppermute | solution.py:326
  81.6 10.6 %collective-permute-start.32 = (bf16[256,512]{1,0:T(8,128)(2,1)S(1)}, bf16[256,512]{1,0:T(8,128)(2,1)S(1)}, u32[]{:S(2)}, u32[]{:S(2)}) collective-permute-start(bf16[256,512]{1,0:T(8,128)(2,1)S(1)} %image.8.refs_6_.refs_2_.refs_4_), channel_id=1, source_target_pairs={{0,4},{4,0},{8,12},{12,8},{16,20},{20,16},{24,28},{28,24},{1,5},{5... | collective-permute-start | bytes 786440 | tf_op jit(solution)/shard_map/ppermute | solution.py:271
  85.8 16.7 %collective-permute-start.29 = (bf16[256,512]{1,0:T(8,128)(2,1)S(1)}, bf16[256,512]{1,0:T(8,128)(2,1)S(1)}, u32[]{:S(2)}, u32[]{:S(2)}) collective-permute-start(bf16[256,512]{1,0:T(8,128)(2,1)S(1)} %image.8.refs_6_.refs_2_.refs_4_), channel_id=1, source_target_pairs={{0,1},{1,0},{2,3},{3,2},{4,5},{5,4},{6,7},{7,6},{8,9},{9,8},{10,11... | collective-permute-start | bytes 786440 | tf_op jit(solution)/shard_map/ppermute | solution.py:236
  86.4 14.0 %collective-permute-start.40 = (bf16[256,512]{1,0:T(8,128)(2,1)S(1)}, bf16[256,512]{1,0:T(8,128)(2,1)S(1)}, u32[]{:S(2)}, u32[]{:S(2)}) collective-permute-start(bf16[256,512]{1,0:T(8,128)(2,1)S(1)} %image.9.refs_8_.refs_2_.refs_12_), channel_id=1, source_target_pairs={{4,8},{12,16},{20,24},{8,4},{16,12},{24,20},{5,9},{13,17},{21,25},... | collective-permute-start | bytes 786440 | tf_op jit(solution)/shard_map/ppermute | solution.py:295
  87.1 15.4 %collective-permute-start.35 = (bf16[256,512]{1,0:T(8,128)(2,1)S(1)}, bf16[256,512]{1,0:T(8,128)(2,1)S(1)}, u32[]{:S(2)}, u32[]{:S(2)}) collective-permute-start(bf16[256,512]{1,0:T(8,128)(2,1)S(1)} %image.9.refs_8_.refs_2_.refs_12_), channel_id=1, source_target_pairs={{0,4},{4,0},{8,12},{12,8},{16,20},{20,16},{24,28},{28,24},{1,5},{5... | collective-permute-start | bytes 786440 | tf_op jit(solution)/shard_map/ppermute | solution.py:279
  92.2 10.9 %collective-permute-start.38 = (bf16[256,512]{1,0:T(8,128)(2,1)S(1)}, bf16[256,512]{1,0:T(8,128)(2,1)S(1)}, u32[]{:S(2)}, u32[]{:S(2)}) collective-permute-start(bf16[256,512]{1,0:T(8,128)(2,1)S(1)} %collective-permute-done.32.refs_10_), channel_id=1, source_target_pairs={{0,8},{8,16},{16,24},{12,4},{20,12},{28,20},{1,9},{9,17},{17,25},{... | collective-permute-start | bytes 786440 | tf_op jit(solution)/shard_map/ppermute | solution.py:294
  108.8 9.0 %collective-permute-start.42 = (bf16[256,512]{1,0:T(8,128)(2,1)S(1)}, bf16[256,512]{1,0:T(8,128)(2,1)S(1)}, u32[]{:S(2)}, u32[]{:S(2)}) collective-permute-start(bf16[256,512]{1,0:T(8,128)(2,1)S(1)} %full.10.a_ref), channel_id=1, source_target_pairs={{0,2},{1,3},{2,0},{3,1},{4,6},{5,7},{6,4},{7,5},{8,10},{9,11},{10,... | collective-permute-start | bytes 786440 | tf_op jit(solution)/shard_map/ppermute | solution.py:326
  114.1 8.8 %collective-permute-start.44 = (bf16[256,512]{1,0:T(8,128)(2,1)S(1)}, bf16[256,512]{1,0:T(8,128)(2,1)S(1)}, u32[]{:S(2)}, u32[]{:S(2)}) collective-permute-start(bf16[256,512]{1,0:T(8,128)(2,1)S(1)} %full.11.a_ref), channel_id=1, source_target_pairs={{0,2},{1,3},{2,0},{3,1},{4,6},{5,7},{6,4},{7,5},{8,10},{9,11},{10,... | collective-permute-start | bytes 786440 | tf_op jit(solution)/shard_map/ppermute | solution.py:326
  119.5 19.0 %collective-permute-start.43 = (bf16[256,512]{1,0:T(8,128)(2,1)S(1)}, bf16[256,512]{1,0:T(8,128)(2,1)S(1)}, u32[]{:S(2)}, u32[]{:S(2)}) collective-permute-start(bf16[256,512]{1,0:T(8,128)(2,1)S(1)} %get-tuple-element.60.refs_6_), channel_id=1, source_target_pairs={{0,1},{1,0},{2,3},{3,2},{4,5},{5,4},{6,7},{7,6},{8,9},{9,8},{10,11... | collective-permute-start | bytes 786440 | tf_op jit(solution)/shard_map/ppermute | solution.py:236
  124.5 14.0 %collective-permute-start.45 = (bf16[256,512]{1,0:T(8,128)(2,1)S(1)}, bf16[256,512]{1,0:T(8,128)(2,1)S(1)}, u32[]{:S(2)}, u32[]{:S(2)}) collective-permute-start(bf16[256,512]{1,0:T(8,128)(2,1)S(1)} %get-tuple-element.62.refs_14_), channel_id=1, source_target_pairs={{0,1},{1,0},{2,3},{3,2},{4,5},{5,4},{6,7},{7,6},{8,9},{9,8},{10,11... | collective-permute-start | bytes 786440 | tf_op jit(solution)/shard_map/ppermute | solution.py:236
  (33 other events, 124.4 us)

commit v5 on v4

v5 whole, which is shorter than its diff:
```python
import functools

import jax
import jax.numpy as jnp
from jax import lax
from jax.experimental import pallas as pl
from jax.experimental.pallas import tpu as pltpu
from jax.sharding import PartitionSpec as P

F32 = jnp.float32
BF16 = jnp.bfloat16
START_SCALE = 2.0**60
VMEM = pl.BlockSpec(memory_space=pltpu.VMEM)
SMEM = pl.BlockSpec(memory_space=pltpu.SMEM)


def call(kernel, name, out, scratch, *operands):
    return pl.pallas_call(
        kernel,
        name=name,
        out_shape=out,
        in_specs=[SMEM if a.dtype == jnp.int32 else VMEM for a in operands],
        out_specs=jax.tree.map(lambda _: VMEM, out),
        scratch_shapes=scratch,
        compiler_params=pltpu.CompilerParams(vmem_limit_bytes=16 << 20),
        cost_estimate=pl.CostEstimate(flops=0, bytes_accessed=0, transcendentals=0),
    )(*operands)


def after(value, *others):
    return lax.optimization_barrier((value, *others))[0]


def my_core():
    return lax.axis_index("op") % 2


def half_of(which, half):
    core = my_core()
    return pl.ds(pl.multiple_of((core if which == 0 else 1 - core) * half, half), half)


def side_of(which, rows, count):
    side = lax.axis_index("op") // (count // 2)
    return pl.ds(pl.multiple_of((side if which == 0 else 1 - side) * rows, rows), rows)


def rows_of(rows_ref, target, sectors):
    return rows_ref[lax.axis_index("sec") * sectors + target]


def live_entries(rows_ref, columns):
    return sum(rows_ref[i] for i in range(rows_ref.shape[0])).astype(F32) * columns


def masked(value, first, rows):
    return jnp.where(lax.broadcasted_iota(jnp.int32, value.shape, 0) + first < rows, value, 0.0)


def inner(stats_ref, row, live):
    return jnp.sum(stats_ref[row : row + 1, :], axis=1, keepdims=True) / live


def write_sums(stats_ref, values, before=None):
    parts = [jnp.zeros((1, 128), F32)] * 8
    for k, value in enumerate(values):
        folded = sum(value[:, i : i + 128] for i in range(0, value.shape[1], 128))
        parts[k] = jnp.sum(folded, axis=0, keepdims=True)
    rows = jnp.concatenate(parts, axis=0)
    stats_ref[...] = rows if before is None else rows + before[...]


def largest(value):
    return jnp.maximum(jnp.max(jnp.abs(value), keepdims=True), 1e-37)


def scaled_sums(pairs):
    sums, lefts, rights = [], [], []
    for left, right in pairs:
        scales = largest(left), largest(right)
        product = (left * (1.0 / scales[0])) * (right * (1.0 / scales[1]))
        folded = sum(product[:, i : i + 128] for i in range(0, product.shape[1], 128))
        sums.append(jnp.sum(folded, axis=0, keepdims=True))
        lefts.append(jnp.broadcast_to(scales[0], (1, 128)))
        rights.append(jnp.broadcast_to(scales[1], (1, 128)))
    fill = [jnp.zeros((1, 128), F32)] * (8 - len(pairs))
    ones = [jnp.full((1, 128), 1e-37, F32)] * (8 - len(pairs))
    return jnp.concatenate(sums + fill + lefts + ones + rights + ones, axis=0)


def merged(a, b):
    left = jnp.maximum(a[8:16], b[8:16])
    right = jnp.maximum(a[16:], b[16:])
    total = sum(t[:8] * (t[8:16] / left) * (t[16:] / right) for t in (a, b))
    return jnp.concatenate([total, left, right], axis=0)


def merge_kernel(axis, bit, own_ref, arrived_ref, out_ref):
    low = lax.axis_index(axis) & bit == 0
    own, arrived = own_ref[...], arrived_ref[...]
    out_ref[...] = merged(jnp.where(low, own, arrived), jnp.where(low, arrived, own))


def first_scalars(tile, live):
    def row(k):
        return (
            jnp.sum(tile[k : k + 1, :], axis=1, keepdims=True) / live,
            tile[8 + k : 9 + k, 0:1],
            tile[16 + k : 17 + k, 0:1],
        )

    square, scale, _ = row(0)
    norm = scale * jnp.sqrt(square)
    cross, image_scale, start_scale = row(1)
    alpha = cross * (image_scale / norm) * (start_scale / norm)
    image_square, image_scale, _ = row(2)
    unit = image_scale / norm
    rest = image_square - (alpha / unit) * (alpha / unit)
    return norm, alpha, unit * jnp.sqrt(jnp.maximum(rest, 0.0))


def form(gram, a, b):
    return sum(a[i] * b[j] * gram[min(i, j)][max(i, j)] for i in a for j in b)


def plus(scale, *terms):
    out = {}
    for c, vector in terms:
        for i, v in vector.items():
            out[i] = out[i] + c * v if i in out else c * v
    return {i: scale * v for i, v in out.items()}


def start_kernel(rows_ref, x_ref, *refs):
    sectors, block_rows, _ = x_ref.shape
    for t in range(sectors):
        for which in range(2):
            part = half_of(which, block_rows // 2)
            value = masked(
                x_ref[t, part, :].astype(F32), part.start, rows_of(rows_ref, t, sectors)
            )
            refs[2 * t + which][...] = (value * START_SCALE).astype(BF16)


def place_of(k):
    pair = jnp.where(lax.axis_index("sec") % 2 == 0, 2, 0)
    return (1, pair, 2 - pair)[k]


def stage_kernel(left_ref, right_ref, left_out, right_out, sems):
    copies = [
        pltpu.make_async_copy(left_ref, left_out, sems.at[0]),
        pltpu.make_async_copy(right_ref, right_out, sems.at[1]),
    ]
    for copy in copies:
        copy.start()
    for copy in copies:
        copy.wait()


def gather_sources(slots, refs, scalars, v_ref):
    half = refs[0].shape[0]
    if scalars:
        rows_ref, tile_ref = scalars
        norm, _, beta = first_scalars(tile_ref, live_entries(rows_ref, v_ref.shape[2]))
        scale = 1.0 / (norm * beta)
    for i, slot in enumerate(slots):
        for which in range(2):
            value = refs[2 * i + which][...]
            if scalars:
                value = (value.astype(F32) * scale).astype(BF16)
            v_ref[slot, half_of(which, half), :] = value


def full_kernel(target, *refs):
    operators, sources, rest = refs[:6], refs[6:18], refs[18:]
    if len(rest) == 2:
        scalars, outs, v_ref = (), rest[:1], rest[1]
    else:
        *scalars, keep_ref, give_ref, v_ref, total_ref = rest
        outs = keep_ref, give_ref
    gather_sources((0, 1, 2, 3, 4, 5), sources, scalars, v_ref)
    far = place_of(2)
    half = sources[0].shape[0]
    total = None
    for shifts_ref, left_ref, right_ref in (operators[:3], operators[3:]):
        for w in range(left_ref.shape[0]):
            offset = target - shifts_ref[w]
            place = (offset >> 1) + 1
            kind = jnp.where(place == 1, 0, jnp.where(place == far, 4, 2))
            part = jnp.dot(
                left_ref[w, target, half_of(0, half), :],
                v_ref[kind + (offset & 1)],
                preferred_element_type=F32,
            ).astype(BF16)
            term = jnp.dot(part, right_ref[w], preferred_element_type=F32)
            total = term if total is None else total + term
    if len(outs) == 1:
        outs[0][...] = total.astype(BF16)
    else:
        total_ref[...] = total.astype(BF16)
        for which, ref in enumerate(outs):
            ref[...] = total_ref[side_of(which, half // 2, lax.axis_size("op")), :]


def add_kernel(a_ref, b_ref, out_ref):
    out_ref[...] = (a_ref[...].astype(F32) + b_ref[...].astype(F32)).astype(BF16)


def image_kernel(product, target, sectors, rows_ref, a_ref, b_ref, *refs):
    out_ref = refs[-2] if product != 1 else refs[-1]
    half, columns = out_ref.shape
    value = a_ref[...].astype(F32) + b_ref[...].astype(F32)
    rows = rows_of(rows_ref, target, sectors)
    first_row = my_core() * half
    part = pl.ds(0, half)
    if product == 2:
        part = side_of(0, half, lax.axis_size("op"))
        first_row = 2 * first_row + part.start
    value = masked(value, first_row, rows)
    if product == 1:
        out_ref[...] = value.astype(BF16)
        return
    stats_ref = refs[-1]
    basis = [r[part, :].astype(F32) for r in refs[: product + 1]]
    if product == 0:
        value = value.astype(BF16)
        out_ref[...] = value
        value = value.astype(F32)
        tile = scaled_sums([(basis[0], basis[0]), (value, basis[0]), (value, value)])
        stats_ref[...] = merged(refs[1][...], tile) if target else tile
        return
    tile_ref, before = refs[product + 1], refs[product + 2] if target else None
    norm, alpha, beta = first_scalars(tile_ref, live_entries(rows_ref, columns))
    zeroth, image, second = (block * (1.0 / norm) for block in basis)
    scale = 1.0 / beta
    first = (image - alpha * zeroth) * scale
    value = (value - (alpha * scale) * second) * scale
    second = (second - alpha * image) * scale
    value = value.astype(BF16)
    out_ref[...] = value
    value = value.astype(F32)
    known = [second * second, second * first, second * zeroth]
    write_sums(stats_ref, known + [value * v for v in (value, second, first, zeroth)], before)


def last_kernel(rows_ref, *refs):
    out_ref, coef_ref = refs[-2:]
    tile_ref, last_stats = refs[-4:-2]
    sectors, block_rows, columns = out_ref.shape
    live = live_entries(rows_ref, columns)
    norm, alpha0, beta0 = first_scalars(tile_ref, live)
    one, none = jnp.ones_like(norm), jnp.zeros_like(norm)
    w11, w1q1, w1q0, zz, zw1, zq1, zq0 = (inner(last_stats, k, live) for k in range(7))
    gram = [[one, none, w1q0, zq0], [None, one, w1q1, zq1], [None, None, w11, zw1], [None] * 3 + [zz]]
    q0, q1, w1 = {0: one}, {1: one}, {2: one}
    alpha1 = w1q1
    r1 = plus(one, (one, w1), (-alpha1, q1), (-beta0, q0))
    beta1 = jnp.sqrt(jnp.maximum(form(gram, r1, r1), 0.0))
    q2 = plus(1.0 / beta1, (one, r1))
    w0 = {0: alpha0, 1: beta0}
    w2 = plus(1.0 / beta1, (beta0, {3: one}), (-alpha1, w1), (-beta0, w0))
    alpha2 = form(gram, q2, w2)
    r2 = plus(one, (one, w2), (-alpha2, q2), (-beta1, q1))
    beta2 = jnp.sqrt(jnp.maximum(form(gram, r2, r2), 0.0))
    q3 = plus(1.0 / beta2, (one, r2))
    c1 = q3[1] / beta0
    c2 = q3[2] / beta0
    coefs = [(q3[0] - alpha0 * c1) / norm, (c1 - alpha0 * c2) / norm, c2 / norm, q3[3]]
    quarter = block_rows // 4
    for t in range(sectors):
        sector_refs = refs[10 * t : 10 * t + 10]
        for which in range(2):
            start = half_of(which, 2 * quarter).start
            for side in range(2):
                part = side_of(side, quarter, lax.axis_size("op"))
                blocks = [sector_refs[2 * k + which][part, :] for k in range(3)]
                blocks.append(sector_refs[6 + 2 * side + which][...])
                vector = sum(c * block.astype(F32) for c, block in zip(coefs, blocks))
                rows = pl.ds(pl.multiple_of(start + part.start, quarter), quarter)
                out_ref[t, rows, :] = vector.astype(BF16)
    row = lax.broadcasted_iota(jnp.int32, coef_ref.shape, 0)
    column = lax.broadcasted_iota(jnp.int32, coef_ref.shape, 1)
    value = jnp.zeros(coef_ref.shape, F32)
    for k, (alpha, beta) in enumerate(((alpha0, beta0), (alpha1, beta1), (alpha2, beta2))):
        value = jnp.where((row == 0) & (column == k), alpha, value)
        value = jnp.where((row == 1) & (column == k), beta, value)
    coef_ref[...] = value


def on_device(wavefunction, left_blocks, right_blocks, charge_shifts, sector_rows):
    sectors, block_rows, columns = wavefunction.shape
    half = block_rows // 2
    n_sec, n_op = lax.axis_size("sec"), lax.axis_size("op")
    assert sectors == 2 and n_sec % 4 == 0 and n_op % 4 == 0
    core_pairs = [(i, i ^ 1) for i in range(n_op)]
    pairs = [(i, i ^ 1) for i in range(n_sec)]
    onward = [(i, i + 2) for i in range(0, n_sec - 2, 2)]
    onward += [(i, i - 2) for i in range(3, n_sec, 2)]
    diagonal = [(i, i + 1) for i in range(1, n_sec - 1, 2)]
    diagonal += [(j, i) for i, j in diagonal]

    def across_cores(value):
        return lax.ppermute(value, "op", core_pairs)

    def flipped_sum(stats, bits):
        for bit in bits:
            stats = stats + lax.ppermute(stats, "sec", [(i, i ^ bit) for i in range(n_sec)])
        return stats

    def flipped_merge(tile, axis, bits):
        for bit in bits:
            flips = [(i, i ^ bit) for i in range(lax.axis_size(axis))]
            arrived = lax.ppermute(tile, axis, flips)
            tile = call(
                functools.partial(merge_kernel, axis, bit), "merge", tile_type, [], tile, arrived
            )
        return tile

    def sum_four(stats, one, two):
        places = range(n_sec * n_op)
        first, second, both = (
            lax.ppermute(stats, ("sec", "op"), [(i, i ^ mask) for i in places])
            for mask in (one, two, one ^ two)
        )
        return (stats + both) + (first + second)

    bits = [1 << k for k in range(n_sec.bit_length() - 1)]

    last_bit = n_op // 2
    half_type = jax.ShapeDtypeStruct((half, columns), BF16)
    quarter_type = jax.ShapeDtypeStruct((half // 2, columns), BF16)
    stats_type = jax.ShapeDtypeStruct((8, 128), F32)
    tile_type = jax.ShapeDtypeStruct((24, 128), F32)
    v_scratch = pltpu.VMEM((6, block_rows, columns), BF16)

    halves = call(
        start_kernel, "start", [half_type] * (2 * sectors), [], sector_rows, wavefunction
    )
    basis = [[(halves[0], halves[1]), (halves[2], halves[3])]]
    pair_0 = lax.ppermute(halves[0], "sec", pairs)
    operators = (charge_shifts, left_blocks, right_blocks)
    others = tuple(across_cores(value) for value in operators)
    stats = []
    hbm = pl.BlockSpec(memory_space=pltpu.HBM)
    left, right = pl.pallas_call(
        stage_kernel,
        name="stage",
        out_shape=[jax.ShapeDtypeStruct(v.shape, v.dtype) for v in operators[1:]],
        in_specs=[hbm] * 2,
        out_specs=[VMEM] * 2,
        scratch_shapes=[pltpu.SemaphoreType.DMA((2,))],
        compiler_params=pltpu.CompilerParams(vmem_limit_bytes=16 << 20),
        cost_estimate=pl.CostEstimate(flops=0, bytes_accessed=0, transcendentals=0),
    )(operators[1], operators[2])
    operators = (charge_shifts, left, right) + others
    pair_0 = after(pair_0, left)

    for product in range(3):
        (mine_0, other_0), (mine_1, other_1) = basis[-1]
        if product:
            pair_0 = lax.ppermute(mine_0, "sec", pairs)
        if product:
            pair_0 = after(pair_0, mine_1)
        else:
            mine_1 = after(mine_1, pair_0)
        if product == 2:
            tile = flipped_merge(after(tile, mine_0), "sec", bits[1:2])
            pair_0 = after(pair_0, tile)
        pair_1 = lax.ppermute(mine_1, "sec", pairs)
        far_0 = lax.ppermute(pair_0, "sec", onward)
        far_1 = lax.ppermute(mine_1, "sec", diagonal)
        if product == 0:
            pair_1 = after(pair_1, far_0)
        if product == 1:
            tile = flipped_merge(flipped_merge(sums, "op", [1]), "sec", bits[:1])
            pair_1 = after(pair_1, tile)
        elif product == 2:
            tile = flipped_merge(after(tile, pair_0), "sec", bits[2:])
            stats.append(tile)
            pair_1 = after(pair_1, tile)
        scalars = (sector_rows, *stats) if product == 2 else ()
        sources = [mine_0, other_0, mine_1, other_1]
        for part in (pair_0, pair_1, far_0, far_1):
            sources += [part, across_cores(part)]
        out, scratch = [half_type], [v_scratch]
        if product == 2:
            out = [quarter_type] * 2
            scratch.append(pltpu.VMEM((half, columns), BF16))
        values = [
            call(
                functools.partial(full_kernel, t), "full", out, scratch,
                *operators, *sources, *scalars,
            )
            for t in range(sectors)
        ]
        image = []
        earlier = []
        for t, parts in enumerate(values):
            bit = 2
            while bit < last_bit:
                flips = [(i, i ^ bit) for i in range(n_op)]
                parts = [
                    call(add_kernel, "add", jax.ShapeDtypeStruct(part.shape, BF16), [], part, lax.ppermute(part, "op", flips))
                    for part in parts
                ]
                bit *= 2
            flips = [(i, i ^ last_bit) for i in range(n_op)]
            arrived = lax.ppermute(parts[-1], "op", flips)
            if t == 0:
                arrived = after(arrived, values[-1][0])
            out = (half_type, half_type, quarter_type)[product]
            needed = () if product == 1 else (*[b[t][0] for b in basis], *stats, *earlier)
            mine, *earlier = call(
                functools.partial(image_kernel, product, t, sectors), "image",
                [out] if product == 1 else [out, stats_type if product else tile_type], [],
                sector_rows, parts[0], arrived, *needed,
            )
            image.append((mine, across_cores(mine)))
            if product == 2:
                other = lax.ppermute(mine, "op", flips)
                image[-1] += (other, across_cores(other))
        basis.append(image)
        if earlier:
            sums = earlier[0]
    sums = sum_four(sum_four(sums, 1, last_bit), n_op, 2 * n_op)
    stats.append(flipped_sum(sums, bits[2:]))

    flat = [h for t in range(sectors) for b in basis for h in b[t]]
    vector_type = jax.ShapeDtypeStruct(wavefunction.shape, BF16)
    coef_type = jax.ShapeDtypeStruct((2, 3), F32)
    vector, coef = call(
        last_kernel, "last", [vector_type, coef_type], [], sector_rows, *flat, *stats
    )
    return vector, coef


def solution(mesh):
    in_specs = (P("sec", None, None), P("op", "sec", None, None), P("op", None, None), P("op"), P())
    out_specs = (P("sec", None, None), P())
    return jax.shard_map(
        on_device, mesh=mesh, in_specs=in_specs, out_specs=out_specs, check_vma=False
    )
```

time: 142 us -> 139 us (0.979)
  waiting for transfers between devices: 43.2 us -> 35.9 us
  starting transfers between devices: 58.2 us -> 63.1 us
    ppermute x8 -> x1, waiting for transfers between devices: 17.7 us -> 2.82 us  [flipped_sum(): lax.ppermute(stats, 'sec', [(i, i ^ bit) for i in range(n_sec)])]
    ppermute x9 -> x18, starting transfers between devices: 9.23 us -> 22.5 us  [the longest x6 8.52 us: sum_four(): lax.ppermute(stats, ('sec', 'op'), [(i, i ^ mask) for i in places])]
    ppermute x8 -> x1, starting transfers between devices: 13.3 us -> 1.68 us  [flipped_sum(): lax.ppermute(stats, 'sec', [(i, i ^ bit) for i in range(n_sec)])]
    ppermute x9 -> x18, waiting for transfers between devices: 16.8 us -> 20.4 us  [the longest x6 10.6 us: on_device(): arrived = lax.ppermute(parts[-1], 'op', flips)]
    ppermute x1, waiting for transfers between devices: 0.01 us -> 2.32 us  [on_device(): pair_0 = lax.ppermute(halves[0], 'sec', pairs)]
    ppermute x3, waiting for transfers between devices: 0.01 us -> 2.12 us  [on_device(): far_0 = lax.ppermute(pair_0, 'sec', onward)]
    ppermute x2, starting transfers between devices: 5.9 us -> 7.91 us  [on_device(): pair_0 = lax.ppermute(mine_0, 'sec', pairs)]
    pallas_call x14 -> x18, Pallas kernels: 33.2 us -> 32.3 us  [call(): pl.pallas_call(kernel, name=name, out_shape=out, in_specs=[SMEM if a.dtyp...]
  transfers between devices with their start and end apart: 51 -> 54, of which waited for: 27 -> 26; matrix products, arithmetic and copies ran while one was open for 0% -> 0% of each run, Pallas kernels for 13% -> 12%
where the time goes in v5:
time: 139 us; the launch traced here: 138 us
  starting transfers between devices  63.1 us (45%)
  waiting for transfers between devices  35.9 us (26%)
  Pallas kernels  32.7 us (24%)
  local copies, waits for them, and re-layouts  5.67 us (4%)
    pallas_call x18, Pallas kernels, call(): pl.pallas_call(kernel, name=name, out_shape=out, in_specs=[SMEM if a.dtyp...  32.3 us
    ppermute x3, starting transfers between devices, on_device(): far_0 = lax.ppermute(pair_0, 'sec', onward)  13.3 us
    ppermute x6, waiting for transfers between devices, on_device(): arrived = lax.ppermute(parts[-1], 'op', flips)  10.6 us
    ppermute x6, starting transfers between devices, sum_four(): lax.ppermute(stats, ('sec', 'op'), [(i, i ^ mask) for i in places])  8.52 us
    ppermute x3, starting transfers between devices, on_device(): pair_1 = lax.ppermute(mine_1, 'sec', pairs)  8.35 us
    ppermute x4, waiting for transfers between devices, flipped_merge(): arrived = lax.ppermute(tile, axis, flips)  8.18 us
    ppermute x2, starting transfers between devices, on_device(): pair_0 = lax.ppermute(mine_0, 'sec', pairs)  7.91 us
    ppermute x6, starting transfers between devices, on_device(): arrived = lax.ppermute(parts[-1], 'op', flips)  6.47 us
  transfers between devices with their start and end apart: 54, of which 26 were waited for; matrix products, arithmetic and copies ran while one was open for 0% of the time, Pallas kernels for 12%

profile of v5, /device:TPU:0, one launch (start us, length us, event | category | flops | bytes accessed | tf_op | source)
XLA Modules:
  0.0 138.4 jit_solution(12829920072125171425)
XLA Ops:
  4.0 3.0 %collective-permute-start.3 = (bf16[256,512]{1,0:T(8,128)(2,1)S(1)}, bf16[256,512]{1,0:T(8,128)(2,1)S(1)}, u32[]{:S(2)}, u32[]{:S(2)}) collective-permute-start(bf16[256,512]{1,0:T(8,128)(2,1)S(1)} %get-tuple-element.33.refs_6_.refs_0_), channel_id=1, source_target_pairs={{0,4},{4,0},{8,12},{12,8},{16,20},{20,16},{24,28},{28,24},{1,5},{5... | collective-permute-start | bytes 786440 | tf_op jit(solution)/shard_map/ppermute | solution.py:341
  11.2 2.3 %collective-permute-done.3.refs_10_ = bf16[256,512]{1,0:T(8,128)(2,1)S(1)} collective-permute-done((bf16[256,512]{1,0:T(8,128)(2,1)S(1)}, bf16[256,512]{1,0:T(8,128)(2,1)S(1)}, u32[]{:S(2)}, u32[]{:S(2)}) %collective-permute-start.3) | collective-permute-done | bytes 262176 | tf_op jit(solution)/shard_map/ppermute | solution.py:341
  15.2 3.5 %collective-permute-start.6 = (bf16[256,512]{1,0:T(8,128)(2,1)S(1)}, bf16[256,512]{1,0:T(8,128)(2,1)S(1)}, u32[]{:S(2)}, u32[]{:S(2)}) collective-permute-start(bf16[256,512]{1,0:T(8,128)(2,1)S(1)} %collective-permute-done.3.refs_10_), channel_id=1, source_target_pairs={{0,8},{8,16},{16,24},{12,4},{20,12},{28,20},{1,9},{9,17},{17,25},{... | collective-permute-start | bytes 786440 | tf_op jit(solution)/shard_map/ppermute | solution.py:371
  26.8 3.7 %full.6.a_ref = bf16[256,512]{1,0:T(8,128)(2,1)S(1)} custom-call(s32[4]{0:T(128)S(1)} %copy-done.5, bf16[4,2,512,512]{3,2,1,0:T(8,128)(2,1)S(1)} %get-tuple-element.35.refs_1_, bf16[4,512,512]{2,1,0:T(8,128)(2,1)S(1)} %get-tuple-element.36.refs_2_, s32[4]{0:T(128)S(1)} %collective-permute-done.refs_3_, ...), custom_call_target="tpu_custom_call" | custom-call | tf_op jit(solution)/shard_map/full/pallas_call | solution.py:18
  32.1 3.7 %full.7.a_ref = bf16[256,512]{1,0:T(8,128)(2,1)S(1)} custom-call(s32[4]{0:T(128)S(1)} %copy-done.5, bf16[4,2,512,512]{3,2,1,0:T(8,128)(2,1)S(1)} %get-tuple-element.35.refs_1_, bf16[4,512,512]{2,1,0:T(8,128)(2,1)S(1)} %get-tuple-element.36.refs_2_, s32[4]{0:T(128)S(1)} %collective-permute-done.refs_3_, ...), custom_call_target="tpu_custom_call" | custom-call | tf_op jit(solution)/shard_map/full/pallas_call | solution.py:18
  36.3 3.2 %collective-permute-done.11.b_ref = bf16[256,512]{1,0:T(8,128)(2,1)S(1)} collective-permute-done((bf16[256,512]{1,0:T(8,128)(2,1)S(1)}, bf16[256,512]{1,0:T(8,128)(2,1)S(1)}, u32[]{:S(2)}, u32[]{:S(2)}) %collective-permute-start.11) | collective-permute-done | bytes 262176 | tf_op jit(solution)/shard_map/ppermute | solution.py:409
  40.5 3.9 %collective-permute-start.15 = (bf16[256,512]{1,0:T(8,128)(2,1)S(1)}, bf16[256,512]{1,0:T(8,128)(2,1)S(1)}, u32[]{:S(2)}, u32[]{:S(2)}) collective-permute-start(bf16[256,512]{1,0:T(8,128)(2,1)S(1)} %get-tuple-element.43.refs_6_.refs_1_.refs_2_), channel_id=1, source_target_pairs={{0,4},{4,0},{8,12},{12,8},{16,20},{20,16},{24,28},{28,24},{1,5},{5... | collective-permute-start | bytes 786440 | tf_op jit(solution)/shard_map/ppermute | solution.py:362
  45.6 3.9 %collective-permute-start.17 = (bf16[256,512]{1,0:T(8,128)(2,1)S(1)}, bf16[256,512]{1,0:T(8,128)(2,1)S(1)}, u32[]{:S(2)}, u32[]{:S(2)}) collective-permute-start(bf16[256,512]{1,0:T(8,128)(2,1)S(1)} %get-tuple-element.45.refs_8_.refs_1_.refs_12_), channel_id=1, source_target_pairs={{0,4},{4,0},{8,12},{12,8},{16,20},{20,16},{24,28},{28,24},{1,5},{5... | collective-permute-start | bytes 786440 | tf_op jit(solution)/shard_map/ppermute | solution.py:370
  50.2 4.7 %collective-permute-start.21 = (bf16[256,512]{1,0:T(8,128)(2,1)S(1)}, bf16[256,512]{1,0:T(8,128)(2,1)S(1)}, u32[]{:S(2)}, u32[]{:S(2)}) collective-permute-start(bf16[256,512]{1,0:T(8,128)(2,1)S(1)} %collective-permute-done.15.refs_10_), channel_id=1, source_target_pairs={{0,8},{8,16},{16,24},{12,4},{20,12},{28,20},{1,9},{9,17},{17,25},{... | collective-permute-start | bytes 786440 | tf_op jit(solution)/shard_map/ppermute | solution.py:371
  57.3 3.4 %collective-permute-done.19.arrived_ref = f32[24,128]{1,0:T(8,128)S(1)} collective-permute-done((f32[24,128]{1,0:T(8,128)S(1)}, f32[24,128]{1,0:T(8,128)S(1)}, u32[]{:S(2)}, u32[]{:S(2)}) %collective-permute-start.19) | collective-permute-done | bytes 12320 | tf_op jit(solution)/shard_map/ppermute | solution.py:314
  63.7 3.7 %full.8.a_ref = bf16[256,512]{1,0:T(8,128)(2,1)S(1)} custom-call(s32[4]{0:T(128)S(1)} %copy-done.5, bf16[4,2,512,512]{3,2,1,0:T(8,128)(2,1)S(1)} %get-tuple-element.35.refs_1_, bf16[4,512,512]{2,1,0:T(8,128)(2,1)S(1)} %get-tuple-element.36.refs_2_, s32[4]{0:T(128)S(1)} %collective-permute-done.refs_3_, ...), custom_call_target="tpu_custom_call" | custom-call | tf_op jit(solution)/shard_map/full/pallas_call | solution.py:18
  68.7 3.7 %full.9.a_ref = bf16[256,512]{1,0:T(8,128)(2,1)S(1)} custom-call(s32[4]{0:T(128)S(1)} %copy-done.5, bf16[4,2,512,512]{3,2,1,0:T(8,128)(2,1)S(1)} %get-tuple-element.35.refs_1_, bf16[4,512,512]{2,1,0:T(8,128)(2,1)S(1)} %get-tuple-element.36.refs_2_, s32[4]{0:T(128)S(1)} %collective-permute-done.refs_3_, ...), custom_call_target="tpu_custom_call" | custom-call | tf_op jit(solution)/shard_map/full/pallas_call | solution.py:18
  73.2 3.4 %collective-permute-done.25.b_ref = bf16[256,512]{1,0:T(8,128)(2,1)S(1)} collective-permute-done((bf16[256,512]{1,0:T(8,128)(2,1)S(1)}, bf16[256,512]{1,0:T(8,128)(2,1)S(1)}, u32[]{:S(2)}, u32[]{:S(2)}) %collective-permute-start.25) | collective-permute-done | bytes 262176 | tf_op jit(solution)/shard_map/ppermute | solution.py:409
  77.2 4.0 %collective-permute-start.29 = (bf16[256,512]{1,0:T(8,128)(2,1)S(1)}, bf16[256,512]{1,0:T(8,128)(2,1)S(1)}, u32[]{:S(2)}, u32[]{:S(2)}) collective-permute-start(bf16[256,512]{1,0:T(8,128)(2,1)S(1)} %image.8.refs_6_.refs_2_.refs_4_), channel_id=1, source_target_pairs={{0,4},{4,0},{8,12},{12,8},{16,20},{20,16},{24,28},{28,24},{1,5},{5... | collective-permute-start | bytes 786440 | tf_op jit(solution)/shard_map/ppermute | solution.py:362
  83.6 2.7 %collective-permute-start.32 = (bf16[256,512]{1,0:T(8,128)(2,1)S(1)}, bf16[256,512]{1,0:T(8,128)(2,1)S(1)}, u32[]{:S(2)}, u32[]{:S(2)}) collective-permute-start(bf16[256,512]{1,0:T(8,128)(2,1)S(1)} %image.9.refs_8_.refs_2_.refs_14_), channel_id=1, source_target_pairs={{0,4},{4,0},{8,12},{12,8},{16,20},{20,16},{24,28},{28,24},{1,5},{5... | collective-permute-start | bytes 786440 | tf_op jit(solution)/shard_map/ppermute | solution.py:370
  87.1 5.1 %collective-permute-start.35 = (bf16[256,512]{1,0:T(8,128)(2,1)S(1)}, bf16[256,512]{1,0:T(8,128)(2,1)S(1)}, u32[]{:S(2)}, u32[]{:S(2)}) collective-permute-start(bf16[256,512]{1,0:T(8,128)(2,1)S(1)} %collective-permute-done.29.refs_10_), channel_id=1, source_target_pairs={{0,8},{8,16},{16,24},{12,4},{20,12},{28,20},{1,9},{9,17},{17,25},{... | collective-permute-start | bytes 786440 | tf_op jit(solution)/shard_map/ppermute | solution.py:371
  92.2 2.4 %collective-permute-start.33 = (f32[24,128]{1,0:T(8,128)S(1)}, f32[24,128]{1,0:T(8,128)S(1)}, u32[]{:S(2)}, u32[]{:S(2)}) collective-permute-start(f32[24,128]{1,0:T(8,128)S(1)} %merge.6.own_ref), channel_id=1, source_target_pairs={{0,16},{4,20},{8,24},{12,28},{16,0},{20,4},{24,8},{28,12},{1,17},{... | collective-permute-start | bytes 36872 | tf_op jit(solution)/shard_map/ppermute | solution.py:314
  94.6 3.8 %collective-permute-done.33.arrived_ref = f32[24,128]{1,0:T(8,128)S(1)} collective-permute-done((f32[24,128]{1,0:T(8,128)S(1)}, f32[24,128]{1,0:T(8,128)S(1)}, u32[]{:S(2)}, u32[]{:S(2)}) %collective-permute-start.33) | collective-permute-done | bytes 12320 | tf_op jit(solution)/shard_map/ppermute | solution.py:314
  101.5 4.1 %full.10 = (bf16[128,512]{1,0:T(8,128)(2,1)S(1)}, bf16[128,512]{1,0:T(8,128)(2,1)S(1)}) custom-call(s32[4]{0:T(128)S(1)} %copy-done.5, bf16[4,2,512,512]{3,2,1,0:T(8,128)(2,1)S(1)} %get-tuple-element.35.refs_1_, bf16[4,512,512]{2,1,0:T(8,128)(2,1)S(1)} %get-tuple-element.36.refs_2_, s32[4]{0:T(128)S(1)} %collective-permute-done.refs_3_, ...), custom_call_target="tpu_custom_call" | custom-call | tf_op jit(solution)/shard_map/full/pallas_call | solution.py:18
  107.2 4.1 %full.11 = (bf16[128,512]{1,0:T(8,128)(2,1)S(1)}, bf16[128,512]{1,0:T(8,128)(2,1)S(1)}) custom-call(s32[4]{0:T(128)S(1)} %copy-done.5, bf16[4,2,512,512]{3,2,1,0:T(8,128)(2,1)S(1)} %get-tuple-element.35.refs_1_, bf16[4,512,512]{2,1,0:T(8,128)(2,1)S(1)} %get-tuple-element.36.refs_2_, s32[4]{0:T(128)S(1)} %collective-permute-done.refs_3_, ...), custom_call_target="tpu_custom_call" | custom-call | tf_op jit(solution)/shard_map/full/pallas_call | solution.py:18
  112.9 3.8 %collective-permute-done.43.b_ref = bf16[128,512]{1,0:T(8,128)(2,1)S(1)} collective-permute-done((bf16[128,512]{1,0:T(8,128)(2,1)S(1)}, bf16[128,512]{1,0:T(8,128)(2,1)S(1)}, u32[]{:S(2)}, u32[]{:S(2)}) %collective-permute-start.43) | collective-permute-done | bytes 131104 | tf_op jit(solution)/shard_map/ppermute | solution.py:409
  122.0 4.2 %collective-permute-start.50 = (f32[8,128]{1,0:T(8,128)S(1)}, f32[8,128]{1,0:T(8,128)S(1)}, u32[]{:S(2)}, u32[]{:S(2)}) collective-permute-start(f32[8,128]{1,0:T(8,128)S(1)} %add_add_fusion.1), channel_id=1, source_target_pairs={{0,12},{1,13},{2,14},{3,15},{4,8},{5,9},{6,10},{7,11},{8,4},{9,5},... | collective-permute-start | bytes 12296 | tf_op jit(solution)/shard_map/ppermute | solution.py:323
  132.2 2.8 %collective-permute-done.53 = f32[8,128]{1,0:T(8,128)S(1)} collective-permute-done((f32[8,128]{1,0:T(8,128)S(1)}, f32[8,128]{1,0:T(8,128)S(1)}, u32[]{:S(2)}, u32[]{:S(2)}) %collective-permute-start.53) | collective-permute-done | bytes 4128 | tf_op jit(solution)/shard_map/ppermute | solution.py:308
  135.1 3.3 %last.1 = (bf16[2,512,512]{2,1,0:T(8,128)(2,1)}, f32[2,3]{1,0:T(2,128)}) custom-call(s32[16]{0:T(128)S(1)} %copy-done.4, bf16[256,512]{1,0:T(8,128)(2,1)S(1)} %get-tuple-element.33.refs_6_.refs_0_, bf16[256,512]{1,0:T(8,128)(2,1)S(1)} %get-tuple-element.34.refs_7_.refs_1_, bf16[256,512]{1,0:T(8,128)(2,1)S(1)} %get-tuple-element.43.refs_6_.refs_1_.refs_2_, ...), custom_call_target="tpu_custom_call" | custom-call | tf_op jit(solution)/shard_map/last/pallas_call | solution.py:18
  (118 shorter events, 51.0 us)
Async XLA Ops:
  0.6 26.2 %collective-permute-start.1 = (bf16[4,2,512,512]{3,2,1,0:T(8,128)(2,1)}, bf16[4,2,512,512]{3,2,1,0:T(8,128)(2,1)S(1)}, u32[]{:S(2)}, u32[]{:S(2)}) collective-permute-start(bf16[4,2,512,512]{3,2,1,0:T(8,128)(2,1)} %left_ref.1), channel_id=1, source_target_pairs={{0,1},{1,0},{2,3},{3,2},{4,5},{5,4},{6,7},{7,6},{8,9},{9,8},{10,11... | collective-permute-start | bytes 12582920 | tf_op jit(solution)/shard_map/ppermute | solution.py:304
  1.1 25.6 %collective-permute-start.2 = (bf16[4,512,512]{2,1,0:T(8,128)(2,1)}, bf16[4,512,512]{2,1,0:T(8,128)(2,1)S(1)}, u32[]{:S(2)}, u32[]{:S(2)}) collective-permute-start(bf16[4,512,512]{2,1,0:T(8,128)(2,1)} %right_ref.1), channel_id=1, source_target_pairs={{0,1},{1,0},{2,3},{3,2},{4,5},{5,4},{6,7},{7,6},{8,9},{9,8},{10,11... | collective-permute-start | bytes 6291464 | tf_op jit(solution)/shard_map/ppermute | solution.py:304
  4.0 9.5 %collective-permute-start.3 = (bf16[256,512]{1,0:T(8,128)(2,1)S(1)}, bf16[256,512]{1,0:T(8,128)(2,1)S(1)}, u32[]{:S(2)}, u32[]{:S(2)}) collective-permute-start(bf16[256,512]{1,0:T(8,128)(2,1)S(1)} %get-tuple-element.33.refs_6_.refs_0_), channel_id=1, source_target_pairs={{0,4},{4,0},{8,12},{12,8},{16,20},{20,16},{24,28},{28,24},{1,5},{5... | collective-permute-start | bytes 786440 | tf_op jit(solution)/shard_map/ppermute | solution.py:341
  13.5 7.8 %collective-permute-start.5 = (bf16[256,512]{1,0:T(8,128)(2,1)S(1)}, bf16[256,512]{1,0:T(8,128)(2,1)S(1)}, u32[]{:S(2)}, u32[]{:S(2)}) collective-permute-start(bf16[256,512]{1,0:T(8,128)(2,1)S(1)} %get-tuple-element.39.refs_8_.refs_0_.refs_10_), channel_id=1, source_target_pairs={{0,4},{4,0},{8,12},{12,8},{16,20},{20,16},{24,28},{28,24},{1,5},{5... | collective-permute-start | bytes 786440 | tf_op jit(solution)/shard_map/ppermute | solution.py:370
  15.2 8.1 %collective-permute-start.6 = (bf16[256,512]{1,0:T(8,128)(2,1)S(1)}, bf16[256,512]{1,0:T(8,128)(2,1)S(1)}, u32[]{:S(2)}, u32[]{:S(2)}) collective-permute-start(bf16[256,512]{1,0:T(8,128)(2,1)S(1)} %collective-permute-done.3.refs_10_), channel_id=1, source_target_pairs={{0,8},{8,16},{16,24},{12,4},{20,12},{28,20},{1,9},{9,17},{17,25},{... | collective-permute-start | bytes 786440 | tf_op jit(solution)/shard_map/ppermute | solution.py:371
  30.5 9.0 %collective-permute-start.11 = (bf16[256,512]{1,0:T(8,128)(2,1)S(1)}, bf16[256,512]{1,0:T(8,128)(2,1)S(1)}, u32[]{:S(2)}, u32[]{:S(2)}) collective-permute-start(bf16[256,512]{1,0:T(8,128)(2,1)S(1)} %full.6.a_ref), channel_id=1, source_target_pairs={{0,2},{1,3},{2,0},{3,1},{4,6},{5,7},{6,4},{7,5},{8,10},{9,11},{10,... | collective-permute-start | bytes 786440 | tf_op jit(solution)/shard_map/ppermute | solution.py:409
  35.8 8.8 %collective-permute-start.13 = (bf16[256,512]{1,0:T(8,128)(2,1)S(1)}, bf16[256,512]{1,0:T(8,128)(2,1)S(1)}, u32[]{:S(2)}, u32[]{:S(2)}) collective-permute-start(bf16[256,512]{1,0:T(8,128)(2,1)S(1)} %full.7.a_ref), channel_id=1, source_target_pairs={{0,2},{1,3},{2,0},{3,1},{4,6},{5,7},{6,4},{7,5},{8,10},{9,11},{10,... | collective-permute-start | bytes 786440 | tf_op jit(solution)/shard_map/ppermute | solution.py:409
  40.5 9.7 %collective-permute-start.15 = (bf16[256,512]{1,0:T(8,128)(2,1)S(1)}, bf16[256,512]{1,0:T(8,128)(2,1)S(1)}, u32[]{:S(2)}, u32[]{:S(2)}) collective-permute-start(bf16[256,512]{1,0:T(8,128)(2,1)S(1)} %get-tuple-element.43.refs_6_.refs_1_.refs_2_), channel_id=1, source_target_pairs={{0,4},{4,0},{8,12},{12,8},{16,20},{20,16},{24,28},{28,24},{1,5},{5... | collective-permute-start | bytes 786440 | tf_op jit(solution)/shard_map/ppermute | solution.py:362
  45.6 15.1 %collective-permute-start.17 = (bf16[256,512]{1,0:T(8,128)(2,1)S(1)}, bf16[256,512]{1,0:T(8,128)(2,1)S(1)}, u32[]{:S(2)}, u32[]{:S(2)}) collective-permute-start(bf16[256,512]{1,0:T(8,128)(2,1)S(1)} %get-tuple-element.45.refs_8_.refs_1_.refs_12_), channel_id=1, source_target_pairs={{0,4},{4,0},{8,12},{12,8},{16,20},{20,16},{24,28},{28,24},{1,5},{5... | collective-permute-start | bytes 786440 | tf_op jit(solution)/shard_map/ppermute | solution.py:370
  49.5 11.8 %collective-permute-start.23 = (bf16[256,512]{1,0:T(8,128)(2,1)S(1)}, bf16[256,512]{1,0:T(8,128)(2,1)S(1)}, u32[]{:S(2)}, u32[]{:S(2)}) collective-permute-start(bf16[256,512]{1,0:T(8,128)(2,1)S(1)} %get-tuple-element.45.refs_8_.refs_1_.refs_12_), channel_id=1, source_target_pairs={{4,8},{12,16},{20,24},{8,4},{16,12},{24,20},{5,9},{13,17},{21,25},... | collective-permute-start | bytes 786440 | tf_op jit(solution)/shard_map/ppermute | solution.py:372
  50.2 11.2 %collective-permute-start.14 = (bf16[256,512]{1,0:T(8,128)(2,1)S(1)}, bf16[256,512]{1,0:T(8,128)(2,1)S(1)}, u32[]{:S(2)}, u32[]{:S(2)}) collective-permute-start(bf16[256,512]{1,0:T(8,128)(2,1)S(1)} %get-tuple-element.45.refs_8_.refs_1_.refs_12_), channel_id=1, source_target_pairs={{0,1},{1,0},{2,3},{3,2},{4,5},{5,4},{6,7},{7,6},{8,9},{9,8},{10,11... | collective-permute-start | bytes 786440 | tf_op jit(solution)/shard_map/ppermute | solution.py:304
  50.2 11.5 %collective-permute-start.21 = (bf16[256,512]{1,0:T(8,128)(2,1)S(1)}, bf16[256,512]{1,0:T(8,128)(2,1)S(1)}, u32[]{:S(2)}, u32[]{:S(2)}) collective-permute-start(bf16[256,512]{1,0:T(8,128)(2,1)S(1)} %collective-permute-done.15.refs_10_), channel_id=1, source_target_pairs={{0,8},{8,16},{16,24},{12,4},{20,12},{28,20},{1,9},{9,17},{17,25},{... | collective-permute-start | bytes 786440 | tf_op jit(solution)/shard_map/ppermute | solution.py:371
  67.4 9.2 %collective-permute-start.25 = (bf16[256,512]{1,0:T(8,128)(2,1)S(1)}, bf16[256,512]{1,0:T(8,128)(2,1)S(1)}, u32[]{:S(2)}, u32[]{:S(2)}) collective-permute-start(bf16[256,512]{1,0:T(8,128)(2,1)S(1)} %full.8.a_ref), channel_id=1, source_target_pairs={{0,2},{1,3},{2,0},{3,1},{4,6},{5,7},{6,4},{7,5},{8,10},{9,11},{10,... | collective-permute-start | bytes 786440 | tf_op jit(solution)/shard_map/ppermute | solution.py:409
  72.4 10.6 %collective-permute-start.27 = (bf16[256,512]{1,0:T(8,128)(2,1)S(1)}, bf16[256,512]{1,0:T(8,128)(2,1)S(1)}, u32[]{:S(2)}, u32[]{:S(2)}) collective-permute-start(bf16[256,512]{1,0:T(8,128)(2,1)S(1)} %full.9.a_ref), channel_id=1, source_target_pairs={{0,2},{1,3},{2,0},{3,1},{4,6},{5,7},{6,4},{7,5},{8,10},{9,11},{10,... | collective-permute-start | bytes 786440 | tf_op jit(solution)/shard_map/ppermute | solution.py:409
  77.2 9.9 %collective-permute-start.29 = (bf16[256,512]{1,0:T(8,128)(2,1)S(1)}, bf16[256,512]{1,0:T(8,128)(2,1)S(1)}, u32[]{:S(2)}, u32[]{:S(2)}) collective-permute-start(bf16[256,512]{1,0:T(8,128)(2,1)S(1)} %image.8.refs_6_.refs_2_.refs_4_), channel_id=1, source_target_pairs={{0,4},{4,0},{8,12},{12,8},{16,20},{20,16},{24,28},{28,24},{1,5},{5... | collective-permute-start | bytes 786440 | tf_op jit(solution)/shard_map/ppermute | solution.py:362
  83.6 14.9 %collective-permute-start.32 = (bf16[256,512]{1,0:T(8,128)(2,1)S(1)}, bf16[256,512]{1,0:T(8,128)(2,1)S(1)}, u32[]{:S(2)}, u32[]{:S(2)}) collective-permute-start(bf16[256,512]{1,0:T(8,128)(2,1)S(1)} %image.9.refs_8_.refs_2_.refs_14_), channel_id=1, source_target_pairs={{0,4},{4,0},{8,12},{12,8},{16,20},{20,16},{24,28},{28,24},{1,5},{5... | collective-permute-start | bytes 786440 | tf_op jit(solution)/shard_map/ppermute | solution.py:370
  86.3 12.7 %collective-permute-start.37 = (bf16[256,512]{1,0:T(8,128)(2,1)S(1)}, bf16[256,512]{1,0:T(8,128)(2,1)S(1)}, u32[]{:S(2)}, u32[]{:S(2)}) collective-permute-start(bf16[256,512]{1,0:T(8,128)(2,1)S(1)} %image.9.refs_8_.refs_2_.refs_14_), channel_id=1, source_target_pairs={{4,8},{12,16},{20,24},{8,4},{16,12},{24,20},{5,9},{13,17},{21,25},... | collective-permute-start | bytes 786440 | tf_op jit(solution)/shard_map/ppermute | solution.py:372
  87.0 12.2 %collective-permute-start.28 = (bf16[256,512]{1,0:T(8,128)(2,1)S(1)}, bf16[256,512]{1,0:T(8,128)(2,1)S(1)}, u32[]{:S(2)}, u32[]{:S(2)}) collective-permute-start(bf16[256,512]{1,0:T(8,128)(2,1)S(1)} %image.9.refs_8_.refs_2_.refs_14_), channel_id=1, source_target_pairs={{0,1},{1,0},{2,3},{3,2},{4,5},{5,4},{6,7},{7,6},{8,9},{9,8},{10,11... | collective-permute-start | bytes 786440 | tf_op jit(solution)/shard_map/ppermute | solution.py:304
  87.1 12.5 %collective-permute-start.35 = (bf16[256,512]{1,0:T(8,128)(2,1)S(1)}, bf16[256,512]{1,0:T(8,128)(2,1)S(1)}, u32[]{:S(2)}, u32[]{:S(2)}) collective-permute-start(bf16[256,512]{1,0:T(8,128)(2,1)S(1)} %collective-permute-done.29.refs_10_), channel_id=1, source_target_pairs={{0,8},{8,16},{16,24},{12,4},{20,12},{28,20},{1,9},{9,17},{17,25},{... | collective-permute-start | bytes 786440 | tf_op jit(solution)/shard_map/ppermute | solution.py:371
  105.6 6.3 %collective-permute-start.39 = (bf16[128,512]{1,0:T(8,128)(2,1)S(1)}, bf16[128,512]{1,0:T(8,128)(2,1)S(1)}, u32[]{:S(2)}, u32[]{:S(2)}) collective-permute-start(bf16[128,512]{1,0:T(8,128)(2,1)S(1)} %get-tuple-element.56), channel_id=1, source_target_pairs={{0,2},{1,3},{2,0},{3,1},{4,6},{5,7},{6,4},{7,5},{8,10},{9,11},{10,... | collective-permute-start | bytes 393224 | tf_op jit(solution)/shard_map/ppermute | solution.py:409
  119.9 9.9 %collective-permute-start.45 = (bf16[128,512]{1,0:T(8,128)(2,1)S(1)}, bf16[128,512]{1,0:T(8,128)(2,1)S(1)}, u32[]{:S(2)}, u32[]{:S(2)}) collective-permute-start(bf16[128,512]{1,0:T(8,128)(2,1)S(1)} %get-tuple-element.62.refs_16_), channel_id=1, source_target_pairs={{0,2},{1,3},{2,0},{3,1},{4,6},{5,7},{6,4},{7,5},{8,10},{9,11},{10,... | collective-permute-start | bytes 393224 | tf_op jit(solution)/shard_map/ppermute | solution.py:421
  120.4 9.9 %collective-permute-start.41 = (bf16[128,512]{1,0:T(8,128)(2,1)S(1)}, bf16[128,512]{1,0:T(8,128)(2,1)S(1)}, u32[]{:S(2)}, u32[]{:S(2)}) collective-permute-start(bf16[128,512]{1,0:T(8,128)(2,1)S(1)} %get-tuple-element.59.refs_6_), channel_id=1, source_target_pairs={{0,2},{1,3},{2,0},{3,1},{4,6},{5,7},{6,4},{7,5},{8,10},{9,11},{10,... | collective-permute-start | bytes 393224 | tf_op jit(solution)/shard_map/ppermute | solution.py:421
  122.0 6.3 %collective-permute-start.50 = (f32[8,128]{1,0:T(8,128)S(1)}, f32[8,128]{1,0:T(8,128)S(1)}, u32[]{:S(2)}, u32[]{:S(2)}) collective-permute-start(f32[8,128]{1,0:T(8,128)S(1)} %add_add_fusion.1), channel_id=1, source_target_pairs={{0,12},{1,13},{2,14},{3,15},{4,8},{5,9},{6,10},{7,11},{8,4},{9,5},... | collective-permute-start | bytes 12296 | tf_op jit(solution)/shard_map/ppermute | solution.py:323
  128.3 6.7 %collective-permute-start.44 = (bf16[128,512]{1,0:T(8,128)(2,1)S(1)}, bf16[128,512]{1,0:T(8,128)(2,1)S(1)}, u32[]{:S(2)}, u32[]{:S(2)}) collective-permute-start(bf16[128,512]{1,0:T(8,128)(2,1)S(1)} %get-tuple-element.62.refs_16_), channel_id=1, source_target_pairs={{0,1},{1,0},{2,3},{3,2},{4,5},{5,4},{6,7},{7,6},{8,9},{9,8},{10,11... | collective-permute-start | bytes 393224 | tf_op jit(solution)/shard_map/ppermute | solution.py:304
  (36 other events, 131.2 us)

commit v6 on v5

--- a/solution.py
+++ b/solution.py
@@ -268,17 +268,20 @@
     c2 = q3[2] / beta0
     coefs = [(q3[0] - alpha0 * c1) / norm, (c1 - alpha0 * c2) / norm, c2 / norm, q3[3]]
     quarter = block_rows // 4
+    chunk = 32
     for t in range(sectors):
         sector_refs = refs[10 * t : 10 * t + 10]
         for which in range(2):
             start = half_of(which, 2 * quarter).start
             for side in range(2):
                 part = side_of(side, quarter, lax.axis_size("op"))
-                blocks = [sector_refs[2 * k + which][part, :] for k in range(3)]
-                blocks.append(sector_refs[6 + 2 * side + which][...])
-                vector = sum(c * block.astype(F32) for c, block in zip(coefs, blocks))
-                rows = pl.ds(pl.multiple_of(start + part.start, quarter), quarter)
-                out_ref[t, rows, :] = vector.astype(BF16)
+                for r in range(0, quarter, chunk):
+                    here = pl.ds(pl.multiple_of(part.start + r, chunk), chunk)
+                    blocks = [sector_refs[2 * k + which][here, :] for k in range(3)]
+                    blocks.append(sector_refs[6 + 2 * side + which][r : r + chunk, :])
+                    vector = sum(c * block.astype(F32) for c, block in zip(coefs, blocks))
+                    rows = pl.ds(pl.multiple_of(start + part.start + r, chunk), chunk)
+                    out_ref[t, rows, :] = vector.astype(BF16)
     row = lax.broadcasted_iota(jnp.int32, coef_ref.shape, 0)
     column = lax.broadcasted_iota(jnp.int32, coef_ref.shape, 1)
     value = jnp.zeros(coef_ref.shape, F32)
@@ -370,8 +373,7 @@
         pair_1 = lax.ppermute(mine_1, "sec", pairs)
         far_0 = lax.ppermute(pair_0, "sec", onward)
         far_1 = lax.ppermute(mine_1, "sec", diagonal)
-        if product == 0:
-            pair_1 = after(pair_1, far_0)
+        pair_1 = after(pair_1, far_0)
         if product == 1:
             tile = flipped_merge(flipped_merge(sums, "op", [1]), "sec", bits[:1])
             pair_1 = after(pair_1, tile)

time: 139 us -> 137 us (0.986)
  waiting for transfers between devices: 35.9 us -> 34.3 us
    ppermute x4, waiting for transfers between devices: 8.18 us -> 6.1 us  [flipped_merge(): arrived = lax.ppermute(tile, axis, flips)]
  transfers between devices with their start and end apart: 54 -> 54, of which waited for: 26 -> 27; matrix products, arithmetic and copies ran while one was open for 0% -> 0% of each run, Pallas kernels for 12% -> 12%
where the time goes in v6:
time: 137 us
  starting transfers between devices  63.2 us (46%)
  waiting for transfers between devices  34.3 us (25%)
  Pallas kernels  32.5 us (24%)
  local copies, waits for them, and re-layouts  5.67 us (4%)
    pallas_call x18, Pallas kernels, call(): pl.pallas_call(kernel, name=name, out_shape=out, in_specs=[SMEM if a.dtyp...  32 us
    ppermute x3, starting transfers between devices, on_device(): far_0 = lax.ppermute(pair_0, 'sec', onward)  13.3 us
    ppermute x6, waiting for transfers between devices, on_device(): arrived = lax.ppermute(parts[-1], 'op', flips)  10.4 us
    ppermute x6, starting transfers between devices, sum_four(): lax.ppermute(stats, ('sec', 'op'), [(i, i ^ mask) for i in places])  8.73 us
    ppermute x3, starting transfers between devices, on_device(): pair_1 = lax.ppermute(mine_1, 'sec', pairs)  8.1 us
    ppermute x2, starting transfers between devices, on_device(): pair_0 = lax.ppermute(mine_0, 'sec', pairs)  6.99 us
    ppermute x4, starting transfers between devices, flipped_merge(): arrived = lax.ppermute(tile, axis, flips)  6.72 us
    ppermute x6, starting transfers between devices, on_device(): arrived = lax.ppermute(parts[-1], 'op', flips)  6.47 us
  transfers between devices with their start and end apart: 54, of which 27 were waited for; matrix products, arithmetic and copies ran while one was open for 0% of the time, Pallas kernels for 12%

profile of v6, /device:TPU:0, one launch (start us, length us, event | category | flops | bytes accessed | tf_op | source)
XLA Modules:
  0.0 136.6 jit_solution(3729624805085086127)
XLA Ops:
  4.0 3.0 %collective-permute-start.3 = (bf16[256,512]{1,0:T(8,128)(2,1)S(1)}, bf16[256,512]{1,0:T(8,128)(2,1)S(1)}, u32[]{:S(2)}, u32[]{:S(2)}) collective-permute-start(bf16[256,512]{1,0:T(8,128)(2,1)S(1)} %get-tuple-element.35.refs_6_.refs_0_), channel_id=1, source_target_pairs={{0,4},{4,0},{8,12},{12,8},{16,20},{20,16},{24,28},{28,24},{1,5},{5... | collective-permute-start | bytes 786440 | tf_op jit(solution)/shard_map/ppermute | solution.py:344
  6.9 2.2 %copy-done = bf16[4,2,512,512]{3,2,1,0:T(8,128)(2,1)S(1)} copy-done((bf16[4,2,512,512]{3,2,1,0:T(8,128)(2,1)S(1)}, bf16[4,2,512,512]{3,2,1,0:T(8,128)(2,1)}, u32[]{:S(2)}) %copy-start) | copy-done | bytes 4194328
  11.2 2.3 %collective-permute-done.3.refs_10_ = bf16[256,512]{1,0:T(8,128)(2,1)S(1)} collective-permute-done((bf16[256,512]{1,0:T(8,128)(2,1)S(1)}, bf16[256,512]{1,0:T(8,128)(2,1)S(1)}, u32[]{:S(2)}, u32[]{:S(2)}) %collective-permute-start.3) | collective-permute-done | bytes 262176 | tf_op jit(solution)/shard_map/ppermute | solution.py:344
  15.2 3.5 %collective-permute-start.6 = (bf16[256,512]{1,0:T(8,128)(2,1)S(1)}, bf16[256,512]{1,0:T(8,128)(2,1)S(1)}, u32[]{:S(2)}, u32[]{:S(2)}) collective-permute-start(bf16[256,512]{1,0:T(8,128)(2,1)S(1)} %collective-permute-done.3.refs_10_), channel_id=1, source_target_pairs={{0,8},{8,16},{16,24},{12,4},{20,12},{28,20},{1,9},{9,17},{17,25},{... | collective-permute-start | bytes 786440 | tf_op jit(solution)/shard_map/ppermute | solution.py:374
  26.8 3.7 %full.6.a_ref = bf16[256,512]{1,0:T(8,128)(2,1)S(1)} custom-call(s32[4]{0:T(128)S(1)} %copy-done.5, bf16[4,2,512,512]{3,2,1,0:T(8,128)(2,1)S(1)} %get-tuple-element.37.refs_1_, bf16[4,512,512]{2,1,0:T(8,128)(2,1)S(1)} %get-tuple-element.38.refs_2_, s32[4]{0:T(128)S(1)} %collective-permute-done.refs_3_, ...), custom_call_target="tpu_custom_call" | custom-call | tf_op jit(solution)/shard_map/full/pallas_call | solution.py:18
  32.1 3.7 %full.7.a_ref = bf16[256,512]{1,0:T(8,128)(2,1)S(1)} custom-call(s32[4]{0:T(128)S(1)} %copy-done.5, bf16[4,2,512,512]{3,2,1,0:T(8,128)(2,1)S(1)} %get-tuple-element.37.refs_1_, bf16[4,512,512]{2,1,0:T(8,128)(2,1)S(1)} %get-tuple-element.38.refs_2_, s32[4]{0:T(128)S(1)} %collective-permute-done.refs_3_, ...), custom_call_target="tpu_custom_call" | custom-call | tf_op jit(solution)/shard_map/full/pallas_call | solution.py:18
  36.3 3.2 %collective-permute-done.11.b_ref = bf16[256,512]{1,0:T(8,128)(2,1)S(1)} collective-permute-done((bf16[256,512]{1,0:T(8,128)(2,1)S(1)}, bf16[256,512]{1,0:T(8,128)(2,1)S(1)}, u32[]{:S(2)}, u32[]{:S(2)}) %collective-permute-start.11) | collective-permute-done | bytes 262176 | tf_op jit(solution)/shard_map/ppermute | solution.py:411
  40.5 3.9 %collective-permute-start.15 = (bf16[256,512]{1,0:T(8,128)(2,1)S(1)}, bf16[256,512]{1,0:T(8,128)(2,1)S(1)}, u32[]{:S(2)}, u32[]{:S(2)}) collective-permute-start(bf16[256,512]{1,0:T(8,128)(2,1)S(1)} %get-tuple-element.45.refs_6_.refs_1_.refs_2_), channel_id=1, source_target_pairs={{0,4},{4,0},{8,12},{12,8},{16,20},{20,16},{24,28},{28,24},{1,5},{5... | collective-permute-start | bytes 786440 | tf_op jit(solution)/shard_map/ppermute | solution.py:365
  45.6 3.9 %collective-permute-start.17 = (bf16[256,512]{1,0:T(8,128)(2,1)S(1)}, bf16[256,512]{1,0:T(8,128)(2,1)S(1)}, u32[]{:S(2)}, u32[]{:S(2)}) collective-permute-start(bf16[256,512]{1,0:T(8,128)(2,1)S(1)} %get-tuple-element.47.refs_8_.refs_1_.refs_12_), channel_id=1, source_target_pairs={{0,4},{4,0},{8,12},{12,8},{16,20},{20,16},{24,28},{28,24},{1,5},{5... | collective-permute-start | bytes 786440 | tf_op jit(solution)/shard_map/ppermute | solution.py:373
  50.2 4.7 %collective-permute-start.18 = (bf16[256,512]{1,0:T(8,128)(2,1)S(1)}, bf16[256,512]{1,0:T(8,128)(2,1)S(1)}, u32[]{:S(2)}, u32[]{:S(2)}) collective-permute-start(bf16[256,512]{1,0:T(8,128)(2,1)S(1)} %collective-permute-done.15.refs_10_), channel_id=1, source_target_pairs={{0,8},{8,16},{16,24},{12,4},{20,12},{28,20},{1,9},{9,17},{17,25},{... | collective-permute-start | bytes 786440 | tf_op jit(solution)/shard_map/ppermute | solution.py:374
  57.4 3.2 %collective-permute-done.20.arrived_ref = f32[24,128]{1,0:T(8,128)S(1)} collective-permute-done((f32[24,128]{1,0:T(8,128)S(1)}, f32[24,128]{1,0:T(8,128)S(1)}, u32[]{:S(2)}, u32[]{:S(2)}) %collective-permute-start.20) | collective-permute-done | bytes 12320 | tf_op jit(solution)/shard_map/ppermute | solution.py:317
  63.7 3.7 %full.8.a_ref = bf16[256,512]{1,0:T(8,128)(2,1)S(1)} custom-call(s32[4]{0:T(128)S(1)} %copy-done.5, bf16[4,2,512,512]{3,2,1,0:T(8,128)(2,1)S(1)} %get-tuple-element.37.refs_1_, bf16[4,512,512]{2,1,0:T(8,128)(2,1)S(1)} %get-tuple-element.38.refs_2_, s32[4]{0:T(128)S(1)} %collective-permute-done.refs_3_, ...), custom_call_target="tpu_custom_call" | custom-call | tf_op jit(solution)/shard_map/full/pallas_call | solution.py:18
  68.7 3.7 %full.9.a_ref = bf16[256,512]{1,0:T(8,128)(2,1)S(1)} custom-call(s32[4]{0:T(128)S(1)} %copy-done.5, bf16[4,2,512,512]{3,2,1,0:T(8,128)(2,1)S(1)} %get-tuple-element.37.refs_1_, bf16[4,512,512]{2,1,0:T(8,128)(2,1)S(1)} %get-tuple-element.38.refs_2_, s32[4]{0:T(128)S(1)} %collective-permute-done.refs_3_, ...), custom_call_target="tpu_custom_call" | custom-call | tf_op jit(solution)/shard_map/full/pallas_call | solution.py:18
  73.2 3.4 %collective-permute-done.25.b_ref = bf16[256,512]{1,0:T(8,128)(2,1)S(1)} collective-permute-done((bf16[256,512]{1,0:T(8,128)(2,1)S(1)}, bf16[256,512]{1,0:T(8,128)(2,1)S(1)}, u32[]{:S(2)}, u32[]{:S(2)}) %collective-permute-start.25) | collective-permute-done | bytes 262176 | tf_op jit(solution)/shard_map/ppermute | solution.py:411
  77.2 3.1 %collective-permute-start.29 = (bf16[256,512]{1,0:T(8,128)(2,1)S(1)}, bf16[256,512]{1,0:T(8,128)(2,1)S(1)}, u32[]{:S(2)}, u32[]{:S(2)}) collective-permute-start(bf16[256,512]{1,0:T(8,128)(2,1)S(1)} %image.8.refs_6_.refs_2_.refs_4_), channel_id=1, source_target_pairs={{0,4},{4,0},{8,12},{12,8},{16,20},{20,16},{24,28},{28,24},{1,5},{5... | collective-permute-start | bytes 786440 | tf_op jit(solution)/shard_map/ppermute | solution.py:365
  82.7 2.4 %collective-permute-start.32 = (bf16[256,512]{1,0:T(8,128)(2,1)S(1)}, bf16[256,512]{1,0:T(8,128)(2,1)S(1)}, u32[]{:S(2)}, u32[]{:S(2)}) collective-permute-start(bf16[256,512]{1,0:T(8,128)(2,1)S(1)} %image.9.refs_8_.refs_2_.refs_14_), channel_id=1, source_target_pairs={{0,4},{4,0},{8,12},{12,8},{16,20},{20,16},{24,28},{28,24},{1,5},{5... | collective-permute-start | bytes 786440 | tf_op jit(solution)/shard_map/ppermute | solution.py:373
  85.9 5.1 %collective-permute-start.33 = (bf16[256,512]{1,0:T(8,128)(2,1)S(1)}, bf16[256,512]{1,0:T(8,128)(2,1)S(1)}, u32[]{:S(2)}, u32[]{:S(2)}) collective-permute-start(bf16[256,512]{1,0:T(8,128)(2,1)S(1)} %collective-permute-done.29.refs_10_), channel_id=1, source_target_pairs={{0,8},{8,16},{16,24},{12,4},{20,12},{28,20},{1,9},{9,17},{17,25},{... | collective-permute-start | bytes 786440 | tf_op jit(solution)/shard_map/ppermute | solution.py:374
  91.0 3.6 %collective-permute-start.34 = (f32[24,128]{1,0:T(8,128)S(1)}, f32[24,128]{1,0:T(8,128)S(1)}, u32[]{:S(2)}, u32[]{:S(2)}) collective-permute-start(f32[24,128]{1,0:T(8,128)S(1)} %merge.6.own_ref), channel_id=1, source_target_pairs={{0,16},{4,20},{8,24},{12,28},{16,0},{20,4},{24,8},{28,12},{1,17},{... | collective-permute-start | bytes 36872 | tf_op jit(solution)/shard_map/ppermute | solution.py:317
  99.5 4.1 %full.10 = (bf16[128,512]{1,0:T(8,128)(2,1)S(1)}, bf16[128,512]{1,0:T(8,128)(2,1)S(1)}) custom-call(s32[4]{0:T(128)S(1)} %copy-done.5, bf16[4,2,512,512]{3,2,1,0:T(8,128)(2,1)S(1)} %get-tuple-element.37.refs_1_, bf16[4,512,512]{2,1,0:T(8,128)(2,1)S(1)} %get-tuple-element.38.refs_2_, s32[4]{0:T(128)S(1)} %collective-permute-done.refs_3_, ...), custom_call_target="tpu_custom_call" | custom-call | tf_op jit(solution)/shard_map/full/pallas_call | solution.py:18
  104.9 4.1 %full.11 = (bf16[128,512]{1,0:T(8,128)(2,1)S(1)}, bf16[128,512]{1,0:T(8,128)(2,1)S(1)}) custom-call(s32[4]{0:T(128)S(1)} %copy-done.5, bf16[4,2,512,512]{3,2,1,0:T(8,128)(2,1)S(1)} %get-tuple-element.37.refs_1_, bf16[4,512,512]{2,1,0:T(8,128)(2,1)S(1)} %get-tuple-element.38.refs_2_, s32[4]{0:T(128)S(1)} %collective-permute-done.refs_3_, ...), custom_call_target="tpu_custom_call" | custom-call | tf_op jit(solution)/shard_map/full/pallas_call | solution.py:18
  110.9 3.6 %collective-permute-done.43.b_ref = bf16[128,512]{1,0:T(8,128)(2,1)S(1)} collective-permute-done((bf16[128,512]{1,0:T(8,128)(2,1)S(1)}, bf16[128,512]{1,0:T(8,128)(2,1)S(1)}, u32[]{:S(2)}, u32[]{:S(2)}) %collective-permute-start.43) | collective-permute-done | bytes 131104 | tf_op jit(solution)/shard_map/ppermute | solution.py:411
  120.0 4.7 %collective-permute-start.50 = (f32[8,128]{1,0:T(8,128)S(1)}, f32[8,128]{1,0:T(8,128)S(1)}, u32[]{:S(2)}, u32[]{:S(2)}) collective-permute-start(f32[8,128]{1,0:T(8,128)S(1)} %add_add_fusion.1), channel_id=1, source_target_pairs={{0,12},{1,13},{2,14},{3,15},{4,8},{5,9},{6,10},{7,11},{8,4},{9,5},... | collective-permute-start | bytes 12296 | tf_op jit(solution)/shard_map/ppermute | solution.py:326
  130.5 3.0 %collective-permute-done.53 = f32[8,128]{1,0:T(8,128)S(1)} collective-permute-done((f32[8,128]{1,0:T(8,128)S(1)}, f32[8,128]{1,0:T(8,128)S(1)}, u32[]{:S(2)}, u32[]{:S(2)}) %collective-permute-start.53) | collective-permute-done | bytes 4128 | tf_op jit(solution)/shard_map/ppermute | solution.py:311
  133.6 3.1 %last.1 = (bf16[2,512,512]{2,1,0:T(8,128)(2,1)}, f32[2,3]{1,0:T(2,128)}) custom-call(s32[16]{0:T(128)S(1)} %copy-done.4, bf16[256,512]{1,0:T(8,128)(2,1)S(1)} %get-tuple-element.35.refs_6_.refs_0_, bf16[256,512]{1,0:T(8,128)(2,1)S(1)} %get-tuple-element.36.refs_7_.refs_1_, bf16[256,512]{1,0:T(8,128)(2,1)S(1)} %get-tuple-element.45.refs_6_.refs_1_.refs_2_, ...), custom_call_target="tpu_custom_call" | custom-call | tf_op jit(solution)/shard_map/last/pallas_call | solution.py:18
  (118 shorter events, 50.8 us)
Async XLA Ops:
  0.6 26.2 %collective-permute-start.1 = (bf16[4,2,512,512]{3,2,1,0:T(8,128)(2,1)}, bf16[4,2,512,512]{3,2,1,0:T(8,128)(2,1)S(1)}, u32[]{:S(2)}, u32[]{:S(2)}) collective-permute-start(bf16[4,2,512,512]{3,2,1,0:T(8,128)(2,1)} %left_ref.1), channel_id=1, source_target_pairs={{0,1},{1,0},{2,3},{3,2},{4,5},{5,4},{6,7},{7,6},{8,9},{9,8},{10,11... | collective-permute-start | bytes 12582920 | tf_op jit(solution)/shard_map/ppermute | solution.py:307
  1.1 25.6 %collective-permute-start.2 = (bf16[4,512,512]{2,1,0:T(8,128)(2,1)}, bf16[4,512,512]{2,1,0:T(8,128)(2,1)S(1)}, u32[]{:S(2)}, u32[]{:S(2)}) collective-permute-start(bf16[4,512,512]{2,1,0:T(8,128)(2,1)} %right_ref.1), channel_id=1, source_target_pairs={{0,1},{1,0},{2,3},{3,2},{4,5},{5,4},{6,7},{7,6},{8,9},{9,8},{10,11... | collective-permute-start | bytes 6291464 | tf_op jit(solution)/shard_map/ppermute | solution.py:307
  4.0 9.5 %collective-permute-start.3 = (bf16[256,512]{1,0:T(8,128)(2,1)S(1)}, bf16[256,512]{1,0:T(8,128)(2,1)S(1)}, u32[]{:S(2)}, u32[]{:S(2)}) collective-permute-start(bf16[256,512]{1,0:T(8,128)(2,1)S(1)} %get-tuple-element.35.refs_6_.refs_0_), channel_id=1, source_target_pairs={{0,4},{4,0},{8,12},{12,8},{16,20},{20,16},{24,28},{28,24},{1,5},{5... | collective-permute-start | bytes 786440 | tf_op jit(solution)/shard_map/ppermute | solution.py:344
  13.5 7.8 %collective-permute-start.5 = (bf16[256,512]{1,0:T(8,128)(2,1)S(1)}, bf16[256,512]{1,0:T(8,128)(2,1)S(1)}, u32[]{:S(2)}, u32[]{:S(2)}) collective-permute-start(bf16[256,512]{1,0:T(8,128)(2,1)S(1)} %get-tuple-element.41.refs_8_.refs_0_.refs_10_), channel_id=1, source_target_pairs={{0,4},{4,0},{8,12},{12,8},{16,20},{20,16},{24,28},{28,24},{1,5},{5... | collective-permute-start | bytes 786440 | tf_op jit(solution)/shard_map/ppermute | solution.py:373
  15.2 8.1 %collective-permute-start.6 = (bf16[256,512]{1,0:T(8,128)(2,1)S(1)}, bf16[256,512]{1,0:T(8,128)(2,1)S(1)}, u32[]{:S(2)}, u32[]{:S(2)}) collective-permute-start(bf16[256,512]{1,0:T(8,128)(2,1)S(1)} %collective-permute-done.3.refs_10_), channel_id=1, source_target_pairs={{0,8},{8,16},{16,24},{12,4},{20,12},{28,20},{1,9},{9,17},{17,25},{... | collective-permute-start | bytes 786440 | tf_op jit(solution)/shard_map/ppermute | solution.py:374
  30.5 9.0 %collective-permute-start.11 = (bf16[256,512]{1,0:T(8,128)(2,1)S(1)}, bf16[256,512]{1,0:T(8,128)(2,1)S(1)}, u32[]{:S(2)}, u32[]{:S(2)}) collective-permute-start(bf16[256,512]{1,0:T(8,128)(2,1)S(1)} %full.6.a_ref), channel_id=1, source_target_pairs={{0,2},{1,3},{2,0},{3,1},{4,6},{5,7},{6,4},{7,5},{8,10},{9,11},{10,... | collective-permute-start | bytes 786440 | tf_op jit(solution)/shard_map/ppermute | solution.py:411
  35.8 8.8 %collective-permute-start.13 = (bf16[256,512]{1,0:T(8,128)(2,1)S(1)}, bf16[256,512]{1,0:T(8,128)(2,1)S(1)}, u32[]{:S(2)}, u32[]{:S(2)}) collective-permute-start(bf16[256,512]{1,0:T(8,128)(2,1)S(1)} %full.7.a_ref), channel_id=1, source_target_pairs={{0,2},{1,3},{2,0},{3,1},{4,6},{5,7},{6,4},{7,5},{8,10},{9,11},{10,... | collective-permute-start | bytes 786440 | tf_op jit(solution)/shard_map/ppermute | solution.py:411
  40.5 9.7 %collective-permute-start.15 = (bf16[256,512]{1,0:T(8,128)(2,1)S(1)}, bf16[256,512]{1,0:T(8,128)(2,1)S(1)}, u32[]{:S(2)}, u32[]{:S(2)}) collective-permute-start(bf16[256,512]{1,0:T(8,128)(2,1)S(1)} %get-tuple-element.45.refs_6_.refs_1_.refs_2_), channel_id=1, source_target_pairs={{0,4},{4,0},{8,12},{12,8},{16,20},{20,16},{24,28},{28,24},{1,5},{5... | collective-permute-start | bytes 786440 | tf_op jit(solution)/shard_map/ppermute | solution.py:365
  45.6 15.1 %collective-permute-start.17 = (bf16[256,512]{1,0:T(8,128)(2,1)S(1)}, bf16[256,512]{1,0:T(8,128)(2,1)S(1)}, u32[]{:S(2)}, u32[]{:S(2)}) collective-permute-start(bf16[256,512]{1,0:T(8,128)(2,1)S(1)} %get-tuple-element.47.refs_8_.refs_1_.refs_12_), channel_id=1, source_target_pairs={{0,4},{4,0},{8,12},{12,8},{16,20},{20,16},{24,28},{28,24},{1,5},{5... | collective-permute-start | bytes 786440 | tf_op jit(solution)/shard_map/ppermute | solution.py:373
  49.5 11.8 %collective-permute-start.23 = (bf16[256,512]{1,0:T(8,128)(2,1)S(1)}, bf16[256,512]{1,0:T(8,128)(2,1)S(1)}, u32[]{:S(2)}, u32[]{:S(2)}) collective-permute-start(bf16[256,512]{1,0:T(8,128)(2,1)S(1)} %get-tuple-element.47.refs_8_.refs_1_.refs_12_), channel_id=1, source_target_pairs={{4,8},{12,16},{20,24},{8,4},{16,12},{24,20},{5,9},{13,17},{21,25},... | collective-permute-start | bytes 786440 | tf_op jit(solution)/shard_map/ppermute | solution.py:375
  50.2 11.2 %collective-permute-start.18 = (bf16[256,512]{1,0:T(8,128)(2,1)S(1)}, bf16[256,512]{1,0:T(8,128)(2,1)S(1)}, u32[]{:S(2)}, u32[]{:S(2)}) collective-permute-start(bf16[256,512]{1,0:T(8,128)(2,1)S(1)} %collective-permute-done.15.refs_10_), channel_id=1, source_target_pairs={{0,8},{8,16},{16,24},{12,4},{20,12},{28,20},{1,9},{9,17},{17,25},{... | collective-permute-start | bytes 786440 | tf_op jit(solution)/shard_map/ppermute | solution.py:374
  54.9 6.9 %collective-permute-start.14 = (bf16[256,512]{1,0:T(8,128)(2,1)S(1)}, bf16[256,512]{1,0:T(8,128)(2,1)S(1)}, u32[]{:S(2)}, u32[]{:S(2)}) collective-permute-start(bf16[256,512]{1,0:T(8,128)(2,1)S(1)} %get-tuple-element.47.refs_8_.refs_1_.refs_12_), channel_id=1, source_target_pairs={{0,1},{1,0},{2,3},{3,2},{4,5},{5,4},{6,7},{7,6},{8,9},{9,8},{10,11... | collective-permute-start | bytes 786440 | tf_op jit(solution)/shard_map/ppermute | solution.py:307
  67.4 9.2 %collective-permute-start.25 = (bf16[256,512]{1,0:T(8,128)(2,1)S(1)}, bf16[256,512]{1,0:T(8,128)(2,1)S(1)}, u32[]{:S(2)}, u32[]{:S(2)}) collective-permute-start(bf16[256,512]{1,0:T(8,128)(2,1)S(1)} %full.8.a_ref), channel_id=1, source_target_pairs={{0,2},{1,3},{2,0},{3,1},{4,6},{5,7},{6,4},{7,5},{8,10},{9,11},{10,... | collective-permute-start | bytes 786440 | tf_op jit(solution)/shard_map/ppermute | solution.py:411
  72.4 9.7 %collective-permute-start.27 = (bf16[256,512]{1,0:T(8,128)(2,1)S(1)}, bf16[256,512]{1,0:T(8,128)(2,1)S(1)}, u32[]{:S(2)}, u32[]{:S(2)}) collective-permute-start(bf16[256,512]{1,0:T(8,128)(2,1)S(1)} %full.9.a_ref), channel_id=1, source_target_pairs={{0,2},{1,3},{2,0},{3,1},{4,6},{5,7},{6,4},{7,5},{8,10},{9,11},{10,... | collective-permute-start | bytes 786440 | tf_op jit(solution)/shard_map/ppermute | solution.py:411
  77.2 8.6 %collective-permute-start.29 = (bf16[256,512]{1,0:T(8,128)(2,1)S(1)}, bf16[256,512]{1,0:T(8,128)(2,1)S(1)}, u32[]{:S(2)}, u32[]{:S(2)}) collective-permute-start(bf16[256,512]{1,0:T(8,128)(2,1)S(1)} %image.8.refs_6_.refs_2_.refs_4_), channel_id=1, source_target_pairs={{0,4},{4,0},{8,12},{12,8},{16,20},{20,16},{24,28},{28,24},{1,5},{5... | collective-permute-start | bytes 786440 | tf_op jit(solution)/shard_map/ppermute | solution.py:365
  82.7 13.8 %collective-permute-start.32 = (bf16[256,512]{1,0:T(8,128)(2,1)S(1)}, bf16[256,512]{1,0:T(8,128)(2,1)S(1)}, u32[]{:S(2)}, u32[]{:S(2)}) collective-permute-start(bf16[256,512]{1,0:T(8,128)(2,1)S(1)} %image.9.refs_8_.refs_2_.refs_14_), channel_id=1, source_target_pairs={{0,4},{4,0},{8,12},{12,8},{16,20},{20,16},{24,28},{28,24},{1,5},{5... | collective-permute-start | bytes 786440 | tf_op jit(solution)/shard_map/ppermute | solution.py:373
  85.1 11.9 %collective-permute-start.37 = (bf16[256,512]{1,0:T(8,128)(2,1)S(1)}, bf16[256,512]{1,0:T(8,128)(2,1)S(1)}, u32[]{:S(2)}, u32[]{:S(2)}) collective-permute-start(bf16[256,512]{1,0:T(8,128)(2,1)S(1)} %image.9.refs_8_.refs_2_.refs_14_), channel_id=1, source_target_pairs={{4,8},{12,16},{20,24},{8,4},{16,12},{24,20},{5,9},{13,17},{21,25},... | collective-permute-start | bytes 786440 | tf_op jit(solution)/shard_map/ppermute | solution.py:375
  85.9 11.3 %collective-permute-start.33 = (bf16[256,512]{1,0:T(8,128)(2,1)S(1)}, bf16[256,512]{1,0:T(8,128)(2,1)S(1)}, u32[]{:S(2)}, u32[]{:S(2)}) collective-permute-start(bf16[256,512]{1,0:T(8,128)(2,1)S(1)} %collective-permute-done.29.refs_10_), channel_id=1, source_target_pairs={{0,8},{8,16},{16,24},{12,4},{20,12},{28,20},{1,9},{9,17},{17,25},{... | collective-permute-start | bytes 786440 | tf_op jit(solution)/shard_map/ppermute | solution.py:374
  90.9 6.6 %collective-permute-start.28 = (bf16[256,512]{1,0:T(8,128)(2,1)S(1)}, bf16[256,512]{1,0:T(8,128)(2,1)S(1)}, u32[]{:S(2)}, u32[]{:S(2)}) collective-permute-start(bf16[256,512]{1,0:T(8,128)(2,1)S(1)} %image.9.refs_8_.refs_2_.refs_14_), channel_id=1, source_target_pairs={{0,1},{1,0},{2,3},{3,2},{4,5},{5,4},{6,7},{7,6},{8,9},{9,8},{10,11... | collective-permute-start | bytes 786440 | tf_op jit(solution)/shard_map/ppermute | solution.py:307
  103.6 6.3 %collective-permute-start.39 = (bf16[128,512]{1,0:T(8,128)(2,1)S(1)}, bf16[128,512]{1,0:T(8,128)(2,1)S(1)}, u32[]{:S(2)}, u32[]{:S(2)}) collective-permute-start(bf16[128,512]{1,0:T(8,128)(2,1)S(1)} %get-tuple-element.60), channel_id=1, source_target_pairs={{0,2},{1,3},{2,0},{3,1},{4,6},{5,7},{6,4},{7,5},{8,10},{9,11},{10,... | collective-permute-start | bytes 393224 | tf_op jit(solution)/shard_map/ppermute | solution.py:411
  117.7 10.7 %collective-permute-start.45 = (bf16[128,512]{1,0:T(8,128)(2,1)S(1)}, bf16[128,512]{1,0:T(8,128)(2,1)S(1)}, u32[]{:S(2)}, u32[]{:S(2)}) collective-permute-start(bf16[128,512]{1,0:T(8,128)(2,1)S(1)} %get-tuple-element.66.refs_16_), channel_id=1, source_target_pairs={{0,2},{1,3},{2,0},{3,1},{4,6},{5,7},{6,4},{7,5},{8,10},{9,11},{10,... | collective-permute-start | bytes 393224 | tf_op jit(solution)/shard_map/ppermute | solution.py:423
  118.4 10.5 %collective-permute-start.41 = (bf16[128,512]{1,0:T(8,128)(2,1)S(1)}, bf16[128,512]{1,0:T(8,128)(2,1)S(1)}, u32[]{:S(2)}, u32[]{:S(2)}) collective-permute-start(bf16[128,512]{1,0:T(8,128)(2,1)S(1)} %get-tuple-element.63.refs_6_), channel_id=1, source_target_pairs={{0,2},{1,3},{2,0},{3,1},{4,6},{5,7},{6,4},{7,5},{8,10},{9,11},{10,... | collective-permute-start | bytes 393224 | tf_op jit(solution)/shard_map/ppermute | solution.py:423
  120.0 6.5 %collective-permute-start.50 = (f32[8,128]{1,0:T(8,128)S(1)}, f32[8,128]{1,0:T(8,128)S(1)}, u32[]{:S(2)}, u32[]{:S(2)}) collective-permute-start(f32[8,128]{1,0:T(8,128)S(1)} %add_add_fusion.1), channel_id=1, source_target_pairs={{0,12},{1,13},{2,14},{3,15},{4,8},{5,9},{6,10},{7,11},{8,4},{9,5},... | collective-permute-start | bytes 12296 | tf_op jit(solution)/shard_map/ppermute | solution.py:326
  126.6 7.0 %collective-permute-start.44 = (bf16[128,512]{1,0:T(8,128)(2,1)S(1)}, bf16[128,512]{1,0:T(8,128)(2,1)S(1)}, u32[]{:S(2)}, u32[]{:S(2)}) collective-permute-start(bf16[128,512]{1,0:T(8,128)(2,1)S(1)} %get-tuple-element.66.refs_16_), channel_id=1, source_target_pairs={{0,1},{1,0},{2,3},{3,2},{4,5},{5,4},{6,7},{7,6},{8,9},{9,8},{10,11... | collective-permute-start | bytes 393224 | tf_op jit(solution)/shard_map/ppermute | solution.py:307
  (36 other events, 129.8 us)

commit v7 on v6

--- a/solution.py
+++ b/solution.py
@@ -119,6 +119,10 @@
     return norm, alpha, unit * jnp.sqrt(jnp.maximum(rest, 0.0))
 
 
+def input_scale(norm, beta):
+    return (1.0 / (norm * beta)).astype(BF16)
+
+
 def form(gram, a, b):
     return sum(a[i] * b[j] * gram[min(i, j)][max(i, j)] for i in a for j in b)
 
@@ -163,12 +167,12 @@
     if scalars:
         rows_ref, tile_ref = scalars
         norm, _, beta = first_scalars(tile_ref, live_entries(rows_ref, v_ref.shape[2]))
-        scale = 1.0 / (norm * beta)
+        scale = input_scale(norm, beta)
     for i, slot in enumerate(slots):
         for which in range(2):
             value = refs[2 * i + which][...]
             if scalars:
-                value = (value.astype(F32) * scale).astype(BF16)
+                value = value * scale
             v_ref[slot, half_of(which, half), :] = value
 
 
@@ -235,6 +239,7 @@
     zeroth, image, second = (block * (1.0 / norm) for block in basis)
     scale = 1.0 / beta
     first = (image - alpha * zeroth) * scale
+    value = value * (scale / (input_scale(norm, beta).astype(F32) * norm))
     value = (value - (alpha * scale) * second) * scale
     second = (second - alpha * image) * scale
     value = value.astype(BF16)

time: 137 us -> 137 us (level)
  no operation moved by 1% of the time
where the time goes in v7:
time: 137 us; the launch traced here: 136 us
  starting transfers between devices  63.3 us (46%)
  waiting for transfers between devices  34.3 us (25%)
  Pallas kernels  32 us (23%)
  local copies, waits for them, and re-layouts  5.67 us (4%)
    pallas_call x18, Pallas kernels, call(): pl.pallas_call(kernel, name=name, out_shape=out, in_specs=[SMEM if a.dtyp...  31.6 us
    ppermute x3, starting transfers between devices, on_device(): far_0 = lax.ppermute(pair_0, 'sec', onward)  13.3 us
    ppermute x6, waiting for transfers between devices, on_device(): arrived = lax.ppermute(parts[-1], 'op', flips)  10.3 us
    ppermute x6, starting transfers between devices, sum_four(): lax.ppermute(stats, ('sec', 'op'), [(i, i ^ mask) for i in places])  8.77 us
    ppermute x3, starting transfers between devices, on_device(): pair_1 = lax.ppermute(mine_1, 'sec', pairs)  8.1 us
    ppermute x2, starting transfers between devices, on_device(): pair_0 = lax.ppermute(mine_0, 'sec', pairs)  7.05 us
    ppermute x4, starting transfers between devices, flipped_merge(): arrived = lax.ppermute(tile, axis, flips)  6.73 us
    ppermute x6, starting transfers between devices, on_device(): arrived = lax.ppermute(parts[-1], 'op', flips)  6.46 us
  transfers between devices with their start and end apart: 54, of which 27 were waited for; matrix products, arithmetic and copies ran while one was open for 0% of the time, Pallas kernels for 12%

profile of v7, /device:TPU:0, one launch (start us, length us, event | category | flops | bytes accessed | tf_op | source)
XLA Modules:
  0.0 136.2 jit_solution(16533684691725133476)
XLA Ops:
  4.0 3.0 %collective-permute-start.3 = (bf16[256,512]{1,0:T(8,128)(2,1)S(1)}, bf16[256,512]{1,0:T(8,128)(2,1)S(1)}, u32[]{:S(2)}, u32[]{:S(2)}) collective-permute-start(bf16[256,512]{1,0:T(8,128)(2,1)S(1)} %get-tuple-element.35.refs_6_.refs_0_), channel_id=1, source_target_pairs={{0,4},{4,0},{8,12},{12,8},{16,20},{20,16},{24,28},{28,24},{1,5},{5... | collective-permute-start | bytes 786440 | tf_op jit(solution)/shard_map/ppermute | solution.py:349
  6.9 2.2 %copy-done = bf16[4,2,512,512]{3,2,1,0:T(8,128)(2,1)S(1)} copy-done((bf16[4,2,512,512]{3,2,1,0:T(8,128)(2,1)S(1)}, bf16[4,2,512,512]{3,2,1,0:T(8,128)(2,1)}, u32[]{:S(2)}) %copy-start) | copy-done | bytes 4194328
  11.2 2.3 %collective-permute-done.3.refs_10_ = bf16[256,512]{1,0:T(8,128)(2,1)S(1)} collective-permute-done((bf16[256,512]{1,0:T(8,128)(2,1)S(1)}, bf16[256,512]{1,0:T(8,128)(2,1)S(1)}, u32[]{:S(2)}, u32[]{:S(2)}) %collective-permute-start.3) | collective-permute-done | bytes 262176 | tf_op jit(solution)/shard_map/ppermute | solution.py:349
  15.2 3.5 %collective-permute-start.6 = (bf16[256,512]{1,0:T(8,128)(2,1)S(1)}, bf16[256,512]{1,0:T(8,128)(2,1)S(1)}, u32[]{:S(2)}, u32[]{:S(2)}) collective-permute-start(bf16[256,512]{1,0:T(8,128)(2,1)S(1)} %collective-permute-done.3.refs_10_), channel_id=1, source_target_pairs={{0,8},{8,16},{16,24},{12,4},{20,12},{28,20},{1,9},{9,17},{17,25},{... | collective-permute-start | bytes 786440 | tf_op jit(solution)/shard_map/ppermute | solution.py:379
  26.8 3.7 %full.6.a_ref = bf16[256,512]{1,0:T(8,128)(2,1)S(1)} custom-call(s32[4]{0:T(128)S(1)} %copy-done.5, bf16[4,2,512,512]{3,2,1,0:T(8,128)(2,1)S(1)} %get-tuple-element.37.refs_1_, bf16[4,512,512]{2,1,0:T(8,128)(2,1)S(1)} %get-tuple-element.38.refs_2_, s32[4]{0:T(128)S(1)} %collective-permute-done.refs_3_, ...), custom_call_target="tpu_custom_call" | custom-call | tf_op jit(solution)/shard_map/full/pallas_call | solution.py:18
  32.1 3.7 %full.7.a_ref = bf16[256,512]{1,0:T(8,128)(2,1)S(1)} custom-call(s32[4]{0:T(128)S(1)} %copy-done.5, bf16[4,2,512,512]{3,2,1,0:T(8,128)(2,1)S(1)} %get-tuple-element.37.refs_1_, bf16[4,512,512]{2,1,0:T(8,128)(2,1)S(1)} %get-tuple-element.38.refs_2_, s32[4]{0:T(128)S(1)} %collective-permute-done.refs_3_, ...), custom_call_target="tpu_custom_call" | custom-call | tf_op jit(solution)/shard_map/full/pallas_call | solution.py:18
  36.3 3.2 %collective-permute-done.11.b_ref = bf16[256,512]{1,0:T(8,128)(2,1)S(1)} collective-permute-done((bf16[256,512]{1,0:T(8,128)(2,1)S(1)}, bf16[256,512]{1,0:T(8,128)(2,1)S(1)}, u32[]{:S(2)}, u32[]{:S(2)}) %collective-permute-start.11) | collective-permute-done | bytes 262176 | tf_op jit(solution)/shard_map/ppermute | solution.py:416
  40.5 4.0 %collective-permute-start.15 = (bf16[256,512]{1,0:T(8,128)(2,1)S(1)}, bf16[256,512]{1,0:T(8,128)(2,1)S(1)}, u32[]{:S(2)}, u32[]{:S(2)}) collective-permute-start(bf16[256,512]{1,0:T(8,128)(2,1)S(1)} %get-tuple-element.45.refs_6_.refs_1_.refs_2_), channel_id=1, source_target_pairs={{0,4},{4,0},{8,12},{12,8},{16,20},{20,16},{24,28},{28,24},{1,5},{5... | collective-permute-start | bytes 786440 | tf_op jit(solution)/shard_map/ppermute | solution.py:370
  45.6 3.9 %collective-permute-start.17 = (bf16[256,512]{1,0:T(8,128)(2,1)S(1)}, bf16[256,512]{1,0:T(8,128)(2,1)S(1)}, u32[]{:S(2)}, u32[]{:S(2)}) collective-permute-start(bf16[256,512]{1,0:T(8,128)(2,1)S(1)} %get-tuple-element.47.refs_8_.refs_1_.refs_12_), channel_id=1, source_target_pairs={{0,4},{4,0},{8,12},{12,8},{16,20},{20,16},{24,28},{28,24},{1,5},{5... | collective-permute-start | bytes 786440 | tf_op jit(solution)/shard_map/ppermute | solution.py:378
  50.2 4.7 %collective-permute-start.18 = (bf16[256,512]{1,0:T(8,128)(2,1)S(1)}, bf16[256,512]{1,0:T(8,128)(2,1)S(1)}, u32[]{:S(2)}, u32[]{:S(2)}) collective-permute-start(bf16[256,512]{1,0:T(8,128)(2,1)S(1)} %collective-permute-done.15.refs_10_), channel_id=1, source_target_pairs={{0,8},{8,16},{16,24},{12,4},{20,12},{28,20},{1,9},{9,17},{17,25},{... | collective-permute-start | bytes 786440 | tf_op jit(solution)/shard_map/ppermute | solution.py:379
  57.4 3.2 %collective-permute-done.20.arrived_ref = f32[24,128]{1,0:T(8,128)S(1)} collective-permute-done((f32[24,128]{1,0:T(8,128)S(1)}, f32[24,128]{1,0:T(8,128)S(1)}, u32[]{:S(2)}, u32[]{:S(2)}) %collective-permute-start.20) | collective-permute-done | bytes 12320 | tf_op jit(solution)/shard_map/ppermute | solution.py:322
  63.7 3.7 %full.8.a_ref = bf16[256,512]{1,0:T(8,128)(2,1)S(1)} custom-call(s32[4]{0:T(128)S(1)} %copy-done.5, bf16[4,2,512,512]{3,2,1,0:T(8,128)(2,1)S(1)} %get-tuple-element.37.refs_1_, bf16[4,512,512]{2,1,0:T(8,128)(2,1)S(1)} %get-tuple-element.38.refs_2_, s32[4]{0:T(128)S(1)} %collective-permute-done.refs_3_, ...), custom_call_target="tpu_custom_call" | custom-call | tf_op jit(solution)/shard_map/full/pallas_call | solution.py:18
  68.7 3.7 %full.9.a_ref = bf16[256,512]{1,0:T(8,128)(2,1)S(1)} custom-call(s32[4]{0:T(128)S(1)} %copy-done.5, bf16[4,2,512,512]{3,2,1,0:T(8,128)(2,1)S(1)} %get-tuple-element.37.refs_1_, bf16[4,512,512]{2,1,0:T(8,128)(2,1)S(1)} %get-tuple-element.38.refs_2_, s32[4]{0:T(128)S(1)} %collective-permute-done.refs_3_, ...), custom_call_target="tpu_custom_call" | custom-call | tf_op jit(solution)/shard_map/full/pallas_call | solution.py:18
  73.2 3.4 %collective-permute-done.25.b_ref = bf16[256,512]{1,0:T(8,128)(2,1)S(1)} collective-permute-done((bf16[256,512]{1,0:T(8,128)(2,1)S(1)}, bf16[256,512]{1,0:T(8,128)(2,1)S(1)}, u32[]{:S(2)}, u32[]{:S(2)}) %collective-permute-start.25) | collective-permute-done | bytes 262176 | tf_op jit(solution)/shard_map/ppermute | solution.py:416
  77.2 3.1 %collective-permute-start.29 = (bf16[256,512]{1,0:T(8,128)(2,1)S(1)}, bf16[256,512]{1,0:T(8,128)(2,1)S(1)}, u32[]{:S(2)}, u32[]{:S(2)}) collective-permute-start(bf16[256,512]{1,0:T(8,128)(2,1)S(1)} %image.8.refs_6_.refs_2_.refs_4_), channel_id=1, source_target_pairs={{0,4},{4,0},{8,12},{12,8},{16,20},{20,16},{24,28},{28,24},{1,5},{5... | collective-permute-start | bytes 786440 | tf_op jit(solution)/shard_map/ppermute | solution.py:370
  82.7 2.4 %collective-permute-start.32 = (bf16[256,512]{1,0:T(8,128)(2,1)S(1)}, bf16[256,512]{1,0:T(8,128)(2,1)S(1)}, u32[]{:S(2)}, u32[]{:S(2)}) collective-permute-start(bf16[256,512]{1,0:T(8,128)(2,1)S(1)} %image.9.refs_8_.refs_2_.refs_14_), channel_id=1, source_target_pairs={{0,4},{4,0},{8,12},{12,8},{16,20},{20,16},{24,28},{28,24},{1,5},{5... | collective-permute-start | bytes 786440 | tf_op jit(solution)/shard_map/ppermute | solution.py:378
  85.8 5.1 %collective-permute-start.33 = (bf16[256,512]{1,0:T(8,128)(2,1)S(1)}, bf16[256,512]{1,0:T(8,128)(2,1)S(1)}, u32[]{:S(2)}, u32[]{:S(2)}) collective-permute-start(bf16[256,512]{1,0:T(8,128)(2,1)S(1)} %collective-permute-done.29.refs_10_), channel_id=1, source_target_pairs={{0,8},{8,16},{16,24},{12,4},{20,12},{28,20},{1,9},{9,17},{17,25},{... | collective-permute-start | bytes 786440 | tf_op jit(solution)/shard_map/ppermute | solution.py:379
  91.0 3.6 %collective-permute-start.34 = (f32[24,128]{1,0:T(8,128)S(1)}, f32[24,128]{1,0:T(8,128)S(1)}, u32[]{:S(2)}, u32[]{:S(2)}) collective-permute-start(f32[24,128]{1,0:T(8,128)S(1)} %merge.6.own_ref), channel_id=1, source_target_pairs={{0,16},{4,20},{8,24},{12,28},{16,0},{20,4},{24,8},{28,12},{1,17},{... | collective-permute-start | bytes 36872 | tf_op jit(solution)/shard_map/ppermute | solution.py:322
  99.5 3.9 %full.10 = (bf16[128,512]{1,0:T(8,128)(2,1)S(1)}, bf16[128,512]{1,0:T(8,128)(2,1)S(1)}) custom-call(s32[4]{0:T(128)S(1)} %copy-done.5, bf16[4,2,512,512]{3,2,1,0:T(8,128)(2,1)S(1)} %get-tuple-element.37.refs_1_, bf16[4,512,512]{2,1,0:T(8,128)(2,1)S(1)} %get-tuple-element.38.refs_2_, s32[4]{0:T(128)S(1)} %collective-permute-done.refs_3_, ...), custom_call_target="tpu_custom_call" | custom-call | tf_op jit(solution)/shard_map/full/pallas_call | solution.py:18
  104.7 3.9 %full.11 = (bf16[128,512]{1,0:T(8,128)(2,1)S(1)}, bf16[128,512]{1,0:T(8,128)(2,1)S(1)}) custom-call(s32[4]{0:T(128)S(1)} %copy-done.5, bf16[4,2,512,512]{3,2,1,0:T(8,128)(2,1)S(1)} %get-tuple-element.37.refs_1_, bf16[4,512,512]{2,1,0:T(8,128)(2,1)S(1)} %get-tuple-element.38.refs_2_, s32[4]{0:T(128)S(1)} %collective-permute-done.refs_3_, ...), custom_call_target="tpu_custom_call" | custom-call | tf_op jit(solution)/shard_map/full/pallas_call | solution.py:18
  110.4 3.6 %collective-permute-done.43.b_ref = bf16[128,512]{1,0:T(8,128)(2,1)S(1)} collective-permute-done((bf16[128,512]{1,0:T(8,128)(2,1)S(1)}, bf16[128,512]{1,0:T(8,128)(2,1)S(1)}, u32[]{:S(2)}, u32[]{:S(2)}) %collective-permute-start.43) | collective-permute-done | bytes 131104 | tf_op jit(solution)/shard_map/ppermute | solution.py:416
  119.5 4.8 %collective-permute-start.50 = (f32[8,128]{1,0:T(8,128)S(1)}, f32[8,128]{1,0:T(8,128)S(1)}, u32[]{:S(2)}, u32[]{:S(2)}) collective-permute-start(f32[8,128]{1,0:T(8,128)S(1)} %add_add_fusion.1), channel_id=1, source_target_pairs={{0,12},{1,13},{2,14},{3,15},{4,8},{5,9},{6,10},{7,11},{8,4},{9,5},... | collective-permute-start | bytes 12296 | tf_op jit(solution)/shard_map/ppermute | solution.py:331
  130.0 3.1 %collective-permute-done.53 = f32[8,128]{1,0:T(8,128)S(1)} collective-permute-done((f32[8,128]{1,0:T(8,128)S(1)}, f32[8,128]{1,0:T(8,128)S(1)}, u32[]{:S(2)}, u32[]{:S(2)}) %collective-permute-start.53) | collective-permute-done | bytes 4128 | tf_op jit(solution)/shard_map/ppermute | solution.py:316
  133.2 3.1 %last.1 = (bf16[2,512,512]{2,1,0:T(8,128)(2,1)}, f32[2,3]{1,0:T(2,128)}) custom-call(s32[16]{0:T(128)S(1)} %copy-done.4, bf16[256,512]{1,0:T(8,128)(2,1)S(1)} %get-tuple-element.35.refs_6_.refs_0_, bf16[256,512]{1,0:T(8,128)(2,1)S(1)} %get-tuple-element.36.refs_7_.refs_1_, bf16[256,512]{1,0:T(8,128)(2,1)S(1)} %get-tuple-element.45.refs_6_.refs_1_.refs_2_, ...), custom_call_target="tpu_custom_call" | custom-call | tf_op jit(solution)/shard_map/last/pallas_call | solution.py:18
  (118 shorter events, 50.7 us)
Async XLA Ops:
  0.6 26.2 %collective-permute-start.1 = (bf16[4,2,512,512]{3,2,1,0:T(8,128)(2,1)}, bf16[4,2,512,512]{3,2,1,0:T(8,128)(2,1)S(1)}, u32[]{:S(2)}, u32[]{:S(2)}) collective-permute-start(bf16[4,2,512,512]{3,2,1,0:T(8,128)(2,1)} %left_ref.1), channel_id=1, source_target_pairs={{0,1},{1,0},{2,3},{3,2},{4,5},{5,4},{6,7},{7,6},{8,9},{9,8},{10,11... | collective-permute-start | bytes 12582920 | tf_op jit(solution)/shard_map/ppermute | solution.py:312
  1.1 25.6 %collective-permute-start.2 = (bf16[4,512,512]{2,1,0:T(8,128)(2,1)}, bf16[4,512,512]{2,1,0:T(8,128)(2,1)S(1)}, u32[]{:S(2)}, u32[]{:S(2)}) collective-permute-start(bf16[4,512,512]{2,1,0:T(8,128)(2,1)} %right_ref.1), channel_id=1, source_target_pairs={{0,1},{1,0},{2,3},{3,2},{4,5},{5,4},{6,7},{7,6},{8,9},{9,8},{10,11... | collective-permute-start | bytes 6291464 | tf_op jit(solution)/shard_map/ppermute | solution.py:312
  4.0 9.5 %collective-permute-start.3 = (bf16[256,512]{1,0:T(8,128)(2,1)S(1)}, bf16[256,512]{1,0:T(8,128)(2,1)S(1)}, u32[]{:S(2)}, u32[]{:S(2)}) collective-permute-start(bf16[256,512]{1,0:T(8,128)(2,1)S(1)} %get-tuple-element.35.refs_6_.refs_0_), channel_id=1, source_target_pairs={{0,4},{4,0},{8,12},{12,8},{16,20},{20,16},{24,28},{28,24},{1,5},{5... | collective-permute-start | bytes 786440 | tf_op jit(solution)/shard_map/ppermute | solution.py:349
  13.5 7.8 %collective-permute-start.5 = (bf16[256,512]{1,0:T(8,128)(2,1)S(1)}, bf16[256,512]{1,0:T(8,128)(2,1)S(1)}, u32[]{:S(2)}, u32[]{:S(2)}) collective-permute-start(bf16[256,512]{1,0:T(8,128)(2,1)S(1)} %get-tuple-element.41.refs_8_.refs_0_.refs_10_), channel_id=1, source_target_pairs={{0,4},{4,0},{8,12},{12,8},{16,20},{20,16},{24,28},{28,24},{1,5},{5... | collective-permute-start | bytes 786440 | tf_op jit(solution)/shard_map/ppermute | solution.py:378
  15.2 8.1 %collective-permute-start.6 = (bf16[256,512]{1,0:T(8,128)(2,1)S(1)}, bf16[256,512]{1,0:T(8,128)(2,1)S(1)}, u32[]{:S(2)}, u32[]{:S(2)}) collective-permute-start(bf16[256,512]{1,0:T(8,128)(2,1)S(1)} %collective-permute-done.3.refs_10_), channel_id=1, source_target_pairs={{0,8},{8,16},{16,24},{12,4},{20,12},{28,20},{1,9},{9,17},{17,25},{... | collective-permute-start | bytes 786440 | tf_op jit(solution)/shard_map/ppermute | solution.py:379
  30.5 9.0 %collective-permute-start.11 = (bf16[256,512]{1,0:T(8,128)(2,1)S(1)}, bf16[256,512]{1,0:T(8,128)(2,1)S(1)}, u32[]{:S(2)}, u32[]{:S(2)}) collective-permute-start(bf16[256,512]{1,0:T(8,128)(2,1)S(1)} %full.6.a_ref), channel_id=1, source_target_pairs={{0,2},{1,3},{2,0},{3,1},{4,6},{5,7},{6,4},{7,5},{8,10},{9,11},{10,... | collective-permute-start | bytes 786440 | tf_op jit(solution)/shard_map/ppermute | solution.py:416
  35.8 8.8 %collective-permute-start.13 = (bf16[256,512]{1,0:T(8,128)(2,1)S(1)}, bf16[256,512]{1,0:T(8,128)(2,1)S(1)}, u32[]{:S(2)}, u32[]{:S(2)}) collective-permute-start(bf16[256,512]{1,0:T(8,128)(2,1)S(1)} %full.7.a_ref), channel_id=1, source_target_pairs={{0,2},{1,3},{2,0},{3,1},{4,6},{5,7},{6,4},{7,5},{8,10},{9,11},{10,... | collective-permute-start | bytes 786440 | tf_op jit(solution)/shard_map/ppermute | solution.py:416
  40.5 9.7 %collective-permute-start.15 = (bf16[256,512]{1,0:T(8,128)(2,1)S(1)}, bf16[256,512]{1,0:T(8,128)(2,1)S(1)}, u32[]{:S(2)}, u32[]{:S(2)}) collective-permute-start(bf16[256,512]{1,0:T(8,128)(2,1)S(1)} %get-tuple-element.45.refs_6_.refs_1_.refs_2_), channel_id=1, source_target_pairs={{0,4},{4,0},{8,12},{12,8},{16,20},{20,16},{24,28},{28,24},{1,5},{5... | collective-permute-start | bytes 786440 | tf_op jit(solution)/shard_map/ppermute | solution.py:370
  45.6 15.1 %collective-permute-start.17 = (bf16[256,512]{1,0:T(8,128)(2,1)S(1)}, bf16[256,512]{1,0:T(8,128)(2,1)S(1)}, u32[]{:S(2)}, u32[]{:S(2)}) collective-permute-start(bf16[256,512]{1,0:T(8,128)(2,1)S(1)} %get-tuple-element.47.refs_8_.refs_1_.refs_12_), channel_id=1, source_target_pairs={{0,4},{4,0},{8,12},{12,8},{16,20},{20,16},{24,28},{28,24},{1,5},{5... | collective-permute-start | bytes 786440 | tf_op jit(solution)/shard_map/ppermute | solution.py:378
  49.5 11.8 %collective-permute-start.23 = (bf16[256,512]{1,0:T(8,128)(2,1)S(1)}, bf16[256,512]{1,0:T(8,128)(2,1)S(1)}, u32[]{:S(2)}, u32[]{:S(2)}) collective-permute-start(bf16[256,512]{1,0:T(8,128)(2,1)S(1)} %get-tuple-element.47.refs_8_.refs_1_.refs_12_), channel_id=1, source_target_pairs={{4,8},{12,16},{20,24},{8,4},{16,12},{24,20},{5,9},{13,17},{21,25},... | collective-permute-start | bytes 786440 | tf_op jit(solution)/shard_map/ppermute | solution.py:380
  50.2 11.2 %collective-permute-start.18 = (bf16[256,512]{1,0:T(8,128)(2,1)S(1)}, bf16[256,512]{1,0:T(8,128)(2,1)S(1)}, u32[]{:S(2)}, u32[]{:S(2)}) collective-permute-start(bf16[256,512]{1,0:T(8,128)(2,1)S(1)} %collective-permute-done.15.refs_10_), channel_id=1, source_target_pairs={{0,8},{8,16},{16,24},{12,4},{20,12},{28,20},{1,9},{9,17},{17,25},{... | collective-permute-start | bytes 786440 | tf_op jit(solution)/shard_map/ppermute | solution.py:379
  54.9 6.8 %collective-permute-start.14 = (bf16[256,512]{1,0:T(8,128)(2,1)S(1)}, bf16[256,512]{1,0:T(8,128)(2,1)S(1)}, u32[]{:S(2)}, u32[]{:S(2)}) collective-permute-start(bf16[256,512]{1,0:T(8,128)(2,1)S(1)} %get-tuple-element.47.refs_8_.refs_1_.refs_12_), channel_id=1, source_target_pairs={{0,1},{1,0},{2,3},{3,2},{4,5},{5,4},{6,7},{7,6},{8,9},{9,8},{10,11... | collective-permute-start | bytes 786440 | tf_op jit(solution)/shard_map/ppermute | solution.py:312
  67.4 9.2 %collective-permute-start.25 = (bf16[256,512]{1,0:T(8,128)(2,1)S(1)}, bf16[256,512]{1,0:T(8,128)(2,1)S(1)}, u32[]{:S(2)}, u32[]{:S(2)}) collective-permute-start(bf16[256,512]{1,0:T(8,128)(2,1)S(1)} %full.8.a_ref), channel_id=1, source_target_pairs={{0,2},{1,3},{2,0},{3,1},{4,6},{5,7},{6,4},{7,5},{8,10},{9,11},{10,... | collective-permute-start | bytes 786440 | tf_op jit(solution)/shard_map/ppermute | solution.py:416
  72.4 9.6 %collective-permute-start.27 = (bf16[256,512]{1,0:T(8,128)(2,1)S(1)}, bf16[256,512]{1,0:T(8,128)(2,1)S(1)}, u32[]{:S(2)}, u32[]{:S(2)}) collective-permute-start(bf16[256,512]{1,0:T(8,128)(2,1)S(1)} %full.9.a_ref), channel_id=1, source_target_pairs={{0,2},{1,3},{2,0},{3,1},{4,6},{5,7},{6,4},{7,5},{8,10},{9,11},{10,... | collective-permute-start | bytes 786440 | tf_op jit(solution)/shard_map/ppermute | solution.py:416
  77.2 8.6 %collective-permute-start.29 = (bf16[256,512]{1,0:T(8,128)(2,1)S(1)}, bf16[256,512]{1,0:T(8,128)(2,1)S(1)}, u32[]{:S(2)}, u32[]{:S(2)}) collective-permute-start(bf16[256,512]{1,0:T(8,128)(2,1)S(1)} %image.8.refs_6_.refs_2_.refs_4_), channel_id=1, source_target_pairs={{0,4},{4,0},{8,12},{12,8},{16,20},{20,16},{24,28},{28,24},{1,5},{5... | collective-permute-start | bytes 786440 | tf_op jit(solution)/shard_map/ppermute | solution.py:370
  82.7 13.8 %collective-permute-start.32 = (bf16[256,512]{1,0:T(8,128)(2,1)S(1)}, bf16[256,512]{1,0:T(8,128)(2,1)S(1)}, u32[]{:S(2)}, u32[]{:S(2)}) collective-permute-start(bf16[256,512]{1,0:T(8,128)(2,1)S(1)} %image.9.refs_8_.refs_2_.refs_14_), channel_id=1, source_target_pairs={{0,4},{4,0},{8,12},{12,8},{16,20},{20,16},{24,28},{28,24},{1,5},{5... | collective-permute-start | bytes 786440 | tf_op jit(solution)/shard_map/ppermute | solution.py:378
  85.1 11.9 %collective-permute-start.37 = (bf16[256,512]{1,0:T(8,128)(2,1)S(1)}, bf16[256,512]{1,0:T(8,128)(2,1)S(1)}, u32[]{:S(2)}, u32[]{:S(2)}) collective-permute-start(bf16[256,512]{1,0:T(8,128)(2,1)S(1)} %image.9.refs_8_.refs_2_.refs_14_), channel_id=1, source_target_pairs={{4,8},{12,16},{20,24},{8,4},{16,12},{24,20},{5,9},{13,17},{21,25},... | collective-permute-start | bytes 786440 | tf_op jit(solution)/shard_map/ppermute | solution.py:380
  85.8 11.3 %collective-permute-start.33 = (bf16[256,512]{1,0:T(8,128)(2,1)S(1)}, bf16[256,512]{1,0:T(8,128)(2,1)S(1)}, u32[]{:S(2)}, u32[]{:S(2)}) collective-permute-start(bf16[256,512]{1,0:T(8,128)(2,1)S(1)} %collective-permute-done.29.refs_10_), channel_id=1, source_target_pairs={{0,8},{8,16},{16,24},{12,4},{20,12},{28,20},{1,9},{9,17},{17,25},{... | collective-permute-start | bytes 786440 | tf_op jit(solution)/shard_map/ppermute | solution.py:379
  90.9 6.7 %collective-permute-start.28 = (bf16[256,512]{1,0:T(8,128)(2,1)S(1)}, bf16[256,512]{1,0:T(8,128)(2,1)S(1)}, u32[]{:S(2)}, u32[]{:S(2)}) collective-permute-start(bf16[256,512]{1,0:T(8,128)(2,1)S(1)} %image.9.refs_8_.refs_2_.refs_14_), channel_id=1, source_target_pairs={{0,1},{1,0},{2,3},{3,2},{4,5},{5,4},{6,7},{7,6},{8,9},{9,8},{10,11... | collective-permute-start | bytes 786440 | tf_op jit(solution)/shard_map/ppermute | solution.py:312
  103.4 6.0 %collective-permute-start.39 = (bf16[128,512]{1,0:T(8,128)(2,1)S(1)}, bf16[128,512]{1,0:T(8,128)(2,1)S(1)}, u32[]{:S(2)}, u32[]{:S(2)}) collective-permute-start(bf16[128,512]{1,0:T(8,128)(2,1)S(1)} %get-tuple-element.60), channel_id=1, source_target_pairs={{0,2},{1,3},{2,0},{3,1},{4,6},{5,7},{6,4},{7,5},{8,10},{9,11},{10,... | collective-permute-start | bytes 393224 | tf_op jit(solution)/shard_map/ppermute | solution.py:416
  117.2 10.8 %collective-permute-start.45 = (bf16[128,512]{1,0:T(8,128)(2,1)S(1)}, bf16[128,512]{1,0:T(8,128)(2,1)S(1)}, u32[]{:S(2)}, u32[]{:S(2)}) collective-permute-start(bf16[128,512]{1,0:T(8,128)(2,1)S(1)} %get-tuple-element.66.refs_16_), channel_id=1, source_target_pairs={{0,2},{1,3},{2,0},{3,1},{4,6},{5,7},{6,4},{7,5},{8,10},{9,11},{10,... | collective-permute-start | bytes 393224 | tf_op jit(solution)/shard_map/ppermute | solution.py:428
  118.0 10.5 %collective-permute-start.41 = (bf16[128,512]{1,0:T(8,128)(2,1)S(1)}, bf16[128,512]{1,0:T(8,128)(2,1)S(1)}, u32[]{:S(2)}, u32[]{:S(2)}) collective-permute-start(bf16[128,512]{1,0:T(8,128)(2,1)S(1)} %get-tuple-element.63.refs_6_), channel_id=1, source_target_pairs={{0,2},{1,3},{2,0},{3,1},{4,6},{5,7},{6,4},{7,5},{8,10},{9,11},{10,... | collective-permute-start | bytes 393224 | tf_op jit(solution)/shard_map/ppermute | solution.py:428
  119.5 6.6 %collective-permute-start.50 = (f32[8,128]{1,0:T(8,128)S(1)}, f32[8,128]{1,0:T(8,128)S(1)}, u32[]{:S(2)}, u32[]{:S(2)}) collective-permute-start(f32[8,128]{1,0:T(8,128)S(1)} %add_add_fusion.1), channel_id=1, source_target_pairs={{0,12},{1,13},{2,14},{3,15},{4,8},{5,9},{6,10},{7,11},{8,4},{9,5},... | collective-permute-start | bytes 12296 | tf_op jit(solution)/shard_map/ppermute | solution.py:331
  126.1 7.0 %collective-permute-start.44 = (bf16[128,512]{1,0:T(8,128)(2,1)S(1)}, bf16[128,512]{1,0:T(8,128)(2,1)S(1)}, u32[]{:S(2)}, u32[]{:S(2)}) collective-permute-start(bf16[128,512]{1,0:T(8,128)(2,1)S(1)} %get-tuple-element.66.refs_16_), channel_id=1, source_target_pairs={{0,1},{1,0},{2,3},{3,2},{4,5},{5,4},{6,7},{7,6},{8,9},{9,8},{10,11... | collective-permute-start | bytes 393224 | tf_op jit(solution)/shard_map/ppermute | solution.py:312
  (36 other events, 129.8 us)

commit v8 on v7

--- a/solution.py
+++ b/solution.py
@@ -212,7 +212,7 @@
 
 
 def image_kernel(product, target, sectors, rows_ref, a_ref, b_ref, *refs):
-    out_ref = refs[-2] if product != 1 else refs[-1]
+    out_ref = refs[-2] if product == 2 else refs[-1]
     half, columns = out_ref.shape
     value = a_ref[...].astype(F32) + b_ref[...].astype(F32)
     rows = rows_of(rows_ref, target, sectors)
@@ -222,18 +222,11 @@
         part = side_of(0, half, lax.axis_size("op"))
         first_row = 2 * first_row + part.start
     value = masked(value, first_row, rows)
-    if product == 1:
+    if product < 2:
         out_ref[...] = value.astype(BF16)
         return
     stats_ref = refs[-1]
     basis = [r[part, :].astype(F32) for r in refs[: product + 1]]
-    if product == 0:
-        value = value.astype(BF16)
-        out_ref[...] = value
-        value = value.astype(F32)
-        tile = scaled_sums([(basis[0], basis[0]), (value, basis[0]), (value, value)])
-        stats_ref[...] = merged(refs[1][...], tile) if target else tile
-        return
     tile_ref, before = refs[product + 1], refs[product + 2] if target else None
     norm, alpha, beta = first_scalars(tile_ref, live_entries(rows_ref, columns))
     zeroth, image, second = (block * (1.0 / norm) for block in basis)
@@ -247,6 +240,16 @@
     value = value.astype(F32)
     known = [second * second, second * first, second * zeroth]
     write_sums(stats_ref, known + [value * v for v in (value, second, first, zeroth)], before)
+
+
+def tile_kernel(*refs):
+    *blocks, tile_ref = refs
+    tile = None
+    for start_ref, image_ref in zip(blocks[::2], blocks[1::2]):
+        start, image = start_ref[...].astype(F32), image_ref[...].astype(F32)
+        part = scaled_sums([(start, start), (image, start), (image, image)])
+        tile = part if tile is None else merged(tile, part)
+    tile_ref[...] = tile
 
 
 def last_kernel(rows_ref, *refs):
@@ -380,6 +383,9 @@
         far_1 = lax.ppermute(mine_1, "sec", diagonal)
         pair_1 = after(pair_1, far_0)
         if product == 1:
+            blocks = [b[t][0] for t in range(sectors) for b in basis]
+            blocks[0] = after(blocks[0], pair_0)
+            sums = call(tile_kernel, "tile", tile_type, [], *blocks)
             tile = flipped_merge(flipped_merge(sums, "op", [1]), "sec", bits[:1])
             pair_1 = after(pair_1, tile)
         elif product == 2:
@@ -417,10 +423,10 @@
             if t == 0:
                 arrived = after(arrived, values[-1][0])
             out = (half_type, half_type, quarter_type)[product]
-            needed = () if product == 1 else (*[b[t][0] for b in basis], *stats, *earlier)
+            needed = () if product < 2 else (*[b[t][0] for b in basis], *stats, *earlier)
             mine, *earlier = call(
                 functools.partial(image_kernel, product, t, sectors), "image",
-                [out] if product == 1 else [out, stats_type if product else tile_type], [],
+                [out] if product < 2 else [out, stats_type], [],
                 sector_rows, parts[0], arrived, *needed,
             )
             image.append((mine, across_cores(mine)))

time: 137 us -> 136 us (level)
    pallas_call x18 -> x19, Pallas kernels: 31.6 us -> 31.6 us  [call(): pl.pallas_call(kernel, name=name, out_shape=out, in_specs=[SMEM if a.dtyp...]
where the time goes in v8:
time: 136 us
  starting transfers between devices  63.4 us (47%)
  waiting for transfers between devices  33.9 us (25%)
  Pallas kernels  32 us (24%)
  local copies, waits for them, and re-layouts  5.67 us (4%)
    pallas_call x19, Pallas kernels, call(): pl.pallas_call(kernel, name=name, out_shape=out, in_specs=[SMEM if a.dtyp...  31.6 us
    ppermute x3, starting transfers between devices, on_device(): far_0 = lax.ppermute(pair_0, 'sec', onward)  13.3 us
    ppermute x6, waiting for transfers between devices, on_device(): arrived = lax.ppermute(parts[-1], 'op', flips)  10.5 us
    ppermute x6, starting transfers between devices, sum_four(): lax.ppermute(stats, ('sec', 'op'), [(i, i ^ mask) for i in places])  8.77 us
    ppermute x3, starting transfers between devices, on_device(): pair_1 = lax.ppermute(mine_1, 'sec', pairs)  8.26 us
    ppermute x2, starting transfers between devices, on_device(): pair_0 = lax.ppermute(mine_0, 'sec', pairs)  7.01 us
    ppermute x4, starting transfers between devices, flipped_merge(): arrived = lax.ppermute(tile, axis, flips)  6.61 us
    ppermute x6, starting transfers between devices, on_device(): arrived = lax.ppermute(parts[-1], 'op', flips)  6.47 us
  transfers between devices with their start and end apart: 54, of which 27 were waited for; matrix products, arithmetic and copies ran while one was open for 0% of the time, Pallas kernels for 12%

profile of v8, /device:TPU:0, one launch (start us, length us, event | category | flops | bytes accessed | tf_op | source)
XLA Modules:
  0.0 135.9 jit_solution(5869705393985719158)
XLA Ops:
  4.0 3.0 %collective-permute-start.3 = (bf16[256,512]{1,0:T(8,128)(2,1)S(1)}, bf16[256,512]{1,0:T(8,128)(2,1)S(1)}, u32[]{:S(2)}, u32[]{:S(2)}) collective-permute-start(bf16[256,512]{1,0:T(8,128)(2,1)S(1)} %get-tuple-element.44.refs_6_.refs_0_), channel_id=1, source_target_pairs={{0,4},{4,0},{8,12},{12,8},{16,20},{20,16},{24,28},{28,24},{1,5},{5... | collective-permute-start | bytes 786440 | tf_op jit(solution)/shard_map/ppermute | solution.py:352
  6.9 2.2 %copy-done = bf16[4,2,512,512]{3,2,1,0:T(8,128)(2,1)S(1)} copy-done((bf16[4,2,512,512]{3,2,1,0:T(8,128)(2,1)S(1)}, bf16[4,2,512,512]{3,2,1,0:T(8,128)(2,1)}, u32[]{:S(2)}) %copy-start) | copy-done | bytes 4194328
  11.2 2.3 %collective-permute-done.3.refs_10_ = bf16[256,512]{1,0:T(8,128)(2,1)S(1)} collective-permute-done((bf16[256,512]{1,0:T(8,128)(2,1)S(1)}, bf16[256,512]{1,0:T(8,128)(2,1)S(1)}, u32[]{:S(2)}, u32[]{:S(2)}) %collective-permute-start.3) | collective-permute-done | bytes 262176 | tf_op jit(solution)/shard_map/ppermute | solution.py:352
  15.2 3.5 %collective-permute-start.6 = (bf16[256,512]{1,0:T(8,128)(2,1)S(1)}, bf16[256,512]{1,0:T(8,128)(2,1)S(1)}, u32[]{:S(2)}, u32[]{:S(2)}) collective-permute-start(bf16[256,512]{1,0:T(8,128)(2,1)S(1)} %collective-permute-done.3.refs_10_), channel_id=1, source_target_pairs={{0,8},{8,16},{16,24},{12,4},{20,12},{28,20},{1,9},{9,17},{17,25},{... | collective-permute-start | bytes 786440 | tf_op jit(solution)/shard_map/ppermute | solution.py:382
  26.8 3.7 %full.6.a_ref = bf16[256,512]{1,0:T(8,128)(2,1)S(1)} custom-call(s32[4]{0:T(128)S(1)} %copy-done.5, bf16[4,2,512,512]{3,2,1,0:T(8,128)(2,1)S(1)} %get-tuple-element.34.refs_1_, bf16[4,512,512]{2,1,0:T(8,128)(2,1)S(1)} %get-tuple-element.35.refs_2_, s32[4]{0:T(128)S(1)} %collective-permute-done.refs_3_, ...), custom_call_target="tpu_custom_call" | custom-call | tf_op jit(solution)/shard_map/full/pallas_call | solution.py:18
  32.1 3.7 %full.7.a_ref = bf16[256,512]{1,0:T(8,128)(2,1)S(1)} custom-call(s32[4]{0:T(128)S(1)} %copy-done.5, bf16[4,2,512,512]{3,2,1,0:T(8,128)(2,1)S(1)} %get-tuple-element.34.refs_1_, bf16[4,512,512]{2,1,0:T(8,128)(2,1)S(1)} %get-tuple-element.35.refs_2_, s32[4]{0:T(128)S(1)} %collective-permute-done.refs_3_, ...), custom_call_target="tpu_custom_call" | custom-call | tf_op jit(solution)/shard_map/full/pallas_call | solution.py:18
  36.3 3.2 %collective-permute-done.11.b_ref = bf16[256,512]{1,0:T(8,128)(2,1)S(1)} collective-permute-done((bf16[256,512]{1,0:T(8,128)(2,1)S(1)}, bf16[256,512]{1,0:T(8,128)(2,1)S(1)}, u32[]{:S(2)}, u32[]{:S(2)}) %collective-permute-start.11) | collective-permute-done | bytes 262176 | tf_op jit(solution)/shard_map/ppermute | solution.py:422
  40.1 3.9 %collective-permute-start.15 = (bf16[256,512]{1,0:T(8,128)(2,1)S(1)}, bf16[256,512]{1,0:T(8,128)(2,1)S(1)}, u32[]{:S(2)}, u32[]{:S(2)}) collective-permute-start(bf16[256,512]{1,0:T(8,128)(2,1)S(1)} %image.6.refs_1_.refs_6_.refs_2_), channel_id=1, source_target_pairs={{0,4},{4,0},{8,12},{12,8},{16,20},{20,16},{24,28},{28,24},{1,5},{5... | collective-permute-start | bytes 786440 | tf_op jit(solution)/shard_map/ppermute | solution.py:373
  45.2 3.9 %collective-permute-start.17 = (bf16[256,512]{1,0:T(8,128)(2,1)S(1)}, bf16[256,512]{1,0:T(8,128)(2,1)S(1)}, u32[]{:S(2)}, u32[]{:S(2)}) collective-permute-start(bf16[256,512]{1,0:T(8,128)(2,1)S(1)} %image.7.refs_3_.refs_8_.refs_1_.refs_12_), channel_id=1, source_target_pairs={{0,4},{4,0},{8,12},{12,8},{16,20},{20,16},{24,28},{28,24},{1,5},{5... | collective-permute-start | bytes 786440 | tf_op jit(solution)/shard_map/ppermute | solution.py:381
  49.8 4.7 %collective-permute-start.18 = (bf16[256,512]{1,0:T(8,128)(2,1)S(1)}, bf16[256,512]{1,0:T(8,128)(2,1)S(1)}, u32[]{:S(2)}, u32[]{:S(2)}) collective-permute-start(bf16[256,512]{1,0:T(8,128)(2,1)S(1)} %collective-permute-done.15.refs_10_), channel_id=1, source_target_pairs={{0,8},{8,16},{16,24},{12,4},{20,12},{28,20},{1,9},{9,17},{17,25},{... | collective-permute-start | bytes 786440 | tf_op jit(solution)/shard_map/ppermute | solution.py:382
  57.6 2.9 %collective-permute-done.20.arrived_ref = f32[24,128]{1,0:T(8,128)S(1)} collective-permute-done((f32[24,128]{1,0:T(8,128)S(1)}, f32[24,128]{1,0:T(8,128)S(1)}, u32[]{:S(2)}, u32[]{:S(2)}) %collective-permute-start.20) | collective-permute-done | bytes 12320 | tf_op jit(solution)/shard_map/ppermute | solution.py:325
  63.5 3.7 %full.8.a_ref = bf16[256,512]{1,0:T(8,128)(2,1)S(1)} custom-call(s32[4]{0:T(128)S(1)} %copy-done.5, bf16[4,2,512,512]{3,2,1,0:T(8,128)(2,1)S(1)} %get-tuple-element.34.refs_1_, bf16[4,512,512]{2,1,0:T(8,128)(2,1)S(1)} %get-tuple-element.35.refs_2_, s32[4]{0:T(128)S(1)} %collective-permute-done.refs_3_, ...), custom_call_target="tpu_custom_call" | custom-call | tf_op jit(solution)/shard_map/full/pallas_call | solution.py:18
  68.8 3.7 %full.9.a_ref = bf16[256,512]{1,0:T(8,128)(2,1)S(1)} custom-call(s32[4]{0:T(128)S(1)} %copy-done.5, bf16[4,2,512,512]{3,2,1,0:T(8,128)(2,1)S(1)} %get-tuple-element.34.refs_1_, bf16[4,512,512]{2,1,0:T(8,128)(2,1)S(1)} %get-tuple-element.35.refs_2_, s32[4]{0:T(128)S(1)} %collective-permute-done.refs_3_, ...), custom_call_target="tpu_custom_call" | custom-call | tf_op jit(solution)/shard_map/full/pallas_call | solution.py:18
  73.0 3.2 %collective-permute-done.25.b_ref = bf16[256,512]{1,0:T(8,128)(2,1)S(1)} collective-permute-done((bf16[256,512]{1,0:T(8,128)(2,1)S(1)}, bf16[256,512]{1,0:T(8,128)(2,1)S(1)}, u32[]{:S(2)}, u32[]{:S(2)}) %collective-permute-start.25) | collective-permute-done | bytes 262176 | tf_op jit(solution)/shard_map/ppermute | solution.py:422
  76.9 3.1 %collective-permute-start.29 = (bf16[256,512]{1,0:T(8,128)(2,1)S(1)}, bf16[256,512]{1,0:T(8,128)(2,1)S(1)}, u32[]{:S(2)}, u32[]{:S(2)}) collective-permute-start(bf16[256,512]{1,0:T(8,128)(2,1)S(1)} %image.8.refs_6_.refs_2_.refs_4_), channel_id=1, source_target_pairs={{0,4},{4,0},{8,12},{12,8},{16,20},{20,16},{24,28},{28,24},{1,5},{5... | collective-permute-start | bytes 786440 | tf_op jit(solution)/shard_map/ppermute | solution.py:373
  82.2 2.6 %collective-permute-start.32 = (bf16[256,512]{1,0:T(8,128)(2,1)S(1)}, bf16[256,512]{1,0:T(8,128)(2,1)S(1)}, u32[]{:S(2)}, u32[]{:S(2)}) collective-permute-start(bf16[256,512]{1,0:T(8,128)(2,1)S(1)} %image.9.refs_8_.refs_2_.refs_14_), channel_id=1, source_target_pairs={{0,4},{4,0},{8,12},{12,8},{16,20},{20,16},{24,28},{28,24},{1,5},{5... | collective-permute-start | bytes 786440 | tf_op jit(solution)/shard_map/ppermute | solution.py:381
  85.5 5.1 %collective-permute-start.33 = (bf16[256,512]{1,0:T(8,128)(2,1)S(1)}, bf16[256,512]{1,0:T(8,128)(2,1)S(1)}, u32[]{:S(2)}, u32[]{:S(2)}) collective-permute-start(bf16[256,512]{1,0:T(8,128)(2,1)S(1)} %collective-permute-done.29.refs_10_), channel_id=1, source_target_pairs={{0,8},{8,16},{16,24},{12,4},{20,12},{28,20},{1,9},{9,17},{17,25},{... | collective-permute-start | bytes 786440 | tf_op jit(solution)/shard_map/ppermute | solution.py:382
  90.7 3.6 %collective-permute-start.34 = (f32[24,128]{1,0:T(8,128)S(1)}, f32[24,128]{1,0:T(8,128)S(1)}, u32[]{:S(2)}, u32[]{:S(2)}) collective-permute-start(f32[24,128]{1,0:T(8,128)S(1)} %merge.6.own_ref), channel_id=1, source_target_pairs={{0,16},{4,20},{8,24},{12,28},{16,0},{20,4},{24,8},{28,12},{1,17},{... | collective-permute-start | bytes 36872 | tf_op jit(solution)/shard_map/ppermute | solution.py:325
  99.2 3.9 %full.10 = (bf16[128,512]{1,0:T(8,128)(2,1)S(1)}, bf16[128,512]{1,0:T(8,128)(2,1)S(1)}) custom-call(s32[4]{0:T(128)S(1)} %copy-done.5, bf16[4,2,512,512]{3,2,1,0:T(8,128)(2,1)S(1)} %get-tuple-element.34.refs_1_, bf16[4,512,512]{2,1,0:T(8,128)(2,1)S(1)} %get-tuple-element.35.refs_2_, s32[4]{0:T(128)S(1)} %collective-permute-done.refs_3_, ...), custom_call_target="tpu_custom_call" | custom-call | tf_op jit(solution)/shard_map/full/pallas_call | solution.py:18
  104.4 3.9 %full.11 = (bf16[128,512]{1,0:T(8,128)(2,1)S(1)}, bf16[128,512]{1,0:T(8,128)(2,1)S(1)}) custom-call(s32[4]{0:T(128)S(1)} %copy-done.5, bf16[4,2,512,512]{3,2,1,0:T(8,128)(2,1)S(1)} %get-tuple-element.34.refs_1_, bf16[4,512,512]{2,1,0:T(8,128)(2,1)S(1)} %get-tuple-element.35.refs_2_, s32[4]{0:T(128)S(1)} %collective-permute-done.refs_3_, ...), custom_call_target="tpu_custom_call" | custom-call | tf_op jit(solution)/shard_map/full/pallas_call | solution.py:18
  110.1 3.6 %collective-permute-done.43.b_ref = bf16[128,512]{1,0:T(8,128)(2,1)S(1)} collective-permute-done((bf16[128,512]{1,0:T(8,128)(2,1)S(1)}, bf16[128,512]{1,0:T(8,128)(2,1)S(1)}, u32[]{:S(2)}, u32[]{:S(2)}) %collective-permute-start.43) | collective-permute-done | bytes 131104 | tf_op jit(solution)/shard_map/ppermute | solution.py:422
  119.3 4.7 %collective-permute-start.50 = (f32[8,128]{1,0:T(8,128)S(1)}, f32[8,128]{1,0:T(8,128)S(1)}, u32[]{:S(2)}, u32[]{:S(2)}) collective-permute-start(f32[8,128]{1,0:T(8,128)S(1)} %add_add_fusion.1), channel_id=1, source_target_pairs={{0,12},{1,13},{2,14},{3,15},{4,8},{5,9},{6,10},{7,11},{8,4},{9,5},... | collective-permute-start | bytes 12296 | tf_op jit(solution)/shard_map/ppermute | solution.py:334
  129.8 3.0 %collective-permute-done.53 = f32[8,128]{1,0:T(8,128)S(1)} collective-permute-done((f32[8,128]{1,0:T(8,128)S(1)}, f32[8,128]{1,0:T(8,128)S(1)}, u32[]{:S(2)}, u32[]{:S(2)}) %collective-permute-start.53) | collective-permute-done | bytes 4128 | tf_op jit(solution)/shard_map/ppermute | solution.py:319
  132.9 3.1 %last.1 = (bf16[2,512,512]{2,1,0:T(8,128)(2,1)}, f32[2,3]{1,0:T(2,128)}) custom-call(s32[16]{0:T(128)S(1)} %copy-done.4, bf16[256,512]{1,0:T(8,128)(2,1)S(1)} %get-tuple-element.44.refs_6_.refs_0_, bf16[256,512]{1,0:T(8,128)(2,1)S(1)} %get-tuple-element.33.refs_7_.refs_1_, bf16[256,512]{1,0:T(8,128)(2,1)S(1)} %image.6.refs_1_.refs_6_.refs_2_, ...), custom_call_target="tpu_custom_call" | custom-call | tf_op jit(solution)/shard_map/last/pallas_call | solution.py:18
  (119 shorter events, 50.9 us)
Async XLA Ops:
  0.6 26.2 %collective-permute-start.1 = (bf16[4,2,512,512]{3,2,1,0:T(8,128)(2,1)}, bf16[4,2,512,512]{3,2,1,0:T(8,128)(2,1)S(1)}, u32[]{:S(2)}, u32[]{:S(2)}) collective-permute-start(bf16[4,2,512,512]{3,2,1,0:T(8,128)(2,1)} %left_ref.1), channel_id=1, source_target_pairs={{0,1},{1,0},{2,3},{3,2},{4,5},{5,4},{6,7},{7,6},{8,9},{9,8},{10,11... | collective-permute-start | bytes 12582920 | tf_op jit(solution)/shard_map/ppermute | solution.py:315
  1.1 25.6 %collective-permute-start.2 = (bf16[4,512,512]{2,1,0:T(8,128)(2,1)}, bf16[4,512,512]{2,1,0:T(8,128)(2,1)S(1)}, u32[]{:S(2)}, u32[]{:S(2)}) collective-permute-start(bf16[4,512,512]{2,1,0:T(8,128)(2,1)} %right_ref.1), channel_id=1, source_target_pairs={{0,1},{1,0},{2,3},{3,2},{4,5},{5,4},{6,7},{7,6},{8,9},{9,8},{10,11... | collective-permute-start | bytes 6291464 | tf_op jit(solution)/shard_map/ppermute | solution.py:315
  4.0 9.5 %collective-permute-start.3 = (bf16[256,512]{1,0:T(8,128)(2,1)S(1)}, bf16[256,512]{1,0:T(8,128)(2,1)S(1)}, u32[]{:S(2)}, u32[]{:S(2)}) collective-permute-start(bf16[256,512]{1,0:T(8,128)(2,1)S(1)} %get-tuple-element.44.refs_6_.refs_0_), channel_id=1, source_target_pairs={{0,4},{4,0},{8,12},{12,8},{16,20},{20,16},{24,28},{28,24},{1,5},{5... | collective-permute-start | bytes 786440 | tf_op jit(solution)/shard_map/ppermute | solution.py:352
  13.5 7.8 %collective-permute-start.5 = (bf16[256,512]{1,0:T(8,128)(2,1)S(1)}, bf16[256,512]{1,0:T(8,128)(2,1)S(1)}, u32[]{:S(2)}, u32[]{:S(2)}) collective-permute-start(bf16[256,512]{1,0:T(8,128)(2,1)S(1)} %get-tuple-element.38.refs_8_.refs_2_.refs_0_.refs_10_), channel_id=1, source_target_pairs={{0,4},{4,0},{8,12},{12,8},{16,20},{20,16},{24,28},{28,24},{1,5},{5... | collective-permute-start | bytes 786440 | tf_op jit(solution)/shard_map/ppermute | solution.py:381
  15.2 8.1 %collective-permute-start.6 = (bf16[256,512]{1,0:T(8,128)(2,1)S(1)}, bf16[256,512]{1,0:T(8,128)(2,1)S(1)}, u32[]{:S(2)}, u32[]{:S(2)}) collective-permute-start(bf16[256,512]{1,0:T(8,128)(2,1)S(1)} %collective-permute-done.3.refs_10_), channel_id=1, source_target_pairs={{0,8},{8,16},{16,24},{12,4},{20,12},{28,20},{1,9},{9,17},{17,25},{... | collective-permute-start | bytes 786440 | tf_op jit(solution)/shard_map/ppermute | solution.py:382
  30.5 9.0 %collective-permute-start.11 = (bf16[256,512]{1,0:T(8,128)(2,1)S(1)}, bf16[256,512]{1,0:T(8,128)(2,1)S(1)}, u32[]{:S(2)}, u32[]{:S(2)}) collective-permute-start(bf16[256,512]{1,0:T(8,128)(2,1)S(1)} %full.6.a_ref), channel_id=1, source_target_pairs={{0,2},{1,3},{2,0},{3,1},{4,6},{5,7},{6,4},{7,5},{8,10},{9,11},{10,... | collective-permute-start | bytes 786440 | tf_op jit(solution)/shard_map/ppermute | solution.py:422
  35.8 8.8 %collective-permute-start.13 = (bf16[256,512]{1,0:T(8,128)(2,1)S(1)}, bf16[256,512]{1,0:T(8,128)(2,1)S(1)}, u32[]{:S(2)}, u32[]{:S(2)}) collective-permute-start(bf16[256,512]{1,0:T(8,128)(2,1)S(1)} %full.7.a_ref), channel_id=1, source_target_pairs={{0,2},{1,3},{2,0},{3,1},{4,6},{5,7},{6,4},{7,5},{8,10},{9,11},{10,... | collective-permute-start | bytes 786440 | tf_op jit(solution)/shard_map/ppermute | solution.py:422
  40.1 9.7 %collective-permute-start.15 = (bf16[256,512]{1,0:T(8,128)(2,1)S(1)}, bf16[256,512]{1,0:T(8,128)(2,1)S(1)}, u32[]{:S(2)}, u32[]{:S(2)}) collective-permute-start(bf16[256,512]{1,0:T(8,128)(2,1)S(1)} %image.6.refs_1_.refs_6_.refs_2_), channel_id=1, source_target_pairs={{0,4},{4,0},{8,12},{12,8},{16,20},{20,16},{24,28},{28,24},{1,5},{5... | collective-permute-start | bytes 786440 | tf_op jit(solution)/shard_map/ppermute | solution.py:373
  45.2 15.3 %collective-permute-start.17 = (bf16[256,512]{1,0:T(8,128)(2,1)S(1)}, bf16[256,512]{1,0:T(8,128)(2,1)S(1)}, u32[]{:S(2)}, u32[]{:S(2)}) collective-permute-start(bf16[256,512]{1,0:T(8,128)(2,1)S(1)} %image.7.refs_3_.refs_8_.refs_1_.refs_12_), channel_id=1, source_target_pairs={{0,4},{4,0},{8,12},{12,8},{16,20},{20,16},{24,28},{28,24},{1,5},{5... | collective-permute-start | bytes 786440 | tf_op jit(solution)/shard_map/ppermute | solution.py:381
  49.1 11.9 %collective-permute-start.23 = (bf16[256,512]{1,0:T(8,128)(2,1)S(1)}, bf16[256,512]{1,0:T(8,128)(2,1)S(1)}, u32[]{:S(2)}, u32[]{:S(2)}) collective-permute-start(bf16[256,512]{1,0:T(8,128)(2,1)S(1)} %image.7.refs_3_.refs_8_.refs_1_.refs_12_), channel_id=1, source_target_pairs={{4,8},{12,16},{20,24},{8,4},{16,12},{24,20},{5,9},{13,17},{21,25},... | collective-permute-start | bytes 786440 | tf_op jit(solution)/shard_map/ppermute | solution.py:383
  49.8 11.3 %collective-permute-start.18 = (bf16[256,512]{1,0:T(8,128)(2,1)S(1)}, bf16[256,512]{1,0:T(8,128)(2,1)S(1)}, u32[]{:S(2)}, u32[]{:S(2)}) collective-permute-start(bf16[256,512]{1,0:T(8,128)(2,1)S(1)} %collective-permute-done.15.refs_10_), channel_id=1, source_target_pairs={{0,8},{8,16},{16,24},{12,4},{20,12},{28,20},{1,9},{9,17},{17,25},{... | collective-permute-start | bytes 786440 | tf_op jit(solution)/shard_map/ppermute | solution.py:382
  54.6 7.0 %collective-permute-start.14 = (bf16[256,512]{1,0:T(8,128)(2,1)S(1)}, bf16[256,512]{1,0:T(8,128)(2,1)S(1)}, u32[]{:S(2)}, u32[]{:S(2)}) collective-permute-start(bf16[256,512]{1,0:T(8,128)(2,1)S(1)} %image.7.refs_3_.refs_8_.refs_1_.refs_12_), channel_id=1, source_target_pairs={{0,1},{1,0},{2,3},{3,2},{4,5},{5,4},{6,7},{7,6},{8,9},{9,8},{10,11... | collective-permute-start | bytes 786440 | tf_op jit(solution)/shard_map/ppermute | solution.py:315
  67.2 9.0 %collective-permute-start.25 = (bf16[256,512]{1,0:T(8,128)(2,1)S(1)}, bf16[256,512]{1,0:T(8,128)(2,1)S(1)}, u32[]{:S(2)}, u32[]{:S(2)}) collective-permute-start(bf16[256,512]{1,0:T(8,128)(2,1)S(1)} %full.8.a_ref), channel_id=1, source_target_pairs={{0,2},{1,3},{2,0},{3,1},{4,6},{5,7},{6,4},{7,5},{8,10},{9,11},{10,... | collective-permute-start | bytes 786440 | tf_op jit(solution)/shard_map/ppermute | solution.py:422
  72.5 9.1 %collective-permute-start.27 = (bf16[256,512]{1,0:T(8,128)(2,1)S(1)}, bf16[256,512]{1,0:T(8,128)(2,1)S(1)}, u32[]{:S(2)}, u32[]{:S(2)}) collective-permute-start(bf16[256,512]{1,0:T(8,128)(2,1)S(1)} %full.9.a_ref), channel_id=1, source_target_pairs={{0,2},{1,3},{2,0},{3,1},{4,6},{5,7},{6,4},{7,5},{8,10},{9,11},{10,... | collective-permute-start | bytes 786440 | tf_op jit(solution)/shard_map/ppermute | solution.py:422
  76.9 8.6 %collective-permute-start.29 = (bf16[256,512]{1,0:T(8,128)(2,1)S(1)}, bf16[256,512]{1,0:T(8,128)(2,1)S(1)}, u32[]{:S(2)}, u32[]{:S(2)}) collective-permute-start(bf16[256,512]{1,0:T(8,128)(2,1)S(1)} %image.8.refs_6_.refs_2_.refs_4_), channel_id=1, source_target_pairs={{0,4},{4,0},{8,12},{12,8},{16,20},{20,16},{24,28},{28,24},{1,5},{5... | collective-permute-start | bytes 786440 | tf_op jit(solution)/shard_map/ppermute | solution.py:373
  82.2 14.0 %collective-permute-start.32 = (bf16[256,512]{1,0:T(8,128)(2,1)S(1)}, bf16[256,512]{1,0:T(8,128)(2,1)S(1)}, u32[]{:S(2)}, u32[]{:S(2)}) collective-permute-start(bf16[256,512]{1,0:T(8,128)(2,1)S(1)} %image.9.refs_8_.refs_2_.refs_14_), channel_id=1, source_target_pairs={{0,4},{4,0},{8,12},{12,8},{16,20},{20,16},{24,28},{28,24},{1,5},{5... | collective-permute-start | bytes 786440 | tf_op jit(solution)/shard_map/ppermute | solution.py:381
  84.8 12.0 %collective-permute-start.37 = (bf16[256,512]{1,0:T(8,128)(2,1)S(1)}, bf16[256,512]{1,0:T(8,128)(2,1)S(1)}, u32[]{:S(2)}, u32[]{:S(2)}) collective-permute-start(bf16[256,512]{1,0:T(8,128)(2,1)S(1)} %image.9.refs_8_.refs_2_.refs_14_), channel_id=1, source_target_pairs={{4,8},{12,16},{20,24},{8,4},{16,12},{24,20},{5,9},{13,17},{21,25},... | collective-permute-start | bytes 786440 | tf_op jit(solution)/shard_map/ppermute | solution.py:383
  85.5 11.3 %collective-permute-start.33 = (bf16[256,512]{1,0:T(8,128)(2,1)S(1)}, bf16[256,512]{1,0:T(8,128)(2,1)S(1)}, u32[]{:S(2)}, u32[]{:S(2)}) collective-permute-start(bf16[256,512]{1,0:T(8,128)(2,1)S(1)} %collective-permute-done.29.refs_10_), channel_id=1, source_target_pairs={{0,8},{8,16},{16,24},{12,4},{20,12},{28,20},{1,9},{9,17},{17,25},{... | collective-permute-start | bytes 786440 | tf_op jit(solution)/shard_map/ppermute | solution.py:382
  90.6 6.7 %collective-permute-start.28 = (bf16[256,512]{1,0:T(8,128)(2,1)S(1)}, bf16[256,512]{1,0:T(8,128)(2,1)S(1)}, u32[]{:S(2)}, u32[]{:S(2)}) collective-permute-start(bf16[256,512]{1,0:T(8,128)(2,1)S(1)} %image.9.refs_8_.refs_2_.refs_14_), channel_id=1, source_target_pairs={{0,1},{1,0},{2,3},{3,2},{4,5},{5,4},{6,7},{7,6},{8,9},{9,8},{10,11... | collective-permute-start | bytes 786440 | tf_op jit(solution)/shard_map/ppermute | solution.py:315
  103.1 6.0 %collective-permute-start.39 = (bf16[128,512]{1,0:T(8,128)(2,1)S(1)}, bf16[128,512]{1,0:T(8,128)(2,1)S(1)}, u32[]{:S(2)}, u32[]{:S(2)}) collective-permute-start(bf16[128,512]{1,0:T(8,128)(2,1)S(1)} %get-tuple-element.54), channel_id=1, source_target_pairs={{0,2},{1,3},{2,0},{3,1},{4,6},{5,7},{6,4},{7,5},{8,10},{9,11},{10,... | collective-permute-start | bytes 393224 | tf_op jit(solution)/shard_map/ppermute | solution.py:422
  116.9 10.8 %collective-permute-start.45 = (bf16[128,512]{1,0:T(8,128)(2,1)S(1)}, bf16[128,512]{1,0:T(8,128)(2,1)S(1)}, u32[]{:S(2)}, u32[]{:S(2)}) collective-permute-start(bf16[128,512]{1,0:T(8,128)(2,1)S(1)} %get-tuple-element.60.refs_16_), channel_id=1, source_target_pairs={{0,2},{1,3},{2,0},{3,1},{4,6},{5,7},{6,4},{7,5},{8,10},{9,11},{10,... | collective-permute-start | bytes 393224 | tf_op jit(solution)/shard_map/ppermute | solution.py:434
  117.7 10.5 %collective-permute-start.41 = (bf16[128,512]{1,0:T(8,128)(2,1)S(1)}, bf16[128,512]{1,0:T(8,128)(2,1)S(1)}, u32[]{:S(2)}, u32[]{:S(2)}) collective-permute-start(bf16[128,512]{1,0:T(8,128)(2,1)S(1)} %get-tuple-element.57.refs_6_), channel_id=1, source_target_pairs={{0,2},{1,3},{2,0},{3,1},{4,6},{5,7},{6,4},{7,5},{8,10},{9,11},{10,... | collective-permute-start | bytes 393224 | tf_op jit(solution)/shard_map/ppermute | solution.py:434
  119.3 6.6 %collective-permute-start.50 = (f32[8,128]{1,0:T(8,128)S(1)}, f32[8,128]{1,0:T(8,128)S(1)}, u32[]{:S(2)}, u32[]{:S(2)}) collective-permute-start(f32[8,128]{1,0:T(8,128)S(1)} %add_add_fusion.1), channel_id=1, source_target_pairs={{0,12},{1,13},{2,14},{3,15},{4,8},{5,9},{6,10},{7,11},{8,4},{9,5},... | collective-permute-start | bytes 12296 | tf_op jit(solution)/shard_map/ppermute | solution.py:334
  125.9 6.9 %collective-permute-start.44 = (bf16[128,512]{1,0:T(8,128)(2,1)S(1)}, bf16[128,512]{1,0:T(8,128)(2,1)S(1)}, u32[]{:S(2)}, u32[]{:S(2)}) collective-permute-start(bf16[128,512]{1,0:T(8,128)(2,1)S(1)} %get-tuple-element.60.refs_16_), channel_id=1, source_target_pairs={{0,1},{1,0},{2,3},{3,2},{4,5},{5,4},{6,7},{7,6},{8,9},{9,8},{10,11... | collective-permute-start | bytes 393224 | tf_op jit(solution)/shard_map/ppermute | solution.py:315
  (36 other events, 128.5 us)

commit v9 on v8

--- a/solution.py
+++ b/solution.py
@@ -276,7 +276,7 @@
     c2 = q3[2] / beta0
     coefs = [(q3[0] - alpha0 * c1) / norm, (c1 - alpha0 * c2) / norm, c2 / norm, q3[3]]
     quarter = block_rows // 4
-    chunk = 32
+    chunk = 16
     for t in range(sectors):
         sector_refs = refs[10 * t : 10 * t + 10]
         for which in range(2):

time: 136 us -> 136 us (level)
  no operation moved by 1% of the time
where the time goes in v9:
time: 136 us
  starting transfers between devices  63.3 us (47%)
  waiting for transfers between devices  34 us (25%)
  Pallas kernels  32 us (24%)
  local copies, waits for them, and re-layouts  5.67 us (4%)
    pallas_call x19, Pallas kernels, call(): pl.pallas_call(kernel, name=name, out_shape=out, in_specs=[SMEM if a.dtyp...  31.5 us
    ppermute x3, starting transfers between devices, on_device(): far_0 = lax.ppermute(pair_0, 'sec', onward)  13.3 us
    ppermute x6, waiting for transfers between devices, on_device(): arrived = lax.ppermute(parts[-1], 'op', flips)  10.5 us
    ppermute x6, starting transfers between devices, sum_four(): lax.ppermute(stats, ('sec', 'op'), [(i, i ^ mask) for i in places])  8.76 us
    ppermute x3, starting transfers between devices, on_device(): pair_1 = lax.ppermute(mine_1, 'sec', pairs)  8.28 us
    ppermute x2, starting transfers between devices, on_device(): pair_0 = lax.ppermute(mine_0, 'sec', pairs)  7.03 us
    ppermute x4, starting transfers between devices, flipped_merge(): arrived = lax.ppermute(tile, axis, flips)  6.59 us
    ppermute x6, starting transfers between devices, on_device(): arrived = lax.ppermute(parts[-1], 'op', flips)  6.47 us
  transfers between devices with their start and end apart: 54, of which 27 were waited for; matrix products, arithmetic and copies ran while one was open for 0% of the time, Pallas kernels for 12%

profile of v9, /device:TPU:0, one launch (start us, length us, event | category | flops | bytes accessed | tf_op | source)
XLA Modules:
  0.0 135.9 jit_solution(18425817285296688939)
XLA Ops:
  4.0 3.0 %collective-permute-start.3 = (bf16[256,512]{1,0:T(8,128)(2,1)S(1)}, bf16[256,512]{1,0:T(8,128)(2,1)S(1)}, u32[]{:S(2)}, u32[]{:S(2)}) collective-permute-start(bf16[256,512]{1,0:T(8,128)(2,1)S(1)} %get-tuple-element.44.refs_6_.refs_0_), channel_id=1, source_target_pairs={{0,4},{4,0},{8,12},{12,8},{16,20},{20,16},{24,28},{28,24},{1,5},{5... | collective-permute-start | bytes 786440 | tf_op jit(solution)/shard_map/ppermute | solution.py:352
  6.9 2.2 %copy-done = bf16[4,2,512,512]{3,2,1,0:T(8,128)(2,1)S(1)} copy-done((bf16[4,2,512,512]{3,2,1,0:T(8,128)(2,1)S(1)}, bf16[4,2,512,512]{3,2,1,0:T(8,128)(2,1)}, u32[]{:S(2)}) %copy-start) | copy-done | bytes 4194328
  11.2 2.3 %collective-permute-done.3.refs_10_ = bf16[256,512]{1,0:T(8,128)(2,1)S(1)} collective-permute-done((bf16[256,512]{1,0:T(8,128)(2,1)S(1)}, bf16[256,512]{1,0:T(8,128)(2,1)S(1)}, u32[]{:S(2)}, u32[]{:S(2)}) %collective-permute-start.3) | collective-permute-done | bytes 262176 | tf_op jit(solution)/shard_map/ppermute | solution.py:352
  15.2 3.5 %collective-permute-start.6 = (bf16[256,512]{1,0:T(8,128)(2,1)S(1)}, bf16[256,512]{1,0:T(8,128)(2,1)S(1)}, u32[]{:S(2)}, u32[]{:S(2)}) collective-permute-start(bf16[256,512]{1,0:T(8,128)(2,1)S(1)} %collective-permute-done.3.refs_10_), channel_id=1, source_target_pairs={{0,8},{8,16},{16,24},{12,4},{20,12},{28,20},{1,9},{9,17},{17,25},{... | collective-permute-start | bytes 786440 | tf_op jit(solution)/shard_map/ppermute | solution.py:382
  26.8 3.7 %full.6.a_ref = bf16[256,512]{1,0:T(8,128)(2,1)S(1)} custom-call(s32[4]{0:T(128)S(1)} %copy-done.5, bf16[4,2,512,512]{3,2,1,0:T(8,128)(2,1)S(1)} %get-tuple-element.34.refs_1_, bf16[4,512,512]{2,1,0:T(8,128)(2,1)S(1)} %get-tuple-element.35.refs_2_, s32[4]{0:T(128)S(1)} %collective-permute-done.refs_3_, ...), custom_call_target="tpu_custom_call" | custom-call | tf_op jit(solution)/shard_map/full/pallas_call | solution.py:18
  32.1 3.7 %full.7.a_ref = bf16[256,512]{1,0:T(8,128)(2,1)S(1)} custom-call(s32[4]{0:T(128)S(1)} %copy-done.5, bf16[4,2,512,512]{3,2,1,0:T(8,128)(2,1)S(1)} %get-tuple-element.34.refs_1_, bf16[4,512,512]{2,1,0:T(8,128)(2,1)S(1)} %get-tuple-element.35.refs_2_, s32[4]{0:T(128)S(1)} %collective-permute-done.refs_3_, ...), custom_call_target="tpu_custom_call" | custom-call | tf_op jit(solution)/shard_map/full/pallas_call | solution.py:18
  36.3 3.2 %collective-permute-done.11.b_ref = bf16[256,512]{1,0:T(8,128)(2,1)S(1)} collective-permute-done((bf16[256,512]{1,0:T(8,128)(2,1)S(1)}, bf16[256,512]{1,0:T(8,128)(2,1)S(1)}, u32[]{:S(2)}, u32[]{:S(2)}) %collective-permute-start.11) | collective-permute-done | bytes 262176 | tf_op jit(solution)/shard_map/ppermute | solution.py:422
  40.1 3.9 %collective-permute-start.15 = (bf16[256,512]{1,0:T(8,128)(2,1)S(1)}, bf16[256,512]{1,0:T(8,128)(2,1)S(1)}, u32[]{:S(2)}, u32[]{:S(2)}) collective-permute-start(bf16[256,512]{1,0:T(8,128)(2,1)S(1)} %image.6.refs_1_.refs_6_.refs_2_), channel_id=1, source_target_pairs={{0,4},{4,0},{8,12},{12,8},{16,20},{20,16},{24,28},{28,24},{1,5},{5... | collective-permute-start | bytes 786440 | tf_op jit(solution)/shard_map/ppermute | solution.py:373
  45.2 3.9 %collective-permute-start.17 = (bf16[256,512]{1,0:T(8,128)(2,1)S(1)}, bf16[256,512]{1,0:T(8,128)(2,1)S(1)}, u32[]{:S(2)}, u32[]{:S(2)}) collective-permute-start(bf16[256,512]{1,0:T(8,128)(2,1)S(1)} %image.7.refs_3_.refs_8_.refs_1_.refs_12_), channel_id=1, source_target_pairs={{0,4},{4,0},{8,12},{12,8},{16,20},{20,16},{24,28},{28,24},{1,5},{5... | collective-permute-start | bytes 786440 | tf_op jit(solution)/shard_map/ppermute | solution.py:381
  49.8 4.7 %collective-permute-start.18 = (bf16[256,512]{1,0:T(8,128)(2,1)S(1)}, bf16[256,512]{1,0:T(8,128)(2,1)S(1)}, u32[]{:S(2)}, u32[]{:S(2)}) collective-permute-start(bf16[256,512]{1,0:T(8,128)(2,1)S(1)} %collective-permute-done.15.refs_10_), channel_id=1, source_target_pairs={{0,8},{8,16},{16,24},{12,4},{20,12},{28,20},{1,9},{9,17},{17,25},{... | collective-permute-start | bytes 786440 | tf_op jit(solution)/shard_map/ppermute | solution.py:382
  57.6 2.9 %collective-permute-done.20.arrived_ref = f32[24,128]{1,0:T(8,128)S(1)} collective-permute-done((f32[24,128]{1,0:T(8,128)S(1)}, f32[24,128]{1,0:T(8,128)S(1)}, u32[]{:S(2)}, u32[]{:S(2)}) %collective-permute-start.20) | collective-permute-done | bytes 12320 | tf_op jit(solution)/shard_map/ppermute | solution.py:325
  63.5 3.7 %full.8.a_ref = bf16[256,512]{1,0:T(8,128)(2,1)S(1)} custom-call(s32[4]{0:T(128)S(1)} %copy-done.5, bf16[4,2,512,512]{3,2,1,0:T(8,128)(2,1)S(1)} %get-tuple-element.34.refs_1_, bf16[4,512,512]{2,1,0:T(8,128)(2,1)S(1)} %get-tuple-element.35.refs_2_, s32[4]{0:T(128)S(1)} %collective-permute-done.refs_3_, ...), custom_call_target="tpu_custom_call" | custom-call | tf_op jit(solution)/shard_map/full/pallas_call | solution.py:18
  68.8 3.7 %full.9.a_ref = bf16[256,512]{1,0:T(8,128)(2,1)S(1)} custom-call(s32[4]{0:T(128)S(1)} %copy-done.5, bf16[4,2,512,512]{3,2,1,0:T(8,128)(2,1)S(1)} %get-tuple-element.34.refs_1_, bf16[4,512,512]{2,1,0:T(8,128)(2,1)S(1)} %get-tuple-element.35.refs_2_, s32[4]{0:T(128)S(1)} %collective-permute-done.refs_3_, ...), custom_call_target="tpu_custom_call" | custom-call | tf_op jit(solution)/shard_map/full/pallas_call | solution.py:18
  73.0 3.2 %collective-permute-done.25.b_ref = bf16[256,512]{1,0:T(8,128)(2,1)S(1)} collective-permute-done((bf16[256,512]{1,0:T(8,128)(2,1)S(1)}, bf16[256,512]{1,0:T(8,128)(2,1)S(1)}, u32[]{:S(2)}, u32[]{:S(2)}) %collective-permute-start.25) | collective-permute-done | bytes 262176 | tf_op jit(solution)/shard_map/ppermute | solution.py:422
  76.9 3.1 %collective-permute-start.29 = (bf16[256,512]{1,0:T(8,128)(2,1)S(1)}, bf16[256,512]{1,0:T(8,128)(2,1)S(1)}, u32[]{:S(2)}, u32[]{:S(2)}) collective-permute-start(bf16[256,512]{1,0:T(8,128)(2,1)S(1)} %image.8.refs_6_.refs_2_.refs_4_), channel_id=1, source_target_pairs={{0,4},{4,0},{8,12},{12,8},{16,20},{20,16},{24,28},{28,24},{1,5},{5... | collective-permute-start | bytes 786440 | tf_op jit(solution)/shard_map/ppermute | solution.py:373
  82.2 2.6 %collective-permute-start.32 = (bf16[256,512]{1,0:T(8,128)(2,1)S(1)}, bf16[256,512]{1,0:T(8,128)(2,1)S(1)}, u32[]{:S(2)}, u32[]{:S(2)}) collective-permute-start(bf16[256,512]{1,0:T(8,128)(2,1)S(1)} %image.9.refs_8_.refs_2_.refs_14_), channel_id=1, source_target_pairs={{0,4},{4,0},{8,12},{12,8},{16,20},{20,16},{24,28},{28,24},{1,5},{5... | collective-permute-start | bytes 786440 | tf_op jit(solution)/shard_map/ppermute | solution.py:381
  85.5 5.1 %collective-permute-start.33 = (bf16[256,512]{1,0:T(8,128)(2,1)S(1)}, bf16[256,512]{1,0:T(8,128)(2,1)S(1)}, u32[]{:S(2)}, u32[]{:S(2)}) collective-permute-start(bf16[256,512]{1,0:T(8,128)(2,1)S(1)} %collective-permute-done.29.refs_10_), channel_id=1, source_target_pairs={{0,8},{8,16},{16,24},{12,4},{20,12},{28,20},{1,9},{9,17},{17,25},{... | collective-permute-start | bytes 786440 | tf_op jit(solution)/shard_map/ppermute | solution.py:382
  90.7 3.6 %collective-permute-start.34 = (f32[24,128]{1,0:T(8,128)S(1)}, f32[24,128]{1,0:T(8,128)S(1)}, u32[]{:S(2)}, u32[]{:S(2)}) collective-permute-start(f32[24,128]{1,0:T(8,128)S(1)} %merge.6.own_ref), channel_id=1, source_target_pairs={{0,16},{4,20},{8,24},{12,28},{16,0},{20,4},{24,8},{28,12},{1,17},{... | collective-permute-start | bytes 36872 | tf_op jit(solution)/shard_map/ppermute | solution.py:325
  99.2 3.9 %full.10 = (bf16[128,512]{1,0:T(8,128)(2,1)S(1)}, bf16[128,512]{1,0:T(8,128)(2,1)S(1)}) custom-call(s32[4]{0:T(128)S(1)} %copy-done.5, bf16[4,2,512,512]{3,2,1,0:T(8,128)(2,1)S(1)} %get-tuple-element.34.refs_1_, bf16[4,512,512]{2,1,0:T(8,128)(2,1)S(1)} %get-tuple-element.35.refs_2_, s32[4]{0:T(128)S(1)} %collective-permute-done.refs_3_, ...), custom_call_target="tpu_custom_call" | custom-call | tf_op jit(solution)/shard_map/full/pallas_call | solution.py:18
  104.4 3.9 %full.11 = (bf16[128,512]{1,0:T(8,128)(2,1)S(1)}, bf16[128,512]{1,0:T(8,128)(2,1)S(1)}) custom-call(s32[4]{0:T(128)S(1)} %copy-done.5, bf16[4,2,512,512]{3,2,1,0:T(8,128)(2,1)S(1)} %get-tuple-element.34.refs_1_, bf16[4,512,512]{2,1,0:T(8,128)(2,1)S(1)} %get-tuple-element.35.refs_2_, s32[4]{0:T(128)S(1)} %collective-permute-done.refs_3_, ...), custom_call_target="tpu_custom_call" | custom-call | tf_op jit(solution)/shard_map/full/pallas_call | solution.py:18
  110.1 3.6 %collective-permute-done.43.b_ref = bf16[128,512]{1,0:T(8,128)(2,1)S(1)} collective-permute-done((bf16[128,512]{1,0:T(8,128)(2,1)S(1)}, bf16[128,512]{1,0:T(8,128)(2,1)S(1)}, u32[]{:S(2)}, u32[]{:S(2)}) %collective-permute-start.43) | collective-permute-done | bytes 131104 | tf_op jit(solution)/shard_map/ppermute | solution.py:422
  119.3 4.8 %collective-permute-start.50 = (f32[8,128]{1,0:T(8,128)S(1)}, f32[8,128]{1,0:T(8,128)S(1)}, u32[]{:S(2)}, u32[]{:S(2)}) collective-permute-start(f32[8,128]{1,0:T(8,128)S(1)} %add_add_fusion.1), channel_id=1, source_target_pairs={{0,12},{1,13},{2,14},{3,15},{4,8},{5,9},{6,10},{7,11},{8,4},{9,5},... | collective-permute-start | bytes 12296 | tf_op jit(solution)/shard_map/ppermute | solution.py:334
  129.8 3.1 %collective-permute-done.53 = f32[8,128]{1,0:T(8,128)S(1)} collective-permute-done((f32[8,128]{1,0:T(8,128)S(1)}, f32[8,128]{1,0:T(8,128)S(1)}, u32[]{:S(2)}, u32[]{:S(2)}) %collective-permute-start.53) | collective-permute-done | bytes 4128 | tf_op jit(solution)/shard_map/ppermute | solution.py:319
  132.9 3.0 %last.1 = (bf16[2,512,512]{2,1,0:T(8,128)(2,1)}, f32[2,3]{1,0:T(2,128)}) custom-call(s32[16]{0:T(128)S(1)} %copy-done.4, bf16[256,512]{1,0:T(8,128)(2,1)S(1)} %get-tuple-element.44.refs_6_.refs_0_, bf16[256,512]{1,0:T(8,128)(2,1)S(1)} %get-tuple-element.33.refs_7_.refs_1_, bf16[256,512]{1,0:T(8,128)(2,1)S(1)} %image.6.refs_1_.refs_6_.refs_2_, ...), custom_call_target="tpu_custom_call" | custom-call | tf_op jit(solution)/shard_map/last/pallas_call | solution.py:18
  (119 shorter events, 50.8 us)
Async XLA Ops:
  0.6 26.2 %collective-permute-start.1 = (bf16[4,2,512,512]{3,2,1,0:T(8,128)(2,1)}, bf16[4,2,512,512]{3,2,1,0:T(8,128)(2,1)S(1)}, u32[]{:S(2)}, u32[]{:S(2)}) collective-permute-start(bf16[4,2,512,512]{3,2,1,0:T(8,128)(2,1)} %left_ref.1), channel_id=1, source_target_pairs={{0,1},{1,0},{2,3},{3,2},{4,5},{5,4},{6,7},{7,6},{8,9},{9,8},{10,11... | collective-permute-start | bytes 12582920 | tf_op jit(solution)/shard_map/ppermute | solution.py:315
  1.1 25.6 %collective-permute-start.2 = (bf16[4,512,512]{2,1,0:T(8,128)(2,1)}, bf16[4,512,512]{2,1,0:T(8,128)(2,1)S(1)}, u32[]{:S(2)}, u32[]{:S(2)}) collective-permute-start(bf16[4,512,512]{2,1,0:T(8,128)(2,1)} %right_ref.1), channel_id=1, source_target_pairs={{0,1},{1,0},{2,3},{3,2},{4,5},{5,4},{6,7},{7,6},{8,9},{9,8},{10,11... | collective-permute-start | bytes 6291464 | tf_op jit(solution)/shard_map/ppermute | solution.py:315
  4.0 9.5 %collective-permute-start.3 = (bf16[256,512]{1,0:T(8,128)(2,1)S(1)}, bf16[256,512]{1,0:T(8,128)(2,1)S(1)}, u32[]{:S(2)}, u32[]{:S(2)}) collective-permute-start(bf16[256,512]{1,0:T(8,128)(2,1)S(1)} %get-tuple-element.44.refs_6_.refs_0_), channel_id=1, source_target_pairs={{0,4},{4,0},{8,12},{12,8},{16,20},{20,16},{24,28},{28,24},{1,5},{5... | collective-permute-start | bytes 786440 | tf_op jit(solution)/shard_map/ppermute | solution.py:352
  13.5 7.8 %collective-permute-start.5 = (bf16[256,512]{1,0:T(8,128)(2,1)S(1)}, bf16[256,512]{1,0:T(8,128)(2,1)S(1)}, u32[]{:S(2)}, u32[]{:S(2)}) collective-permute-start(bf16[256,512]{1,0:T(8,128)(2,1)S(1)} %get-tuple-element.38.refs_8_.refs_2_.refs_0_.refs_10_), channel_id=1, source_target_pairs={{0,4},{4,0},{8,12},{12,8},{16,20},{20,16},{24,28},{28,24},{1,5},{5... | collective-permute-start | bytes 786440 | tf_op jit(solution)/shard_map/ppermute | solution.py:381
  15.2 8.1 %collective-permute-start.6 = (bf16[256,512]{1,0:T(8,128)(2,1)S(1)}, bf16[256,512]{1,0:T(8,128)(2,1)S(1)}, u32[]{:S(2)}, u32[]{:S(2)}) collective-permute-start(bf16[256,512]{1,0:T(8,128)(2,1)S(1)} %collective-permute-done.3.refs_10_), channel_id=1, source_target_pairs={{0,8},{8,16},{16,24},{12,4},{20,12},{28,20},{1,9},{9,17},{17,25},{... | collective-permute-start | bytes 786440 | tf_op jit(solution)/shard_map/ppermute | solution.py:382
  30.5 9.0 %collective-permute-start.11 = (bf16[256,512]{1,0:T(8,128)(2,1)S(1)}, bf16[256,512]{1,0:T(8,128)(2,1)S(1)}, u32[]{:S(2)}, u32[]{:S(2)}) collective-permute-start(bf16[256,512]{1,0:T(8,128)(2,1)S(1)} %full.6.a_ref), channel_id=1, source_target_pairs={{0,2},{1,3},{2,0},{3,1},{4,6},{5,7},{6,4},{7,5},{8,10},{9,11},{10,... | collective-permute-start | bytes 786440 | tf_op jit(solution)/shard_map/ppermute | solution.py:422
  35.8 8.8 %collective-permute-start.13 = (bf16[256,512]{1,0:T(8,128)(2,1)S(1)}, bf16[256,512]{1,0:T(8,128)(2,1)S(1)}, u32[]{:S(2)}, u32[]{:S(2)}) collective-permute-start(bf16[256,512]{1,0:T(8,128)(2,1)S(1)} %full.7.a_ref), channel_id=1, source_target_pairs={{0,2},{1,3},{2,0},{3,1},{4,6},{5,7},{6,4},{7,5},{8,10},{9,11},{10,... | collective-permute-start | bytes 786440 | tf_op jit(solution)/shard_map/ppermute | solution.py:422
  40.1 9.7 %collective-permute-start.15 = (bf16[256,512]{1,0:T(8,128)(2,1)S(1)}, bf16[256,512]{1,0:T(8,128)(2,1)S(1)}, u32[]{:S(2)}, u32[]{:S(2)}) collective-permute-start(bf16[256,512]{1,0:T(8,128)(2,1)S(1)} %image.6.refs_1_.refs_6_.refs_2_), channel_id=1, source_target_pairs={{0,4},{4,0},{8,12},{12,8},{16,20},{20,16},{24,28},{28,24},{1,5},{5... | collective-permute-start | bytes 786440 | tf_op jit(solution)/shard_map/ppermute | solution.py:373
  45.2 15.3 %collective-permute-start.17 = (bf16[256,512]{1,0:T(8,128)(2,1)S(1)}, bf16[256,512]{1,0:T(8,128)(2,1)S(1)}, u32[]{:S(2)}, u32[]{:S(2)}) collective-permute-start(bf16[256,512]{1,0:T(8,128)(2,1)S(1)} %image.7.refs_3_.refs_8_.refs_1_.refs_12_), channel_id=1, source_target_pairs={{0,4},{4,0},{8,12},{12,8},{16,20},{20,16},{24,28},{28,24},{1,5},{5... | collective-permute-start | bytes 786440 | tf_op jit(solution)/shard_map/ppermute | solution.py:381
  49.1 11.9 %collective-permute-start.23 = (bf16[256,512]{1,0:T(8,128)(2,1)S(1)}, bf16[256,512]{1,0:T(8,128)(2,1)S(1)}, u32[]{:S(2)}, u32[]{:S(2)}) collective-permute-start(bf16[256,512]{1,0:T(8,128)(2,1)S(1)} %image.7.refs_3_.refs_8_.refs_1_.refs_12_), channel_id=1, source_target_pairs={{4,8},{12,16},{20,24},{8,4},{16,12},{24,20},{5,9},{13,17},{21,25},... | collective-permute-start | bytes 786440 | tf_op jit(solution)/shard_map/ppermute | solution.py:383
  49.8 11.3 %collective-permute-start.18 = (bf16[256,512]{1,0:T(8,128)(2,1)S(1)}, bf16[256,512]{1,0:T(8,128)(2,1)S(1)}, u32[]{:S(2)}, u32[]{:S(2)}) collective-permute-start(bf16[256,512]{1,0:T(8,128)(2,1)S(1)} %collective-permute-done.15.refs_10_), channel_id=1, source_target_pairs={{0,8},{8,16},{16,24},{12,4},{20,12},{28,20},{1,9},{9,17},{17,25},{... | collective-permute-start | bytes 786440 | tf_op jit(solution)/shard_map/ppermute | solution.py:382
  54.6 7.0 %collective-permute-start.14 = (bf16[256,512]{1,0:T(8,128)(2,1)S(1)}, bf16[256,512]{1,0:T(8,128)(2,1)S(1)}, u32[]{:S(2)}, u32[]{:S(2)}) collective-permute-start(bf16[256,512]{1,0:T(8,128)(2,1)S(1)} %image.7.refs_3_.refs_8_.refs_1_.refs_12_), channel_id=1, source_target_pairs={{0,1},{1,0},{2,3},{3,2},{4,5},{5,4},{6,7},{7,6},{8,9},{9,8},{10,11... | collective-permute-start | bytes 786440 | tf_op jit(solution)/shard_map/ppermute | solution.py:315
  67.2 9.0 %collective-permute-start.25 = (bf16[256,512]{1,0:T(8,128)(2,1)S(1)}, bf16[256,512]{1,0:T(8,128)(2,1)S(1)}, u32[]{:S(2)}, u32[]{:S(2)}) collective-permute-start(bf16[256,512]{1,0:T(8,128)(2,1)S(1)} %full.8.a_ref), channel_id=1, source_target_pairs={{0,2},{1,3},{2,0},{3,1},{4,6},{5,7},{6,4},{7,5},{8,10},{9,11},{10,... | collective-permute-start | bytes 786440 | tf_op jit(solution)/shard_map/ppermute | solution.py:422
  72.5 9.1 %collective-permute-start.27 = (bf16[256,512]{1,0:T(8,128)(2,1)S(1)}, bf16[256,512]{1,0:T(8,128)(2,1)S(1)}, u32[]{:S(2)}, u32[]{:S(2)}) collective-permute-start(bf16[256,512]{1,0:T(8,128)(2,1)S(1)} %full.9.a_ref), channel_id=1, source_target_pairs={{0,2},{1,3},{2,0},{3,1},{4,6},{5,7},{6,4},{7,5},{8,10},{9,11},{10,... | collective-permute-start | bytes 786440 | tf_op jit(solution)/shard_map/ppermute | solution.py:422
  76.9 8.6 %collective-permute-start.29 = (bf16[256,512]{1,0:T(8,128)(2,1)S(1)}, bf16[256,512]{1,0:T(8,128)(2,1)S(1)}, u32[]{:S(2)}, u32[]{:S(2)}) collective-permute-start(bf16[256,512]{1,0:T(8,128)(2,1)S(1)} %image.8.refs_6_.refs_2_.refs_4_), channel_id=1, source_target_pairs={{0,4},{4,0},{8,12},{12,8},{16,20},{20,16},{24,28},{28,24},{1,5},{5... | collective-permute-start | bytes 786440 | tf_op jit(solution)/shard_map/ppermute | solution.py:373
  82.2 14.0 %collective-permute-start.32 = (bf16[256,512]{1,0:T(8,128)(2,1)S(1)}, bf16[256,512]{1,0:T(8,128)(2,1)S(1)}, u32[]{:S(2)}, u32[]{:S(2)}) collective-permute-start(bf16[256,512]{1,0:T(8,128)(2,1)S(1)} %image.9.refs_8_.refs_2_.refs_14_), channel_id=1, source_target_pairs={{0,4},{4,0},{8,12},{12,8},{16,20},{20,16},{24,28},{28,24},{1,5},{5... | collective-permute-start | bytes 786440 | tf_op jit(solution)/shard_map/ppermute | solution.py:381
  84.8 12.0 %collective-permute-start.37 = (bf16[256,512]{1,0:T(8,128)(2,1)S(1)}, bf16[256,512]{1,0:T(8,128)(2,1)S(1)}, u32[]{:S(2)}, u32[]{:S(2)}) collective-permute-start(bf16[256,512]{1,0:T(8,128)(2,1)S(1)} %image.9.refs_8_.refs_2_.refs_14_), channel_id=1, source_target_pairs={{4,8},{12,16},{20,24},{8,4},{16,12},{24,20},{5,9},{13,17},{21,25},... | collective-permute-start | bytes 786440 | tf_op jit(solution)/shard_map/ppermute | solution.py:383
  85.5 11.3 %collective-permute-start.33 = (bf16[256,512]{1,0:T(8,128)(2,1)S(1)}, bf16[256,512]{1,0:T(8,128)(2,1)S(1)}, u32[]{:S(2)}, u32[]{:S(2)}) collective-permute-start(bf16[256,512]{1,0:T(8,128)(2,1)S(1)} %collective-permute-done.29.refs_10_), channel_id=1, source_target_pairs={{0,8},{8,16},{16,24},{12,4},{20,12},{28,20},{1,9},{9,17},{17,25},{... | collective-permute-start | bytes 786440 | tf_op jit(solution)/shard_map/ppermute | solution.py:382
  90.6 6.7 %collective-permute-start.28 = (bf16[256,512]{1,0:T(8,128)(2,1)S(1)}, bf16[256,512]{1,0:T(8,128)(2,1)S(1)}, u32[]{:S(2)}, u32[]{:S(2)}) collective-permute-start(bf16[256,512]{1,0:T(8,128)(2,1)S(1)} %image.9.refs_8_.refs_2_.refs_14_), channel_id=1, source_target_pairs={{0,1},{1,0},{2,3},{3,2},{4,5},{5,4},{6,7},{7,6},{8,9},{9,8},{10,11... | collective-permute-start | bytes 786440 | tf_op jit(solution)/shard_map/ppermute | solution.py:315
  103.1 6.0 %collective-permute-start.39 = (bf16[128,512]{1,0:T(8,128)(2,1)S(1)}, bf16[128,512]{1,0:T(8,128)(2,1)S(1)}, u32[]{:S(2)}, u32[]{:S(2)}) collective-permute-start(bf16[128,512]{1,0:T(8,128)(2,1)S(1)} %get-tuple-element.54), channel_id=1, source_target_pairs={{0,2},{1,3},{2,0},{3,1},{4,6},{5,7},{6,4},{7,5},{8,10},{9,11},{10,... | collective-permute-start | bytes 393224 | tf_op jit(solution)/shard_map/ppermute | solution.py:422
  116.9 10.8 %collective-permute-start.45 = (bf16[128,512]{1,0:T(8,128)(2,1)S(1)}, bf16[128,512]{1,0:T(8,128)(2,1)S(1)}, u32[]{:S(2)}, u32[]{:S(2)}) collective-permute-start(bf16[128,512]{1,0:T(8,128)(2,1)S(1)} %get-tuple-element.60.refs_16_), channel_id=1, source_target_pairs={{0,2},{1,3},{2,0},{3,1},{4,6},{5,7},{6,4},{7,5},{8,10},{9,11},{10,... | collective-permute-start | bytes 393224 | tf_op jit(solution)/shard_map/ppermute | solution.py:434
  117.7 10.5 %collective-permute-start.41 = (bf16[128,512]{1,0:T(8,128)(2,1)S(1)}, bf16[128,512]{1,0:T(8,128)(2,1)S(1)}, u32[]{:S(2)}, u32[]{:S(2)}) collective-permute-start(bf16[128,512]{1,0:T(8,128)(2,1)S(1)} %get-tuple-element.57.refs_6_), channel_id=1, source_target_pairs={{0,2},{1,3},{2,0},{3,1},{4,6},{5,7},{6,4},{7,5},{8,10},{9,11},{10,... | collective-permute-start | bytes 393224 | tf_op jit(solution)/shard_map/ppermute | solution.py:434
  119.3 6.6 %collective-permute-start.50 = (f32[8,128]{1,0:T(8,128)S(1)}, f32[8,128]{1,0:T(8,128)S(1)}, u32[]{:S(2)}, u32[]{:S(2)}) collective-permute-start(f32[8,128]{1,0:T(8,128)S(1)} %add_add_fusion.1), channel_id=1, source_target_pairs={{0,12},{1,13},{2,14},{3,15},{4,8},{5,9},{6,10},{7,11},{8,4},{9,5},... | collective-permute-start | bytes 12296 | tf_op jit(solution)/shard_map/ppermute | solution.py:334
  125.8 7.0 %collective-permute-start.44 = (bf16[128,512]{1,0:T(8,128)(2,1)S(1)}, bf16[128,512]{1,0:T(8,128)(2,1)S(1)}, u32[]{:S(2)}, u32[]{:S(2)}) collective-permute-start(bf16[128,512]{1,0:T(8,128)(2,1)S(1)} %get-tuple-element.60.refs_16_), channel_id=1, source_target_pairs={{0,1},{1,0},{2,3},{3,2},{4,5},{5,4},{6,7},{7,6},{8,9},{9,8},{10,11... | collective-permute-start | bytes 393224 | tf_op jit(solution)/shard_map/ppermute | solution.py:315
  (36 other events, 128.5 us)
